TPU v7x, 32 devices: a whole 2x2x4 slice. The times are simulated.
32 devices in a mesh: tok: 4 (over z), row: 2 (over x), col: 4 (over y, core).
Axes of the slice: x: 2, y: 2, z: 4, core: 2. Of those that a mesh axis runs over, the one named last changes fastest.
Arguments:
- tokens: bfloat16 [512, 8192], P('tok', 'row'), may hold values from -6 to 6
- w1_blocks: bfloat16 [2, 4, 8, 128, 128], P('row', 'col'), may hold values from -0.5 to 0.5
- w1_rows: int32 [2, 4, 8], P('row', 'col'), may hold values from 0 to 31
- w1_cols: int32 [2, 4, 8], P('row', 'col'), may hold values from 0 to 63
- w2_blocks: bfloat16 [2, 4, 8, 128, 128], P('row', 'col'), may hold values from -0.5 to 0.5
- w2_hidden: int32 [2, 4, 8], P('row', 'col'), may hold values from 0 to 63
- w2_outs: int32 [2, 4, 8], P('row', 'col'), may hold values from 0 to 31
- grad_out: bfloat16 [512, 8192], P('tok', 'row'), may hold values from -6 to 6
Outputs:
- output: bfloat16 [512, 8192], P(('tok', 'col'), 'row')
- grad_in: bfloat16 [512, 8192], P(('tok', 'col'), 'row')
- grad_w1: float32 [2, 4, 8, 128, 128], P('row', 'col', None, 'tok')
- grad_w2: float32 [2, 4, 8, 128, 128], P('row', 'col', None, 'tok')
All inputs are finite; a program needn't handle non-finite values.
Results may differ from a plain program's by a relative error of at most 0.0049.
Values may be sent and summed in bfloat16 or wider, within the bound.
No kernel may reach another device: no remote copies, remote signals or barrier semaphores. Data moves between devices by JAX's collectives and lax.ppermute only.
A program may use at most 64 MiB of HBM per device.

v0:
```python
import jax
import jax.numpy as jnp
from jax import lax
from jax.sharding import PartitionSpec as P

FF = 32768


highest = lax.Precision.HIGHEST


def gelu_value(value):
    return value * (0.5 * (1.0 + jax.scipy.special.erf(value / jnp.sqrt(2.0))))


def gelu_slope(value):
    cdf_part = 0.5 * (1.0 + jax.scipy.special.erf(value / jnp.sqrt(2.0)))
    return cdf_part + value * jnp.exp(-0.5 * value * value) / jnp.sqrt(2.0 * jnp.pi)


def select_blocks(source, indices, count):
    block = source.shape[1] // count
    onehot = (indices[:, None] == jnp.arange(count, dtype=jnp.int32)[None, :]).astype(jnp.bfloat16)
    shaped = source.reshape(source.shape[0], count, block)
    taken = jnp.einsum("kr,trb->ktb", onehot, shaped, preferred_element_type=jnp.float32)
    return taken.astype(jnp.bfloat16)


def place_blocks(product, indices, count):
    onehot = (indices[:, None] == jnp.arange(count, dtype=jnp.int32)[None, :]).astype(jnp.float32)
    placed = jnp.einsum("kc,ktj->tcj", onehot, product, precision=highest)
    return placed.reshape(product.shape[1], count * product.shape[2])


def apply_blocks(taken, weights, index_out, count_out, flip):
    form = "ktb,kjb->ktj" if flip else "ktb,kbj->ktj"
    product = jnp.einsum(form, taken, weights, preferred_element_type=jnp.float32)
    return place_blocks(product, index_out, count_out)


def shards(tokens, w1_blocks, w1_rows, w1_cols, w2_blocks, w2_hidden, w2_outs, grad_out):
    slots = w1_blocks.shape[2]
    block = w1_blocks.shape[-1]
    row_blocks = tokens.shape[1] // block
    col_blocks = FF // lax.axis_size("col") // block
    first = w1_blocks.reshape(slots, block, block)
    second = w2_blocks.reshape(slots, block, block)
    first_rows = w1_rows.reshape(slots)
    first_cols = w1_cols.reshape(slots)
    second_hidden = w2_hidden.reshape(slots)
    second_outs = w2_outs.reshape(slots)
    token_taken = select_blocks(tokens, first_rows, row_blocks)
    partial_value = apply_blocks(token_taken, first, first_cols, col_blocks, False)
    hidden_part = lax.psum_scatter(partial_value, "row", scatter_dimension=0, tiled=True)
    active = lax.all_gather(gelu_value(hidden_part).astype(jnp.bfloat16), "row", axis=0, tiled=True)
    active_taken = select_blocks(active, second_hidden, col_blocks)
    out_part = apply_blocks(active_taken, second, second_outs, row_blocks, False)
    output = lax.psum_scatter(out_part, "col", scatter_dimension=0, tiled=True).astype(jnp.bfloat16)
    cotangent_taken = select_blocks(grad_out, second_outs, row_blocks)
    back_part = apply_blocks(cotangent_taken, second, second_hidden, col_blocks, True)
    back_part_sum = lax.psum_scatter(back_part, "row", scatter_dimension=0, tiled=True)
    grad_part = (back_part_sum * gelu_slope(hidden_part)).astype(jnp.bfloat16)
    grad_hidden = lax.all_gather(grad_part, "row", axis=0, tiled=True)
    grad_taken = select_blocks(grad_hidden, first_cols, col_blocks)
    input_part = apply_blocks(grad_taken, first, first_rows, row_blocks, True)
    grad_in = lax.psum_scatter(input_part, "col", scatter_dimension=0, tiled=True).astype(
        jnp.bfloat16
    )
    first_grad = jnp.einsum(
        "ktb,ktj->kbj", token_taken, grad_taken, preferred_element_type=jnp.float32
    )
    second_grad = jnp.einsum(
        "ktb,ktj->kbj", active_taken, cotangent_taken, preferred_element_type=jnp.float32
    )
    summed = (
        lax.psum_scatter(
            first_grad.reshape(1, 1, slots, block, block), "tok", scatter_dimension=3, tiled=True
        ),
        lax.psum_scatter(
            second_grad.reshape(1, 1, slots, block, block), "tok", scatter_dimension=3, tiled=True
        ),
    )
    return (output, grad_in, summed[0], summed[1])


def solution(mesh):
    placed = (
        P("tok", "row"),
        P("row", "col", None, None, None),
        P("row", "col", None),
        P("row", "col", None),
        P("row", "col", None, None, None),
        P("row", "col", None),
        P("row", "col", None),
        P("tok", "row"),
    )
    return jax.shard_map(
        shards,
        mesh=mesh,
        in_specs=placed,
        out_specs=(
            P(("tok", "col"), "row"),
            P(("tok", "col"), "row"),
            P("row", "col", None, "tok", None),
            P("row", "col", None, "tok", None),
        ),
        check_vma=False,
    )
```

profile of v0, /device:TPU:0, one launch (start us, length us, event | category | flops | bytes accessed | tf_op | source)
XLA Modules:
  0.0 323.9 jit_solution(11852339798552320495)
XLA Ops:
  7.2 0.0 reduce-scatter.11.cloned.1.call-start
  7.3 1.5 copy.26
  8.8 0.3 convolution_convert_fusion.1
  9.1 0.3 fusion.14
  9.4 1.9 fusion.8
  11.3 5.2 %copy.50 = f32[16,8,64,128]{3,1,2,0:T(8,128)} copy(f32[16,8,64,128]{3,2,1,0:T(8,128)S(1)} %bitcast.72) | data formatting | bytes 8388608
  16.6 0.0 reduce-scatter.11.cloned.1.call-update
  16.6 0.2 reduce-scatter.7.cloned.1.call-start
  16.8 1.0 copy-done.1
  17.8 0.2 copy.22
  18.0 0.3 convolution_convert_fusion.3
  18.4 0.2 copy.12
  18.6 0.3 fusion.20
  18.9 1.9 fusion.12
  20.8 5.4 %copy.51 = f32[16,8,64,128]{3,1,2,0:T(8,128)} copy(f32[16,8,64,128]{3,2,1,0:T(8,128)S(1)} %bitcast.73) | data formatting | bytes 8388608
  26.2 0.0 all-gather.5.cloned.1.call-start
  26.3 47.4 %reduce-scatter.11.cloned.1.call-done = f32[64,8192]{1,0:T(8,128)} async-done(((f32[128,8192]{1,0:T(8,128)}), f32[64,8192]{1,0:T(8,128)}) %reduce-scatter.11.cloned.1.call-update) | async-done | bytes 2097168 | tf_op jit(solution)/shard_map/reduce_scatter | solution.py:61
  73.7 56.7 %reduce-scatter.7.cloned.1.call-done = f32[64,8192]{1,0:T(8,128)} async-done(((f32[128,8192]{1,0:T(8,128)}), f32[64,8192]{1,0:T(8,128)}) %reduce-scatter.7.cloned.1.call-update) | async-done | bytes 2097168 | tf_op jit(solution)/shard_map/reduce_scatter | solution.py:54
  130.5 3.6 %fusion.5 = (bf16[64,8192]{1,0:T(8,128)(2,1)}, bf16[64,8192]{1,0:T(8,128)(2,1)}) fusion(f32[64,8192]{1,0:T(8,128)} %reduce-scatter.11.cloned.1.call-done, f32[64,8192]{1,0:T(8,128)} %reduce-scatter.7.cloned.1.call-done), kind=kLoop, calls=%fused_computation.8 | loop fusion | flops 6291456 | bytes 6291456 | tf_op jit(solution)/shard_map/convert_element_type | solution.py:62
  134.1 0.0 all-gather.5.cloned.1.call-update
  134.1 0.0 all-gather.3.cloned.1.call-start
  134.2 0.5 all-gather.3.cloned.1.call-update
  134.7 0.0 reduce-scatter.13.cloned.1.call-start
  134.7 32.7 %all-gather.5.cloned.1.call-done = bf16[128,8192]{1,0:T(8,128)(2,1)} async-done(((bf16[64,8192]{1,0:T(8,128)(2,1)}), bf16[128,8192]{1,0:T(8,128)(2,1)}) %all-gather.5.cloned.1.call-update) | async-done | bytes 2097168 | tf_op jit(solution)/shard_map/all_gather | solution.py:63
  167.4 2.2 copy.28
  169.6 0.4 convolution_convert_fusion
  170.0 0.3 fusion.18
  170.3 1.1 fusion.6
  171.5 3.0 copy.52
  174.5 0.3 reduce-scatter.9.cloned.1.call-start
  174.7 27.2 %all-gather.3.cloned.1.call-done = bf16[128,8192]{1,0:T(8,128)(2,1)} async-done(((bf16[64,8192]{1,0:T(8,128)(2,1)}), bf16[128,8192]{1,0:T(8,128)(2,1)}) %all-gather.3.cloned.1.call-update) | async-done | bytes 2097168 | tf_op jit(solution)/shard_map/all_gather | solution.py:55
  201.9 2.2 copy.24
  204.1 0.4 convolution_convert_fusion.2
  204.6 0.2 copy.14
  204.8 0.3 fusion.16
  205.1 1.1 fusion.10
  206.2 3.0 copy.53
  209.2 0.0 reduce-scatter.9.cloned.1.call-update
  209.2 0.0 reduce-scatter.17.cloned.1.call-start
  209.3 1.0 convolution_bitcast_fusion
  210.3 0.0 reduce-scatter.15.cloned.1.call-start
  210.4 1.0 convolution_bitcast_fusion.1
  211.4 24.4 %reduce-scatter.13.cloned.1.call-done = f32[32,4096]{1,0:T(8,128)} async-done(((f32[128,4096]{1,0:T(8,128)}), f32[32,4096]{1,0:T(8,128)}) %reduce-scatter.13.cloned.1.call-update) | async-done | bytes 524304 | tf_op jit(solution)/shard_map/reduce_scatter | solution.py:66
  235.8 1.8 convert_element_type.39
  237.6 32.2 %reduce-scatter.9.cloned.1.call-done = f32[32,4096]{1,0:T(8,128)} async-done(((f32[128,4096]{1,0:T(8,128)}), f32[32,4096]{1,0:T(8,128)}) %reduce-scatter.9.cloned.1.call-update) | async-done | bytes 524304 | tf_op jit(solution)/shard_map/reduce_scatter | solution.py:58
  269.8 1.8 convert_element_type.35
  271.5 22.7 %reduce-scatter.17.cloned.1.call-done = f32[1,1,8,32,128]{4,3,2,1,0:T(8,128)} async-done(((f32[1,1,8,128,128]{4,3,2,1,0:T(8,128)}), f32[1,1,8,32,128]{4,3,2,1,0:T(8,128)}) %reduce-scatter.17.cloned.1.call-update) | async-done | bytes 131088 | tf_op jit(solution)/shard_map/reduce_scatter | solution.py:79
  294.3 22.8 %reduce-scatter.15.cloned.1.call-done = f32[1,1,8,32,128]{4,3,2,1,0:T(8,128)} async-done(((f32[1,1,8,128,128]{4,3,2,1,0:T(8,128)}), f32[1,1,8,32,128]{4,3,2,1,0:T(8,128)}) %reduce-scatter.15.cloned.1.call-update) | async-done | bytes 131088 | tf_op jit(solution)/shard_map/reduce_scatter | solution.py:76
  (17 shorter events, 0.1 us)
Async XLA Ops:
  7.2 11.4 %copy-start = (bf16[1,1,8,128,128]{4,3,2,1,0:T(8,128)(2,1)S(1)}, bf16[1,1,8,128,128]{4,3,2,1,0:T(8,128)(2,1)}, u32[]{:S(2)}) copy-start(bf16[1,1,8,128,128]{4,3,2,1,0:T(8,128)(2,1)} %param.9) | copy-start | bytes 786436
  7.2 1.6 copy-start.6
  7.2 1.9 copy-start.2
  7.2 66.5 %reduce-scatter.11.cloned.1.call-start = ((), (), s32[]{:S(2)}) async-start(), calls=%async_computation.9 | async-start | bytes 6291456 | tf_op jit(solution)/shard_map/reduce_scatter | solution.py:61
  7.2 2.2 copy-start.4
  16.6 1.2 copy-start.1
  16.6 1.5 copy-start.5
  16.6 113.9 %reduce-scatter.7.cloned.1.call-start = ((), (), s32[]{:S(2)}) async-start(), calls=%async_computation.6 | async-start | bytes 6291456 | tf_op jit(solution)/shard_map/reduce_scatter | solution.py:54
  17.8 1.1 copy-start.3
  26.2 141.2 %all-gather.5.cloned.1.call-start = ((), (), s32[]{:S(2)}) async-start(), calls=%async_computation.10 | async-start | bytes 3145728 | tf_op jit(solution)/shard_map/all_gather | solution.py:63
  134.1 67.8 %all-gather.3.cloned.1.call-start = ((), (), s32[]{:S(2)}) async-start(), calls=%async_computation.7 | async-start | bytes 3145728 | tf_op jit(solution)/shard_map/all_gather | solution.py:55
  134.7 101.1 %reduce-scatter.13.cloned.1.call-start = ((), (), s32[]{:S(2)}) async-start(), calls=%async_computation.11 | async-start | bytes 2621440 | tf_op jit(solution)/shard_map/reduce_scatter | solution.py:66
  174.5 95.3 %reduce-scatter.9.cloned.1.call-start = ((), (), s32[]{:S(2)}) async-start(), calls=%async_computation.8 | async-start | bytes 2621440 | tf_op jit(solution)/shard_map/reduce_scatter | solution.py:58
  209.2 85.1 %reduce-scatter.17.cloned.1.call-start = ((), (), s32[]{:S(2)}) async-start(), calls=%async_computation.13 | async-start | bytes 655360 | tf_op jit(solution)/shard_map/reduce_scatter | solution.py:79
  210.3 106.7 %reduce-scatter.15.cloned.1.call-start = ((), (), s32[]{:S(2)}) async-start(), calls=%async_computation.12 | async-start | bytes 655360 | tf_op jit(solution)/shard_map/reduce_scatter | solution.py:76
Sparse Core Ops, SparseCore 0:
  16.7 56.9 reduce-scatter.10
  76.1 54.3 reduce-scatter.6
  134.2 33.1 all-gather.4
  168.8 33.1 all-gather.2
  204.3 31.4 reduce-scatter.12
  238.3 31.3 reduce-scatter.8
  272.6 21.6 reduce-scatter.16
  297.1 19.9 reduce-scatter.14
where the time goes:
time: 324 us
  waiting for transfers between devices  267 us (82%)
  local copies, waits for them, and re-layouts  24.1 us (7%)
  between operations  14.3 us (4%)
  matrix products  10.8 us (3%)
  other arithmetic  7.16 us (2%)
    reduce_scatter x1, waiting for transfers between devices, shards(): lax.psum_scatter(partial_value, 'row', scatter_dimension=0, tiled=True)  56.7 us
    reduce_scatter x1, waiting for transfers between devices, shards(): lax.psum_scatter(back_part, 'row', scatter_dimension=0, tiled=True)  47.4 us
    all_gather x1, waiting for transfers between devices, shards(): grad_hidden = lax.all_gather(grad_part, 'row', axis=0, tiled=True)  32.7 us
    reduce_scatter x1, waiting for transfers between devices, shards(): lax.psum_scatter(out_part, 'col', scatter_dimension=0, tiled=True)  32.2 us
    all_gather x1, waiting for transfers between devices, shards(): lax.all_gather(gelu_value(hidden_part).astype(jnp.bfloat16), 'row', axis=...  27.2 us
    reduce_scatter x1, waiting for transfers between devices, shards(): lax.psum_scatter(input_part, 'col', scatter_dimension=0, tiled=True)  24.4 us
    unnamed x22, local copies, waits for them, and re-layouts  23.6 us
    reduce_scatter x1, waiting for transfers between devices, shards(): lax.psum_scatter(first_grad.reshape(1, 1, slots, block, block), 'tok', sc...  22.8 us
  transfers between devices with their start and end apart: 8, of which 8 were waited for; matrix products, arithmetic and copies ran while one was open for 9% of the time, Pallas kernels for 0%

commit v1 on v0

v1 whole, which is shorter than its diff:
```python
import functools
import math

import jax
import jax.numpy as jnp
from jax import lax
from jax.experimental import pallas as pl
from jax.experimental.pallas import tpu as pltpu
from jax.sharding import PartitionSpec as P

FF = 32768
f32 = jnp.float32
bf16 = jnp.bfloat16
VMEM = pl.BlockSpec(memory_space=pltpu.VMEM)
SMEM = pl.BlockSpec(memory_space=pltpu.SMEM)
ANY = pl.BlockSpec(memory_space=pl.ANY)
PARAMS = pltpu.CompilerParams(vmem_limit_bytes=32 * 1024 * 1024)

W1_ROW, W1_COL, W2_HID, W2_OUT = range(4)


def dot(a, b, contract):
    return lax.dot_general(a, b, ((contract[:1], contract[1:]), ((), ())), preferred_element_type=f32)


def shift(x, axis, by):
    n = lax.axis_size(axis)
    if by % n == 0:
        return x
    return lax.ppermute(x, axis, [(i, (i + by) % n) for i in range(n)])


def cdf(v):
    return 0.5 * (1.0 + lax.erf(v * math.sqrt(0.5)))


def first_kernel(slots, blk, tab, tokens, grad_out, w1, w2, p_own, p_send, b_own, b_send, taken, cot, w1_v, w2_v, sems):
    def block_of(source, index, target, sem):
        start = pl.multiple_of(index * blk, blk)
        return pltpu.make_async_copy(source.at[:, pl.ds(start, blk)], target, sem)

    w1_copy = pltpu.make_async_copy(w1, w1_v, sems.at[2 * slots])
    w2_copy = pltpu.make_async_copy(w2, w2_v, sems.at[2 * slots + 1])
    w1_copy.start()
    t_copies = [block_of(tokens, tab[W1_ROW, k], taken.at[k], sems.at[k]) for k in range(slots)]
    g_copies = [block_of(grad_out, tab[W2_OUT, k], cot.at[k], sems.at[slots + k]) for k in range(slots)]
    for c in t_copies:
        c.start()
    w2_copy.start()
    for c in g_copies:
        c.start()
    w1_copy.wait()
    for k in range(slots):
        t_copies[k].wait()
        value = dot(taken[k], w1_v[k], (1, 0))
        p_own[k] = value
        p_send[k] = value.astype(bf16)
    w2_copy.wait()
    for k in range(slots):
        g_copies[k].wait()
        value = dot(cot[k], w2_v[k], (1, 1))
        b_own[k] = value
        b_send[k] = value.astype(bf16)


def peer_tables(tabs, n_row, n_col):
    me_r, me_c = lax.axis_index("row"), lax.axis_index("col")

    def entry(d, which, k):
        r = lax.rem(me_r + (n_row - d), n_row)
        return tabs[r * n_col + me_c, which, k]

    return entry


def sum_at(acc, entry, targets, sources, own, peers, slots):
    for which in targets:
        for k in range(slots):
            acc[entry(0, which, k)] = jnp.zeros(acc.shape[1:], f32)
    for d, ref in enumerate([own] + list(peers)):
        for k in range(slots):
            at = entry(d, sources, k)
            acc[at] = acc[at] + ref[k].astype(f32)


def send_shares(value, refs, k, me, n):
    share = value.shape[0] // n
    for d in range(n):
        start = pl.multiple_of(lax.rem(me + d, n) * share, share)
        refs[d][k] = value[pl.ds(start, share), :].astype(refs[d].dtype)


def hidden_kernel(dims, tabs, p_own, *refs):
    slots, n_row, n_col, n_tok = dims
    p_peers, refs = refs[: n_row - 1], refs[n_row - 1 :]
    cot, w2, slope = refs[:3]
    outs, grads = refs[3 : 3 + n_col], refs[3 + n_col : 3 + n_col + n_tok]
    acc, value, grad = refs[3 + n_col + n_tok :]
    entry = peer_tables(tabs, n_row, n_col)
    me_c, me_t = lax.axis_index("col"), lax.axis_index("tok")
    sum_at(acc, entry, (W1_COL, W2_HID), W1_COL, p_own, p_peers, slots)
    for k in range(slots):
        h = acc[entry(0, W2_HID, k)]
        active = (h * cdf(h)).astype(bf16)
        value[...] = dot(active, w2[k], (1, 0))
        send_shares(value, outs, k, me_c, n_col)
        grad[...] = dot(active, cot[k], (0, 0))
        send_shares(grad, grads, k, me_t, n_tok)
    for k in range(slots):
        h = acc[entry(0, W1_COL, k)]
        slope[k] = cdf(h) + h * jnp.exp(-0.5 * h * h) * (1.0 / math.sqrt(2.0 * math.pi))


def back_kernel(dims, tabs, b_own, *refs):
    slots, n_row, n_col, n_tok = dims
    b_peers, refs = refs[: n_row - 1], refs[n_row - 1 :]
    slope, taken, w1 = refs[:3]
    outs, grads = refs[3 : 3 + n_col], refs[3 + n_col : 3 + n_col + n_tok]
    acc, value, grad = refs[3 + n_col + n_tok :]
    entry = peer_tables(tabs, n_row, n_col)
    me_c, me_t = lax.axis_index("col"), lax.axis_index("tok")
    sum_at(acc, entry, (W1_COL,), W2_HID, b_own, b_peers, slots)
    for k in range(slots):
        g = (acc[entry(0, W1_COL, k)] * slope[k]).astype(bf16)
        value[...] = dot(g, w1[k], (1, 1))
        send_shares(value, outs, k, me_c, n_col)
        grad[...] = dot(taken[k], g, (0, 0))
        send_shares(grad, grads, k, me_t, n_tok)


def last_kernel(dims, tabs, *refs):
    slots, n_row, n_col, n_tok = dims
    o_parts, refs = refs[:n_col], refs[n_col:]
    i_parts, refs = refs[:n_col], refs[n_col:]
    g2_parts, refs = refs[:n_tok], refs[n_tok:]
    g1_parts, refs = refs[:n_tok], refs[n_tok:]
    output, grad_in, gw1, gw2, acc = refs
    me_r, me_c = lax.axis_index("row"), lax.axis_index("col")
    blk = acc.shape[-1]
    for parts, which, result in ((o_parts, W2_OUT, output), (i_parts, W1_ROW, grad_in)):
        acc[...] = jnp.zeros(acc.shape, f32)
        for d, ref in enumerate(parts):
            src = me_r * n_col + lax.rem(me_c + (n_col - d), n_col)
            for k in range(slots):
                at = tabs[src, which, k]
                acc[at] = acc[at] + ref[k].astype(f32)
        for b in range(acc.shape[0]):
            result[:, b * blk : (b + 1) * blk] = acc[b].astype(bf16)
    for parts, result in ((g2_parts, gw2), (g1_parts, gw1)):
        for k in range(slots):
            total = parts[0][k].astype(f32)
            for ref in parts[1:]:
                total = total + ref[k].astype(f32)
            result[k] = total


def shards(tokens, w1_blocks, w1_rows, w1_cols, w2_blocks, w2_hidden, w2_outs, grad_out):
    slots, blk = w1_blocks.shape[2], w1_blocks.shape[-1]
    rows = tokens.shape[0]
    n_row, n_col, n_tok = (lax.axis_size(a) for a in ("row", "col", "tok"))
    dims = (slots, n_row, n_col, n_tok)
    row_blocks = tokens.shape[1] // blk
    col_blocks = FF // n_col // blk
    share, part = rows // n_col, blk // n_tok
    w1 = w1_blocks.reshape(slots, blk, blk)
    w2 = w2_blocks.reshape(slots, blk, blk)
    tab = jnp.concatenate([t.reshape(1, slots) for t in (w1_rows, w1_cols, w2_hidden, w2_outs)])
    tabs = lax.all_gather(tab, ("row", "col"))

    S = jax.ShapeDtypeStruct
    wide, narrow = S((slots, rows, blk), f32), S((slots, rows, blk), bf16)
    p_own, p_send, b_own, b_send, taken, cot = pl.pallas_call(
        functools.partial(first_kernel, slots, blk),
        out_shape=(wide, narrow, wide, narrow, narrow, narrow),
        in_specs=[SMEM, ANY, ANY, ANY, ANY],
        out_specs=(VMEM,) * 6,
        scratch_shapes=[
            pltpu.VMEM((slots, blk, blk), bf16),
            pltpu.VMEM((slots, blk, blk), bf16),
            pltpu.SemaphoreType.DMA((2 * slots + 2,)),
        ],
        compiler_params=PARAMS,
        name="take_and_multiply",
    )(tab, tokens, grad_out, w1, w2)

    p_peers = [shift(p_send, "row", d) for d in range(1, n_row)]
    b_peers = [shift(b_send, "row", d) for d in range(1, n_row)]

    shares = (S((slots, share, blk), bf16),) * n_col
    parts = (S((slots, part, blk), bf16),) * n_tok
    scratch = [
        pltpu.VMEM((col_blocks, rows, blk), f32),
        pltpu.VMEM((rows, blk), f32),
        pltpu.VMEM((blk, blk), f32),
    ]
    slope, *sent = pl.pallas_call(
        functools.partial(hidden_kernel, dims),
        out_shape=(wide,) + shares + parts,
        in_specs=[SMEM] + [VMEM] * (n_row + 2),
        out_specs=(VMEM,) * (1 + n_col + n_tok),
        scratch_shapes=scratch,
        compiler_params=PARAMS,
        name="hidden",
    )(tabs, p_own, *p_peers, cot, w2)
    o_parts = [shift(x, "col", d) for d, x in enumerate(sent[:n_col])]
    g2_parts = [shift(x, "tok", d) for d, x in enumerate(sent[n_col:])]

    sent = pl.pallas_call(
        functools.partial(back_kernel, dims),
        out_shape=shares + parts,
        in_specs=[SMEM] + [VMEM] * (n_row + 3),
        out_specs=(VMEM,) * (n_col + n_tok),
        scratch_shapes=scratch,
        compiler_params=PARAMS,
        name="back",
    )(tabs, b_own, *b_peers, slope, taken, w1)
    i_parts = [shift(x, "col", d) for d, x in enumerate(sent[:n_col])]
    g1_parts = [shift(x, "tok", d) for d, x in enumerate(sent[n_col:])]

    summed = S((slots, part, blk), f32)
    output, grad_in, gw1, gw2 = pl.pallas_call(
        functools.partial(last_kernel, dims),
        out_shape=(
            S((share, row_blocks * blk), bf16),
            S((share, row_blocks * blk), bf16),
            summed,
            summed,
        ),
        in_specs=[SMEM] + [VMEM] * (2 * n_col + 2 * n_tok),
        out_specs=(VMEM,) * 4,
        scratch_shapes=[pltpu.VMEM((row_blocks, share, blk), f32)],
        compiler_params=PARAMS,
        name="add_up",
    )(tabs, *o_parts, *i_parts, *g2_parts, *g1_parts)
    return (output, grad_in, gw1.reshape(1, 1, slots, part, blk), gw2.reshape(1, 1, slots, part, blk))


def solution(mesh):
    placed = (
        P("tok", "row"),
        P("row", "col", None, None, None),
        P("row", "col", None),
        P("row", "col", None),
        P("row", "col", None, None, None),
        P("row", "col", None),
        P("row", "col", None),
        P("tok", "row"),
    )
    return jax.shard_map(
        shards,
        mesh=mesh,
        in_specs=placed,
        out_specs=(
            P(("tok", "col"), "row"),
            P(("tok", "col"), "row"),
            P("row", "col", None, "tok", None),
            P("row", "col", None, "tok", None),
        ),
        check_vma=False,
    )
```

time: 324 us -> 53.1 us (0.16)
  waiting for transfers between devices: 267 us -> 5.31 us
  local copies, waits for them, and re-layouts: 24.1 us -> 5.02 us
  starting transfers between devices: 0.73 us -> 17.1 us
  blocking collectives: 0 us -> 16.1 us
  between operations: 14.3 us -> 0.72 us
  matrix products: 10.8 us -> 0 us
  Pallas kernels: 0 us -> 8.52 us
  other arithmetic: 7.16 us -> 0.01 us
    reduce_scatter x6 -> x0, waiting for transfers between devices: 206 us -> none  [the longest x1 56.7 us: shards(): lax.psum_scatter(partial_value, 'row', scatter_dimension=0, tiled=True)]
    all_gather x2 -> x0, waiting for transfers between devices: 59.9 us -> none  [the longest x1 32.7 us: shards(): grad_hidden = lax.all_gather(grad_part, 'row', axis=0, tiled=True)]
    unnamed x22 -> x20, local copies, waits for them, and re-layouts: 23.6 us -> 5.02 us
    ppermute x0 -> x14, starting transfers between devices: none -> 17.1 us  [shift(): return lax.ppermute(x, axis, [(i, (i + by) % n) for i in range(n)])]
    all_gather x0 -> x1, blocking collectives: none -> 16.1 us  [shards(): tabs = lax.all_gather(tab, ('row', 'col'))]
    dot_general x14 -> x0, matrix products: 10.8 us -> none  [the longest x4 6.07 us: place_blocks(): placed = jnp.einsum('kc,ktj->tcj', onehot, product, precision=highest)]
    pallas_call x0 -> x4, Pallas kernels: none -> 8.52 us  [the longest x1 3.44 us: shards(): pl.pallas_call(functools.partial(first_kernel, slots, blk), out_shape=(wi...]
    convert_element_type x3 -> x0, other arithmetic: 7.16 us -> none  [the longest x1 3.62 us: shards(): grad_part = (back_part_sum * gelu_slope(hidden_part)).astype(jnp.bfloat16)]
  transfers between devices with their start and end apart: 8 -> 14, of which waited for: 8 -> 4; matrix products, arithmetic and copies ran while one was open for 9% -> 0% of each run, Pallas kernels for 0% -> 6%
where the time goes in v1:
time: 53.1 us; the launch traced here: 52.8 us
  starting transfers between devices  17.1 us (32%)
  blocking collectives  16.1 us (30%)
  Pallas kernels  8.52 us (16%)
  waiting for transfers between devices  5.31 us (10%)
  local copies, waits for them, and re-layouts  5.02 us (9%)
  between operations  0.72 us (1%)
    ppermute x14, starting transfers between devices, shift(): return lax.ppermute(x, axis, [(i, (i + by) % n) for i in range(n)])  17.1 us
    all_gather x1, blocking collectives, shards(): tabs = lax.all_gather(tab, ('row', 'col'))  16.1 us
    ppermute x14, waiting for transfers between devices, shift(): return lax.ppermute(x, axis, [(i, (i + by) % n) for i in range(n)])  5.31 us
    unnamed x20, local copies, waits for them, and re-layouts  5.02 us
    pallas_call x1, Pallas kernels, shards(): pl.pallas_call(functools.partial(first_kernel, slots, blk), out_shape=(wi...  3.44 us
    pallas_call x1, Pallas kernels, shards(): pl.pallas_call(functools.partial(last_kernel, dims), out_shape=(S((share,...  2.08 us
    pallas_call x1, Pallas kernels, shards(): pl.pallas_call(functools.partial(hidden_kernel, dims), out_shape=(wide,)...  1.59 us
    pallas_call x1, Pallas kernels, shards(): pl.pallas_call(functools.partial(back_kernel, dims), out_shape=shares + p...  1.41 us
  transfers between devices with their start and end apart: 14, of which 4 were waited for; matrix products, arithmetic and copies ran while one was open for 0% of the time, Pallas kernels for 6%

profile of v1, /device:TPU:0, one launch (start us, length us, event | category | flops | bytes accessed | tf_op | source)
XLA Modules:
  0.0 52.8 jit_solution(2913524705974242044)
XLA Ops:
  0.6 0.0 copy-start.9
  0.6 0.0 copy-start.6
  0.7 0.0 copy-start.7
  0.7 0.0 copy-start.8
  0.7 0.6 %copy-done.9 = s32[1,1,8]{2,1,0:T(1,128)S(1)} copy-done((s32[1,1,8]{2,1,0:T(1,128)S(1)}, s32[1,1,8]{2,1,0:T(1,128)}, u32[]{:S(2)}) %copy-start.9) | copy-done | bytes 56
  1.3 0.0 copy-done.6
  1.3 0.0 copy-done.7
  1.3 0.0 copy-done.8
  1.3 0.0 copy-start
  1.4 0.9 %copy-done = bf16[1,1,8,128,128]{4,3,2,1,0:T(8,128)(2,1)S(1)} copy-done((bf16[1,1,8,128,128]{4,3,2,1,0:T(8,128)(2,1)S(1)}, bf16[1,1,8,128,128]{4,3,2,1,0:T(8,128)(2,1)}, u32[]{:S(2)}) %copy-start) | copy-done | bytes 262168
  2.3 1.2 %copy-done.2 = bf16[128,4096]{1,0:T(8,128)(2,1)S(1)} copy-done((bf16[128,4096]{1,0:T(8,128)(2,1)S(1)}, bf16[128,4096]{1,0:T(8,128)(2,1)}, u32[]{:S(2)}) %copy-start.2) | copy-done | bytes 1048600
  3.5 1.2 %copy-done.3 = bf16[128,4096]{1,0:T(8,128)(2,1)S(1)} copy-done((bf16[128,4096]{1,0:T(8,128)(2,1)S(1)}, bf16[128,4096]{1,0:T(8,128)(2,1)}, u32[]{:S(2)}) %copy-start.3) | copy-done | bytes 1048600
  4.8 0.9 %copy-done.4 = bf16[1,1,8,128,128]{4,3,2,1,0:T(8,128)(2,1)S(1)} copy-done((bf16[1,1,8,128,128]{4,3,2,1,0:T(8,128)(2,1)S(1)}, bf16[1,1,8,128,128]{4,3,2,1,0:T(8,128)(2,1)}, u32[]{:S(2)}) %copy-start.4) | copy-done | bytes 262168
  5.7 3.4 %take_and_multiply.1 = (f32[8,128,128]{2,1,0:T(8,128)S(1)}, bf16[8,128,128]{2,1,0:T(8,128)(2,1)S(1)}, f32[8,128,128]{2,1,0:T(8,128)S(1)}, bf16[8,128,128]{2,1,0:...) custom-call(s32[4,8]{1,0:T(4,128)S(1)} %get-tuple-element.58.tab, ...), custom_call_target="tpu_custom_call" | custom-call | tf_op jit(solution)/shard_map/take_and_multiply/pallas_call | solution.py:172
  9.2 3.0 %collective-permute-start = (bf16[8,128,128]{2,1,0:T(8,128)(2,1)S(1)}, bf16[8,128,128]{2,1,0:T(8,128)(2,1)S(1)}, u32[]{:S(2)}, u32[]{:S(2)}) collective-permute-start(bf16[8,128,128]{2,1,0:T(8,128)(2,1)S(1)} %get-tuple-element.32), channel_id=1, source_target_pairs={{0,4},{4,0},{1,5},{5,1},{2,6},{6,2},{3,7},{7,3},{8,12},{12,8},{9,1... | collective-permute-start | bytes 786440 | tf_op jit(solution)/shard_map/ppermute | solution.py:30
  12.2 0.1 collective-permute-start.4
  12.2 16.1 %all-gather.1.tabs = s32[8,4,8]{2,1,0:T(4,128)S(1)} all-gather(s32[1,4,8]{2,1,0:T(4,128)S(1)} %get-tuple-element.59), channel_id=2, replica_groups=mesh['tok'=4,'row'=2,'col'=4] {'row','col'}, dimensions={0}, use_global_device_ids=true | all-gather | bytes 1152 | tf_op jit(solution)/shard_map/all_gather | solution.py:168
  28.4 0.0 collective-permute-done.refs_0_
  28.4 0.0 copy-done.5
  28.4 1.6 %hidden.1 = (f32[8,128,128]{2,1,0:T(8,128)S(1)}, bf16[8,32,128]{2,1,0:T(8,128)(2,1)S(1)}, bf16[8,32,128]{2,1,0:T(8,128)(2,1)S(1)}, bf16[8,32,128]{2,1,0:T(8,128)...) custom-call(s32[8,4,8]{2,1,0:T(4,128)S(1)} %all-gather.1.tabs, ...), custom_call_target="tpu_custom_call" | custom-call | tf_op jit(solution)/shard_map/hidden/pallas_call | solution.py:196
  30.0 0.4 collective-permute-start.1
  30.4 1.5 %collective-permute-start.2 = (bf16[8,32,128]{2,1,0:T(8,128)(2,1)S(1)}, bf16[8,32,128]{2,1,0:T(8,128)(2,1)S(1)}, u32[]{:S(2)}, u32[]{:S(2)}) collective-permute-start(bf16[8,32,128]{2,1,0:T(8,128)(2,1)S(1)} %get-tuple-element.36), channel_id=1, source_target_pairs={{0,2},{1,3},{2,0},{3,1},{4,6},{5,7},{6,4},{7,5},{8,10},{9,11},{10,... | collective-permute-start | bytes 196616 | tf_op jit(solution)/shard_map/ppermute | solution.py:30
  31.9 1.1 %collective-permute-start.3 = (bf16[8,32,128]{2,1,0:T(8,128)(2,1)S(1)}, bf16[8,32,128]{2,1,0:T(8,128)(2,1)S(1)}, u32[]{:S(2)}, u32[]{:S(2)}) collective-permute-start(bf16[8,32,128]{2,1,0:T(8,128)(2,1)S(1)} %get-tuple-element.37), channel_id=1, source_target_pairs={{0,3},{1,0},{2,1},{3,2},{4,7},{5,4},{6,5},{7,6},{8,11},{9,8},{10,9... | collective-permute-start | bytes 196616 | tf_op jit(solution)/shard_map/ppermute | solution.py:30
  33.0 1.6 %collective-permute-start.8 = (bf16[8,32,128]{2,1,0:T(8,128)(2,1)S(1)}, bf16[8,32,128]{2,1,0:T(8,128)(2,1)S(1)}, u32[]{:S(2)}, u32[]{:S(2)}) collective-permute-start(bf16[8,32,128]{2,1,0:T(8,128)(2,1)S(1)} %get-tuple-element.47), channel_id=1, source_target_pairs={{0,8},{8,16},{16,24},{24,0},{1,9},{9,17},{17,25},{25,1},{2,10},{10... | collective-permute-start | bytes 196616 | tf_op jit(solution)/shard_map/ppermute | solution.py:30
  34.6 0.0 collective-permute-done.4.refs_0_
  34.6 2.6 %collective-permute-start.9 = (bf16[8,32,128]{2,1,0:T(8,128)(2,1)S(1)}, bf16[8,32,128]{2,1,0:T(8,128)(2,1)S(1)}, u32[]{:S(2)}, u32[]{:S(2)}) collective-permute-start(bf16[8,32,128]{2,1,0:T(8,128)(2,1)S(1)} %get-tuple-element.48), channel_id=1, source_target_pairs={{0,16},{8,24},{16,0},{24,8},{1,17},{9,25},{17,1},{25,9},{2,18},{10... | collective-permute-start | bytes 196616 | tf_op jit(solution)/shard_map/ppermute | solution.py:30
  37.2 0.0 copy-done.1
  37.2 1.4 %back.1 = (bf16[8,32,128]{2,1,0:T(8,128)(2,1)S(1)}, bf16[8,32,128]{2,1,0:T(8,128)(2,1)S(1)}, bf16[8,32,128]{2,1,0:T(8,128)(2,1)S(1)}, bf16[8,32,128]{2,1,0:T(8,1...) custom-call(s32[8,4,8]{2,1,0:T(4,128)S(1)} %all-gather.1.tabs, ...), custom_call_target="tpu_custom_call" | custom-call | tf_op jit(solution)/shard_map/back/pallas_call | solution.py:208
  38.6 0.0 collective-permute-done.1.refs_1_
  38.6 1.4 %collective-permute-start.10 = (bf16[8,32,128]{2,1,0:T(8,128)(2,1)S(1)}, bf16[8,32,128]{2,1,0:T(8,128)(2,1)S(1)}, u32[]{:S(2)}, u32[]{:S(2)}) collective-permute-start(bf16[8,32,128]{2,1,0:T(8,128)(2,1)S(1)} %get-tuple-element.49), channel_id=1, source_target_pairs={{0,24},{8,0},{16,8},{24,16},{1,25},{9,1},{17,9},{25,17},{2,26},{10... | collective-permute-start | bytes 196616 | tf_op jit(solution)/shard_map/ppermute | solution.py:30
  40.0 0.0 collective-permute-done.2.refs_2_
  40.0 0.0 collective-permute-start.5
  40.0 0.0 collective-permute-done.3.refs_3_
  40.0 0.6 %collective-permute-start.6 = (bf16[8,32,128]{2,1,0:T(8,128)(2,1)S(1)}, bf16[8,32,128]{2,1,0:T(8,128)(2,1)S(1)}, u32[]{:S(2)}, u32[]{:S(2)}) collective-permute-start(bf16[8,32,128]{2,1,0:T(8,128)(2,1)S(1)} %get-tuple-element.44), channel_id=1, source_target_pairs={{0,2},{1,3},{2,0},{3,1},{4,6},{5,7},{6,4},{7,5},{8,10},{9,11},{10,... | collective-permute-start | bytes 196616 | tf_op jit(solution)/shard_map/ppermute | solution.py:30
  40.6 0.0 collective-permute-done.8.refs_9_
  40.6 1.4 %collective-permute-start.7 = (bf16[8,32,128]{2,1,0:T(8,128)(2,1)S(1)}, bf16[8,32,128]{2,1,0:T(8,128)(2,1)S(1)}, u32[]{:S(2)}, u32[]{:S(2)}) collective-permute-start(bf16[8,32,128]{2,1,0:T(8,128)(2,1)S(1)} %get-tuple-element.45), channel_id=1, source_target_pairs={{0,3},{1,0},{2,1},{3,2},{4,7},{5,4},{6,5},{7,6},{8,11},{9,8},{10,9... | collective-permute-start | bytes 196616 | tf_op jit(solution)/shard_map/ppermute | solution.py:30
  42.0 0.0 collective-permute-done.9.refs_10_
  42.0 0.7 %collective-permute-start.11 = (bf16[8,32,128]{2,1,0:T(8,128)(2,1)S(1)}, bf16[8,32,128]{2,1,0:T(8,128)(2,1)S(1)}, u32[]{:S(2)}, u32[]{:S(2)}) collective-permute-start(bf16[8,32,128]{2,1,0:T(8,128)(2,1)S(1)} %get-tuple-element.51), channel_id=1, source_target_pairs={{0,8},{8,16},{16,24},{24,0},{1,9},{9,17},{17,25},{25,1},{2,10},{10... | collective-permute-start | bytes 196616 | tf_op jit(solution)/shard_map/ppermute | solution.py:30
  42.7 0.2 collective-permute-done.10.refs_11_
  42.9 0.3 collective-permute-start.12
  43.2 0.5 %collective-permute-done.5.refs_5_ = bf16[8,32,128]{2,1,0:T(8,128)(2,1)S(1)} collective-permute-done((bf16[8,32,128]{2,1,0:T(8,128)(2,1)S(1)}, bf16[8,32,128]{2,1,0:T(8,128)(2,1)S(1)}, u32[]{:S(2)}, u32[]{:S(2)}) %collective-permute-start.5) | collective-permute-done | bytes 65568 | tf_op jit(solution)/shard_map/ppermute | solution.py:30
  43.8 2.4 %collective-permute-start.13 = (bf16[8,32,128]{2,1,0:T(8,128)(2,1)S(1)}, bf16[8,32,128]{2,1,0:T(8,128)(2,1)S(1)}, u32[]{:S(2)}, u32[]{:S(2)}) collective-permute-start(bf16[8,32,128]{2,1,0:T(8,128)(2,1)S(1)} %get-tuple-element.53), channel_id=1, source_target_pairs={{0,24},{8,0},{16,8},{24,16},{1,25},{9,1},{17,9},{25,17},{2,26},{10... | collective-permute-start | bytes 196616 | tf_op jit(solution)/shard_map/ppermute | solution.py:30
  46.2 0.0 collective-permute-done.6.refs_6_
  46.2 0.0 collective-permute-done.7.refs_7_
  46.2 2.6 %collective-permute-done.11.refs_13_ = bf16[8,32,128]{2,1,0:T(8,128)(2,1)S(1)} collective-permute-done((bf16[8,32,128]{2,1,0:T(8,128)(2,1)S(1)}, bf16[8,32,128]{2,1,0:T(8,128)(2,1)S(1)}, u32[]{:S(2)}, u32[]{:S(2)}) %collective-permute-start.11) | collective-permute-done | bytes 65568 | tf_op jit(solution)/shard_map/ppermute | solution.py:30
  48.8 1.9 %collective-permute-done.12.refs_14_ = bf16[8,32,128]{2,1,0:T(8,128)(2,1)S(1)} collective-permute-done((bf16[8,32,128]{2,1,0:T(8,128)(2,1)S(1)}, bf16[8,32,128]{2,1,0:T(8,128)(2,1)S(1)}, u32[]{:S(2)}, u32[]{:S(2)}) %collective-permute-start.12) | collective-permute-done | bytes 65568 | tf_op jit(solution)/shard_map/ppermute | solution.py:30
  50.7 0.0 collective-permute-done.13.refs_15_
  50.7 2.1 %add_up.1 = (bf16[32,4096]{1,0:T(8,128)(2,1)}, bf16[32,4096]{1,0:T(8,128)(2,1)}, f32[8,32,128]{2,1,0:T(8,128)}, f32[8,32,128]{2,1,0:T(8,128)}) custom-call(s32[8,4,8]{2,1,0:T(4,128)S(1)} %all-gather.1.tabs, bf16[8,32,128]{2,1,0:T(8,128)(2,1)S(1)} %get-tuple-element.34.refs_0_, bf16[8,32,128]{2,1,0:T(8,128)(2,1)S(1)} %collective-permute-done.1.refs_1_, ...), custom_call_target="tpu_custom_call" | custom-call | tf_op jit(solution)/shard_map/add_up/pallas_call | solution.py:221
  (6 shorter events, 0.0 us)
Async XLA Ops:
  0.6 0.7 %copy-start.9 = (s32[1,1,8]{2,1,0:T(1,128)S(1)}, s32[1,1,8]{2,1,0:T(1,128)}, u32[]{:S(2)}) copy-start(s32[1,1,8]{2,1,0:T(1,128)} %param.10) | copy-start | bytes 100
  0.6 0.7 %copy-start.6 = (s32[1,1,8]{2,1,0:T(1,128)S(1)}, s32[1,1,8]{2,1,0:T(1,128)}, u32[]{:S(2)}) copy-start(s32[1,1,8]{2,1,0:T(1,128)} %param.14) | copy-start | bytes 100
  0.7 0.7 %copy-start.7 = (s32[1,1,8]{2,1,0:T(1,128)S(1)}, s32[1,1,8]{2,1,0:T(1,128)}, u32[]{:S(2)}) copy-start(s32[1,1,8]{2,1,0:T(1,128)} %param.13) | copy-start | bytes 100
  0.7 0.7 %copy-start.8 = (s32[1,1,8]{2,1,0:T(1,128)S(1)}, s32[1,1,8]{2,1,0:T(1,128)}, u32[]{:S(2)}) copy-start(s32[1,1,8]{2,1,0:T(1,128)} %param.11) | copy-start | bytes 100
  1.3 1.0 %copy-start = (bf16[1,1,8,128,128]{4,3,2,1,0:T(8,128)(2,1)S(1)}, bf16[1,1,8,128,128]{4,3,2,1,0:T(8,128)(2,1)}, u32[]{:S(2)}) copy-start(bf16[1,1,8,128,128]{4,3,2,1,0:T(8,128)(2,1)} %param.9) | copy-start | bytes 786436
  2.3 1.2 %copy-start.2 = (bf16[128,4096]{1,0:T(8,128)(2,1)S(1)}, bf16[128,4096]{1,0:T(8,128)(2,1)}, u32[]{:S(2)}) copy-start(bf16[128,4096]{1,0:T(8,128)(2,1)} %tokens.1) | copy-start | bytes 3145732
  3.5 1.2 %copy-start.3 = (bf16[128,4096]{1,0:T(8,128)(2,1)S(1)}, bf16[128,4096]{1,0:T(8,128)(2,1)}, u32[]{:S(2)}) copy-start(bf16[128,4096]{1,0:T(8,128)(2,1)} %grad_out.1) | copy-start | bytes 3145732
  4.8 0.9 %copy-start.4 = (bf16[1,1,8,128,128]{4,3,2,1,0:T(8,128)(2,1)S(1)}, bf16[1,1,8,128,128]{4,3,2,1,0:T(8,128)(2,1)}, u32[]{:S(2)}) copy-start(bf16[1,1,8,128,128]{4,3,2,1,0:T(8,128)(2,1)} %param.12) | copy-start | bytes 786436
  5.7 22.7 %copy-start.5 = (bf16[1,1,8,128,128]{4,3,2,1,0:T(8,128)(2,1)S(1)}, bf16[1,1,8,128,128]{4,3,2,1,0:T(8,128)(2,1)}, u32[]{:S(2)}) copy-start(bf16[1,1,8,128,128]{4,3,2,1,0:T(8,128)(2,1)} %param.12) | copy-start | bytes 786436
  9.2 19.2 %collective-permute-start = (bf16[8,128,128]{2,1,0:T(8,128)(2,1)S(1)}, bf16[8,128,128]{2,1,0:T(8,128)(2,1)S(1)}, u32[]{:S(2)}, u32[]{:S(2)}) collective-permute-start(bf16[8,128,128]{2,1,0:T(8,128)(2,1)S(1)} %get-tuple-element.32), channel_id=1, source_target_pairs={{0,4},{4,0},{1,5},{5,1},{2,6},{6,2},{3,7},{7,3},{8,12},{12,8},{9,1... | collective-permute-start | bytes 786440 | tf_op jit(solution)/shard_map/ppermute | solution.py:30
  12.2 22.4 %collective-permute-start.4 = (bf16[8,128,128]{2,1,0:T(8,128)(2,1)S(1)}, bf16[8,128,128]{2,1,0:T(8,128)(2,1)S(1)}, u32[]{:S(2)}, u32[]{:S(2)}) collective-permute-start(bf16[8,128,128]{2,1,0:T(8,128)(2,1)S(1)} %get-tuple-element.39), channel_id=1, source_target_pairs={{0,4},{4,0},{1,5},{5,1},{2,6},{6,2},{3,7},{7,3},{8,12},{12,8},{9,1... | collective-permute-start | bytes 786440 | tf_op jit(solution)/shard_map/ppermute | solution.py:30
  28.4 8.8 %copy-start.1 = (bf16[1,1,8,128,128]{4,3,2,1,0:T(8,128)(2,1)S(1)}, bf16[1,1,8,128,128]{4,3,2,1,0:T(8,128)(2,1)}, u32[]{:S(2)}) copy-start(bf16[1,1,8,128,128]{4,3,2,1,0:T(8,128)(2,1)} %param.9) | copy-start | bytes 786436
  30.0 8.6 %collective-permute-start.1 = (bf16[8,32,128]{2,1,0:T(8,128)(2,1)S(1)}, bf16[8,32,128]{2,1,0:T(8,128)(2,1)S(1)}, u32[]{:S(2)}, u32[]{:S(2)}) collective-permute-start(bf16[8,32,128]{2,1,0:T(8,128)(2,1)S(1)} %get-tuple-element.35), channel_id=1, source_target_pairs={{0,1},{1,2},{2,3},{3,0},{4,5},{5,6},{6,7},{7,4},{8,9},{9,10},{10,1... | collective-permute-start | bytes 196616 | tf_op jit(solution)/shard_map/ppermute | solution.py:30
  30.4 9.6 %collective-permute-start.2 = (bf16[8,32,128]{2,1,0:T(8,128)(2,1)S(1)}, bf16[8,32,128]{2,1,0:T(8,128)(2,1)S(1)}, u32[]{:S(2)}, u32[]{:S(2)}) collective-permute-start(bf16[8,32,128]{2,1,0:T(8,128)(2,1)S(1)} %get-tuple-element.36), channel_id=1, source_target_pairs={{0,2},{1,3},{2,0},{3,1},{4,6},{5,7},{6,4},{7,5},{8,10},{9,11},{10,... | collective-permute-start | bytes 196616 | tf_op jit(solution)/shard_map/ppermute | solution.py:30
  31.9 8.1 %collective-permute-start.3 = (bf16[8,32,128]{2,1,0:T(8,128)(2,1)S(1)}, bf16[8,32,128]{2,1,0:T(8,128)(2,1)S(1)}, u32[]{:S(2)}, u32[]{:S(2)}) collective-permute-start(bf16[8,32,128]{2,1,0:T(8,128)(2,1)S(1)} %get-tuple-element.37), channel_id=1, source_target_pairs={{0,3},{1,0},{2,1},{3,2},{4,7},{5,4},{6,5},{7,6},{8,11},{9,8},{10,9... | collective-permute-start | bytes 196616 | tf_op jit(solution)/shard_map/ppermute | solution.py:30
  33.0 7.6 %collective-permute-start.8 = (bf16[8,32,128]{2,1,0:T(8,128)(2,1)S(1)}, bf16[8,32,128]{2,1,0:T(8,128)(2,1)S(1)}, u32[]{:S(2)}, u32[]{:S(2)}) collective-permute-start(bf16[8,32,128]{2,1,0:T(8,128)(2,1)S(1)} %get-tuple-element.47), channel_id=1, source_target_pairs={{0,8},{8,16},{16,24},{24,0},{1,9},{9,17},{17,25},{25,1},{2,10},{10... | collective-permute-start | bytes 196616 | tf_op jit(solution)/shard_map/ppermute | solution.py:30
  34.6 7.4 %collective-permute-start.9 = (bf16[8,32,128]{2,1,0:T(8,128)(2,1)S(1)}, bf16[8,32,128]{2,1,0:T(8,128)(2,1)S(1)}, u32[]{:S(2)}, u32[]{:S(2)}) collective-permute-start(bf16[8,32,128]{2,1,0:T(8,128)(2,1)S(1)} %get-tuple-element.48), channel_id=1, source_target_pairs={{0,16},{8,24},{16,0},{24,8},{1,17},{9,25},{17,1},{25,9},{2,18},{10... | collective-permute-start | bytes 196616 | tf_op jit(solution)/shard_map/ppermute | solution.py:30
  38.6 4.3 %collective-permute-start.10 = (bf16[8,32,128]{2,1,0:T(8,128)(2,1)S(1)}, bf16[8,32,128]{2,1,0:T(8,128)(2,1)S(1)}, u32[]{:S(2)}, u32[]{:S(2)}) collective-permute-start(bf16[8,32,128]{2,1,0:T(8,128)(2,1)S(1)} %get-tuple-element.49), channel_id=1, source_target_pairs={{0,24},{8,0},{16,8},{24,16},{1,25},{9,1},{17,9},{25,17},{2,26},{10... | collective-permute-start | bytes 196616 | tf_op jit(solution)/shard_map/ppermute | solution.py:30
  40.0 3.8 %collective-permute-start.5 = (bf16[8,32,128]{2,1,0:T(8,128)(2,1)S(1)}, bf16[8,32,128]{2,1,0:T(8,128)(2,1)S(1)}, u32[]{:S(2)}, u32[]{:S(2)}) collective-permute-start(bf16[8,32,128]{2,1,0:T(8,128)(2,1)S(1)} %get-tuple-element.43), channel_id=1, source_target_pairs={{0,1},{1,2},{2,3},{3,0},{4,5},{5,6},{6,7},{7,4},{8,9},{9,10},{10,1... | collective-permute-start | bytes 196616 | tf_op jit(solution)/shard_map/ppermute | solution.py:30
  40.0 6.2 %collective-permute-start.6 = (bf16[8,32,128]{2,1,0:T(8,128)(2,1)S(1)}, bf16[8,32,128]{2,1,0:T(8,128)(2,1)S(1)}, u32[]{:S(2)}, u32[]{:S(2)}) collective-permute-start(bf16[8,32,128]{2,1,0:T(8,128)(2,1)S(1)} %get-tuple-element.44), channel_id=1, source_target_pairs={{0,2},{1,3},{2,0},{3,1},{4,6},{5,7},{6,4},{7,5},{8,10},{9,11},{10,... | collective-permute-start | bytes 196616 | tf_op jit(solution)/shard_map/ppermute | solution.py:30
  40.6 5.6 %collective-permute-start.7 = (bf16[8,32,128]{2,1,0:T(8,128)(2,1)S(1)}, bf16[8,32,128]{2,1,0:T(8,128)(2,1)S(1)}, u32[]{:S(2)}, u32[]{:S(2)}) collective-permute-start(bf16[8,32,128]{2,1,0:T(8,128)(2,1)S(1)} %get-tuple-element.45), channel_id=1, source_target_pairs={{0,3},{1,0},{2,1},{3,2},{4,7},{5,4},{6,5},{7,6},{8,11},{9,8},{10,9... | collective-permute-start | bytes 196616 | tf_op jit(solution)/shard_map/ppermute | solution.py:30
  42.0 6.8 %collective-permute-start.11 = (bf16[8,32,128]{2,1,0:T(8,128)(2,1)S(1)}, bf16[8,32,128]{2,1,0:T(8,128)(2,1)S(1)}, u32[]{:S(2)}, u32[]{:S(2)}) collective-permute-start(bf16[8,32,128]{2,1,0:T(8,128)(2,1)S(1)} %get-tuple-element.51), channel_id=1, source_target_pairs={{0,8},{8,16},{16,24},{24,0},{1,9},{9,17},{17,25},{25,1},{2,10},{10... | collective-permute-start | bytes 196616 | tf_op jit(solution)/shard_map/ppermute | solution.py:30
  42.9 7.8 %collective-permute-start.12 = (bf16[8,32,128]{2,1,0:T(8,128)(2,1)S(1)}, bf16[8,32,128]{2,1,0:T(8,128)(2,1)S(1)}, u32[]{:S(2)}, u32[]{:S(2)}) collective-permute-start(bf16[8,32,128]{2,1,0:T(8,128)(2,1)S(1)} %get-tuple-element.52), channel_id=1, source_target_pairs={{0,16},{8,24},{16,0},{24,8},{1,17},{9,25},{17,1},{25,9},{2,18},{10... | collective-permute-start | bytes 196616 | tf_op jit(solution)/shard_map/ppermute | solution.py:30
  43.8 6.9 %collective-permute-start.13 = (bf16[8,32,128]{2,1,0:T(8,128)(2,1)S(1)}, bf16[8,32,128]{2,1,0:T(8,128)(2,1)S(1)}, u32[]{:S(2)}, u32[]{:S(2)}) collective-permute-start(bf16[8,32,128]{2,1,0:T(8,128)(2,1)S(1)} %get-tuple-element.53), channel_id=1, source_target_pairs={{0,24},{8,0},{16,8},{24,16},{1,25},{9,1},{17,9},{25,17},{2,26},{10... | collective-permute-start | bytes 196616 | tf_op jit(solution)/shard_map/ppermute | solution.py:30

commit v2 on v1

v2 whole, which is shorter than its diff:
```python
import functools
import math

import jax
import jax.numpy as jnp
from jax import lax
from jax.experimental import pallas as pl
from jax.experimental.pallas import tpu as pltpu
from jax.sharding import PartitionSpec as P

FF = 32768
f32 = jnp.float32
bf16 = jnp.bfloat16
VMEM = pl.BlockSpec(memory_space=pltpu.VMEM)
SMEM = pl.BlockSpec(memory_space=pltpu.SMEM)
HBM = pl.BlockSpec(memory_space=pltpu.HBM)
LANES = 128
PARAMS = pltpu.CompilerParams(vmem_limit_bytes=32 * 1024 * 1024)

W1_ROW, W1_COL, W2_HID, W2_OUT = range(4)


def dot(a, b, contract):
    return lax.dot_general(a, b, ((contract[:1], contract[1:]), ((), ())), preferred_element_type=f32)


def shift(x, axis, by):
    n = lax.axis_size(axis)
    if by % n == 0:
        return x
    return lax.ppermute(x, axis, [(i, (i + by) % n) for i in range(n)])


def cdf(v):
    return 0.5 * (1.0 + lax.erf(v * math.sqrt(0.5)))


def table_row(tables, slots):
    lane = lax.broadcasted_iota(jnp.int32, (16, LANES), 1)
    row = jnp.zeros((16, LANES), f32)
    for which, table in enumerate(tables):
        for k in range(slots):
            row = jnp.where(lane == which * slots + k, table[k].astype(f32), row)
    return row.astype(bf16)


def decode_tables(refs, rows, ints, scalars, sem):
    for i, ref in enumerate(refs):
        ints[i * 8 : i * 8 + 8] = ref[rows : rows + 16, :].astype(f32)[:8].astype(jnp.int32)
    copy = pltpu.make_async_copy(ints, scalars, sem)
    copy.start()
    return copy


def take_kernel(slots, blk, flip, at, c0, c1, c2, c3, source, weights, own, send, taken, w_v, sems):
    tables = (c0, c1, c2, c3)
    w_copy = pltpu.make_async_copy(weights, w_v, sems.at[slots])
    copies = []
    for k in range(slots):
        begin = pl.multiple_of(tables[at][k] * blk, blk)
        copies.append(pltpu.make_async_copy(source.at[:, pl.ds(begin, blk)], taken.at[k], sems.at[k]))
    for c in copies[:1] + [w_copy] + copies[1:]:
        c.start()
    rows = taken.shape[1]
    send[slots * rows :, :] = table_row(tables, slots)
    w_copy.wait()
    for k in range(slots):
        copies[k].wait()
        value = dot(taken[k], w_v[k], (1, 1) if flip else (1, 0))
        own[k] = value
        send[k * rows : (k + 1) * rows, :] = value.astype(bf16)


def sum_at(acc, targets, tables, own_at, own, peers, peer_at, slots, scratch):
    ints, scalars, sem = scratch
    rows = acc.shape[1]
    copy = decode_tables(peers, slots * rows, ints, scalars, sem) if peers else None
    for which in targets:
        for k in range(slots):
            acc[tables[which][k]] = jnp.zeros(acc.shape[1:], f32)
    for k in range(slots):
        at = tables[own_at][k]
        acc[at] = acc[at] + own[k]
    if peers:
        copy.wait()
    for i, ref in enumerate(peers):
        for k in range(slots):
            at = scalars[i * 8, peer_at * slots + k]
            acc[at] = acc[at] + ref[k * rows : (k + 1) * rows, :].astype(f32)


def send_shares(value, ref, k):
    n = ref.shape[0]
    share = value.shape[0] // n
    for d in range(n):
        ref[d, k * share : (k + 1) * share, :] = value[d * share : (d + 1) * share].astype(ref.dtype)


def hidden_kernel(dims, c0, c1, c2, c3, p_own, *refs):
    slots, n_row, n_col, n_tok = dims
    p_peers, refs = refs[: n_row - 1], refs[n_row - 1 :]
    cot, w2, slope, outs, grads, acc, *scratch = refs
    tables = (c0, c1, c2, c3)
    row = table_row(tables, slots)
    for d in range(n_col):
        outs[d, outs.shape[1] - 16 :, :] = row
    sum_at(acc, (W1_COL, W2_HID), tables, W1_COL, p_own, p_peers, W1_COL, slots, scratch)
    for k in range(slots):
        h = acc[tables[W2_HID][k]]
        active = (h * cdf(h)).astype(bf16)
        send_shares(dot(active, w2[k], (1, 0)), outs, k)
        send_shares(dot(active, cot[k], (0, 0)), grads, k)
    for k in range(slots):
        h = acc[tables[W1_COL][k]]
        slope[k] = cdf(h) + h * jnp.exp(-0.5 * h * h) * (1.0 / math.sqrt(2.0 * math.pi))


def back_kernel(dims, c0, c1, c2, c3, b_own, *refs):
    slots, n_row, n_col, n_tok = dims
    b_peers, refs = refs[: n_row - 1], refs[n_row - 1 :]
    slope, taken, w1, outs, grads, acc, *scratch = refs
    tables = (c0, c1, c2, c3)
    sum_at(acc, (W1_COL,), tables, W2_HID, b_own, b_peers, W2_HID, slots, scratch)
    for k in range(slots):
        g = (acc[tables[W1_COL][k]] * slope[k]).astype(bf16)
        send_shares(dot(g, w1[k], (1, 1)), outs, k)
        send_shares(dot(taken[k], g, (0, 0)), grads, k)


def last_kernel(dims, o_parts, i_parts, g2_parts, g1_parts, output, grad_in, gw1, gw2, acc, ints, scalars, sem):
    slots, n_row, n_col, n_tok = dims
    blk, share = acc.shape[-1], acc.shape[1]
    copy = decode_tables([o_parts.at[c] for c in range(n_col)], slots * share, ints, scalars, sem)
    for parts, result in ((g2_parts, gw2), (g1_parts, gw1)):
        for k in range(slots):
            here = slice(k * result.shape[1], (k + 1) * result.shape[1])
            total = parts[0, here, :].astype(f32)
            for d in range(1, n_tok):
                total = total + parts[d, here, :].astype(f32)
            result[k] = total
    copy.wait()
    for parts, which, result in ((o_parts, W2_OUT, output), (i_parts, W1_ROW, grad_in)):
        acc[...] = jnp.zeros(acc.shape, f32)
        for c in range(n_col):
            for k in range(slots):
                at = scalars[c * 8, which * slots + k]
                acc[at] = acc[at] + parts[c, k * share : (k + 1) * share, :].astype(f32)
        for b in range(acc.shape[0]):
            result[:, b * blk : (b + 1) * blk] = acc[b].astype(bf16)


def shards(tokens, w1_blocks, w1_rows, w1_cols, w2_blocks, w2_hidden, w2_outs, grad_out):
    slots, blk = w1_blocks.shape[2], w1_blocks.shape[-1]
    rows = tokens.shape[0]
    n_row, n_col, n_tok = (lax.axis_size(a) for a in ("row", "col", "tok"))
    dims = (slots, n_row, n_col, n_tok)
    row_blocks = tokens.shape[1] // blk
    col_blocks = FF // n_col // blk
    share, part = rows // n_col, blk // n_tok
    w1 = w1_blocks.reshape(slots, blk, blk)
    w2 = w2_blocks.reshape(slots, blk, blk)
    tables = [t.reshape(slots) for t in (w1_rows, w1_cols, w2_hidden, w2_outs)]

    S = jax.ShapeDtypeStruct
    wide, narrow = S((slots, rows, blk), f32), S((slots, rows, blk), bf16)
    message = S((slots * rows + 16, blk), bf16)

    def take(source, weights, flip, at, name):
        return pl.pallas_call(
            functools.partial(take_kernel, slots, blk, flip, at),
            out_shape=(wide, message, narrow),
            in_specs=[SMEM] * 4 + [HBM, HBM],
            out_specs=(VMEM,) * 3,
            scratch_shapes=[
                pltpu.VMEM((slots, blk, blk), bf16),
                pltpu.SemaphoreType.DMA((slots + 1,)),
            ],
            compiler_params=PARAMS,
            name=name,
        )(*tables, source, weights)

    p_own, p_send, taken = take(tokens, w1, False, W1_ROW, "take_tokens")
    p_peers = [shift(p_send, "row", d) for d in range(1, n_row)]
    b_own, b_send, cot = take(grad_out, w2, True, W2_OUT, "take_cotangent")
    b_peers = [shift(b_send, "row", d) for d in range(1, n_row)]

    parts = S((n_tok, slots * part, blk), bf16)
    scratch = [
        pltpu.VMEM((col_blocks, rows, blk), f32),
        pltpu.VMEM((8 * max(1, n_row - 1), LANES), jnp.int32),
        pltpu.SMEM((8 * max(1, n_row - 1), LANES), jnp.int32),
        pltpu.SemaphoreType.DMA,
    ]
    slope, o_sent, g2_sent = pl.pallas_call(
        functools.partial(hidden_kernel, dims),
        out_shape=(wide, S((n_col, slots * share + 16, blk), bf16), parts),
        in_specs=[SMEM] * 4 + [VMEM] * (n_row + 2),
        out_specs=(VMEM,) * 3,
        scratch_shapes=scratch,
        compiler_params=PARAMS,
        name="hidden",
    )(*tables, p_own, *p_peers, cot, w2)
    o_parts = lax.all_to_all(o_sent, "col", 0, 0, tiled=True)
    g2_parts = lax.all_to_all(g2_sent, "tok", 0, 0, tiled=True)

    i_sent, g1_sent = pl.pallas_call(
        functools.partial(back_kernel, dims),
        out_shape=(S((n_col, slots * share, blk), bf16), parts),
        in_specs=[SMEM] * 4 + [VMEM] * (n_row + 3),
        out_specs=(VMEM,) * 2,
        scratch_shapes=scratch,
        compiler_params=PARAMS,
        name="back",
    )(*tables, b_own, *b_peers, slope, taken, w1)
    i_parts = lax.all_to_all(i_sent, "col", 0, 0, tiled=True)
    g1_parts = lax.all_to_all(g1_sent, "tok", 0, 0, tiled=True)

    summed = S((slots, part, blk), f32)
    output, grad_in, gw1, gw2 = pl.pallas_call(
        functools.partial(last_kernel, dims),
        out_shape=(
            S((share, row_blocks * blk), bf16),
            S((share, row_blocks * blk), bf16),
            summed,
            summed,
        ),
        in_specs=[VMEM] * 4,
        out_specs=(VMEM,) * 4,
        scratch_shapes=[
            pltpu.VMEM((row_blocks, share, blk), f32),
            pltpu.VMEM((8 * n_col, LANES), jnp.int32),
            pltpu.SMEM((8 * n_col, LANES), jnp.int32),
            pltpu.SemaphoreType.DMA,
        ],
        compiler_params=PARAMS,
        name="add_up",
    )(o_parts, i_parts, g2_parts, g1_parts)
    return (output, grad_in, gw1.reshape(1, 1, slots, part, blk), gw2.reshape(1, 1, slots, part, blk))


def solution(mesh):
    placed = (
        P("tok", "row"),
        P("row", "col", None, None, None),
        P("row", "col", None),
        P("row", "col", None),
        P("row", "col", None, None, None),
        P("row", "col", None),
        P("row", "col", None),
        P("tok", "row"),
    )
    return jax.shard_map(
        shards,
        mesh=mesh,
        in_specs=placed,
        out_specs=(
            P(("tok", "col"), "row"),
            P(("tok", "col"), "row"),
            P("row", "col", None, "tok", None),
            P("row", "col", None, "tok", None),
        ),
        check_vma=False,
    )
```

time: 53.1 us -> 66.6 us (1.25)
  blocking collectives: 16.1 us -> 42 us
  starting transfers between devices: 17.1 us -> 3.1 us
  waiting for transfers between devices: 5.31 us -> 8.19 us
  local copies, waits for them, and re-layouts: 5.02 us -> 2.86 us
  Pallas kernels: 8.52 us -> 9.38 us
    all_to_all x0 -> x4, blocking collectives: none -> 42 us  [the longest x1 13.7 us: shards(): g2_parts = lax.all_to_all(g2_sent, 'tok', 0, 0, tiled=True)]
    all_gather x1 -> x0, blocking collectives: 16.1 us -> none  [shards(): tabs = lax.all_gather(tab, ('row', 'col'))]
    ppermute x14 -> x2, starting transfers between devices: 17.1 us -> 3.1 us  [shift(): return lax.ppermute(x, axis, [(i, (i + by) % n) for i in range(n)])]
    ppermute x14 -> x2, waiting for transfers between devices: 5.31 us -> 8.19 us  [shift(): return lax.ppermute(x, axis, [(i, (i + by) % n) for i in range(n)])]
    unnamed x20 -> x18, local copies, waits for them, and re-layouts: 5.02 us -> 2.86 us
    pallas_call x3 -> x4, Pallas kernels: 6.45 us -> 7.4 us  [the longest x2 4.04 us: take(): pl.pallas_call(functools.partial(take_kernel, slots, blk, flip, at), out_...]
  transfers between devices with their start and end apart: 14 -> 2, of which waited for: 4 -> 2; matrix products, arithmetic and copies ran while one was open for 0% -> 0% of each run, Pallas kernels for 6% -> 6%
where the time goes in v2:
time: 66.6 us; the launch traced here: 66.2 us
  blocking collectives  42 us (63%)
  Pallas kernels  9.38 us (14%)
  waiting for transfers between devices  8.19 us (12%)
  starting transfers between devices  3.1 us (5%)
  local copies, waits for them, and re-layouts  2.86 us (4%)
  between operations  0.71 us (1%)
    all_to_all x1, blocking collectives, shards(): g2_parts = lax.all_to_all(g2_sent, 'tok', 0, 0, tiled=True)  13.7 us
    all_to_all x1, blocking collectives, shards(): g1_parts = lax.all_to_all(g1_sent, 'tok', 0, 0, tiled=True)  10.8 us
    all_to_all x1, blocking collectives, shards(): i_parts = lax.all_to_all(i_sent, 'col', 0, 0, tiled=True)  8.88 us
    all_to_all x1, blocking collectives, shards(): o_parts = lax.all_to_all(o_sent, 'col', 0, 0, tiled=True)  8.56 us
    ppermute x2, waiting for transfers between devices, shift(): return lax.ppermute(x, axis, [(i, (i + by) % n) for i in range(n)])  8.19 us
    pallas_call x2, Pallas kernels, take(): pl.pallas_call(functools.partial(take_kernel, slots, blk, flip, at), out_...  4.04 us
    ppermute x2, starting transfers between devices, shift(): return lax.ppermute(x, axis, [(i, (i + by) % n) for i in range(n)])  3.1 us
    unnamed x18, local copies, waits for them, and re-layouts  2.86 us
  transfers between devices with their start and end apart: 2, of which 2 were waited for; matrix products, arithmetic and copies ran while one was open for 0% of the time, Pallas kernels for 6%

profile of v2, /device:TPU:0, one launch (start us, length us, event | category | flops | bytes accessed | tf_op | source)
XLA Modules:
  0.0 66.2 jit_solution(11395526818687800250)
XLA Ops:
  0.6 0.0 copy-start.8
  0.6 0.0 copy-start.5
  0.7 0.0 copy-start.6
  0.7 0.0 copy-start.7
  0.7 0.6 copy-done.8
  1.3 0.0 copy-done.5
  1.3 0.0 copy-done.6
  1.3 0.0 copy-done.7
  1.3 0.0 copy-start.1
  1.3 1.2 %copy-done.1 = bf16[128,4096]{1,0:T(8,128)(2,1)S(1)} copy-done((bf16[128,4096]{1,0:T(8,128)(2,1)S(1)}, bf16[128,4096]{1,0:T(8,128)(2,1)}, u32[]{:S(2)}) %copy-start.1) | copy-done | bytes 1048600
  2.6 0.0 copy-start.3
  2.6 0.9 %copy-done.3 = bf16[1,1,8,128,128]{4,3,2,1,0:T(8,128)(2,1)S(1)} copy-done((bf16[1,1,8,128,128]{4,3,2,1,0:T(8,128)(2,1)S(1)}, bf16[1,1,8,128,128]{4,3,2,1,0:T(8,128)(2,1)}, u32[]{:S(2)}) %copy-start.3) | copy-done | bytes 262168
  3.5 0.0 copy-start
  3.5 0.0 copy-start.2
  3.5 2.0 %take_tokens.1 = (f32[8,128,128]{2,1,0:T(8,128)S(1)}, bf16[1040,128]{1,0:T(8,128)(2,1)S(1)}, bf16[8,128,128]{2,1,0:T(8,128)(2,1)S(1)}) custom-call(s32[8]{0:T(128)S(1)} %bitcast.12, s32[8]{0:T(128)S(1)} %bitcast.16, s32[8]{0:T(128)S(1)} %bitcast.20, s32[8]{0:T(128)S(1)} %bitcast.24, bf16[128,4096]{1,0:T(8,128)(2,1)S(1)} %copy-done.1, ...), custom_call_target="tpu_custom_call" | custom-call | tf_op jit(solution)/shard_map/take_tokens/pallas_call | solution.py:169
  5.5 3.0 %collective-permute-start = (bf16[1040,128]{1,0:T(8,128)(2,1)S(1)}, bf16[1040,128]{1,0:T(8,128)(2,1)S(1)}, u32[]{:S(2)}, u32[]{:S(2)}) collective-permute-start(bf16[1040,128]{1,0:T(8,128)(2,1)S(1)} %get-tuple-element.20), channel_id=1, source_target_pairs={{0,4},{4,0},{1,5},{5,1},{2,6},{6,2},{3,7},{7,3},{8,12},{12,8},{9,1... | collective-permute-start | bytes 798728 | tf_op jit(solution)/shard_map/ppermute | solution.py:31
  8.5 0.0 copy-done
  8.5 0.0 copy-done.2
  8.5 2.1 %take_cotangent.1 = (f32[8,128,128]{2,1,0:T(8,128)S(1)}, bf16[1040,128]{1,0:T(8,128)(2,1)S(1)}, bf16[8,128,128]{2,1,0:T(8,128)(2,1)S(1)}) custom-call(s32[8]{0:T(128)S(1)} %bitcast.13, s32[8]{0:T(128)S(1)} %bitcast.17, s32[8]{0:T(128)S(1)} %bitcast.21, s32[8]{0:T(128)S(1)} %bitcast.25, bf16[128,4096]{1,0:T(8,128)(2,1)S(1)} %copy-done.2, ...), custom_call_target="tpu_custom_call" | custom-call | tf_op jit(solution)/shard_map/take_cotangent/pallas_call | solution.py:169
  10.6 0.1 collective-permute-start.1
  10.7 5.0 %collective-permute-done.refs_0_ = bf16[1040,128]{1,0:T(8,128)(2,1)S(1)} collective-permute-done((bf16[1040,128]{1,0:T(8,128)(2,1)S(1)}, bf16[1040,128]{1,0:T(8,128)(2,1)S(1)}, u32[]{:S(2)}, u32[]{:S(2)}) %collective-permute-start) | collective-permute-done | bytes 266272 | tf_op jit(solution)/shard_map/ppermute | solution.py:31
  15.7 0.0 copy-start.4
  15.7 1.7 %hidden.1 = (f32[8,128,128]{2,1,0:T(8,128)S(1)}, bf16[4,272,128]{2,1,0:T(8,128)(2,1)S(1)}, bf16[4,256,128]{2,1,0:T(8,128)(2,1)S(1)}) custom-call(s32[8]{0:T(128)S(1)} %bitcast.14, s32[8]{0:T(128)S(1)} %bitcast.18, s32[8]{0:T(128)S(1)} %bitcast.22, s32[8]{0:T(128)S(1)} %bitcast.26, f32[8,128,128]{2,1,0:T(8,128)S(1)} %get-tuple-element.19.p_own, ...), custom_call_target="tpu_custom_call" | custom-call | tf_op jit(solution)/shard_map/hidden/pallas_call | solution.py:194
  17.4 3.2 %collective-permute-done.1.refs_0_ = bf16[1040,128]{1,0:T(8,128)(2,1)S(1)} collective-permute-done((bf16[1040,128]{1,0:T(8,128)(2,1)S(1)}, bf16[1040,128]{1,0:T(8,128)(2,1)S(1)}, u32[]{:S(2)}, u32[]{:S(2)}) %collective-permute-start.1) | collective-permute-done | bytes 266272 | tf_op jit(solution)/shard_map/ppermute | solution.py:31
  20.6 0.0 copy-done.4
  20.6 1.7 %back.1 = (bf16[4,256,128]{2,1,0:T(8,128)(2,1)S(1)}, bf16[4,256,128]{2,1,0:T(8,128)(2,1)S(1)}) custom-call(s32[8]{0:T(128)S(1)} %bitcast.15, s32[8]{0:T(128)S(1)} %bitcast.19, s32[8]{0:T(128)S(1)} %bitcast.23, s32[8]{0:T(128)S(1)} %bitcast.27, f32[8,128,128]{2,1,0:T(8,128)S(1)} %get-tuple-element.23.b_own, ...), custom_call_target="tpu_custom_call" | custom-call | tf_op jit(solution)/shard_map/back/pallas_call | solution.py:206
  22.2 8.9 %all_to_all.20.i_parts = bf16[4,256,128]{2,1,0:T(8,128)(2,1)S(1)} all-to-all(bf16[4,256,128]{2,1,0:T(8,128)(2,1)S(1)} %get-tuple-element.27), channel_id=1, replica_groups=mesh['tok'=4,'row'=2,'col'=4] {'col'}, dimensions={0} | all-to-all | bytes 524288 | tf_op jit(solution)/shard_map/all_to_all | solution.py:215
  31.1 8.6 %all_to_all.21.o_parts = bf16[4,272,128]{2,1,0:T(8,128)(2,1)S(1)} all-to-all(bf16[4,272,128]{2,1,0:T(8,128)(2,1)S(1)} %get-tuple-element.22), channel_id=1, replica_groups=mesh['tok'=4,'row'=2,'col'=4] {'col'}, dimensions={0} | all-to-all | bytes 557056 | tf_op jit(solution)/shard_map/all_to_all | solution.py:203
  39.7 13.7 %all_to_all.22.g2_parts = bf16[4,256,128]{2,1,0:T(8,128)(2,1)S(1)} all-to-all(bf16[4,256,128]{2,1,0:T(8,128)(2,1)S(1)} %get-tuple-element.28), channel_id=1, replica_groups=mesh['tok'=4,'row'=2,'col'=4] {'tok'}, dimensions={0} | all-to-all | bytes 524288 | tf_op jit(solution)/shard_map/all_to_all | solution.py:204
  53.4 10.8 %all_to_all.23.g1_parts = bf16[4,256,128]{2,1,0:T(8,128)(2,1)S(1)} all-to-all(bf16[4,256,128]{2,1,0:T(8,128)(2,1)S(1)} %get-tuple-element.29), channel_id=1, replica_groups=mesh['tok'=4,'row'=2,'col'=4] {'tok'}, dimensions={0} | all-to-all | bytes 524288 | tf_op jit(solution)/shard_map/all_to_all | solution.py:216
  64.2 2.0 %add_up.1 = (bf16[32,4096]{1,0:T(8,128)(2,1)}, bf16[32,4096]{1,0:T(8,128)(2,1)}, f32[8,32,128]{2,1,0:T(8,128)}, f32[8,32,128]{2,1,0:T(8,128)}) custom-call(bf16[4,272,128]{2,1,0:T(8,128)(2,1)S(1)} %all_to_all.21.o_parts, bf16[4,256,128]{2,1,0:T(8,128)(2,1)S(1)} %all_to_all.20.i_parts, bf16[4,256,128]{2,1,0:T(8,128)(2,1)S(1)} %all_to_all.22.g2_parts, ...), custom_call_target="tpu_custom_call" | custom-call | tf_op jit(solution)/shard_map/add_up/pallas_call | solution.py:219
Async XLA Ops:
  0.6 0.7 copy-start.8
  0.6 0.7 copy-start.5
  0.7 0.7 %copy-start.6 = (s32[1,1,8]{2,1,0:T(1,128)S(1)}, s32[1,1,8]{2,1,0:T(1,128)}, u32[]{:S(2)}) copy-start(s32[1,1,8]{2,1,0:T(1,128)} %param.11) | copy-start | bytes 100
  0.7 0.7 %copy-start.7 = (s32[1,1,8]{2,1,0:T(1,128)S(1)}, s32[1,1,8]{2,1,0:T(1,128)}, u32[]{:S(2)}) copy-start(s32[1,1,8]{2,1,0:T(1,128)} %param.13) | copy-start | bytes 100
  1.3 1.2 %copy-start.1 = (bf16[128,4096]{1,0:T(8,128)(2,1)S(1)}, bf16[128,4096]{1,0:T(8,128)(2,1)}, u32[]{:S(2)}) copy-start(bf16[128,4096]{1,0:T(8,128)(2,1)} %source.2) | copy-start | bytes 3145732
  2.6 0.9 %copy-start.3 = (bf16[1,1,8,128,128]{4,3,2,1,0:T(8,128)(2,1)S(1)}, bf16[1,1,8,128,128]{4,3,2,1,0:T(8,128)(2,1)}, u32[]{:S(2)}) copy-start(bf16[1,1,8,128,128]{4,3,2,1,0:T(8,128)(2,1)} %param.9) | copy-start | bytes 786436
  3.5 5.0 %copy-start = (bf16[1,1,8,128,128]{4,3,2,1,0:T(8,128)(2,1)S(1)}, bf16[1,1,8,128,128]{4,3,2,1,0:T(8,128)(2,1)}, u32[]{:S(2)}) copy-start(bf16[1,1,8,128,128]{4,3,2,1,0:T(8,128)(2,1)} %param.12) | copy-start | bytes 786436
  3.5 5.0 %copy-start.2 = (bf16[128,4096]{1,0:T(8,128)(2,1)S(1)}, bf16[128,4096]{1,0:T(8,128)(2,1)}, u32[]{:S(2)}) copy-start(bf16[128,4096]{1,0:T(8,128)(2,1)} %source.3) | copy-start | bytes 3145732
  5.5 10.2 %collective-permute-start = (bf16[1040,128]{1,0:T(8,128)(2,1)S(1)}, bf16[1040,128]{1,0:T(8,128)(2,1)S(1)}, u32[]{:S(2)}, u32[]{:S(2)}) collective-permute-start(bf16[1040,128]{1,0:T(8,128)(2,1)S(1)} %get-tuple-element.20), channel_id=1, source_target_pairs={{0,4},{4,0},{1,5},{5,1},{2,6},{6,2},{3,7},{7,3},{8,12},{12,8},{9,1... | collective-permute-start | bytes 798728 | tf_op jit(solution)/shard_map/ppermute | solution.py:31
  10.6 10.0 %collective-permute-start.1 = (bf16[1040,128]{1,0:T(8,128)(2,1)S(1)}, bf16[1040,128]{1,0:T(8,128)(2,1)S(1)}, u32[]{:S(2)}, u32[]{:S(2)}) collective-permute-start(bf16[1040,128]{1,0:T(8,128)(2,1)S(1)} %get-tuple-element.24), channel_id=1, source_target_pairs={{0,4},{4,0},{1,5},{5,1},{2,6},{6,2},{3,7},{7,3},{8,12},{12,8},{9,1... | collective-permute-start | bytes 798728 | tf_op jit(solution)/shard_map/ppermute | solution.py:31
  15.7 4.9 %copy-start.4 = (bf16[1,1,8,128,128]{4,3,2,1,0:T(8,128)(2,1)S(1)}, bf16[1,1,8,128,128]{4,3,2,1,0:T(8,128)(2,1)}, u32[]{:S(2)}) copy-start(bf16[1,1,8,128,128]{4,3,2,1,0:T(8,128)(2,1)} %param.9) | copy-start | bytes 786436

commit v3 on v2

--- a/solution.py
+++ b/solution.py
@@ -17,6 +17,8 @@
 LANES = 128
 PARAMS = pltpu.CompilerParams(vmem_limit_bytes=32 * 1024 * 1024)
 
+TAKE_LIMIT = 62 * 1024 * 1024
+
 W1_ROW, W1_COL, W2_HID, W2_OUT = range(4)
 
 
@@ -24,11 +26,19 @@
     return lax.dot_general(a, b, ((contract[:1], contract[1:]), ((), ())), preferred_element_type=f32)
 
 
-def shift(x, axis, by):
+def partner(i, d, n):
+    return i ^ d if n & (n - 1) == 0 else (i + d) % n
+
+
+def send(x, axis, d):
     n = lax.axis_size(axis)
-    if by % n == 0:
-        return x
-    return lax.ppermute(x, axis, [(i, (i + by) % n) for i in range(n)])
+    return lax.ppermute(x, axis, [(i, partner(i, d, n)) for i in range(n)]) if d else x
+
+
+def target(axis, d):
+    n = lax.axis_size(axis)
+    me = lax.axis_index(axis)
+    return jnp.bitwise_xor(me, d) if n & (n - 1) == 0 else lax.rem(me + d, n)
 
 
 def cdf(v):
@@ -52,7 +62,7 @@
     return copy
 
 
-def take_kernel(slots, blk, flip, at, c0, c1, c2, c3, source, weights, own, send, taken, w_v, sems):
+def take_kernel(slots, blk, flip, at, c0, c1, c2, c3, source, weights, own, message, taken, w_v, sems):
     tables = (c0, c1, c2, c3)
     w_copy = pltpu.make_async_copy(weights, w_v, sems.at[slots])
     copies = []
@@ -62,13 +72,13 @@
     for c in copies[:1] + [w_copy] + copies[1:]:
         c.start()
     rows = taken.shape[1]
-    send[slots * rows :, :] = table_row(tables, slots)
+    message[slots * rows :, :] = table_row(tables, slots)
     w_copy.wait()
     for k in range(slots):
         copies[k].wait()
         value = dot(taken[k], w_v[k], (1, 1) if flip else (1, 0))
         own[k] = value
-        send[k * rows : (k + 1) * rows, :] = value.astype(bf16)
+        message[k * rows : (k + 1) * rows, :] = value.astype(bf16)
 
 
 def sum_at(acc, targets, tables, own_at, own, peers, peer_at, slots, scratch):
@@ -89,27 +99,27 @@
             acc[at] = acc[at] + ref[k * rows : (k + 1) * rows, :].astype(f32)
 
 
-def send_shares(value, ref, k):
-    n = ref.shape[0]
-    share = value.shape[0] // n
-    for d in range(n):
-        ref[d, k * share : (k + 1) * share, :] = value[d * share : (d + 1) * share].astype(ref.dtype)
+def cut(value, refs, k, axis):
+    share = value.shape[0] // len(refs)
+    for d, ref in enumerate(refs):
+        begin = pl.multiple_of(target(axis, d) * share, share)
+        ref[k * share : (k + 1) * share, :] = value[pl.ds(begin, share), :].astype(ref.dtype)
 
 
 def hidden_kernel(dims, c0, c1, c2, c3, p_own, *refs):
     slots, n_row, n_col, n_tok = dims
     p_peers, refs = refs[: n_row - 1], refs[n_row - 1 :]
-    cot, w2, slope, outs, grads, acc, *scratch = refs
+    cot, w2, slope, out = refs[:4]
+    grads, refs = refs[4 : 4 + n_tok], refs[4 + n_tok :]
+    acc, value, grad, *scratch = refs
     tables = (c0, c1, c2, c3)
-    row = table_row(tables, slots)
-    for d in range(n_col):
-        outs[d, outs.shape[1] - 16 :, :] = row
     sum_at(acc, (W1_COL, W2_HID), tables, W1_COL, p_own, p_peers, W1_COL, slots, scratch)
     for k in range(slots):
         h = acc[tables[W2_HID][k]]
         active = (h * cdf(h)).astype(bf16)
-        send_shares(dot(active, w2[k], (1, 0)), outs, k)
-        send_shares(dot(active, cot[k], (0, 0)), grads, k)
+        grad[k] = dot(active, cot[k], (0, 0))
+        cut(grad.at[k], grads, k, "tok")
+        out[k] = dot(active, w2[k], (1, 0)).astype(bf16)
     for k in range(slots):
         h = acc[tables[W1_COL][k]]
         slope[k] = cdf(h) + h * jnp.exp(-0.5 * h * h) * (1.0 / math.sqrt(2.0 * math.pi))
@@ -118,33 +128,48 @@
 def back_kernel(dims, c0, c1, c2, c3, b_own, *refs):
     slots, n_row, n_col, n_tok = dims
     b_peers, refs = refs[: n_row - 1], refs[n_row - 1 :]
-    slope, taken, w1, outs, grads, acc, *scratch = refs
+    slope, taken, w1, out = refs[:4]
+    refs = refs[4:]
+    outs, refs = refs[:n_col], refs[n_col:]
+    grads, refs = refs[:n_tok], refs[n_tok:]
+    acc, value, grad, *scratch = refs
     tables = (c0, c1, c2, c3)
+    row = table_row(tables, slots)
+    for ref in outs:
+        ref[ref.shape[0] - 16 :, :] = row
     sum_at(acc, (W1_COL,), tables, W2_HID, b_own, b_peers, W2_HID, slots, scratch)
     for k in range(slots):
         g = (acc[tables[W1_COL][k]] * slope[k]).astype(bf16)
-        send_shares(dot(g, w1[k], (1, 1)), outs, k)
-        send_shares(dot(taken[k], g, (0, 0)), grads, k)
-
-
-def last_kernel(dims, o_parts, i_parts, g2_parts, g1_parts, output, grad_in, gw1, gw2, acc, ints, scalars, sem):
+        grad[k] = dot(taken[k], g, (0, 0))
+        cut(grad.at[k], grads, k, "tok")
+        value[...] = dot(g, w1[k], (1, 1))
+        cut(out.at[k], outs, k, "col")
+        cut(value, outs, slots + k, "col")
+
+
+def last_kernel(dims, *refs):
     slots, n_row, n_col, n_tok = dims
+    o_parts, refs = refs[:n_col], refs[n_col:]
+    g2_parts, refs = refs[:n_tok], refs[n_tok:]
+    g1_parts, refs = refs[:n_tok], refs[n_tok:]
+    output, grad_in, gw1, gw2, acc, ints, scalars, sem = refs
     blk, share = acc.shape[-1], acc.shape[1]
-    copy = decode_tables([o_parts.at[c] for c in range(n_col)], slots * share, ints, scalars, sem)
+    copy = decode_tables(o_parts, 2 * slots * share, ints, scalars, sem)
     for parts, result in ((g2_parts, gw2), (g1_parts, gw1)):
         for k in range(slots):
             here = slice(k * result.shape[1], (k + 1) * result.shape[1])
-            total = parts[0, here, :].astype(f32)
-            for d in range(1, n_tok):
-                total = total + parts[d, here, :].astype(f32)
+            total = parts[0][here, :].astype(f32)
+            for ref in parts[1:]:
+                total = total + ref[here, :].astype(f32)
             result[k] = total
     copy.wait()
-    for parts, which, result in ((o_parts, W2_OUT, output), (i_parts, W1_ROW, grad_in)):
+    for first, which, result in ((0, W2_OUT, output), (slots, W1_ROW, grad_in)):
         acc[...] = jnp.zeros(acc.shape, f32)
-        for c in range(n_col):
+        for c, ref in enumerate(o_parts):
             for k in range(slots):
                 at = scalars[c * 8, which * slots + k]
-                acc[at] = acc[at] + parts[c, k * share : (k + 1) * share, :].astype(f32)
+                here = slice((first + k) * share, (first + k + 1) * share)
+                acc[at] = acc[at] + ref[here, :].astype(f32)
         for b in range(acc.shape[0]):
             result[:, b * blk : (b + 1) * blk] = acc[b].astype(bf16)
 
@@ -175,45 +200,47 @@
                 pltpu.VMEM((slots, blk, blk), bf16),
                 pltpu.SemaphoreType.DMA((slots + 1,)),
             ],
-            compiler_params=PARAMS,
+            compiler_params=pltpu.CompilerParams(vmem_limit_bytes=TAKE_LIMIT),
             name=name,
         )(*tables, source, weights)
 
     p_own, p_send, taken = take(tokens, w1, False, W1_ROW, "take_tokens")
-    p_peers = [shift(p_send, "row", d) for d in range(1, n_row)]
+    p_peers = [send(p_send, "row", d) for d in range(1, n_row)]
     b_own, b_send, cot = take(grad_out, w2, True, W2_OUT, "take_cotangent")
-    b_peers = [shift(b_send, "row", d) for d in range(1, n_row)]
-
-    parts = S((n_tok, slots * part, blk), bf16)
+    b_peers = [send(b_send, "row", d) for d in range(1, n_row)]
+
+    parts = (S((slots * part, blk), bf16),) * n_tok
+    outs = (S((2 * slots * share + 16, blk), bf16),) * n_col
     scratch = [
         pltpu.VMEM((col_blocks, rows, blk), f32),
+        pltpu.VMEM((rows, blk), f32),
+        pltpu.VMEM((slots, blk, blk), f32),
         pltpu.VMEM((8 * max(1, n_row - 1), LANES), jnp.int32),
         pltpu.SMEM((8 * max(1, n_row - 1), LANES), jnp.int32),
         pltpu.SemaphoreType.DMA,
     ]
-    slope, o_sent, g2_sent = pl.pallas_call(
+    slope, out, *g2_sent = pl.pallas_call(
         functools.partial(hidden_kernel, dims),
-        out_shape=(wide, S((n_col, slots * share + 16, blk), bf16), parts),
+        out_shape=(wide, narrow) + parts,
         in_specs=[SMEM] * 4 + [VMEM] * (n_row + 2),
-        out_specs=(VMEM,) * 3,
+        out_specs=(VMEM,) * (2 + n_tok),
         scratch_shapes=scratch,
         compiler_params=PARAMS,
         name="hidden",
     )(*tables, p_own, *p_peers, cot, w2)
-    o_parts = lax.all_to_all(o_sent, "col", 0, 0, tiled=True)
-    g2_parts = lax.all_to_all(g2_sent, "tok", 0, 0, tiled=True)
-
-    i_sent, g1_sent = pl.pallas_call(
+    g2_parts = [send(x, "tok", d) for d, x in enumerate(g2_sent)]
+
+    sent = pl.pallas_call(
         functools.partial(back_kernel, dims),
-        out_shape=(S((n_col, slots * share, blk), bf16), parts),
-        in_specs=[SMEM] * 4 + [VMEM] * (n_row + 3),
-        out_specs=(VMEM,) * 2,
+        out_shape=outs + parts,
+        in_specs=[SMEM] * 4 + [VMEM] * (n_row + 4),
+        out_specs=(VMEM,) * (n_col + n_tok),
         scratch_shapes=scratch,
         compiler_params=PARAMS,
         name="back",
-    )(*tables, b_own, *b_peers, slope, taken, w1)
-    i_parts = lax.all_to_all(i_sent, "col", 0, 0, tiled=True)
-    g1_parts = lax.all_to_all(g1_sent, "tok", 0, 0, tiled=True)
+    )(*tables, b_own, *b_peers, slope, taken, w1, out)
+    g1_parts = [send(x, "tok", d) for d, x in enumerate(sent[n_col:])]
+    o_parts = [send(x, "col", d) for d, x in enumerate(sent[:n_col])]
 
     summed = S((slots, part, blk), f32)
     output, grad_in, gw1, gw2 = pl.pallas_call(
@@ -224,7 +251,7 @@
             summed,
             summed,
         ),
-        in_specs=[VMEM] * 4,
+        in_specs=[VMEM] * (n_col + 2 * n_tok),
         out_specs=(VMEM,) * 4,
         scratch_shapes=[
             pltpu.VMEM((row_blocks, share, blk), f32),
@@ -234,7 +261,7 @@
         ],
         compiler_params=PARAMS,
         name="add_up",
-    )(o_parts, i_parts, g2_parts, g1_parts)
+    )(*o_parts, *g2_parts, *g1_parts)
     return (output, grad_in, gw1.reshape(1, 1, slots, part, blk), gw2.reshape(1, 1, slots, part, blk))
 
 

time: 66.6 us -> 41.6 us (0.62)
  blocking collectives: 42 us -> 0 us
  starting transfers between devices: 3.1 us -> 12.8 us
  waiting for transfers between devices: 8.19 us -> 12.7 us
  Pallas kernels: 9.38 us -> 13.5 us
  local copies, waits for them, and re-layouts: 2.86 us -> 1.63 us
    all_to_all x4 -> x0, blocking collectives: 42 us -> none  [the longest x1 13.7 us: shards(): g2_parts = lax.all_to_all(g2_sent, 'tok', 0, 0, tiled=True)]
    ppermute x2 -> x11, starting transfers between devices: 3.1 us -> 12.8 us  [send(): lax.ppermute(x, axis, [(i, partner(i, d, n)) for i in range(n)])]
    ppermute x2 -> x11, waiting for transfers between devices: 8.19 us -> 12.7 us  [send(): lax.ppermute(x, axis, [(i, partner(i, d, n)) for i in range(n)])]
    pallas_call x2, Pallas kernels: 4.04 us -> 8.04 us  [take(): pl.pallas_call(functools.partial(take_kernel, slots, blk, flip, at), out_...]
    unnamed x18 -> x20, local copies, waits for them, and re-layouts: 2.86 us -> 1.63 us
  transfers between devices with their start and end apart: 2 -> 11, of which waited for: 2 -> 4; matrix products, arithmetic and copies ran while one was open for 0% -> 0% of each run, Pallas kernels for 6% -> 18%
where the time goes in v3:
time: 41.6 us; the launch traced here: 41.4 us
  Pallas kernels  13.5 us (32%)
  starting transfers between devices  12.8 us (31%)
  waiting for transfers between devices  12.7 us (31%)
  local copies, waits for them, and re-layouts  1.63 us (4%)
  between operations  0.73 us (2%)
    ppermute x11, starting transfers between devices, send(): lax.ppermute(x, axis, [(i, partner(i, d, n)) for i in range(n)])  12.8 us
    ppermute x11, waiting for transfers between devices, send(): lax.ppermute(x, axis, [(i, partner(i, d, n)) for i in range(n)])  12.7 us
    pallas_call x2, Pallas kernels, take(): pl.pallas_call(functools.partial(take_kernel, slots, blk, flip, at), out_...  8.04 us
    pallas_call x1, Pallas kernels, shards(): pl.pallas_call(functools.partial(last_kernel, dims), out_shape=(S((share,...  2.05 us
    pallas_call x1, Pallas kernels, shards(): pl.pallas_call(functools.partial(back_kernel, dims), out_shape=outs + par...  1.72 us
    pallas_call x1, Pallas kernels, shards(): pl.pallas_call(functools.partial(hidden_kernel, dims), out_shape=(wide, n...  1.69 us
    unnamed x20, local copies, waits for them, and re-layouts  1.63 us
  transfers between devices with their start and end apart: 11, of which 4 were waited for; matrix products, arithmetic and copies ran while one was open for 0% of the time, Pallas kernels for 18%

profile of v3, /device:TPU:0, one launch (start us, length us, event | category | flops | bytes accessed | tf_op | source)
XLA Modules:
  0.0 41.4 jit_solution(3764561191353239745)
XLA Ops:
  0.6 3.9 %take_tokens.1 = (f32[8,128,128]{2,1,0:T(8,128)}, bf16[1040,128]{1,0:T(8,128)(2,1)}, bf16[8,128,128]{2,1,0:T(8,128)(2,1)}) custom-call(s32[8]{0:T(128)} %bitcast.12, s32[8]{0:T(128)} %bitcast.16, s32[8]{0:T(128)} %bitcast.20, s32[8]{0:T(128)} %bitcast.24, bf16[128,4096]{1,0:T(8,128)(2,1)} %source.3, bf16[8,128,128]{2,1,0:T(8,128)(2,1)} %bitcast.10), custom_call_target="tpu_custom_call" | custom-call | tf_op jit(solution)/shard_map/take_tokens/pallas_call | solution.py:194
  4.5 3.0 %collective-permute-start.1 = (bf16[1040,128]{1,0:T(8,128)(2,1)}, bf16[1040,128]{1,0:T(8,128)(2,1)S(1)}, u32[]{:S(2)}, u32[]{:S(2)}) collective-permute-start(bf16[1040,128]{1,0:T(8,128)(2,1)} %get-tuple-element.31), channel_id=1, source_target_pairs={{0,4},{4,0},{1,5},{5,1},{2,6},{6,2},{3,7},{7,3},{8,12},{12,8},{9,1... | collective-permute-start | bytes 798728 | tf_op jit(solution)/shard_map/ppermute | solution.py:35
  7.5 0.0 copy-start
  7.5 0.0 copy-start.3
  7.5 0.0 copy-start.9
  7.5 4.1 %take_cotangent.1 = (f32[8,128,128]{2,1,0:T(8,128)}, bf16[1040,128]{1,0:T(8,128)(2,1)}, bf16[8,128,128]{2,1,0:T(8,128)(2,1)}) custom-call(s32[8]{0:T(128)} %bitcast.13, s32[8]{0:T(128)} %bitcast.17, s32[8]{0:T(128)} %bitcast.21, s32[8]{0:T(128)} %bitcast.25, bf16[128,4096]{1,0:T(8,128)(2,1)} %source.2, bf16[8,128,128]{2,1,0:T(8,128)(2,1)} %bitcast.8), custom_call_target="tpu_custom_call" | custom-call | tf_op jit(solution)/shard_map/take_cotangent/pallas_call | solution.py:194
  11.7 0.1 collective-permute-start
  11.8 2.8 %collective-permute-done.1.refs_0_ = bf16[1040,128]{1,0:T(8,128)(2,1)S(1)} collective-permute-done((bf16[1040,128]{1,0:T(8,128)(2,1)}, bf16[1040,128]{1,0:T(8,128)(2,1)S(1)}, u32[]{:S(2)}, u32[]{:S(2)}) %collective-permute-start.1) | collective-permute-done | bytes 266272 | tf_op jit(solution)/shard_map/ppermute | solution.py:35
  14.6 0.0 copy-start.6
  14.6 0.0 copy-start.7
  14.6 0.0 copy-start.8
  14.6 0.0 copy-done
  14.7 0.0 copy-done.3
  14.7 0.0 copy-done.9
  14.7 0.6 %copy-done.6 = s32[1,1,8]{2,1,0:T(1,128)S(1)} copy-done((s32[1,1,8]{2,1,0:T(1,128)S(1)}, s32[1,1,8]{2,1,0:T(1,128)}, u32[]{:S(2)}) %copy-start.6) | copy-done | bytes 56
  15.3 0.0 copy-done.7
  15.3 0.0 copy-done.8
  15.3 0.0 copy-start.5
  15.3 0.9 %copy-done.5 = bf16[8,128,128]{2,1,0:T(8,128)(2,1)S(1)} copy-done((bf16[8,128,128]{2,1,0:T(8,128)(2,1)S(1)}, bf16[8,128,128]{2,1,0:T(8,128)(2,1)}, u32[]{:S(2)}) %copy-start.5) | copy-done | bytes 262168
  16.3 0.0 copy-start.1
  16.3 0.0 copy-start.2
  16.3 0.0 copy-start.4
  16.3 1.7 %hidden.1 = (f32[8,128,128]{2,1,0:T(8,128)S(1)}, bf16[8,128,128]{2,1,0:T(8,128)(2,1)S(1)}, bf16[256,128]{1,0:T(8,128)(2,1)S(1)}, bf16[256,128]{1,0:T(8,128)(2,1)...) custom-call(s32[8]{0:T(128)S(1)} %bitcast.14, s32[8]{0:T(128)S(1)} %bitcast.18, s32[8]{0:T(128)S(1)} %bitcast.22, ...), custom_call_target="tpu_custom_call" | custom-call | tf_op jit(solution)/shard_map/hidden/pallas_call | solution.py:222
  18.0 1.6 %collective-permute-start.5 = (bf16[256,128]{1,0:T(8,128)(2,1)S(1)}, bf16[256,128]{1,0:T(8,128)(2,1)S(1)}, u32[]{:S(2)}, u32[]{:S(2)}) collective-permute-start(bf16[256,128]{1,0:T(8,128)(2,1)S(1)} %get-tuple-element.41), channel_id=1, source_target_pairs={{0,8},{8,0},{16,24},{24,16},{1,9},{9,1},{17,25},{25,17},{2,10},{10... | collective-permute-start | bytes 196616 | tf_op jit(solution)/shard_map/ppermute | solution.py:35
  19.6 2.6 %collective-permute-start.6 = (bf16[256,128]{1,0:T(8,128)(2,1)S(1)}, bf16[256,128]{1,0:T(8,128)(2,1)S(1)}, u32[]{:S(2)}, u32[]{:S(2)}) collective-permute-start(bf16[256,128]{1,0:T(8,128)(2,1)S(1)} %get-tuple-element.42), channel_id=1, source_target_pairs={{0,16},{8,24},{16,0},{24,8},{1,17},{9,25},{17,1},{25,9},{2,18},{10... | collective-permute-start | bytes 196616 | tf_op jit(solution)/shard_map/ppermute | solution.py:35
  22.2 0.0 collective-permute-done.refs_0_
  22.2 0.0 copy-done.1
  22.2 0.0 copy-done.2
  22.2 0.0 copy-done.4
  22.2 1.7 %back.1 = (bf16[528,128]{1,0:T(8,128)(2,1)S(1)}, bf16[528,128]{1,0:T(8,128)(2,1)S(1)}, bf16[528,128]{1,0:T(8,128)(2,1)S(1)}, bf16[528,128]{1,0:T(8,128)(2,1)S(1)...) custom-call(s32[8]{0:T(128)S(1)} %bitcast.15, ...), custom_call_target="tpu_custom_call" | custom-call | tf_op jit(solution)/shard_map/back/pallas_call | solution.py:233
  24.0 0.1 collective-permute-start.2
  24.0 1.6 %collective-permute-start.3 = (bf16[528,128]{1,0:T(8,128)(2,1)S(1)}, bf16[528,128]{1,0:T(8,128)(2,1)S(1)}, u32[]{:S(2)}, u32[]{:S(2)}) collective-permute-start(bf16[528,128]{1,0:T(8,128)(2,1)S(1)} %get-tuple-element.38), channel_id=1, source_target_pairs={{0,2},{1,3},{2,0},{3,1},{4,6},{5,7},{6,4},{7,5},{8,10},{9,11},{10,... | collective-permute-start | bytes 405512 | tf_op jit(solution)/shard_map/ppermute | solution.py:35
  25.6 0.3 collective-permute-start.4
  25.9 0.0 collective-permute-done.5.refs_5_
  25.9 1.5 %collective-permute-start.7 = (bf16[256,128]{1,0:T(8,128)(2,1)S(1)}, bf16[256,128]{1,0:T(8,128)(2,1)S(1)}, u32[]{:S(2)}, u32[]{:S(2)}) collective-permute-start(bf16[256,128]{1,0:T(8,128)(2,1)S(1)} %get-tuple-element.43), channel_id=1, source_target_pairs={{0,24},{8,16},{16,8},{24,0},{1,25},{9,17},{17,9},{25,1},{2,26},{10... | collective-permute-start | bytes 196616 | tf_op jit(solution)/shard_map/ppermute | solution.py:35
  27.4 0.0 collective-permute-done.6.refs_6_
  27.4 0.0 collective-permute-start.8
  27.4 5.2 %collective-permute-done.7.refs_7_ = bf16[256,128]{1,0:T(8,128)(2,1)S(1)} collective-permute-done((bf16[256,128]{1,0:T(8,128)(2,1)S(1)}, bf16[256,128]{1,0:T(8,128)(2,1)S(1)}, u32[]{:S(2)}, u32[]{:S(2)}) %collective-permute-start.7) | collective-permute-done | bytes 65568 | tf_op jit(solution)/shard_map/ppermute | solution.py:35
  32.6 0.0 collective-permute-start.9
  32.6 0.2 collective-permute-done.8.refs_9_
  32.8 2.1 %collective-permute-start.10 = (bf16[256,128]{1,0:T(8,128)(2,1)S(1)}, bf16[256,128]{1,0:T(8,128)(2,1)S(1)}, u32[]{:S(2)}, u32[]{:S(2)}) collective-permute-start(bf16[256,128]{1,0:T(8,128)(2,1)S(1)} %get-tuple-element.47), channel_id=1, source_target_pairs={{0,24},{8,16},{16,8},{24,0},{1,25},{9,17},{17,9},{25,1},{2,26},{10... | collective-permute-start | bytes 196616 | tf_op jit(solution)/shard_map/ppermute | solution.py:35
  34.9 4.4 %collective-permute-done.9.refs_10_ = bf16[256,128]{1,0:T(8,128)(2,1)S(1)} collective-permute-done((bf16[256,128]{1,0:T(8,128)(2,1)S(1)}, bf16[256,128]{1,0:T(8,128)(2,1)S(1)}, u32[]{:S(2)}, u32[]{:S(2)}) %collective-permute-start.9) | collective-permute-done | bytes 65568 | tf_op jit(solution)/shard_map/ppermute | solution.py:35
  39.3 0.0 collective-permute-done.10.refs_11_
  39.3 0.0 collective-permute-done.2.refs_1_
  39.3 0.0 collective-permute-done.3.refs_2_
  39.3 0.0 collective-permute-done.4.refs_3_
  39.3 2.1 %add_up.1 = (bf16[32,4096]{1,0:T(8,128)(2,1)}, bf16[32,4096]{1,0:T(8,128)(2,1)}, f32[8,32,128]{2,1,0:T(8,128)}, f32[8,32,128]{2,1,0:T(8,128)}) custom-call(bf16[528,128]{1,0:T(8,128)(2,1)S(1)} %get-tuple-element.36.refs_0_, bf16[528,128]{1,0:T(8,128)(2,1)S(1)} %collective-permute-done.2.refs_1_, bf16[528,128]{1,0:T(8,128)(2,1)S(1)} %collective-permute-done.3.refs_2_, ...), custom_call_target="tpu_custom_call" | custom-call | tf_op jit(solution)/shard_map/add_up/pallas_call | solution.py:246
Async XLA Ops:
  4.5 10.1 %collective-permute-start.1 = (bf16[1040,128]{1,0:T(8,128)(2,1)}, bf16[1040,128]{1,0:T(8,128)(2,1)S(1)}, u32[]{:S(2)}, u32[]{:S(2)}) collective-permute-start(bf16[1040,128]{1,0:T(8,128)(2,1)} %get-tuple-element.31), channel_id=1, source_target_pairs={{0,4},{4,0},{1,5},{5,1},{2,6},{6,2},{3,7},{7,3},{8,12},{12,8},{9,1... | collective-permute-start | bytes 798728 | tf_op jit(solution)/shard_map/ppermute | solution.py:35
  7.5 7.1 %copy-start = (bf16[1,1,8,128,128]{4,3,2,1,0:T(8,128)(2,1)S(1)}, bf16[1,1,8,128,128]{4,3,2,1,0:T(8,128)(2,1)}, u32[]{:S(2)}) copy-start(bf16[1,1,8,128,128]{4,3,2,1,0:T(8,128)(2,1)} %param.12) | copy-start | bytes 786436
  7.5 7.1 %copy-start.3 = (f32[8,128,128]{2,1,0:T(8,128)S(1)}, f32[8,128,128]{2,1,0:T(8,128)}, u32[]{:S(2)}) copy-start(f32[8,128,128]{2,1,0:T(8,128)} %get-tuple-element.30.p_own) | copy-start | bytes 1572868
  7.5 7.1 %copy-start.9 = (s32[1,1,8]{2,1,0:T(1,128)S(1)}, s32[1,1,8]{2,1,0:T(1,128)}, u32[]{:S(2)}) copy-start(s32[1,1,8]{2,1,0:T(1,128)} %param.14) | copy-start | bytes 100
  11.7 10.5 %collective-permute-start = (bf16[1040,128]{1,0:T(8,128)(2,1)}, bf16[1040,128]{1,0:T(8,128)(2,1)S(1)}, u32[]{:S(2)}, u32[]{:S(2)}) collective-permute-start(bf16[1040,128]{1,0:T(8,128)(2,1)} %get-tuple-element.29), channel_id=1, source_target_pairs={{0,4},{4,0},{1,5},{5,1},{2,6},{6,2},{3,7},{7,3},{8,12},{12,8},{9,1... | collective-permute-start | bytes 798728 | tf_op jit(solution)/shard_map/ppermute | solution.py:35
  14.6 0.7 %copy-start.6 = (s32[1,1,8]{2,1,0:T(1,128)S(1)}, s32[1,1,8]{2,1,0:T(1,128)}, u32[]{:S(2)}) copy-start(s32[1,1,8]{2,1,0:T(1,128)} %param.10) | copy-start | bytes 100
  14.6 0.7 %copy-start.7 = (s32[1,1,8]{2,1,0:T(1,128)S(1)}, s32[1,1,8]{2,1,0:T(1,128)}, u32[]{:S(2)}) copy-start(s32[1,1,8]{2,1,0:T(1,128)} %param.11) | copy-start | bytes 100
  14.6 0.7 %copy-start.8 = (s32[1,1,8]{2,1,0:T(1,128)S(1)}, s32[1,1,8]{2,1,0:T(1,128)}, u32[]{:S(2)}) copy-start(s32[1,1,8]{2,1,0:T(1,128)} %param.13) | copy-start | bytes 100
  15.3 0.9 %copy-start.5 = (bf16[8,128,128]{2,1,0:T(8,128)(2,1)S(1)}, bf16[8,128,128]{2,1,0:T(8,128)(2,1)}, u32[]{:S(2)}) copy-start(bf16[8,128,128]{2,1,0:T(8,128)(2,1)} %get-tuple-element.32.refs_1_) | copy-start | bytes 786436
  16.3 5.9 %copy-start.1 = (bf16[1,1,8,128,128]{4,3,2,1,0:T(8,128)(2,1)S(1)}, bf16[1,1,8,128,128]{4,3,2,1,0:T(8,128)(2,1)}, u32[]{:S(2)}) copy-start(bf16[1,1,8,128,128]{4,3,2,1,0:T(8,128)(2,1)} %param.9) | copy-start | bytes 786436
  16.3 5.9 %copy-start.2 = (f32[8,128,128]{2,1,0:T(8,128)S(1)}, f32[8,128,128]{2,1,0:T(8,128)}, u32[]{:S(2)}) copy-start(f32[8,128,128]{2,1,0:T(8,128)} %get-tuple-element.28.b_own) | copy-start | bytes 1572868
  16.3 5.9 %copy-start.4 = (bf16[8,128,128]{2,1,0:T(8,128)(2,1)S(1)}, bf16[8,128,128]{2,1,0:T(8,128)(2,1)}, u32[]{:S(2)}) copy-start(bf16[8,128,128]{2,1,0:T(8,128)(2,1)} %get-tuple-element.34.refs_2_) | copy-start | bytes 786436
  18.0 7.9 %collective-permute-start.5 = (bf16[256,128]{1,0:T(8,128)(2,1)S(1)}, bf16[256,128]{1,0:T(8,128)(2,1)S(1)}, u32[]{:S(2)}, u32[]{:S(2)}) collective-permute-start(bf16[256,128]{1,0:T(8,128)(2,1)S(1)} %get-tuple-element.41), channel_id=1, source_target_pairs={{0,8},{8,0},{16,24},{24,16},{1,9},{9,1},{17,25},{25,17},{2,10},{10... | collective-permute-start | bytes 196616 | tf_op jit(solution)/shard_map/ppermute | solution.py:35
  19.6 7.8 %collective-permute-start.6 = (bf16[256,128]{1,0:T(8,128)(2,1)S(1)}, bf16[256,128]{1,0:T(8,128)(2,1)S(1)}, u32[]{:S(2)}, u32[]{:S(2)}) collective-permute-start(bf16[256,128]{1,0:T(8,128)(2,1)S(1)} %get-tuple-element.42), channel_id=1, source_target_pairs={{0,16},{8,24},{16,0},{24,8},{1,17},{9,25},{17,1},{25,9},{2,18},{10... | collective-permute-start | bytes 196616 | tf_op jit(solution)/shard_map/ppermute | solution.py:35
  24.0 15.3 %collective-permute-start.2 = (bf16[528,128]{1,0:T(8,128)(2,1)S(1)}, bf16[528,128]{1,0:T(8,128)(2,1)S(1)}, u32[]{:S(2)}, u32[]{:S(2)}) collective-permute-start(bf16[528,128]{1,0:T(8,128)(2,1)S(1)} %get-tuple-element.37), channel_id=1, source_target_pairs={{0,1},{1,0},{2,3},{3,2},{4,5},{5,4},{6,7},{7,6},{8,9},{9,8},{10,11... | collective-permute-start | bytes 405512 | tf_op jit(solution)/shard_map/ppermute | solution.py:35
  24.0 15.3 %collective-permute-start.3 = (bf16[528,128]{1,0:T(8,128)(2,1)S(1)}, bf16[528,128]{1,0:T(8,128)(2,1)S(1)}, u32[]{:S(2)}, u32[]{:S(2)}) collective-permute-start(bf16[528,128]{1,0:T(8,128)(2,1)S(1)} %get-tuple-element.38), channel_id=1, source_target_pairs={{0,2},{1,3},{2,0},{3,1},{4,6},{5,7},{6,4},{7,5},{8,10},{9,11},{10,... | collective-permute-start | bytes 405512 | tf_op jit(solution)/shard_map/ppermute | solution.py:35
  25.6 13.7 %collective-permute-start.4 = (bf16[528,128]{1,0:T(8,128)(2,1)S(1)}, bf16[528,128]{1,0:T(8,128)(2,1)S(1)}, u32[]{:S(2)}, u32[]{:S(2)}) collective-permute-start(bf16[528,128]{1,0:T(8,128)(2,1)S(1)} %get-tuple-element.39), channel_id=1, source_target_pairs={{0,3},{1,2},{2,1},{3,0},{4,7},{5,6},{6,5},{7,4},{8,11},{9,10},{10,... | collective-permute-start | bytes 405512 | tf_op jit(solution)/shard_map/ppermute | solution.py:35
  25.9 6.7 %collective-permute-start.7 = (bf16[256,128]{1,0:T(8,128)(2,1)S(1)}, bf16[256,128]{1,0:T(8,128)(2,1)S(1)}, u32[]{:S(2)}, u32[]{:S(2)}) collective-permute-start(bf16[256,128]{1,0:T(8,128)(2,1)S(1)} %get-tuple-element.43), channel_id=1, source_target_pairs={{0,24},{8,16},{16,8},{24,0},{1,25},{9,17},{17,9},{25,1},{2,26},{10... | collective-permute-start | bytes 196616 | tf_op jit(solution)/shard_map/ppermute | solution.py:35
  27.4 5.5 %collective-permute-start.8 = (bf16[256,128]{1,0:T(8,128)(2,1)S(1)}, bf16[256,128]{1,0:T(8,128)(2,1)S(1)}, u32[]{:S(2)}, u32[]{:S(2)}) collective-permute-start(bf16[256,128]{1,0:T(8,128)(2,1)S(1)} %get-tuple-element.45), channel_id=1, source_target_pairs={{0,8},{8,0},{16,24},{24,16},{1,9},{9,1},{17,25},{25,17},{2,10},{10... | collective-permute-start | bytes 196616 | tf_op jit(solution)/shard_map/ppermute | solution.py:35
  32.6 6.7 %collective-permute-start.9 = (bf16[256,128]{1,0:T(8,128)(2,1)S(1)}, bf16[256,128]{1,0:T(8,128)(2,1)S(1)}, u32[]{:S(2)}, u32[]{:S(2)}) collective-permute-start(bf16[256,128]{1,0:T(8,128)(2,1)S(1)} %get-tuple-element.46), channel_id=1, source_target_pairs={{0,16},{8,24},{16,0},{24,8},{1,17},{9,25},{17,1},{25,9},{2,18},{10... | collective-permute-start | bytes 196616 | tf_op jit(solution)/shard_map/ppermute | solution.py:35
  32.8 6.5 %collective-permute-start.10 = (bf16[256,128]{1,0:T(8,128)(2,1)S(1)}, bf16[256,128]{1,0:T(8,128)(2,1)S(1)}, u32[]{:S(2)}, u32[]{:S(2)}) collective-permute-start(bf16[256,128]{1,0:T(8,128)(2,1)S(1)} %get-tuple-element.47), channel_id=1, source_target_pairs={{0,24},{8,16},{16,8},{24,0},{1,25},{9,17},{17,9},{25,1},{2,26},{10... | collective-permute-start | bytes 196616 | tf_op jit(solution)/shard_map/ppermute | solution.py:35

commit v4 on v3

v4 whole, which is shorter than its diff:
```python
import functools
import math

import jax
import jax.numpy as jnp
from jax import lax
from jax.experimental import pallas as pl
from jax.experimental.pallas import tpu as pltpu
from jax.sharding import PartitionSpec as P

FF = 32768
f32 = jnp.float32
bf16 = jnp.bfloat16
VMEM = pl.BlockSpec(memory_space=pltpu.VMEM)
SMEM = pl.BlockSpec(memory_space=pltpu.SMEM)
HBM = pl.BlockSpec(memory_space=pltpu.HBM)
LANES = 128
PARAMS = pltpu.CompilerParams(vmem_limit_bytes=32 * 1024 * 1024)

TAKE_LIMIT = 62 * 1024 * 1024

W1_ROW, W1_COL, W2_HID, W2_OUT = range(4)


def dot(a, b, contract):
    return lax.dot_general(a, b, ((contract[:1], contract[1:]), ((), ())), preferred_element_type=f32)


def partner(i, d, n):
    return i ^ d if n & (n - 1) == 0 else (i + d) % n


def send(x, axis, d):
    n = lax.axis_size(axis)
    return lax.ppermute(x, axis, [(i, partner(i, d, n)) for i in range(n)]) if d else x


def target(axis, d):
    n = lax.axis_size(axis)
    me = lax.axis_index(axis)
    return jnp.bitwise_xor(me, d) if n & (n - 1) == 0 else lax.rem(me + d, n)


def cdf(v):
    return 0.5 * (1.0 + lax.erf(v * math.sqrt(0.5)))


def table_row(tables, slots):
    lane = lax.broadcasted_iota(jnp.int32, (16, LANES), 1)
    row = jnp.zeros((16, LANES), f32)
    for which, table in enumerate(tables):
        for k in range(slots):
            row = jnp.where(lane == which * slots + k, table[k].astype(f32), row)
    return row.astype(bf16)


def decode_tables(refs, rows, ints, scalars, sem):
    for i, ref in enumerate(refs):
        ints[i * 8 : i * 8 + 8] = ref[rows : rows + 16, :].astype(f32)[:8].astype(jnp.int32)
    copy = pltpu.make_async_copy(ints, scalars, sem)
    copy.start()
    return copy


def start_taking(source, table, taken, sems):
    slots, _, blk = taken.shape
    copies = []
    for k in range(slots):
        begin = pl.multiple_of(table[k] * blk, blk)
        copies.append(pltpu.make_async_copy(source.at[:, pl.ds(begin, blk)], taken.at[k], sems.at[k]))
        copies[-1].start()
    return copies


def token_kernel(t0, t1, t2, t3, tokens, w1, message, taken, w_v, c0, c1, c2, c3, sems):
    slots, rows, blk = taken.shape
    tables = (c0, c1, c2, c3)
    loads = [pltpu.make_async_copy(t, c, sems.at[slots + 1 + i]) for i, (t, c) in enumerate(zip((t0, t1, t2, t3), tables))]
    w_copy = pltpu.make_async_copy(w1, w_v, sems.at[slots])
    for c in loads:
        c.start()
    w_copy.start()
    loads[W1_ROW].wait()
    copies = start_taking(tokens, c0, taken, sems)
    for c in loads[1:]:
        c.wait()
    message[slots * rows :, :] = table_row(tables, slots)
    w_copy.wait()
    for k in range(slots):
        copies[k].wait()
        message[k * rows : (k + 1) * rows, :] = dot(taken[k], w_v[k], (1, 0)).astype(bf16)


def cotangent_kernel(c0, c1, c2, c3, grad_out, w1, w2, taken, message, cot, p_own, b_own, tab, sems):
    slots, rows, blk = cot.shape
    copies = start_taking(grad_out, c3, cot, sems)
    for which, table in enumerate((c0, c1, c2, c3)):
        for k in range(slots):
            tab[which * slots + k] = table[k]
    for k in range(slots):
        copies[k].wait()
        value = dot(cot[k], w2[k], (1, 1))
        b_own[k] = value
        message[k * rows : (k + 1) * rows, :] = value.astype(bf16)
    message[slots * rows :, :] = jnp.zeros((16, blk), bf16)
    for k in range(slots):
        p_own[k] = dot(taken[k], w1[k], (1, 0))


def sum_at(acc, targets, tab, own_at, own, peers, peer_at, slots, scratch):
    ints, scalars, sem = scratch
    rows = acc.shape[1]
    copy = decode_tables(peers, slots * rows, ints, scalars, sem) if peers else None
    for which in targets:
        for k in range(slots):
            acc[tab[which * slots + k]] = jnp.zeros(acc.shape[1:], f32)
    for k in range(slots):
        at = tab[own_at * slots + k]
        acc[at] = acc[at] + own[k]
    if peers:
        copy.wait()
    for i, ref in enumerate(peers):
        for k in range(slots):
            at = scalars[i * 8, peer_at * slots + k]
            acc[at] = acc[at] + ref[k * rows : (k + 1) * rows, :].astype(f32)


def cut(value, refs, k, axis):
    share = value.shape[0] // len(refs)
    for d, ref in enumerate(refs):
        begin = pl.multiple_of(target(axis, d) * share, share)
        ref[k * share : (k + 1) * share, :] = value[pl.ds(begin, share), :].astype(ref.dtype)


def hidden_kernel(dims, tab, p_own, *refs):
    slots, n_row, n_col, n_tok = dims
    p_peers, refs = refs[: n_row - 1], refs[n_row - 1 :]
    cot, active, hidden, peer_tabs = refs[:4]
    grads, refs = refs[4 : 4 + n_tok], refs[4 + n_tok :]
    acc, grad, *scratch = refs
    sum_at(acc, (W1_COL, W2_HID), tab, W1_COL, p_own, p_peers, W1_COL, slots, scratch)
    for k in range(slots):
        h = acc[tab[W2_HID * slots + k]]
        active[k] = (h * cdf(h)).astype(bf16)
        grad[k] = dot(active[k], cot[k], (0, 0))
        cut(grad.at[k], grads, k, "tok")
    for k in range(slots):
        hidden[k] = acc[tab[W1_COL * slots + k]]
    peer_tabs[...] = scratch[0][...]


def slope_kernel(dims, active, hidden, w2, out, slope):
    slots = dims[0]
    for k in range(slots):
        out[k] = dot(active[k], w2[k], (1, 0)).astype(bf16)
    for k in range(slots):
        h = hidden[k]
        slope[k] = cdf(h) + h * jnp.exp(-0.5 * h * h) * (1.0 / math.sqrt(2.0 * math.pi))


def back_kernel(dims, tab, peer_tabs, b_own, *refs):
    slots, n_row, n_col, n_tok = dims
    b_peers, refs = refs[: n_row - 1], refs[n_row - 1 :]
    slope, taken, w1, out = refs[:4]
    refs = refs[4:]
    outs, refs = refs[:n_col], refs[n_col:]
    grads, refs = refs[:n_tok], refs[n_tok:]
    acc, value, grad = refs
    rows = acc.shape[1]
    for k in range(slots):
        acc[tab[W1_COL * slots + k]] = jnp.zeros(acc.shape[1:], f32)
    for k in range(slots):
        at = tab[W2_HID * slots + k]
        acc[at] = acc[at] + b_own[k]
    for i, ref in enumerate(b_peers):
        for k in range(slots):
            at = peer_tabs[i * 8, W2_HID * slots + k]
            acc[at] = acc[at] + ref[k * rows : (k + 1) * rows, :].astype(f32)
    for k in range(slots):
        g = (acc[tab[W1_COL * slots + k]] * slope[k]).astype(bf16)
        grad[k] = dot(taken[k], g, (0, 0))
        cut(grad.at[k], grads, k, "tok")
        value[k] = dot(g, w1[k], (1, 1))
        cut(value.at[k], outs, slots + k, "col")
    for k in range(slots):
        cut(out.at[k], outs, k, "col")
    row = table_row([[tab[which * slots + k] for k in range(slots)] for which in range(4)], slots)
    for ref in outs:
        ref[ref.shape[0] - 16 :, :] = row


def add_shares(parts, result):
    for k in range(result.shape[0]):
        here = slice(k * result.shape[1], (k + 1) * result.shape[1])
        total = parts[0][here, :].astype(f32)
        for ref in parts[1:]:
            total = total + ref[here, :].astype(f32)
        result[k] = total


def output_kernel(dims, *refs):
    slots, n_row, n_col, n_tok = dims
    o_parts, refs = refs[:n_col], refs[n_col:]
    g2_parts, refs = refs[:n_tok], refs[n_tok:]
    output, grad_in, gw2, acc, ints, scalars, sem = refs
    blk, share = acc.shape[-1], acc.shape[1]
    copy = decode_tables(o_parts, 2 * slots * share, ints, scalars, sem)
    add_shares(g2_parts, gw2)
    copy.wait()
    for first, which, result in ((0, W2_OUT, output), (slots, W1_ROW, grad_in)):
        acc[...] = jnp.zeros(acc.shape, f32)
        for c, ref in enumerate(o_parts):
            for k in range(slots):
                at = scalars[c * 8, which * slots + k]
                here = slice((first + k) * share, (first + k + 1) * share)
                acc[at] = acc[at] + ref[here, :].astype(f32)
        for b in range(acc.shape[0]):
            result[:, b * blk : (b + 1) * blk] = acc[b].astype(bf16)


def grad_kernel(*refs):
    add_shares(refs[:-1], refs[-1])


def shards(tokens, w1_blocks, w1_rows, w1_cols, w2_blocks, w2_hidden, w2_outs, grad_out):
    slots, blk = w1_blocks.shape[2], w1_blocks.shape[-1]
    rows = tokens.shape[0]
    n_row, n_col, n_tok = (lax.axis_size(a) for a in ("row", "col", "tok"))
    dims = (slots, n_row, n_col, n_tok)
    row_blocks = tokens.shape[1] // blk
    col_blocks = FF // n_col // blk
    share, part = rows // n_col, blk // n_tok
    w1 = w1_blocks.reshape(slots, blk, blk)
    w2 = w2_blocks.reshape(slots, blk, blk)
    tables = [t.reshape(slots) for t in (w1_rows, w1_cols, w2_hidden, w2_outs)]

    S = jax.ShapeDtypeStruct
    message = S((slots * rows + 16, blk), bf16)
    wide, narrow = S((slots, rows, blk), f32), S((slots, rows, blk), bf16)
    p_send, taken = pl.pallas_call(
        token_kernel,
        out_shape=(message, narrow),
        in_specs=[HBM] * 6,
        out_specs=(VMEM,) * 2,
        scratch_shapes=[pltpu.VMEM((slots, blk, blk), bf16)]
        + [pltpu.SMEM((slots,), jnp.int32)] * 4
        + [pltpu.SemaphoreType.DMA((slots + 5,))],
        compiler_params=pltpu.CompilerParams(vmem_limit_bytes=TAKE_LIMIT),
        name="take_tokens",
    )(*tables, tokens, w1)
    p_peers = [send(p_send, "row", d) for d in range(1, n_row)]
    b_send, cot, p_own, b_own, tab = pl.pallas_call(
        cotangent_kernel,
        out_shape=(message, narrow, wide, wide, S((4 * slots,), jnp.int32)),
        in_specs=[SMEM] * 4 + [HBM] + [VMEM] * 3,
        out_specs=(VMEM,) * 4 + (SMEM,),
        scratch_shapes=[pltpu.SemaphoreType.DMA((slots,))],
        compiler_params=PARAMS,
        name="take_cotangent",
    )(*tables, grad_out, w1, w2, taken)
    b_peers = [send(b_send, "row", d) for d in range(1, n_row)]

    parts = (S((slots * part, blk), bf16),) * n_tok
    outs = (S((2 * slots * share + 16, blk), bf16),) * n_col
    peer_rows = 8 * max(1, n_row - 1)
    active, hidden, peer_tabs, *g2_sent = pl.pallas_call(
        functools.partial(hidden_kernel, dims),
        out_shape=(narrow, wide, S((peer_rows, LANES), jnp.int32)) + parts,
        in_specs=[SMEM] + [VMEM] * (n_row + 1),
        out_specs=(VMEM,) * (3 + n_tok),
        scratch_shapes=[
            pltpu.VMEM((col_blocks, rows, blk), f32),
            pltpu.VMEM((slots, blk, blk), f32),
            pltpu.VMEM((peer_rows, LANES), jnp.int32),
            pltpu.SMEM((peer_rows, LANES), jnp.int32),
            pltpu.SemaphoreType.DMA,
        ],
        compiler_params=PARAMS,
        name="hidden",
    )(tab, p_own, *p_peers, cot)
    g2_parts = [send(x, "tok", d) for d, x in enumerate(g2_sent)]
    out, slope = pl.pallas_call(
        functools.partial(slope_kernel, dims),
        out_shape=(narrow, wide),
        in_specs=[VMEM] * 3,
        out_specs=(VMEM,) * 2,
        compiler_params=PARAMS,
        name="slope",
    )(active, hidden, w2)

    sent = pl.pallas_call(
        functools.partial(back_kernel, dims),
        out_shape=outs + parts,
        in_specs=[SMEM] * 2 + [VMEM] * (n_row + 4),
        out_specs=(VMEM,) * (n_col + n_tok),
        scratch_shapes=[
            pltpu.VMEM((col_blocks, rows, blk), f32),
            pltpu.VMEM((slots, rows, blk), f32),
            pltpu.VMEM((slots, blk, blk), f32),
        ],
        compiler_params=PARAMS,
        name="back",
    )(tab, peer_tabs, b_own, *b_peers, slope, taken, w1, out)
    g1_parts = [send(x, "tok", d) for d, x in enumerate(sent[n_col:])]
    o_parts = [send(x, "col", d) for d, x in enumerate(sent[:n_col])]

    summed = S((slots, part, blk), f32)
    result = S((share, row_blocks * blk), bf16)
    output, grad_in, gw2 = pl.pallas_call(
        functools.partial(output_kernel, dims),
        out_shape=(result, result, summed),
        in_specs=[VMEM] * (n_col + n_tok),
        out_specs=(VMEM,) * 3,
        scratch_shapes=[
            pltpu.VMEM((row_blocks, share, blk), f32),
            pltpu.VMEM((8 * n_col, LANES), jnp.int32),
            pltpu.SMEM((8 * n_col, LANES), jnp.int32),
            pltpu.SemaphoreType.DMA,
        ],
        compiler_params=PARAMS,
        name="add_outputs",
    )(*o_parts, *g2_parts)
    gw1 = pl.pallas_call(
        grad_kernel,
        out_shape=summed,
        in_specs=[VMEM] * n_tok,
        out_specs=VMEM,
        compiler_params=PARAMS,
        name="add_grads",
    )(*g1_parts)
    return (output, grad_in, gw1.reshape(1, 1, slots, part, blk), gw2.reshape(1, 1, slots, part, blk))


def solution(mesh):
    placed = (
        P("tok", "row"),
        P("row", "col", None, None, None),
        P("row", "col", None),
        P("row", "col", None),
        P("row", "col", None, None, None),
        P("row", "col", None),
        P("row", "col", None),
        P("tok", "row"),
    )
    return jax.shard_map(
        shards,
        mesh=mesh,
        in_specs=placed,
        out_specs=(
            P(("tok", "col"), "row"),
            P(("tok", "col"), "row"),
            P("row", "col", None, "tok", None),
            P("row", "col", None, "tok", None),
        ),
        check_vma=False,
    )
```

time: 41.6 us -> 42.8 us (1.029)
  starting transfers between devices: 12.8 us -> 16.7 us
  waiting for transfers between devices: 12.7 us -> 10.7 us
  Pallas kernels: 13.5 us -> 12 us
  local copies, waits for them, and re-layouts: 1.63 us -> 2.58 us
    ppermute x11, starting transfers between devices: 12.8 us -> 16.7 us  [send(): lax.ppermute(x, axis, [(i, partner(i, d, n)) for i in range(n)])]
    ppermute x11, waiting for transfers between devices: 12.7 us -> 10.7 us  [send(): lax.ppermute(x, axis, [(i, partner(i, d, n)) for i in range(n)])]
    pallas_call x4 -> x6, Pallas kernels: 11.8 us -> 10.8 us  [the longest x1 3.58 us: shards(): pl.pallas_call(token_kernel, out_shape=(message, narrow), in_specs=[HBM]...]
    unnamed x20, local copies, waits for them, and re-layouts: 1.63 us -> 2.58 us
    pallas_call x1, Pallas kernels: 1.72 us -> 1.19 us  [shards(): pl.pallas_call(functools.partial(back_kernel, dims), out_shape=outs + par...]
  transfers between devices with their start and end apart: 11 -> 11, of which waited for: 4 -> 5; matrix products, arithmetic and copies ran while one was open for 0% -> 0% of each run, Pallas kernels for 18% -> 15%
where the time goes in v4:
time: 42.8 us; the launch traced here: 42.6 us
  starting transfers between devices  16.7 us (39%)
  Pallas kernels  12 us (28%)
  waiting for transfers between devices  10.7 us (25%)
  local copies, waits for them, and re-layouts  2.58 us (6%)
  between operations  0.73 us (2%)
    ppermute x11, starting transfers between devices, send(): lax.ppermute(x, axis, [(i, partner(i, d, n)) for i in range(n)])  16.7 us
    ppermute x11, waiting for transfers between devices, send(): lax.ppermute(x, axis, [(i, partner(i, d, n)) for i in range(n)])  10.7 us
    pallas_call x1, Pallas kernels, shards(): pl.pallas_call(token_kernel, out_shape=(message, narrow), in_specs=[HBM]...  3.58 us
    unnamed x20, local copies, waits for them, and re-layouts  2.58 us
    pallas_call x1, Pallas kernels, shards(): pl.pallas_call(cotangent_kernel, out_shape=(message, narrow, wide, wide,...  2.52 us
    pallas_call x1, Pallas kernels, shards(): pl.pallas_call(functools.partial(output_kernel, dims), out_shape=(result,...  2.05 us
    pallas_call x1, Pallas kernels, shards(): pl.pallas_call(functools.partial(hidden_kernel, dims), out_shape=(narrow,...  1.58 us
    pallas_call x1, Pallas kernels, shards(): pl.pallas_call(functools.partial(back_kernel, dims), out_shape=outs + par...  1.19 us
  transfers between devices with their start and end apart: 11, of which 5 were waited for; matrix products, arithmetic and copies ran while one was open for 0% of the time, Pallas kernels for 15%

profile of v4, /device:TPU:0, one launch (start us, length us, event | category | flops | bytes accessed | tf_op | source)
XLA Modules:
  0.0 42.6 jit_solution(356547057635225879)
XLA Ops:
  0.6 0.0 copy-start.1
  0.6 0.0 copy-start
  0.7 0.0 copy-start.9
  0.7 3.6 %take_tokens.1 = (bf16[1040,128]{1,0:T(8,128)(2,1)}, bf16[8,128,128]{2,1,0:T(8,128)(2,1)}) custom-call(s32[8]{0:T(128)} %bitcast.13, s32[8]{0:T(128)} %bitcast.15, s32[8]{0:T(128)} %bitcast.17, s32[8]{0:T(128)} %bitcast.19, bf16[128,4096]{1,0:T(8,128)(2,1)} %tokens.1, bf16[8,128,128]{2,1,0:T(8,128)(2,1)} %bitcast.8), custom_call_target="tpu_custom_call" | custom-call | tf_op jit(solution)/shard_map/take_tokens/pallas_call | solution.py:240
  4.2 3.0 %collective-permute-start = (bf16[1040,128]{1,0:T(8,128)(2,1)}, bf16[1040,128]{1,0:T(8,128)(2,1)S(1)}, u32[]{:S(2)}, u32[]{:S(2)}) collective-permute-start(bf16[1040,128]{1,0:T(8,128)(2,1)} %get-tuple-element.34), channel_id=1, source_target_pairs={{0,4},{4,0},{1,5},{5,1},{2,6},{6,2},{3,7},{7,3},{8,12},{12,8},{9,1... | collective-permute-start | bytes 798728 | tf_op jit(solution)/shard_map/ppermute | solution.py:35
  7.2 0.0 copy-start.6
  7.3 0.0 copy-start.7
  7.3 0.0 copy-start.8
  7.3 0.0 copy-done.1
  7.3 0.0 copy-done
  7.3 0.0 copy-done.9
  7.3 0.6 %copy-done.6 = s32[1,1,8]{2,1,0:T(1,128)S(1)} copy-done((s32[1,1,8]{2,1,0:T(1,128)S(1)}, s32[1,1,8]{2,1,0:T(1,128)}, u32[]{:S(2)}) %copy-start.6) | copy-done | bytes 56
  7.9 0.0 copy-done.7
  7.9 0.0 copy-done.8
  7.9 0.0 copy-start.2
  7.9 0.9 %copy-done.2 = bf16[8,128,128]{2,1,0:T(8,128)(2,1)S(1)} copy-done((bf16[8,128,128]{2,1,0:T(8,128)(2,1)S(1)}, bf16[8,128,128]{2,1,0:T(8,128)(2,1)}, u32[]{:S(2)}) %copy-start.2) | copy-done | bytes 262168
  8.9 0.0 copy-start.4
  8.9 0.9 %copy-done.4 = bf16[1,1,8,128,128]{4,3,2,1,0:T(8,128)(2,1)S(1)} copy-done((bf16[1,1,8,128,128]{4,3,2,1,0:T(8,128)(2,1)S(1)}, bf16[1,1,8,128,128]{4,3,2,1,0:T(8,128)(2,1)}, u32[]{:S(2)}) %copy-start.4) | copy-done | bytes 262168
  9.8 2.5 %take_cotangent.1 = (bf16[1040,128]{1,0:T(8,128)(2,1)S(1)}, bf16[8,128,128]{2,1,0:T(8,128)(2,1)S(1)}, f32[8,128,128]{2,1,0:T(8,128)S(1)}, f32[8,128,128]{2,1,0:T(8,128)S(1)}, s32[32]{0:T(128)S(1)}) custom-call(s32[8]{0:T(128)S(1)} %bitcast.14, s32[8]{0:T(128)S(1)} %bitcast.16, s32[8]{0:T(128)S(1)} %bitcast.18, s32[8]{0:T(128)S(1)} %bitcast.20, ...), custom_call_target="tpu_custom_call" | custom-call | tf_op jit(solution)/shard_map/take_cotangent/pallas_call | solution.py:252
  12.4 0.1 collective-permute-start.1
  12.4 1.4 %collective-permute-done.refs_0_ = bf16[1040,128]{1,0:T(8,128)(2,1)S(1)} collective-permute-done((bf16[1040,128]{1,0:T(8,128)(2,1)}, bf16[1040,128]{1,0:T(8,128)(2,1)S(1)}, u32[]{:S(2)}, u32[]{:S(2)}) %collective-permute-start) | collective-permute-done | bytes 266272 | tf_op jit(solution)/shard_map/ppermute | solution.py:35
  13.9 0.0 copy-start.5
  13.9 1.6 %hidden.1 = (bf16[8,128,128]{2,1,0:T(8,128)(2,1)S(1)}, f32[8,128,128]{2,1,0:T(8,128)S(1)}, s32[8,128]{1,0:T(8,128)S(1)}, bf16[256,128]{1,0:T(8,128)(2,1)S(1)}, b...) custom-call(s32[32]{0:T(128)S(1)} %get-tuple-element.32.tab, ...), custom_call_target="tpu_custom_call" | custom-call | tf_op jit(solution)/shard_map/hidden/pallas_call | solution.py:266
  15.5 1.9 %collective-permute-start.5 = (bf16[256,128]{1,0:T(8,128)(2,1)S(1)}, bf16[256,128]{1,0:T(8,128)(2,1)S(1)}, u32[]{:S(2)}, u32[]{:S(2)}) collective-permute-start(bf16[256,128]{1,0:T(8,128)(2,1)S(1)} %get-tuple-element.48), channel_id=1, source_target_pairs={{0,8},{8,0},{16,24},{24,16},{1,9},{9,1},{17,25},{25,17},{2,10},{10... | collective-permute-start | bytes 196616 | tf_op jit(solution)/shard_map/ppermute | solution.py:35
  17.3 0.0 copy-done.5
  17.3 0.3 slope.1
  17.7 2.6 %collective-permute-done.1.refs_0_ = bf16[1040,128]{1,0:T(8,128)(2,1)S(1)} collective-permute-done((bf16[1040,128]{1,0:T(8,128)(2,1)S(1)}, bf16[1040,128]{1,0:T(8,128)(2,1)S(1)}, u32[]{:S(2)}, u32[]{:S(2)}) %collective-permute-start.1) | collective-permute-done | bytes 266272 | tf_op jit(solution)/shard_map/ppermute | solution.py:35
  20.3 0.0 copy-done.3
  20.3 1.2 %back.1 = (bf16[528,128]{1,0:T(8,128)(2,1)S(1)}, bf16[528,128]{1,0:T(8,128)(2,1)S(1)}, bf16[528,128]{1,0:T(8,128)(2,1)S(1)}, bf16[528,128]{1,0:T(8,128)(2,1)S(1)...) custom-call(s32[32]{0:T(128)S(1)} %get-tuple-element.32.tab, ...), custom_call_target="tpu_custom_call" | custom-call | tf_op jit(solution)/shard_map/back/pallas_call | solution.py:291
  21.5 1.7 %collective-permute-start.8 = (bf16[256,128]{1,0:T(8,128)(2,1)S(1)}, bf16[256,128]{1,0:T(8,128)(2,1)S(1)}, u32[]{:S(2)}, u32[]{:S(2)}) collective-permute-start(bf16[256,128]{1,0:T(8,128)(2,1)S(1)} %get-tuple-element.54), channel_id=1, source_target_pairs={{0,8},{8,0},{16,24},{24,16},{1,9},{9,1},{17,25},{25,17},{2,10},{10... | collective-permute-start | bytes 196616 | tf_op jit(solution)/shard_map/ppermute | solution.py:35
  23.1 0.0 collective-permute-start.2
  23.1 1.5 %collective-permute-start.3 = (bf16[528,128]{1,0:T(8,128)(2,1)S(1)}, bf16[528,128]{1,0:T(8,128)(2,1)S(1)}, u32[]{:S(2)}, u32[]{:S(2)}) collective-permute-start(bf16[528,128]{1,0:T(8,128)(2,1)S(1)} %get-tuple-element.45), channel_id=1, source_target_pairs={{0,2},{1,3},{2,0},{3,1},{4,6},{5,7},{6,4},{7,5},{8,10},{9,11},{10,... | collective-permute-start | bytes 405512 | tf_op jit(solution)/shard_map/ppermute | solution.py:35
  24.7 0.3 collective-permute-start.4
  25.0 0.0 collective-permute-done.5.refs_5_
  25.0 2.6 %collective-permute-start.9 = (bf16[256,128]{1,0:T(8,128)(2,1)S(1)}, bf16[256,128]{1,0:T(8,128)(2,1)S(1)}, u32[]{:S(2)}, u32[]{:S(2)}) collective-permute-start(bf16[256,128]{1,0:T(8,128)(2,1)S(1)} %get-tuple-element.55), channel_id=1, source_target_pairs={{0,16},{8,24},{16,0},{24,8},{1,17},{9,25},{17,1},{25,9},{2,18},{10... | collective-permute-start | bytes 196616 | tf_op jit(solution)/shard_map/ppermute | solution.py:35
  27.6 0.0 collective-permute-done.8.refs_1_
  27.6 1.8 %collective-permute-start.10 = (bf16[256,128]{1,0:T(8,128)(2,1)S(1)}, bf16[256,128]{1,0:T(8,128)(2,1)S(1)}, u32[]{:S(2)}, u32[]{:S(2)}) collective-permute-start(bf16[256,128]{1,0:T(8,128)(2,1)S(1)} %get-tuple-element.56), channel_id=1, source_target_pairs={{0,24},{8,16},{16,8},{24,0},{1,25},{9,17},{17,9},{25,1},{2,26},{10... | collective-permute-start | bytes 196616 | tf_op jit(solution)/shard_map/ppermute | solution.py:35
  29.4 2.1 %collective-permute-done.9.refs_2_ = bf16[256,128]{1,0:T(8,128)(2,1)S(1)} collective-permute-done((bf16[256,128]{1,0:T(8,128)(2,1)S(1)}, bf16[256,128]{1,0:T(8,128)(2,1)S(1)}, u32[]{:S(2)}, u32[]{:S(2)}) %collective-permute-start.9) | collective-permute-done | bytes 65568 | tf_op jit(solution)/shard_map/ppermute | solution.py:35
  31.5 2.0 %collective-permute-start.6 = (bf16[256,128]{1,0:T(8,128)(2,1)S(1)}, bf16[256,128]{1,0:T(8,128)(2,1)S(1)}, u32[]{:S(2)}, u32[]{:S(2)}) collective-permute-start(bf16[256,128]{1,0:T(8,128)(2,1)S(1)} %get-tuple-element.49), channel_id=1, source_target_pairs={{0,16},{8,24},{16,0},{24,8},{1,17},{9,25},{17,1},{25,9},{2,18},{10... | collective-permute-start | bytes 196616 | tf_op jit(solution)/shard_map/ppermute | solution.py:35
  33.5 0.8 %collective-permute-done.10.refs_3_ = bf16[256,128]{1,0:T(8,128)(2,1)S(1)} collective-permute-done((bf16[256,128]{1,0:T(8,128)(2,1)S(1)}, bf16[256,128]{1,0:T(8,128)(2,1)S(1)}, u32[]{:S(2)}, u32[]{:S(2)}) %collective-permute-start.10) | collective-permute-done | bytes 65568 | tf_op jit(solution)/shard_map/ppermute | solution.py:35
  34.4 1.8 %collective-permute-start.7 = (bf16[256,128]{1,0:T(8,128)(2,1)S(1)}, bf16[256,128]{1,0:T(8,128)(2,1)S(1)}, u32[]{:S(2)}, u32[]{:S(2)}) collective-permute-start(bf16[256,128]{1,0:T(8,128)(2,1)S(1)} %get-tuple-element.50), channel_id=1, source_target_pairs={{0,24},{8,16},{16,8},{24,0},{1,25},{9,17},{17,9},{25,1},{2,26},{10... | collective-permute-start | bytes 196616 | tf_op jit(solution)/shard_map/ppermute | solution.py:35
  36.1 0.7 %add_grads.1 = f32[8,32,128]{2,1,0:T(8,128)} custom-call(bf16[256,128]{1,0:T(8,128)(2,1)S(1)} %get-tuple-element.53.refs_0_, bf16[256,128]{1,0:T(8,128)(2,1)S(1)} %collective-permute-done.8.refs_1_, bf16[256,128]{1,0:T(8,128)(2,1)S(1)} %collective-permute-done.9.refs_2_, bf16[256,128]{1,0:T(8,128)(2,1)S(1)} %collective-permute-done.10.refs_3_), custom_call_target="tpu_custom_call" | custom-call | tf_op jit(solution)/shard_map/add_grads/pallas_call | solution.py:323
  36.8 0.0 collective-permute-done.6.refs_6_
  36.8 3.7 %collective-permute-done.7.refs_7_ = bf16[256,128]{1,0:T(8,128)(2,1)S(1)} collective-permute-done((bf16[256,128]{1,0:T(8,128)(2,1)S(1)}, bf16[256,128]{1,0:T(8,128)(2,1)S(1)}, u32[]{:S(2)}, u32[]{:S(2)}) %collective-permute-start.7) | collective-permute-done | bytes 65568 | tf_op jit(solution)/shard_map/ppermute | solution.py:35
  40.5 0.0 collective-permute-done.2.refs_1_
  40.5 0.0 collective-permute-done.3.refs_2_
  40.5 0.0 collective-permute-done.4.refs_3_
  40.5 2.1 %add_outputs.1 = (bf16[32,4096]{1,0:T(8,128)(2,1)}, bf16[32,4096]{1,0:T(8,128)(2,1)}, f32[8,32,128]{2,1,0:T(8,128)}) custom-call(bf16[528,128]{1,0:T(8,128)(2,1)S(1)} %get-tuple-element.43.refs_0_, bf16[528,128]{1,0:T(8,128)(2,1)S(1)} %collective-permute-done.2.refs_1_, bf16[528,128]{1,0:T(8,128)(2,1)S(1)} %collective-permute-done.3.refs_2_, ...), custom_call_target="tpu_custom_call" | custom-call | tf_op jit(solution)/shard_map/add_outputs/pallas_call | solution.py:309
  (1 shorter events, 0.0 us)
Async XLA Ops:
  0.6 6.6 %copy-start.1 = (bf16[128,4096]{1,0:T(8,128)(2,1)S(1)}, bf16[128,4096]{1,0:T(8,128)(2,1)}, u32[]{:S(2)}) copy-start(bf16[128,4096]{1,0:T(8,128)(2,1)} %grad_out.1) | copy-start | bytes 3145732
  0.6 6.6 %copy-start = (bf16[1,1,8,128,128]{4,3,2,1,0:T(8,128)(2,1)S(1)}, bf16[1,1,8,128,128]{4,3,2,1,0:T(8,128)(2,1)}, u32[]{:S(2)}) copy-start(bf16[1,1,8,128,128]{4,3,2,1,0:T(8,128)(2,1)} %param.9) | copy-start | bytes 786436
  0.7 6.6 %copy-start.9 = (s32[1,1,8]{2,1,0:T(1,128)S(1)}, s32[1,1,8]{2,1,0:T(1,128)}, u32[]{:S(2)}) copy-start(s32[1,1,8]{2,1,0:T(1,128)} %param.14) | copy-start | bytes 100
  4.2 9.6 %collective-permute-start = (bf16[1040,128]{1,0:T(8,128)(2,1)}, bf16[1040,128]{1,0:T(8,128)(2,1)S(1)}, u32[]{:S(2)}, u32[]{:S(2)}) collective-permute-start(bf16[1040,128]{1,0:T(8,128)(2,1)} %get-tuple-element.34), channel_id=1, source_target_pairs={{0,4},{4,0},{1,5},{5,1},{2,6},{6,2},{3,7},{7,3},{8,12},{12,8},{9,1... | collective-permute-start | bytes 798728 | tf_op jit(solution)/shard_map/ppermute | solution.py:35
  7.2 0.7 %copy-start.6 = (s32[1,1,8]{2,1,0:T(1,128)S(1)}, s32[1,1,8]{2,1,0:T(1,128)}, u32[]{:S(2)}) copy-start(s32[1,1,8]{2,1,0:T(1,128)} %param.10) | copy-start | bytes 100
  7.3 0.7 %copy-start.7 = (s32[1,1,8]{2,1,0:T(1,128)S(1)}, s32[1,1,8]{2,1,0:T(1,128)}, u32[]{:S(2)}) copy-start(s32[1,1,8]{2,1,0:T(1,128)} %param.11) | copy-start | bytes 100
  7.3 0.7 %copy-start.8 = (s32[1,1,8]{2,1,0:T(1,128)S(1)}, s32[1,1,8]{2,1,0:T(1,128)}, u32[]{:S(2)}) copy-start(s32[1,1,8]{2,1,0:T(1,128)} %param.13) | copy-start | bytes 100
  7.9 0.9 %copy-start.2 = (bf16[8,128,128]{2,1,0:T(8,128)(2,1)S(1)}, bf16[8,128,128]{2,1,0:T(8,128)(2,1)}, u32[]{:S(2)}) copy-start(bf16[8,128,128]{2,1,0:T(8,128)(2,1)} %get-tuple-element.31.taken.refs_2_) | copy-start | bytes 786436
  8.9 0.9 %copy-start.4 = (bf16[1,1,8,128,128]{4,3,2,1,0:T(8,128)(2,1)S(1)}, bf16[1,1,8,128,128]{4,3,2,1,0:T(8,128)(2,1)}, u32[]{:S(2)}) copy-start(bf16[1,1,8,128,128]{4,3,2,1,0:T(8,128)(2,1)} %param.12) | copy-start | bytes 786436
  12.4 7.9 %collective-permute-start.1 = (bf16[1040,128]{1,0:T(8,128)(2,1)S(1)}, bf16[1040,128]{1,0:T(8,128)(2,1)S(1)}, u32[]{:S(2)}, u32[]{:S(2)}) collective-permute-start(bf16[1040,128]{1,0:T(8,128)(2,1)S(1)} %get-tuple-element.38), channel_id=1, source_target_pairs={{0,4},{4,0},{1,5},{5,1},{2,6},{6,2},{3,7},{7,3},{8,12},{12,8},{9,1... | collective-permute-start | bytes 798728 | tf_op jit(solution)/shard_map/ppermute | solution.py:35
  13.9 3.5 %copy-start.5 = (bf16[1,1,8,128,128]{4,3,2,1,0:T(8,128)(2,1)S(1)}, bf16[1,1,8,128,128]{4,3,2,1,0:T(8,128)(2,1)}, u32[]{:S(2)}) copy-start(bf16[1,1,8,128,128]{4,3,2,1,0:T(8,128)(2,1)} %param.12) | copy-start | bytes 786436
  15.5 9.5 %collective-permute-start.5 = (bf16[256,128]{1,0:T(8,128)(2,1)S(1)}, bf16[256,128]{1,0:T(8,128)(2,1)S(1)}, u32[]{:S(2)}, u32[]{:S(2)}) collective-permute-start(bf16[256,128]{1,0:T(8,128)(2,1)S(1)} %get-tuple-element.48), channel_id=1, source_target_pairs={{0,8},{8,0},{16,24},{24,16},{1,9},{9,1},{17,25},{25,17},{2,10},{10... | collective-permute-start | bytes 196616 | tf_op jit(solution)/shard_map/ppermute | solution.py:35
  17.3 2.9 %copy-start.3 = (bf16[8,128,128]{2,1,0:T(8,128)(2,1)S(1)}, bf16[8,128,128]{2,1,0:T(8,128)(2,1)}, u32[]{:S(2)}) copy-start(bf16[8,128,128]{2,1,0:T(8,128)(2,1)} %get-tuple-element.31.taken.refs_2_) | copy-start | bytes 786436
  21.5 6.1 %collective-permute-start.8 = (bf16[256,128]{1,0:T(8,128)(2,1)S(1)}, bf16[256,128]{1,0:T(8,128)(2,1)S(1)}, u32[]{:S(2)}, u32[]{:S(2)}) collective-permute-start(bf16[256,128]{1,0:T(8,128)(2,1)S(1)} %get-tuple-element.54), channel_id=1, source_target_pairs={{0,8},{8,0},{16,24},{24,16},{1,9},{9,1},{17,25},{25,17},{2,10},{10... | collective-permute-start | bytes 196616 | tf_op jit(solution)/shard_map/ppermute | solution.py:35
  23.1 17.4 %collective-permute-start.2 = (bf16[528,128]{1,0:T(8,128)(2,1)S(1)}, bf16[528,128]{1,0:T(8,128)(2,1)S(1)}, u32[]{:S(2)}, u32[]{:S(2)}) collective-permute-start(bf16[528,128]{1,0:T(8,128)(2,1)S(1)} %get-tuple-element.44), channel_id=1, source_target_pairs={{0,1},{1,0},{2,3},{3,2},{4,5},{5,4},{6,7},{7,6},{8,9},{9,8},{10,11... | collective-permute-start | bytes 405512 | tf_op jit(solution)/shard_map/ppermute | solution.py:35
  23.1 17.4 %collective-permute-start.3 = (bf16[528,128]{1,0:T(8,128)(2,1)S(1)}, bf16[528,128]{1,0:T(8,128)(2,1)S(1)}, u32[]{:S(2)}, u32[]{:S(2)}) collective-permute-start(bf16[528,128]{1,0:T(8,128)(2,1)S(1)} %get-tuple-element.45), channel_id=1, source_target_pairs={{0,2},{1,3},{2,0},{3,1},{4,6},{5,7},{6,4},{7,5},{8,10},{9,11},{10,... | collective-permute-start | bytes 405512 | tf_op jit(solution)/shard_map/ppermute | solution.py:35
  24.7 15.9 %collective-permute-start.4 = (bf16[528,128]{1,0:T(8,128)(2,1)S(1)}, bf16[528,128]{1,0:T(8,128)(2,1)S(1)}, u32[]{:S(2)}, u32[]{:S(2)}) collective-permute-start(bf16[528,128]{1,0:T(8,128)(2,1)S(1)} %get-tuple-element.46), channel_id=1, source_target_pairs={{0,3},{1,2},{2,1},{3,0},{4,7},{5,6},{6,5},{7,4},{8,11},{9,10},{10,... | collective-permute-start | bytes 405512 | tf_op jit(solution)/shard_map/ppermute | solution.py:35
  25.0 6.5 %collective-permute-start.9 = (bf16[256,128]{1,0:T(8,128)(2,1)S(1)}, bf16[256,128]{1,0:T(8,128)(2,1)S(1)}, u32[]{:S(2)}, u32[]{:S(2)}) collective-permute-start(bf16[256,128]{1,0:T(8,128)(2,1)S(1)} %get-tuple-element.55), channel_id=1, source_target_pairs={{0,16},{8,24},{16,0},{24,8},{1,17},{9,25},{17,1},{25,9},{2,18},{10... | collective-permute-start | bytes 196616 | tf_op jit(solution)/shard_map/ppermute | solution.py:35
  27.6 6.8 %collective-permute-start.10 = (bf16[256,128]{1,0:T(8,128)(2,1)S(1)}, bf16[256,128]{1,0:T(8,128)(2,1)S(1)}, u32[]{:S(2)}, u32[]{:S(2)}) collective-permute-start(bf16[256,128]{1,0:T(8,128)(2,1)S(1)} %get-tuple-element.56), channel_id=1, source_target_pairs={{0,24},{8,16},{16,8},{24,0},{1,25},{9,17},{17,9},{25,1},{2,26},{10... | collective-permute-start | bytes 196616 | tf_op jit(solution)/shard_map/ppermute | solution.py:35
  31.5 5.3 %collective-permute-start.6 = (bf16[256,128]{1,0:T(8,128)(2,1)S(1)}, bf16[256,128]{1,0:T(8,128)(2,1)S(1)}, u32[]{:S(2)}, u32[]{:S(2)}) collective-permute-start(bf16[256,128]{1,0:T(8,128)(2,1)S(1)} %get-tuple-element.49), channel_id=1, source_target_pairs={{0,16},{8,24},{16,0},{24,8},{1,17},{9,25},{17,1},{25,9},{2,18},{10... | collective-permute-start | bytes 196616 | tf_op jit(solution)/shard_map/ppermute | solution.py:35
  34.4 6.2 %collective-permute-start.7 = (bf16[256,128]{1,0:T(8,128)(2,1)S(1)}, bf16[256,128]{1,0:T(8,128)(2,1)S(1)}, u32[]{:S(2)}, u32[]{:S(2)}) collective-permute-start(bf16[256,128]{1,0:T(8,128)(2,1)S(1)} %get-tuple-element.50), channel_id=1, source_target_pairs={{0,24},{8,16},{16,8},{24,0},{1,25},{9,17},{17,9},{25,1},{2,26},{10... | collective-permute-start | bytes 196616 | tf_op jit(solution)/shard_map/ppermute | solution.py:35

commit v5 on v4

--- a/solution.py
+++ b/solution.py
@@ -13,6 +13,7 @@
 bf16 = jnp.bfloat16
 VMEM = pl.BlockSpec(memory_space=pltpu.VMEM)
 SMEM = pl.BlockSpec(memory_space=pltpu.SMEM)
+ANY = pl.BlockSpec(memory_space=pl.ANY)
 HBM = pl.BlockSpec(memory_space=pltpu.HBM)
 LANES = 128
 PARAMS = pltpu.CompilerParams(vmem_limit_bytes=32 * 1024 * 1024)
@@ -33,6 +34,10 @@
 def send(x, axis, d):
     n = lax.axis_size(axis)
     return lax.ppermute(x, axis, [(i, partner(i, d, n)) for i in range(n)]) if d else x
+
+
+def exchange(shares, axis):
+    return [send(x, axis, d) for d, x in reversed(list(enumerate(shares)))][::-1]
 
 
 def target(axis, d):
@@ -161,11 +166,8 @@
 def back_kernel(dims, tab, peer_tabs, b_own, *refs):
     slots, n_row, n_col, n_tok = dims
     b_peers, refs = refs[: n_row - 1], refs[n_row - 1 :]
-    slope, taken, w1, out = refs[:4]
-    refs = refs[4:]
-    outs, refs = refs[:n_col], refs[n_col:]
-    grads, refs = refs[:n_tok], refs[n_tok:]
-    acc, value, grad = refs
+    slope, w1, out, grad_hidden = refs[:4]
+    outs, (acc, value) = refs[4 : 4 + n_col], refs[4 + n_col :]
     rows = acc.shape[1]
     for k in range(slots):
         acc[tab[W1_COL * slots + k]] = jnp.zeros(acc.shape[1:], f32)
@@ -178,8 +180,7 @@
             acc[at] = acc[at] + ref[k * rows : (k + 1) * rows, :].astype(f32)
     for k in range(slots):
         g = (acc[tab[W1_COL * slots + k]] * slope[k]).astype(bf16)
-        grad[k] = dot(taken[k], g, (0, 0))
-        cut(grad.at[k], grads, k, "tok")
+        grad_hidden[k] = g
         value[k] = dot(g, w1[k], (1, 1))
         cut(value.at[k], outs, slots + k, "col")
     for k in range(slots):
@@ -198,15 +199,24 @@
         result[k] = total
 
 
+def grads_kernel(dims, taken, grad_hidden, *refs):
+    slots, n_row, n_col, n_tok = dims
+    g2_parts, gw2 = refs[:n_tok], refs[n_tok]
+    grads, grad = refs[n_tok + 1 : -1], refs[-1]
+    for k in range(slots):
+        grad[k] = dot(taken[k], grad_hidden[k], (0, 0))
+        cut(grad.at[k], grads, k, "tok")
+    add_shares(g2_parts, gw2)
+
+
 def output_kernel(dims, *refs):
     slots, n_row, n_col, n_tok = dims
     o_parts, refs = refs[:n_col], refs[n_col:]
-    g2_parts, refs = refs[:n_tok], refs[n_tok:]
-    output, grad_in, gw2, acc, ints, scalars, sem = refs
+    output, grad_in, tabs, acc, ints, scalars, sem = refs
     blk, share = acc.shape[-1], acc.shape[1]
     copy = decode_tables(o_parts, 2 * slots * share, ints, scalars, sem)
-    add_shares(g2_parts, gw2)
     copy.wait()
+    tabs[...] = ints[...]
     for first, which, result in ((0, W2_OUT, output), (slots, W1_ROW, grad_in)):
         acc[...] = jnp.zeros(acc.shape, f32)
         for c, ref in enumerate(o_parts):
@@ -218,7 +228,8 @@
             result[:, b * blk : (b + 1) * blk] = acc[b].astype(bf16)
 
 
-def grad_kernel(*refs):
+def grad_kernel(after, *refs):
+    del after
     add_shares(refs[:-1], refs[-1])
 
 
@@ -278,7 +289,7 @@
         compiler_params=PARAMS,
         name="hidden",
     )(tab, p_own, *p_peers, cot)
-    g2_parts = [send(x, "tok", d) for d, x in enumerate(g2_sent)]
+    g2_parts = exchange(g2_sent, "tok")
     out, slope = pl.pallas_call(
         functools.partial(slope_kernel, dims),
         out_shape=(narrow, wide),
@@ -288,28 +299,37 @@
         name="slope",
     )(active, hidden, w2)
 
-    sent = pl.pallas_call(
+    grad_hidden, *o_sent = pl.pallas_call(
         functools.partial(back_kernel, dims),
-        out_shape=outs + parts,
-        in_specs=[SMEM] * 2 + [VMEM] * (n_row + 4),
-        out_specs=(VMEM,) * (n_col + n_tok),
+        out_shape=(narrow,) + outs,
+        in_specs=[SMEM] * 2 + [VMEM] * (n_row + 3),
+        out_specs=(VMEM,) * (1 + n_col),
         scratch_shapes=[
             pltpu.VMEM((col_blocks, rows, blk), f32),
             pltpu.VMEM((slots, rows, blk), f32),
-            pltpu.VMEM((slots, blk, blk), f32),
         ],
         compiler_params=PARAMS,
         name="back",
-    )(tab, peer_tabs, b_own, *b_peers, slope, taken, w1, out)
-    g1_parts = [send(x, "tok", d) for d, x in enumerate(sent[n_col:])]
-    o_parts = [send(x, "col", d) for d, x in enumerate(sent[:n_col])]
+    )(tab, peer_tabs, b_own, *b_peers, slope, w1, out)
+    o_parts = exchange(o_sent, "col")
 
     summed = S((slots, part, blk), f32)
+    gw2, *g1_sent = pl.pallas_call(
+        functools.partial(grads_kernel, dims),
+        out_shape=(summed,) + parts,
+        in_specs=[VMEM] * (2 + n_tok),
+        out_specs=(VMEM,) * (1 + n_tok),
+        scratch_shapes=[pltpu.VMEM((slots, blk, blk), f32)],
+        compiler_params=PARAMS,
+        name="grads",
+    )(taken, grad_hidden, *g2_parts)
+    g1_parts = exchange(g1_sent, "tok")
+
     result = S((share, row_blocks * blk), bf16)
-    output, grad_in, gw2 = pl.pallas_call(
+    output, grad_in, tabs = pl.pallas_call(
         functools.partial(output_kernel, dims),
-        out_shape=(result, result, summed),
-        in_specs=[VMEM] * (n_col + n_tok),
+        out_shape=(result, result, S((8 * n_col, LANES), jnp.int32)),
+        in_specs=[VMEM] * n_col,
         out_specs=(VMEM,) * 3,
         scratch_shapes=[
             pltpu.VMEM((row_blocks, share, blk), f32),
@@ -319,15 +339,15 @@
         ],
         compiler_params=PARAMS,
         name="add_outputs",
-    )(*o_parts, *g2_parts)
+    )(*o_parts)
     gw1 = pl.pallas_call(
         grad_kernel,
         out_shape=summed,
-        in_specs=[VMEM] * n_tok,
+        in_specs=[ANY] + [VMEM] * n_tok,
         out_specs=VMEM,
         compiler_params=PARAMS,
         name="add_grads",
-    )(*g1_parts)
+    )(tabs, *g1_parts)
     return (output, grad_in, gw1.reshape(1, 1, slots, part, blk), gw2.reshape(1, 1, slots, part, blk))
 
 

time: 42.8 us -> 44.7 us (1.044)
  waiting for transfers between devices: 10.7 us -> 12.9 us
  starting transfers between devices: 16.7 us -> 15.6 us
  Pallas kernels: 12 us -> 12.6 us
    ppermute x11, waiting for transfers between devices: 10.7 us -> 12.9 us  [send(): lax.ppermute(x, axis, [(i, partner(i, d, n)) for i in range(n)])]
    ppermute x11, starting transfers between devices: 16.7 us -> 15.6 us  [send(): lax.ppermute(x, axis, [(i, partner(i, d, n)) for i in range(n)])]
    pallas_call x2 -> x3, Pallas kernels: 1.88 us -> 2.65 us  [the longest x1 1.07 us: shards(): pl.pallas_call(functools.partial(back_kernel, dims), out_shape=(narrow,)...]
  transfers between devices with their start and end apart: 11 -> 11, of which waited for: 5 -> 5; matrix products, arithmetic and copies ran while one was open for 0% -> 0% of each run, Pallas kernels for 15% -> 16%
where the time goes in v5:
time: 44.7 us; the launch traced here: 44.4 us
  starting transfers between devices  15.6 us (35%)
  waiting for transfers between devices  12.9 us (29%)
  Pallas kernels  12.6 us (28%)
  local copies, waits for them, and re-layouts  2.58 us (6%)
  between operations  0.76 us (2%)
    ppermute x11, starting transfers between devices, send(): lax.ppermute(x, axis, [(i, partner(i, d, n)) for i in range(n)])  15.6 us
    ppermute x11, waiting for transfers between devices, send(): lax.ppermute(x, axis, [(i, partner(i, d, n)) for i in range(n)])  12.9 us
    pallas_call x1, Pallas kernels, shards(): pl.pallas_call(token_kernel, out_shape=(message, narrow), in_specs=[HBM]...  3.57 us
    unnamed x20, local copies, waits for them, and re-layouts  2.58 us
    pallas_call x1, Pallas kernels, shards(): pl.pallas_call(cotangent_kernel, out_shape=(message, narrow, wide, wide,...  2.52 us
    pallas_call x1, Pallas kernels, shards(): pl.pallas_call(functools.partial(output_kernel, dims), out_shape=(result,...  1.89 us
    pallas_call x1, Pallas kernels, shards(): pl.pallas_call(functools.partial(hidden_kernel, dims), out_shape=(narrow,...  1.58 us
    pallas_call x1, Pallas kernels, shards(): pl.pallas_call(functools.partial(back_kernel, dims), out_shape=(narrow,)...  1.07 us
  transfers between devices with their start and end apart: 11, of which 5 were waited for; matrix products, arithmetic and copies ran while one was open for 0% of the time, Pallas kernels for 16%

profile of v5, /device:TPU:0, one launch (start us, length us, event | category | flops | bytes accessed | tf_op | source)
XLA Modules:
  0.0 44.4 jit_solution(9622209351613718423)
XLA Ops:
  0.6 0.0 copy-start.1
  0.6 0.0 copy-start
  0.7 0.0 copy-start.9
  0.7 3.6 %take_tokens.1 = (bf16[1040,128]{1,0:T(8,128)(2,1)}, bf16[8,128,128]{2,1,0:T(8,128)(2,1)}) custom-call(s32[8]{0:T(128)} %bitcast.13, s32[8]{0:T(128)} %bitcast.15, s32[8]{0:T(128)} %bitcast.17, s32[8]{0:T(128)} %bitcast.19, bf16[128,4096]{1,0:T(8,128)(2,1)} %tokens.1, bf16[8,128,128]{2,1,0:T(8,128)(2,1)} %bitcast.8), custom_call_target="tpu_custom_call" | custom-call | tf_op jit(solution)/shard_map/take_tokens/pallas_call | solution.py:251
  4.2 3.0 %collective-permute-start = (bf16[1040,128]{1,0:T(8,128)(2,1)}, bf16[1040,128]{1,0:T(8,128)(2,1)S(1)}, u32[]{:S(2)}, u32[]{:S(2)}) collective-permute-start(bf16[1040,128]{1,0:T(8,128)(2,1)} %get-tuple-element.36), channel_id=1, source_target_pairs={{0,4},{4,0},{1,5},{5,1},{2,6},{6,2},{3,7},{7,3},{8,12},{12,8},{9,1... | collective-permute-start | bytes 798728 | tf_op jit(solution)/shard_map/ppermute | solution.py:36
  7.2 0.0 copy-start.6
  7.2 0.0 copy-start.7
  7.2 0.0 copy-start.8
  7.2 0.0 copy-done.1
  7.3 0.0 copy-done
  7.3 0.0 copy-done.9
  7.3 0.6 %copy-done.6 = s32[1,1,8]{2,1,0:T(1,128)S(1)} copy-done((s32[1,1,8]{2,1,0:T(1,128)S(1)}, s32[1,1,8]{2,1,0:T(1,128)}, u32[]{:S(2)}) %copy-start.6) | copy-done | bytes 56
  7.9 0.0 copy-done.7
  7.9 0.0 copy-done.8
  7.9 0.0 copy-start.2
  7.9 0.9 %copy-done.2 = bf16[8,128,128]{2,1,0:T(8,128)(2,1)S(1)} copy-done((bf16[8,128,128]{2,1,0:T(8,128)(2,1)S(1)}, bf16[8,128,128]{2,1,0:T(8,128)(2,1)}, u32[]{:S(2)}) %copy-start.2) | copy-done | bytes 262168
  8.9 0.0 copy-start.4
  8.9 0.9 %copy-done.4 = bf16[1,1,8,128,128]{4,3,2,1,0:T(8,128)(2,1)S(1)} copy-done((bf16[1,1,8,128,128]{4,3,2,1,0:T(8,128)(2,1)S(1)}, bf16[1,1,8,128,128]{4,3,2,1,0:T(8,128)(2,1)}, u32[]{:S(2)}) %copy-start.4) | copy-done | bytes 262168
  9.8 2.5 %take_cotangent.1 = (bf16[1040,128]{1,0:T(8,128)(2,1)S(1)}, bf16[8,128,128]{2,1,0:T(8,128)(2,1)S(1)}, f32[8,128,128]{2,1,0:T(8,128)S(1)}, f32[8,128,128]{2,1,0:T(8,128)S(1)}, s32[32]{0:T(128)S(1)}) custom-call(s32[8]{0:T(128)S(1)} %bitcast.14, s32[8]{0:T(128)S(1)} %bitcast.16, s32[8]{0:T(128)S(1)} %bitcast.18, s32[8]{0:T(128)S(1)} %bitcast.20, ...), custom_call_target="tpu_custom_call" | custom-call | tf_op jit(solution)/shard_map/take_cotangent/pallas_call | solution.py:263
  12.4 0.1 collective-permute-start.1
  12.4 1.4 %collective-permute-done.refs_0_ = bf16[1040,128]{1,0:T(8,128)(2,1)S(1)} collective-permute-done((bf16[1040,128]{1,0:T(8,128)(2,1)}, bf16[1040,128]{1,0:T(8,128)(2,1)S(1)}, u32[]{:S(2)}, u32[]{:S(2)}) %collective-permute-start) | collective-permute-done | bytes 266272 | tf_op jit(solution)/shard_map/ppermute | solution.py:36
  13.9 1.6 %hidden.1 = (bf16[8,128,128]{2,1,0:T(8,128)(2,1)S(1)}, f32[8,128,128]{2,1,0:T(8,128)S(1)}, s32[8,128]{1,0:T(8,128)S(1)}, bf16[256,128]{1,0:T(8,128)(2,1)S(1)}, b...) custom-call(s32[32]{0:T(128)S(1)} %get-tuple-element.34.tab, ...), custom_call_target="tpu_custom_call" | custom-call | tf_op jit(solution)/shard_map/hidden/pallas_call | solution.py:277
  15.4 0.0 copy-done.5
  15.5 0.4 slope.1
  15.8 4.5 %collective-permute-done.1.refs_0_ = bf16[1040,128]{1,0:T(8,128)(2,1)S(1)} collective-permute-done((bf16[1040,128]{1,0:T(8,128)(2,1)S(1)}, bf16[1040,128]{1,0:T(8,128)(2,1)S(1)}, u32[]{:S(2)}, u32[]{:S(2)}) %collective-permute-start.1) | collective-permute-done | bytes 266272 | tf_op jit(solution)/shard_map/ppermute | solution.py:36
  20.3 1.1 %back.1 = (bf16[8,128,128]{2,1,0:T(8,128)(2,1)S(1)}, bf16[528,128]{1,0:T(8,128)(2,1)S(1)}, bf16[528,128]{1,0:T(8,128)(2,1)S(1)}, bf16[528,128]{1,0:T(8,128)(2,1)S(1)}, bf16[528,128]{1,0:T(8,128)(2,1)S(1)}) custom-call(s32[32]{0:T(128)S(1)} %get-tuple-element.34.tab, s32[8,128]{1,0:T(8,128)S(1)} %get-tuple-element.38.peer_tabs, ...), custom_call_target="tpu_custom_call" | custom-call | tf_op jit(solution)/shard_map/back/pallas_call | solution.py:302
  21.4 0.1 collective-permute-start.2
  21.4 1.6 %collective-permute-start.5 = (bf16[256,128]{1,0:T(8,128)(2,1)S(1)}, bf16[256,128]{1,0:T(8,128)(2,1)S(1)}, u32[]{:S(2)}, u32[]{:S(2)}) collective-permute-start(bf16[256,128]{1,0:T(8,128)(2,1)S(1)} %get-tuple-element.54), channel_id=1, source_target_pairs={{0,8},{8,0},{16,24},{24,16},{1,9},{9,1},{17,25},{25,17},{2,10},{10... | collective-permute-start | bytes 196616 | tf_op jit(solution)/shard_map/ppermute | solution.py:36
  23.1 1.6 %collective-permute-start.3 = (bf16[528,128]{1,0:T(8,128)(2,1)S(1)}, bf16[528,128]{1,0:T(8,128)(2,1)S(1)}, u32[]{:S(2)}, u32[]{:S(2)}) collective-permute-start(bf16[528,128]{1,0:T(8,128)(2,1)S(1)} %get-tuple-element.47), channel_id=1, source_target_pairs={{0,2},{1,3},{2,0},{3,1},{4,6},{5,7},{6,4},{7,5},{8,10},{9,11},{10,... | collective-permute-start | bytes 405512 | tf_op jit(solution)/shard_map/ppermute | solution.py:36
  24.6 0.0 collective-permute-start.4
  24.6 2.6 %collective-permute-start.6 = (bf16[256,128]{1,0:T(8,128)(2,1)S(1)}, bf16[256,128]{1,0:T(8,128)(2,1)S(1)}, u32[]{:S(2)}, u32[]{:S(2)}) collective-permute-start(bf16[256,128]{1,0:T(8,128)(2,1)S(1)} %get-tuple-element.55), channel_id=1, source_target_pairs={{0,16},{8,24},{16,0},{24,8},{1,17},{9,25},{17,1},{25,9},{2,18},{10... | collective-permute-start | bytes 196616 | tf_op jit(solution)/shard_map/ppermute | solution.py:36
  27.2 0.0 collective-permute-done.5.refs_1_
  27.2 2.3 %collective-permute-start.7 = (bf16[256,128]{1,0:T(8,128)(2,1)S(1)}, bf16[256,128]{1,0:T(8,128)(2,1)S(1)}, u32[]{:S(2)}, u32[]{:S(2)}) collective-permute-start(bf16[256,128]{1,0:T(8,128)(2,1)S(1)} %get-tuple-element.56), channel_id=1, source_target_pairs={{0,24},{8,16},{16,8},{24,0},{1,25},{9,17},{17,9},{25,1},{2,26},{10... | collective-permute-start | bytes 196616 | tf_op jit(solution)/shard_map/ppermute | solution.py:36
  29.5 1.9 %collective-permute-done.6.refs_2_ = bf16[256,128]{1,0:T(8,128)(2,1)S(1)} collective-permute-done((bf16[256,128]{1,0:T(8,128)(2,1)S(1)}, bf16[256,128]{1,0:T(8,128)(2,1)S(1)}, u32[]{:S(2)}, u32[]{:S(2)}) %collective-permute-start.6) | collective-permute-done | bytes 65568 | tf_op jit(solution)/shard_map/ppermute | solution.py:36
  31.4 2.0 %collective-permute-done.7.refs_3_ = bf16[256,128]{1,0:T(8,128)(2,1)S(1)} collective-permute-done((bf16[256,128]{1,0:T(8,128)(2,1)S(1)}, bf16[256,128]{1,0:T(8,128)(2,1)S(1)}, u32[]{:S(2)}, u32[]{:S(2)}) %collective-permute-start.7) | collective-permute-done | bytes 65568 | tf_op jit(solution)/shard_map/ppermute | solution.py:36
  33.4 0.0 copy-done.3
  33.4 0.9 %grads.1 = (f32[8,32,128]{2,1,0:T(8,128)}, bf16[256,128]{1,0:T(8,128)(2,1)S(1)}, bf16[256,128]{1,0:T(8,128)(2,1)S(1)}, bf16[256,128]{1,0:T(8,128)(2,1)S(1)}, bf16[256,128]{1,0:T(8,128)(2,1)S(1)}) custom-call(bf16[8,128,128]{2,1,0:T(8,128)(2,1)S(1)} %copy-done.3, bf16[8,128,128]{2,1,0:T(8,128)(2,1)S(1)} %get-tuple-element.52.grad_hidden, ...), custom_call_target="tpu_custom_call" | custom-call | tf_op jit(solution)/shard_map/grads/pallas_call | solution.py:317
  34.3 1.3 %collective-permute-start.8 = (bf16[256,128]{1,0:T(8,128)(2,1)S(1)}, bf16[256,128]{1,0:T(8,128)(2,1)S(1)}, u32[]{:S(2)}, u32[]{:S(2)}) collective-permute-start(bf16[256,128]{1,0:T(8,128)(2,1)S(1)} %get-tuple-element.58), channel_id=1, source_target_pairs={{0,8},{8,0},{16,24},{24,16},{1,9},{9,1},{17,25},{25,17},{2,10},{10... | collective-permute-start | bytes 196616 | tf_op jit(solution)/shard_map/ppermute | solution.py:36
  35.7 1.5 %collective-permute-start.9 = (bf16[256,128]{1,0:T(8,128)(2,1)S(1)}, bf16[256,128]{1,0:T(8,128)(2,1)S(1)}, u32[]{:S(2)}, u32[]{:S(2)}) collective-permute-start(bf16[256,128]{1,0:T(8,128)(2,1)S(1)} %get-tuple-element.59), channel_id=1, source_target_pairs={{0,16},{8,24},{16,0},{24,8},{1,17},{9,25},{17,1},{25,9},{2,18},{10... | collective-permute-start | bytes 196616 | tf_op jit(solution)/shard_map/ppermute | solution.py:36
  37.2 0.0 collective-permute-done.2.refs_1_
  37.2 1.5 %collective-permute-start.10 = (bf16[256,128]{1,0:T(8,128)(2,1)S(1)}, bf16[256,128]{1,0:T(8,128)(2,1)S(1)}, u32[]{:S(2)}, u32[]{:S(2)}) collective-permute-start(bf16[256,128]{1,0:T(8,128)(2,1)S(1)} %get-tuple-element.60), channel_id=1, source_target_pairs={{0,24},{8,16},{16,8},{24,0},{1,25},{9,17},{17,9},{25,1},{2,26},{10... | collective-permute-start | bytes 196616 | tf_op jit(solution)/shard_map/ppermute | solution.py:36
  38.7 0.0 collective-permute-done.3.refs_2_
  38.7 0.0 collective-permute-done.4.refs_3_
  38.7 1.9 %add_outputs.1 = (bf16[32,4096]{1,0:T(8,128)(2,1)}, bf16[32,4096]{1,0:T(8,128)(2,1)}, s32[32,128]{1,0:T(8,128)S(1)}) custom-call(bf16[528,128]{1,0:T(8,128)(2,1)S(1)} %get-tuple-element.45.refs_0_, bf16[528,128]{1,0:T(8,128)(2,1)S(1)} %collective-permute-done.2.refs_1_, bf16[528,128]{1,0:T(8,128)(2,1)S(1)} %collective-permute-done.3.refs_2_, ...), custom_call_target="tpu_custom_call" | custom-call | tf_op jit(solution)/shard_map/add_outputs/pallas_call | solution.py:329
  40.6 0.0 collective-permute-done.8.refs_1_
  40.6 3.1 %collective-permute-done.9.refs_2_ = bf16[256,128]{1,0:T(8,128)(2,1)S(1)} collective-permute-done((bf16[256,128]{1,0:T(8,128)(2,1)S(1)}, bf16[256,128]{1,0:T(8,128)(2,1)S(1)}, u32[]{:S(2)}, u32[]{:S(2)}) %collective-permute-start.9) | collective-permute-done | bytes 65568 | tf_op jit(solution)/shard_map/ppermute | solution.py:36
  43.7 0.0 collective-permute-done.10.refs_3_
  43.7 0.7 %add_grads.1 = f32[8,32,128]{2,1,0:T(8,128)} custom-call(s32[32,128]{1,0:T(8,128)S(1)} %get-tuple-element.51.after, bf16[256,128]{1,0:T(8,128)(2,1)S(1)} %get-tuple-element.57.refs_0_, bf16[256,128]{1,0:T(8,128)(2,1)S(1)} %collective-permute-done.8.refs_1_, bf16[256,128]{1,0:T(8,128)(2,1)S(1)} %collective-permute-done.9.refs_2_, ...), custom_call_target="tpu_custom_call" | custom-call | tf_op jit(solution)/shard_map/add_grads/pallas_call | solution.py:343
  (2 shorter events, 0.0 us)
Async XLA Ops:
  0.6 6.6 %copy-start.1 = (bf16[128,4096]{1,0:T(8,128)(2,1)S(1)}, bf16[128,4096]{1,0:T(8,128)(2,1)}, u32[]{:S(2)}) copy-start(bf16[128,4096]{1,0:T(8,128)(2,1)} %grad_out.1) | copy-start | bytes 3145732
  0.6 6.6 %copy-start = (bf16[1,1,8,128,128]{4,3,2,1,0:T(8,128)(2,1)S(1)}, bf16[1,1,8,128,128]{4,3,2,1,0:T(8,128)(2,1)}, u32[]{:S(2)}) copy-start(bf16[1,1,8,128,128]{4,3,2,1,0:T(8,128)(2,1)} %param.9) | copy-start | bytes 786436
  0.7 6.6 %copy-start.9 = (s32[1,1,8]{2,1,0:T(1,128)S(1)}, s32[1,1,8]{2,1,0:T(1,128)}, u32[]{:S(2)}) copy-start(s32[1,1,8]{2,1,0:T(1,128)} %param.14) | copy-start | bytes 100
  4.2 9.6 %collective-permute-start = (bf16[1040,128]{1,0:T(8,128)(2,1)}, bf16[1040,128]{1,0:T(8,128)(2,1)S(1)}, u32[]{:S(2)}, u32[]{:S(2)}) collective-permute-start(bf16[1040,128]{1,0:T(8,128)(2,1)} %get-tuple-element.36), channel_id=1, source_target_pairs={{0,4},{4,0},{1,5},{5,1},{2,6},{6,2},{3,7},{7,3},{8,12},{12,8},{9,1... | collective-permute-start | bytes 798728 | tf_op jit(solution)/shard_map/ppermute | solution.py:36
  7.2 0.7 %copy-start.6 = (s32[1,1,8]{2,1,0:T(1,128)S(1)}, s32[1,1,8]{2,1,0:T(1,128)}, u32[]{:S(2)}) copy-start(s32[1,1,8]{2,1,0:T(1,128)} %param.10) | copy-start | bytes 100
  7.2 0.7 %copy-start.7 = (s32[1,1,8]{2,1,0:T(1,128)S(1)}, s32[1,1,8]{2,1,0:T(1,128)}, u32[]{:S(2)}) copy-start(s32[1,1,8]{2,1,0:T(1,128)} %param.11) | copy-start | bytes 100
  7.2 0.7 %copy-start.8 = (s32[1,1,8]{2,1,0:T(1,128)S(1)}, s32[1,1,8]{2,1,0:T(1,128)}, u32[]{:S(2)}) copy-start(s32[1,1,8]{2,1,0:T(1,128)} %param.13) | copy-start | bytes 100
  7.9 0.9 %copy-start.2 = (bf16[8,128,128]{2,1,0:T(8,128)(2,1)S(1)}, bf16[8,128,128]{2,1,0:T(8,128)(2,1)}, u32[]{:S(2)}) copy-start(bf16[8,128,128]{2,1,0:T(8,128)(2,1)} %get-tuple-element.33.taken) | copy-start | bytes 786436
  8.9 0.9 %copy-start.4 = (bf16[1,1,8,128,128]{4,3,2,1,0:T(8,128)(2,1)S(1)}, bf16[1,1,8,128,128]{4,3,2,1,0:T(8,128)(2,1)}, u32[]{:S(2)}) copy-start(bf16[1,1,8,128,128]{4,3,2,1,0:T(8,128)(2,1)} %param.12) | copy-start | bytes 786436
  12.4 7.9 %collective-permute-start.1 = (bf16[1040,128]{1,0:T(8,128)(2,1)S(1)}, bf16[1040,128]{1,0:T(8,128)(2,1)S(1)}, u32[]{:S(2)}, u32[]{:S(2)}) collective-permute-start(bf16[1040,128]{1,0:T(8,128)(2,1)S(1)} %get-tuple-element.40), channel_id=1, source_target_pairs={{0,4},{4,0},{1,5},{5,1},{2,6},{6,2},{3,7},{7,3},{8,12},{12,8},{9,1... | collective-permute-start | bytes 798728 | tf_op jit(solution)/shard_map/ppermute | solution.py:36
  13.9 1.6 %copy-start.5 = (bf16[1,1,8,128,128]{4,3,2,1,0:T(8,128)(2,1)S(1)}, bf16[1,1,8,128,128]{4,3,2,1,0:T(8,128)(2,1)}, u32[]{:S(2)}) copy-start(bf16[1,1,8,128,128]{4,3,2,1,0:T(8,128)(2,1)} %param.12) | copy-start | bytes 786436
  20.3 13.2 %copy-start.3 = (bf16[8,128,128]{2,1,0:T(8,128)(2,1)S(1)}, bf16[8,128,128]{2,1,0:T(8,128)(2,1)}, u32[]{:S(2)}) copy-start(bf16[8,128,128]{2,1,0:T(8,128)(2,1)} %get-tuple-element.33.taken) | copy-start | bytes 786436
  21.4 15.8 %collective-permute-start.2 = (bf16[528,128]{1,0:T(8,128)(2,1)S(1)}, bf16[528,128]{1,0:T(8,128)(2,1)S(1)}, u32[]{:S(2)}, u32[]{:S(2)}) collective-permute-start(bf16[528,128]{1,0:T(8,128)(2,1)S(1)} %get-tuple-element.46), channel_id=1, source_target_pairs={{0,1},{1,0},{2,3},{3,2},{4,5},{5,4},{6,7},{7,6},{8,9},{9,8},{10,11... | collective-permute-start | bytes 405512 | tf_op jit(solution)/shard_map/ppermute | solution.py:36
  21.4 5.8 %collective-permute-start.5 = (bf16[256,128]{1,0:T(8,128)(2,1)S(1)}, bf16[256,128]{1,0:T(8,128)(2,1)S(1)}, u32[]{:S(2)}, u32[]{:S(2)}) collective-permute-start(bf16[256,128]{1,0:T(8,128)(2,1)S(1)} %get-tuple-element.54), channel_id=1, source_target_pairs={{0,8},{8,0},{16,24},{24,16},{1,9},{9,1},{17,25},{25,17},{2,10},{10... | collective-permute-start | bytes 196616 | tf_op jit(solution)/shard_map/ppermute | solution.py:36
  23.1 15.7 %collective-permute-start.3 = (bf16[528,128]{1,0:T(8,128)(2,1)S(1)}, bf16[528,128]{1,0:T(8,128)(2,1)S(1)}, u32[]{:S(2)}, u32[]{:S(2)}) collective-permute-start(bf16[528,128]{1,0:T(8,128)(2,1)S(1)} %get-tuple-element.47), channel_id=1, source_target_pairs={{0,2},{1,3},{2,0},{3,1},{4,6},{5,7},{6,4},{7,5},{8,10},{9,11},{10,... | collective-permute-start | bytes 405512 | tf_op jit(solution)/shard_map/ppermute | solution.py:36
  24.6 14.1 %collective-permute-start.4 = (bf16[528,128]{1,0:T(8,128)(2,1)S(1)}, bf16[528,128]{1,0:T(8,128)(2,1)S(1)}, u32[]{:S(2)}, u32[]{:S(2)}) collective-permute-start(bf16[528,128]{1,0:T(8,128)(2,1)S(1)} %get-tuple-element.48), channel_id=1, source_target_pairs={{0,3},{1,2},{2,1},{3,0},{4,7},{5,6},{6,5},{7,4},{8,11},{9,10},{10,... | collective-permute-start | bytes 405512 | tf_op jit(solution)/shard_map/ppermute | solution.py:36
  24.6 6.8 %collective-permute-start.6 = (bf16[256,128]{1,0:T(8,128)(2,1)S(1)}, bf16[256,128]{1,0:T(8,128)(2,1)S(1)}, u32[]{:S(2)}, u32[]{:S(2)}) collective-permute-start(bf16[256,128]{1,0:T(8,128)(2,1)S(1)} %get-tuple-element.55), channel_id=1, source_target_pairs={{0,16},{8,24},{16,0},{24,8},{1,17},{9,25},{17,1},{25,9},{2,18},{10... | collective-permute-start | bytes 196616 | tf_op jit(solution)/shard_map/ppermute | solution.py:36
  27.2 6.2 %collective-permute-start.7 = (bf16[256,128]{1,0:T(8,128)(2,1)S(1)}, bf16[256,128]{1,0:T(8,128)(2,1)S(1)}, u32[]{:S(2)}, u32[]{:S(2)}) collective-permute-start(bf16[256,128]{1,0:T(8,128)(2,1)S(1)} %get-tuple-element.56), channel_id=1, source_target_pairs={{0,24},{8,16},{16,8},{24,0},{1,25},{9,17},{17,9},{25,1},{2,26},{10... | collective-permute-start | bytes 196616 | tf_op jit(solution)/shard_map/ppermute | solution.py:36
  34.3 6.3 %collective-permute-start.8 = (bf16[256,128]{1,0:T(8,128)(2,1)S(1)}, bf16[256,128]{1,0:T(8,128)(2,1)S(1)}, u32[]{:S(2)}, u32[]{:S(2)}) collective-permute-start(bf16[256,128]{1,0:T(8,128)(2,1)S(1)} %get-tuple-element.58), channel_id=1, source_target_pairs={{0,8},{8,0},{16,24},{24,16},{1,9},{9,1},{17,25},{25,17},{2,10},{10... | collective-permute-start | bytes 196616 | tf_op jit(solution)/shard_map/ppermute | solution.py:36
  35.7 8.1 %collective-permute-start.9 = (bf16[256,128]{1,0:T(8,128)(2,1)S(1)}, bf16[256,128]{1,0:T(8,128)(2,1)S(1)}, u32[]{:S(2)}, u32[]{:S(2)}) collective-permute-start(bf16[256,128]{1,0:T(8,128)(2,1)S(1)} %get-tuple-element.59), channel_id=1, source_target_pairs={{0,16},{8,24},{16,0},{24,8},{1,17},{9,25},{17,1},{25,9},{2,18},{10... | collective-permute-start | bytes 196616 | tf_op jit(solution)/shard_map/ppermute | solution.py:36
  37.2 6.6 %collective-permute-start.10 = (bf16[256,128]{1,0:T(8,128)(2,1)S(1)}, bf16[256,128]{1,0:T(8,128)(2,1)S(1)}, u32[]{:S(2)}, u32[]{:S(2)}) collective-permute-start(bf16[256,128]{1,0:T(8,128)(2,1)S(1)} %get-tuple-element.60), channel_id=1, source_target_pairs={{0,24},{8,16},{16,8},{24,0},{1,25},{9,17},{17,9},{25,1},{2,26},{10... | collective-permute-start | bytes 196616 | tf_op jit(solution)/shard_map/ppermute | solution.py:36

commit v6 on v4

--- a/solution.py
+++ b/solution.py
@@ -13,6 +13,7 @@
 bf16 = jnp.bfloat16
 VMEM = pl.BlockSpec(memory_space=pltpu.VMEM)
 SMEM = pl.BlockSpec(memory_space=pltpu.SMEM)
+ANY = pl.BlockSpec(memory_space=pl.ANY)
 HBM = pl.BlockSpec(memory_space=pltpu.HBM)
 LANES = 128
 PARAMS = pltpu.CompilerParams(vmem_limit_bytes=32 * 1024 * 1024)
@@ -33,6 +34,10 @@
 def send(x, axis, d):
     n = lax.axis_size(axis)
     return lax.ppermute(x, axis, [(i, partner(i, d, n)) for i in range(n)]) if d else x
+
+
+def exchange(shares, axis):
+    return [send(x, axis, d) for d, x in reversed(list(enumerate(shares)))][::-1]
 
 
 def target(axis, d):
@@ -135,15 +140,18 @@
 def hidden_kernel(dims, tab, p_own, *refs):
     slots, n_row, n_col, n_tok = dims
     p_peers, refs = refs[: n_row - 1], refs[n_row - 1 :]
-    cot, active, hidden, peer_tabs = refs[:4]
-    grads, refs = refs[4 : 4 + n_tok], refs[4 + n_tok :]
-    acc, grad, *scratch = refs
+    cot, active, hidden, peer_tabs, grad, half, acc, *scratch = refs
+    part = grad.shape[1] // n_tok
+    other = 1 - lax.rem(lax.axis_index("tok"), 2)
     sum_at(acc, (W1_COL, W2_HID), tab, W1_COL, p_own, p_peers, W1_COL, slots, scratch)
     for k in range(slots):
         h = acc[tab[W2_HID * slots + k]]
         active[k] = (h * cdf(h)).astype(bf16)
         grad[k] = dot(active[k], cot[k], (0, 0))
-        cut(grad.at[k], grads, k, "tok")
+        for j in range(n_tok // 2):
+            begin = pl.multiple_of((2 * j + other) * part, part)
+            here = (j * slots + k) * part
+            half[here : here + part, :] = grad[k, pl.ds(begin, part), :].astype(bf16)
     for k in range(slots):
         hidden[k] = acc[tab[W1_COL * slots + k]]
     peer_tabs[...] = scratch[0][...]
@@ -161,11 +169,11 @@
 def back_kernel(dims, tab, peer_tabs, b_own, *refs):
     slots, n_row, n_col, n_tok = dims
     b_peers, refs = refs[: n_row - 1], refs[n_row - 1 :]
-    slope, taken, w1, out = refs[:4]
-    refs = refs[4:]
+    slope, w1, out, taken, grad2, half = refs[:6]
+    refs = refs[6:]
     outs, refs = refs[:n_col], refs[n_col:]
-    grads, refs = refs[:n_tok], refs[n_tok:]
-    acc, value, grad = refs
+    grads, (acc, value, grad) = refs[:n_tok], refs[n_tok:]
+    part = grad.shape[1] // n_tok
     rows = acc.shape[1]
     for k in range(slots):
         acc[tab[W1_COL * slots + k]] = jnp.zeros(acc.shape[1:], f32)
@@ -184,14 +192,23 @@
         cut(value.at[k], outs, slots + k, "col")
     for k in range(slots):
         cut(out.at[k], outs, k, "col")
+    for d in range(0, n_tok, 2 if n_tok % 2 == 0 else 1):
+        to = target("tok", d)
+        begin = pl.multiple_of(to * part, part)
+        for k in range(slots):
+            total = grad2[k, pl.ds(begin, part), :]
+            if n_tok % 2 == 0:
+                there = pl.multiple_of((lax.div(to, 2) * slots + k) * part, part)
+                total = total + half[pl.ds(there, part), :].astype(f32)
+            grads[d][(slots + k) * part : (slots + k + 1) * part, :] = total.astype(bf16)
     row = table_row([[tab[which * slots + k] for k in range(slots)] for which in range(4)], slots)
     for ref in outs:
         ref[ref.shape[0] - 16 :, :] = row
 
 
-def add_shares(parts, result):
+def add_shares(parts, result, first):
     for k in range(result.shape[0]):
-        here = slice(k * result.shape[1], (k + 1) * result.shape[1])
+        here = slice((first + k) * result.shape[1], (first + k + 1) * result.shape[1])
         total = parts[0][here, :].astype(f32)
         for ref in parts[1:]:
             total = total + ref[here, :].astype(f32)
@@ -201,12 +218,11 @@
 def output_kernel(dims, *refs):
     slots, n_row, n_col, n_tok = dims
     o_parts, refs = refs[:n_col], refs[n_col:]
-    g2_parts, refs = refs[:n_tok], refs[n_tok:]
-    output, grad_in, gw2, acc, ints, scalars, sem = refs
+    output, grad_in, tabs, acc, ints, scalars, sem = refs
     blk, share = acc.shape[-1], acc.shape[1]
     copy = decode_tables(o_parts, 2 * slots * share, ints, scalars, sem)
-    add_shares(g2_parts, gw2)
     copy.wait()
+    tabs[...] = ints[...]
     for first, which, result in ((0, W2_OUT, output), (slots, W1_ROW, grad_in)):
         acc[...] = jnp.zeros(acc.shape, f32)
         for c, ref in enumerate(o_parts):
@@ -218,8 +234,12 @@
             result[:, b * blk : (b + 1) * blk] = acc[b].astype(bf16)
 
 
-def grad_kernel(*refs):
-    add_shares(refs[:-1], refs[-1])
+def grad_kernel(after, *refs):
+    del after
+    parts, gw1, gw2 = refs[:-2], refs[-2], refs[-1]
+    slots = gw1.shape[0]
+    add_shares(parts, gw1, 0)
+    add_shares([ref for ref in parts if ref.shape[0] > slots * gw1.shape[1]], gw2, slots)
 
 
 def shards(tokens, w1_blocks, w1_rows, w1_cols, w2_blocks, w2_hidden, w2_outs, grad_out):
@@ -260,17 +280,18 @@
     )(*tables, grad_out, w1, w2, taken)
     b_peers = [send(b_send, "row", d) for d in range(1, n_row)]
 
-    parts = (S((slots * part, blk), bf16),) * n_tok
+    both = [n_tok % 2 == 1 or d % 2 == 0 for d in range(n_tok)]
+    grads = tuple(S(((2 if b else 1) * slots * part, blk), bf16) for b in both)
+    half = S((max(1, n_tok // 2) * slots * part, blk), bf16)
     outs = (S((2 * slots * share + 16, blk), bf16),) * n_col
     peer_rows = 8 * max(1, n_row - 1)
-    active, hidden, peer_tabs, *g2_sent = pl.pallas_call(
+    active, hidden, peer_tabs, grad2, half = pl.pallas_call(
         functools.partial(hidden_kernel, dims),
-        out_shape=(narrow, wide, S((peer_rows, LANES), jnp.int32)) + parts,
+        out_shape=(narrow, wide, S((peer_rows, LANES), jnp.int32), S((slots, blk, blk), f32), half),
         in_specs=[SMEM] + [VMEM] * (n_row + 1),
-        out_specs=(VMEM,) * (3 + n_tok),
+        out_specs=(VMEM,) * 5,
         scratch_shapes=[
             pltpu.VMEM((col_blocks, rows, blk), f32),
-            pltpu.VMEM((slots, blk, blk), f32),
             pltpu.VMEM((peer_rows, LANES), jnp.int32),
             pltpu.SMEM((peer_rows, LANES), jnp.int32),
             pltpu.SemaphoreType.DMA,
@@ -278,7 +299,8 @@
         compiler_params=PARAMS,
         name="hidden",
     )(tab, p_own, *p_peers, cot)
-    g2_parts = [send(x, "tok", d) for d, x in enumerate(g2_sent)]
+    if n_tok % 2 == 0:
+        half = lax.ppermute(half, "tok", [(i, i ^ 1) for i in range(n_tok)])
     out, slope = pl.pallas_call(
         functools.partial(slope_kernel, dims),
         out_shape=(narrow, wide),
@@ -290,8 +312,8 @@
 
     sent = pl.pallas_call(
         functools.partial(back_kernel, dims),
-        out_shape=outs + parts,
-        in_specs=[SMEM] * 2 + [VMEM] * (n_row + 4),
+        out_shape=outs + grads,
+        in_specs=[SMEM] * 2 + [VMEM] * (n_row + 6),
         out_specs=(VMEM,) * (n_col + n_tok),
         scratch_shapes=[
             pltpu.VMEM((col_blocks, rows, blk), f32),
@@ -300,16 +322,15 @@
         ],
         compiler_params=PARAMS,
         name="back",
-    )(tab, peer_tabs, b_own, *b_peers, slope, taken, w1, out)
-    g1_parts = [send(x, "tok", d) for d, x in enumerate(sent[n_col:])]
-    o_parts = [send(x, "col", d) for d, x in enumerate(sent[:n_col])]
-
-    summed = S((slots, part, blk), f32)
+    )(tab, peer_tabs, b_own, *b_peers, slope, w1, out, taken, grad2, half)
+    g_parts = exchange(sent[n_col:], "tok")
+    o_parts = exchange(sent[:n_col], "col")
+
     result = S((share, row_blocks * blk), bf16)
-    output, grad_in, gw2 = pl.pallas_call(
+    output, grad_in, tabs = pl.pallas_call(
         functools.partial(output_kernel, dims),
-        out_shape=(result, result, summed),
-        in_specs=[VMEM] * (n_col + n_tok),
+        out_shape=(result, result, S((8 * n_col, LANES), jnp.int32)),
+        in_specs=[VMEM] * n_col,
         out_specs=(VMEM,) * 3,
         scratch_shapes=[
             pltpu.VMEM((row_blocks, share, blk), f32),
@@ -319,15 +340,16 @@
         ],
         compiler_params=PARAMS,
         name="add_outputs",
-    )(*o_parts, *g2_parts)
-    gw1 = pl.pallas_call(
+    )(*o_parts)
+    summed = S((slots, part, blk), f32)
+    gw1, gw2 = pl.pallas_call(
         grad_kernel,
-        out_shape=summed,
-        in_specs=[VMEM] * n_tok,
-        out_specs=VMEM,
+        out_shape=(summed, summed),
+        in_specs=[ANY] + [VMEM] * n_tok,
+        out_specs=(VMEM,) * 2,
         compiler_params=PARAMS,
         name="add_grads",
-    )(*g1_parts)
+    )(tabs, *g_parts)
     return (output, grad_in, gw1.reshape(1, 1, slots, part, blk), gw2.reshape(1, 1, slots, part, blk))
 
 

time: 42.8 us -> 36.3 us (0.85)
  starting transfers between devices: 16.7 us -> 11.3 us
  waiting for transfers between devices: 10.7 us -> 9.32 us
    ppermute x11 -> x8, starting transfers between devices: 16.7 us -> 9.44 us  [send(): lax.ppermute(x, axis, [(i, partner(i, d, n)) for i in range(n)])]
    ppermute x0 -> x1, starting transfers between devices: none -> 1.88 us  [shards(): half = lax.ppermute(half, 'tok', [(i, i ^ 1) for i in range(n_tok)])]
    ppermute x11 -> x8, waiting for transfers between devices: 10.7 us -> 9.11 us  [send(): lax.ppermute(x, axis, [(i, partner(i, d, n)) for i in range(n)])]
  transfers between devices with their start and end apart: 11 -> 9, of which waited for: 5 -> 7; matrix products, arithmetic and copies ran while one was open for 0% -> 0% of each run, Pallas kernels for 15% -> 18%
where the time goes in v6:
time: 36.3 us; the launch traced here: 35.8 us
  Pallas kernels  11.9 us (33%)
  starting transfers between devices  11.3 us (31%)
  waiting for transfers between devices  9.32 us (26%)
  local copies, waits for them, and re-layouts  2.58 us (7%)
  between operations  0.75 us (2%)
    ppermute x8, starting transfers between devices, send(): lax.ppermute(x, axis, [(i, partner(i, d, n)) for i in range(n)])  9.44 us
    ppermute x8, waiting for transfers between devices, send(): lax.ppermute(x, axis, [(i, partner(i, d, n)) for i in range(n)])  9.11 us
    pallas_call x1, Pallas kernels, shards(): pl.pallas_call(token_kernel, out_shape=(message, narrow), in_specs=[HBM]...  3.57 us
    unnamed x20, local copies, waits for them, and re-layouts  2.58 us
    pallas_call x1, Pallas kernels, shards(): pl.pallas_call(cotangent_kernel, out_shape=(message, narrow, wide, wide,...  2.52 us
    pallas_call x1, Pallas kernels, shards(): pl.pallas_call(functools.partial(output_kernel, dims), out_shape=(result,...  1.89 us
    ppermute x1, starting transfers between devices, shards(): half = lax.ppermute(half, 'tok', [(i, i ^ 1) for i in range(n_tok)])  1.88 us
    pallas_call x1, Pallas kernels, shards(): pl.pallas_call(functools.partial(hidden_kernel, dims), out_shape=(narrow,...  1.59 us
  transfers between devices with their start and end apart: 9, of which 7 were waited for; matrix products, arithmetic and copies ran while one was open for 0% of the time, Pallas kernels for 18%

profile of v6, /device:TPU:0, one launch (start us, length us, event | category | flops | bytes accessed | tf_op | source)
XLA Modules:
  0.0 35.8 jit_solution(9514559642261187311)
XLA Ops:
  0.6 0.0 copy-start.1
  0.6 0.0 copy-start
  0.7 0.0 copy-start.9
  0.7 3.6 %take_tokens.1 = (bf16[1040,128]{1,0:T(8,128)(2,1)}, bf16[8,128,128]{2,1,0:T(8,128)(2,1)}) custom-call(s32[8]{0:T(128)} %bitcast.13, s32[8]{0:T(128)} %bitcast.15, s32[8]{0:T(128)} %bitcast.17, s32[8]{0:T(128)} %bitcast.19, bf16[128,4096]{1,0:T(8,128)(2,1)} %tokens.1, bf16[8,128,128]{2,1,0:T(8,128)(2,1)} %bitcast.8), custom_call_target="tpu_custom_call" | custom-call | tf_op jit(solution)/shard_map/take_tokens/pallas_call | solution.py:260
  4.2 3.0 %collective-permute-start = (bf16[1040,128]{1,0:T(8,128)(2,1)}, bf16[1040,128]{1,0:T(8,128)(2,1)S(1)}, u32[]{:S(2)}, u32[]{:S(2)}) collective-permute-start(bf16[1040,128]{1,0:T(8,128)(2,1)} %get-tuple-element.34), channel_id=1, source_target_pairs={{0,4},{4,0},{1,5},{5,1},{2,6},{6,2},{3,7},{7,3},{8,12},{12,8},{9,1... | collective-permute-start | bytes 798728 | tf_op jit(solution)/shard_map/ppermute | solution.py:36
  7.2 0.0 copy-start.6
  7.2 0.0 copy-start.7
  7.3 0.0 copy-start.8
  7.3 0.0 copy-done.1
  7.3 0.0 copy-done
  7.3 0.0 copy-done.9
  7.3 0.6 %copy-done.6 = s32[1,1,8]{2,1,0:T(1,128)S(1)} copy-done((s32[1,1,8]{2,1,0:T(1,128)S(1)}, s32[1,1,8]{2,1,0:T(1,128)}, u32[]{:S(2)}) %copy-start.6) | copy-done | bytes 56
  7.9 0.0 copy-done.7
  7.9 0.0 copy-done.8
  7.9 0.0 copy-start.2
  7.9 0.9 %copy-done.2 = bf16[8,128,128]{2,1,0:T(8,128)(2,1)S(1)} copy-done((bf16[8,128,128]{2,1,0:T(8,128)(2,1)S(1)}, bf16[8,128,128]{2,1,0:T(8,128)(2,1)}, u32[]{:S(2)}) %copy-start.2) | copy-done | bytes 262168
  8.9 0.0 copy-start.4
  8.9 0.9 %copy-done.4 = bf16[1,1,8,128,128]{4,3,2,1,0:T(8,128)(2,1)S(1)} copy-done((bf16[1,1,8,128,128]{4,3,2,1,0:T(8,128)(2,1)S(1)}, bf16[1,1,8,128,128]{4,3,2,1,0:T(8,128)(2,1)}, u32[]{:S(2)}) %copy-start.4) | copy-done | bytes 262168
  9.8 2.5 %take_cotangent.1 = (bf16[1040,128]{1,0:T(8,128)(2,1)S(1)}, bf16[8,128,128]{2,1,0:T(8,128)(2,1)S(1)}, f32[8,128,128]{2,1,0:T(8,128)S(1)}, f32[8,128,128]{2,1,0:T(8,128)S(1)}, s32[32]{0:T(128)S(1)}) custom-call(s32[8]{0:T(128)S(1)} %bitcast.14, s32[8]{0:T(128)S(1)} %bitcast.16, s32[8]{0:T(128)S(1)} %bitcast.18, s32[8]{0:T(128)S(1)} %bitcast.20, ...), custom_call_target="tpu_custom_call" | custom-call | tf_op jit(solution)/shard_map/take_cotangent/pallas_call | solution.py:272
  12.4 0.1 collective-permute-start.1
  12.4 1.4 %collective-permute-done.refs_0_ = bf16[1040,128]{1,0:T(8,128)(2,1)S(1)} collective-permute-done((bf16[1040,128]{1,0:T(8,128)(2,1)}, bf16[1040,128]{1,0:T(8,128)(2,1)S(1)}, u32[]{:S(2)}, u32[]{:S(2)}) %collective-permute-start) | collective-permute-done | bytes 266272 | tf_op jit(solution)/shard_map/ppermute | solution.py:36
  13.9 0.0 copy-start.5
  13.9 1.6 %hidden.1 = (bf16[8,128,128]{2,1,0:T(8,128)(2,1)S(1)}, f32[8,128,128]{2,1,0:T(8,128)S(1)}, s32[8,128]{1,0:T(8,128)S(1)}, f32[8,128,128]{2,1,0:T(8,128)S(1)}, bf16[512,128]{1,0:T(8,128)(2,1)S(1)}) custom-call(s32[32]{0:T(128)S(1)} %get-tuple-element.32.tab, f32[8,128,128]{2,1,0:T(8,128)S(1)} %get-tuple-element.33.p_own, ...), custom_call_target="tpu_custom_call" | custom-call | tf_op jit(solution)/shard_map/hidden/pallas_call | solution.py:288
  15.5 1.9 %collective-permute-start.2 = (bf16[512,128]{1,0:T(8,128)(2,1)S(1)}, bf16[512,128]{1,0:T(8,128)(2,1)S(1)}, u32[]{:S(2)}, u32[]{:S(2)}) collective-permute-start(bf16[512,128]{1,0:T(8,128)(2,1)S(1)} %get-tuple-element.44), channel_id=1, source_target_pairs={{0,8},{8,0},{16,24},{24,16},{1,9},{9,1},{17,25},{25,17},{2,10},{10... | collective-permute-start | bytes 393224 | tf_op jit(solution)/shard_map/ppermute | solution.py:303
  17.3 0.0 copy-done.5
  17.3 0.0 copy-start.3
  17.4 0.3 slope.1
  17.7 2.6 %collective-permute-done.1.refs_0_ = bf16[1040,128]{1,0:T(8,128)(2,1)S(1)} collective-permute-done((bf16[1040,128]{1,0:T(8,128)(2,1)S(1)}, bf16[1040,128]{1,0:T(8,128)(2,1)S(1)}, u32[]{:S(2)}, u32[]{:S(2)}) %collective-permute-start.1) | collective-permute-done | bytes 266272 | tf_op jit(solution)/shard_map/ppermute | solution.py:36
  20.3 0.2 collective-permute-done.2.refs_6_
  20.5 0.0 copy-done.3
  20.5 1.2 %back.1 = (bf16[528,128]{1,0:T(8,128)(2,1)S(1)}, bf16[528,128]{1,0:T(8,128)(2,1)S(1)}, bf16[528,128]{1,0:T(8,128)(2,1)S(1)}, bf16[528,128]{1,0:T(8,128)(2,1)S(1)...) custom-call(s32[32]{0:T(128)S(1)} %get-tuple-element.32.tab, ...), custom_call_target="tpu_custom_call" | custom-call | tf_op jit(solution)/shard_map/back/pallas_call | solution.py:313
  21.7 0.1 collective-permute-start.3
  21.8 1.8 %collective-permute-start.4 = (bf16[528,128]{1,0:T(8,128)(2,1)S(1)}, bf16[528,128]{1,0:T(8,128)(2,1)S(1)}, u32[]{:S(2)}, u32[]{:S(2)}) collective-permute-start(bf16[528,128]{1,0:T(8,128)(2,1)S(1)} %get-tuple-element.47), channel_id=1, source_target_pairs={{0,2},{1,3},{2,0},{3,1},{4,6},{5,7},{6,4},{7,5},{8,10},{9,11},{10,... | collective-permute-start | bytes 405512 | tf_op jit(solution)/shard_map/ppermute | solution.py:36
  23.6 0.1 collective-permute-start.5
  23.7 2.8 %collective-permute-start.7 = (bf16[512,128]{1,0:T(8,128)(2,1)S(1)}, bf16[512,128]{1,0:T(8,128)(2,1)S(1)}, u32[]{:S(2)}, u32[]{:S(2)}) collective-permute-start(bf16[512,128]{1,0:T(8,128)(2,1)S(1)} %get-tuple-element.54), channel_id=1, source_target_pairs={{0,16},{8,24},{16,0},{24,8},{1,17},{9,25},{17,1},{25,9},{2,18},{10... | collective-permute-start | bytes 393224 | tf_op jit(solution)/shard_map/ppermute | solution.py:36
  26.5 1.6 %collective-permute-start.6 = (bf16[256,128]{1,0:T(8,128)(2,1)S(1)}, bf16[256,128]{1,0:T(8,128)(2,1)S(1)}, u32[]{:S(2)}, u32[]{:S(2)}) collective-permute-start(bf16[256,128]{1,0:T(8,128)(2,1)S(1)} %get-tuple-element.53), channel_id=1, source_target_pairs={{0,8},{8,0},{16,24},{24,16},{1,9},{9,1},{17,25},{25,17},{2,10},{10... | collective-permute-start | bytes 196616 | tf_op jit(solution)/shard_map/ppermute | solution.py:36
  28.1 0.0 collective-permute-done.3.refs_1_
  28.1 0.0 collective-permute-start.8
  28.1 0.2 collective-permute-done.4.refs_2_
  28.2 2.0 %collective-permute-done.5.refs_3_ = bf16[528,128]{1,0:T(8,128)(2,1)S(1)} collective-permute-done((bf16[528,128]{1,0:T(8,128)(2,1)S(1)}, bf16[528,128]{1,0:T(8,128)(2,1)S(1)}, u32[]{:S(2)}, u32[]{:S(2)}) %collective-permute-start.5) | collective-permute-done | bytes 135200 | tf_op jit(solution)/shard_map/ppermute | solution.py:36
  30.2 1.9 %add_outputs.1 = (bf16[32,4096]{1,0:T(8,128)(2,1)}, bf16[32,4096]{1,0:T(8,128)(2,1)}, s32[32,128]{1,0:T(8,128)S(1)}) custom-call(bf16[528,128]{1,0:T(8,128)(2,1)S(1)} %get-tuple-element.45.refs_0_, bf16[528,128]{1,0:T(8,128)(2,1)S(1)} %collective-permute-done.3.refs_1_, bf16[528,128]{1,0:T(8,128)(2,1)S(1)} %collective-permute-done.4.refs_2_, ...), custom_call_target="tpu_custom_call" | custom-call | tf_op jit(solution)/shard_map/add_outputs/pallas_call | solution.py:330
  32.1 0.0 collective-permute-done.6.refs_1_
  32.1 2.3 %collective-permute-done.8.refs_3_ = bf16[256,128]{1,0:T(8,128)(2,1)S(1)} collective-permute-done((bf16[256,128]{1,0:T(8,128)(2,1)S(1)}, bf16[256,128]{1,0:T(8,128)(2,1)S(1)}, u32[]{:S(2)}, u32[]{:S(2)}) %collective-permute-start.8) | collective-permute-done | bytes 65568 | tf_op jit(solution)/shard_map/ppermute | solution.py:36
  34.4 0.7 %collective-permute-done.7.refs_2_ = bf16[512,128]{1,0:T(8,128)(2,1)S(1)} collective-permute-done((bf16[512,128]{1,0:T(8,128)(2,1)S(1)}, bf16[512,128]{1,0:T(8,128)(2,1)S(1)}, u32[]{:S(2)}, u32[]{:S(2)}) %collective-permute-start.7) | collective-permute-done | bytes 131104 | tf_op jit(solution)/shard_map/ppermute | solution.py:36
  35.1 0.7 %add_grads.1 = (f32[8,32,128]{2,1,0:T(8,128)}, f32[8,32,128]{2,1,0:T(8,128)}) custom-call(s32[32,128]{1,0:T(8,128)S(1)} %get-tuple-element.51.after, bf16[512,128]{1,0:T(8,128)(2,1)S(1)} %get-tuple-element.52.refs_0_, bf16[256,128]{1,0:T(8,128)(2,1)S(1)} %collective-permute-done.6.refs_1_, bf16[512,128]{1,0:T(8,128)(2,1)S(1)} %collective-permute-done.7.refs_2_, ...), custom_call_target="tpu_custom_call" | custom-call | tf_op jit(solution)/shard_map/add_grads/pallas_call | solution.py:345
Async XLA Ops:
  0.6 6.6 %copy-start.1 = (bf16[128,4096]{1,0:T(8,128)(2,1)S(1)}, bf16[128,4096]{1,0:T(8,128)(2,1)}, u32[]{:S(2)}) copy-start(bf16[128,4096]{1,0:T(8,128)(2,1)} %grad_out.1) | copy-start | bytes 3145732
  0.6 6.6 %copy-start = (bf16[1,1,8,128,128]{4,3,2,1,0:T(8,128)(2,1)S(1)}, bf16[1,1,8,128,128]{4,3,2,1,0:T(8,128)(2,1)}, u32[]{:S(2)}) copy-start(bf16[1,1,8,128,128]{4,3,2,1,0:T(8,128)(2,1)} %param.9) | copy-start | bytes 786436
  0.7 6.6 %copy-start.9 = (s32[1,1,8]{2,1,0:T(1,128)S(1)}, s32[1,1,8]{2,1,0:T(1,128)}, u32[]{:S(2)}) copy-start(s32[1,1,8]{2,1,0:T(1,128)} %param.14) | copy-start | bytes 100
  4.2 9.6 %collective-permute-start = (bf16[1040,128]{1,0:T(8,128)(2,1)}, bf16[1040,128]{1,0:T(8,128)(2,1)S(1)}, u32[]{:S(2)}, u32[]{:S(2)}) collective-permute-start(bf16[1040,128]{1,0:T(8,128)(2,1)} %get-tuple-element.34), channel_id=1, source_target_pairs={{0,4},{4,0},{1,5},{5,1},{2,6},{6,2},{3,7},{7,3},{8,12},{12,8},{9,1... | collective-permute-start | bytes 798728 | tf_op jit(solution)/shard_map/ppermute | solution.py:36
  7.2 0.7 %copy-start.6 = (s32[1,1,8]{2,1,0:T(1,128)S(1)}, s32[1,1,8]{2,1,0:T(1,128)}, u32[]{:S(2)}) copy-start(s32[1,1,8]{2,1,0:T(1,128)} %param.10) | copy-start | bytes 100
  7.2 0.7 %copy-start.7 = (s32[1,1,8]{2,1,0:T(1,128)S(1)}, s32[1,1,8]{2,1,0:T(1,128)}, u32[]{:S(2)}) copy-start(s32[1,1,8]{2,1,0:T(1,128)} %param.11) | copy-start | bytes 100
  7.3 0.7 %copy-start.8 = (s32[1,1,8]{2,1,0:T(1,128)S(1)}, s32[1,1,8]{2,1,0:T(1,128)}, u32[]{:S(2)}) copy-start(s32[1,1,8]{2,1,0:T(1,128)} %param.13) | copy-start | bytes 100
  7.9 0.9 %copy-start.2 = (bf16[8,128,128]{2,1,0:T(8,128)(2,1)S(1)}, bf16[8,128,128]{2,1,0:T(8,128)(2,1)}, u32[]{:S(2)}) copy-start(bf16[8,128,128]{2,1,0:T(8,128)(2,1)} %get-tuple-element.31.taken.refs_4_) | copy-start | bytes 786436
  8.9 0.9 %copy-start.4 = (bf16[1,1,8,128,128]{4,3,2,1,0:T(8,128)(2,1)S(1)}, bf16[1,1,8,128,128]{4,3,2,1,0:T(8,128)(2,1)}, u32[]{:S(2)}) copy-start(bf16[1,1,8,128,128]{4,3,2,1,0:T(8,128)(2,1)} %param.12) | copy-start | bytes 786436
  12.4 7.9 %collective-permute-start.1 = (bf16[1040,128]{1,0:T(8,128)(2,1)S(1)}, bf16[1040,128]{1,0:T(8,128)(2,1)S(1)}, u32[]{:S(2)}, u32[]{:S(2)}) collective-permute-start(bf16[1040,128]{1,0:T(8,128)(2,1)S(1)} %get-tuple-element.38), channel_id=1, source_target_pairs={{0,4},{4,0},{1,5},{5,1},{2,6},{6,2},{3,7},{7,3},{8,12},{12,8},{9,1... | collective-permute-start | bytes 798728 | tf_op jit(solution)/shard_map/ppermute | solution.py:36
  13.9 3.5 %copy-start.5 = (bf16[1,1,8,128,128]{4,3,2,1,0:T(8,128)(2,1)S(1)}, bf16[1,1,8,128,128]{4,3,2,1,0:T(8,128)(2,1)}, u32[]{:S(2)}) copy-start(bf16[1,1,8,128,128]{4,3,2,1,0:T(8,128)(2,1)} %param.12) | copy-start | bytes 786436
  15.5 5.0 %collective-permute-start.2 = (bf16[512,128]{1,0:T(8,128)(2,1)S(1)}, bf16[512,128]{1,0:T(8,128)(2,1)S(1)}, u32[]{:S(2)}, u32[]{:S(2)}) collective-permute-start(bf16[512,128]{1,0:T(8,128)(2,1)S(1)} %get-tuple-element.44), channel_id=1, source_target_pairs={{0,8},{8,0},{16,24},{24,16},{1,9},{9,1},{17,25},{25,17},{2,10},{10... | collective-permute-start | bytes 393224 | tf_op jit(solution)/shard_map/ppermute | solution.py:303
  17.3 3.1 %copy-start.3 = (bf16[8,128,128]{2,1,0:T(8,128)(2,1)S(1)}, bf16[8,128,128]{2,1,0:T(8,128)(2,1)}, u32[]{:S(2)}) copy-start(bf16[8,128,128]{2,1,0:T(8,128)(2,1)} %get-tuple-element.31.taken.refs_4_) | copy-start | bytes 786436
  21.7 6.4 %collective-permute-start.3 = (bf16[528,128]{1,0:T(8,128)(2,1)S(1)}, bf16[528,128]{1,0:T(8,128)(2,1)S(1)}, u32[]{:S(2)}, u32[]{:S(2)}) collective-permute-start(bf16[528,128]{1,0:T(8,128)(2,1)S(1)} %get-tuple-element.46), channel_id=1, source_target_pairs={{0,1},{1,0},{2,3},{3,2},{4,5},{5,4},{6,7},{7,6},{8,9},{9,8},{10,11... | collective-permute-start | bytes 405512 | tf_op jit(solution)/shard_map/ppermute | solution.py:36
  21.8 6.5 %collective-permute-start.4 = (bf16[528,128]{1,0:T(8,128)(2,1)S(1)}, bf16[528,128]{1,0:T(8,128)(2,1)S(1)}, u32[]{:S(2)}, u32[]{:S(2)}) collective-permute-start(bf16[528,128]{1,0:T(8,128)(2,1)S(1)} %get-tuple-element.47), channel_id=1, source_target_pairs={{0,2},{1,3},{2,0},{3,1},{4,6},{5,7},{6,4},{7,5},{8,10},{9,11},{10,... | collective-permute-start | bytes 405512 | tf_op jit(solution)/shard_map/ppermute | solution.py:36
  23.6 6.6 %collective-permute-start.5 = (bf16[528,128]{1,0:T(8,128)(2,1)S(1)}, bf16[528,128]{1,0:T(8,128)(2,1)S(1)}, u32[]{:S(2)}, u32[]{:S(2)}) collective-permute-start(bf16[528,128]{1,0:T(8,128)(2,1)S(1)} %get-tuple-element.48), channel_id=1, source_target_pairs={{0,3},{1,2},{2,1},{3,0},{4,7},{5,6},{6,5},{7,4},{8,11},{9,10},{10,... | collective-permute-start | bytes 405512 | tf_op jit(solution)/shard_map/ppermute | solution.py:36
  23.7 11.4 %collective-permute-start.7 = (bf16[512,128]{1,0:T(8,128)(2,1)S(1)}, bf16[512,128]{1,0:T(8,128)(2,1)S(1)}, u32[]{:S(2)}, u32[]{:S(2)}) collective-permute-start(bf16[512,128]{1,0:T(8,128)(2,1)S(1)} %get-tuple-element.54), channel_id=1, source_target_pairs={{0,16},{8,24},{16,0},{24,8},{1,17},{9,25},{17,1},{25,9},{2,18},{10... | collective-permute-start | bytes 393224 | tf_op jit(solution)/shard_map/ppermute | solution.py:36
  26.5 5.7 %collective-permute-start.6 = (bf16[256,128]{1,0:T(8,128)(2,1)S(1)}, bf16[256,128]{1,0:T(8,128)(2,1)S(1)}, u32[]{:S(2)}, u32[]{:S(2)}) collective-permute-start(bf16[256,128]{1,0:T(8,128)(2,1)S(1)} %get-tuple-element.53), channel_id=1, source_target_pairs={{0,8},{8,0},{16,24},{24,16},{1,9},{9,1},{17,25},{25,17},{2,10},{10... | collective-permute-start | bytes 196616 | tf_op jit(solution)/shard_map/ppermute | solution.py:36
  28.1 6.3 %collective-permute-start.8 = (bf16[256,128]{1,0:T(8,128)(2,1)S(1)}, bf16[256,128]{1,0:T(8,128)(2,1)S(1)}, u32[]{:S(2)}, u32[]{:S(2)}) collective-permute-start(bf16[256,128]{1,0:T(8,128)(2,1)S(1)} %get-tuple-element.55), channel_id=1, source_target_pairs={{0,24},{8,16},{16,8},{24,0},{1,25},{9,17},{17,9},{25,1},{2,26},{10... | collective-permute-start | bytes 196616 | tf_op jit(solution)/shard_map/ppermute | solution.py:36

commit v7 on v6

--- a/solution.py
+++ b/solution.py
@@ -77,28 +77,40 @@
     return copies
 
 
-def token_kernel(t0, t1, t2, t3, tokens, w1, message, taken, w_v, c0, c1, c2, c3, sems):
-    slots, rows, blk = taken.shape
+def token_kernel(t0, t1, t2, t3, tokens, w1, message, tokens_v, w_v, sent, c0, c1, c2, c3, sems):
+    slots, blk, _ = w_v.shape
+    rows = tokens_v.shape[0]
     tables = (c0, c1, c2, c3)
-    loads = [pltpu.make_async_copy(t, c, sems.at[slots + 1 + i]) for i, (t, c) in enumerate(zip((t0, t1, t2, t3), tables))]
-    w_copy = pltpu.make_async_copy(w1, w_v, sems.at[slots])
+    loads = [pltpu.make_async_copy(t, c, sems.at[i]) for i, (t, c) in enumerate(zip((t0, t1, t2, t3), tables))]
+    loads.append(pltpu.make_async_copy(tokens, tokens_v, sems.at[4]))
+    loads.append(pltpu.make_async_copy(w1, w_v, sems.at[5]))
+    stores = []
+
+    def store(begin, size):
+        here = pl.ds(begin, size)
+        stores.append(pltpu.make_async_copy(sent.at[here], message.at[here], sems.at[6 + len(stores)]))
+        stores[-1].start()
+
     for c in loads:
         c.start()
-    w_copy.start()
-    loads[W1_ROW].wait()
-    copies = start_taking(tokens, c0, taken, sems)
-    for c in loads[1:]:
+    for c in loads[:4]:
         c.wait()
-    message[slots * rows :, :] = table_row(tables, slots)
-    w_copy.wait()
-    for k in range(slots):
-        copies[k].wait()
-        message[k * rows : (k + 1) * rows, :] = dot(taken[k], w_v[k], (1, 0)).astype(bf16)
-
-
-def cotangent_kernel(c0, c1, c2, c3, grad_out, w1, w2, taken, message, cot, p_own, b_own, tab, sems):
+    sent[slots * rows :, :] = table_row(tables, slots)
+    store(slots * rows, 16)
+    for c in loads[4:]:
+        c.wait()
+    for k in range(slots):
+        here = pl.ds(pl.multiple_of(c0[k] * blk, blk), blk)
+        sent[k * rows : (k + 1) * rows, :] = dot(tokens_v[:, here], w_v[k], (1, 0)).astype(bf16)
+        store(k * rows, rows)
+    for c in stores:
+        c.wait()
+
+
+def cotangent_kernel(c0, c1, c2, c3, tokens, grad_out, w1, w2, message, taken, cot, p_own, b_own, tab, sems):
     slots, rows, blk = cot.shape
-    copies = start_taking(grad_out, c3, cot, sems)
+    copies = start_taking(grad_out, c3, cot, sems.at[0])
+    copies_t = start_taking(tokens, c0, taken, sems.at[1])
     for which, table in enumerate((c0, c1, c2, c3)):
         for k in range(slots):
             tab[which * slots + k] = table[k]
@@ -109,6 +121,7 @@
         message[k * rows : (k + 1) * rows, :] = value.astype(bf16)
     message[slots * rows :, :] = jnp.zeros((16, blk), bf16)
     for k in range(slots):
+        copies_t[k].wait()
         p_own[k] = dot(taken[k], w1[k], (1, 0))
 
 
@@ -217,14 +230,15 @@
 
 def output_kernel(dims, *refs):
     slots, n_row, n_col, n_tok = dims
-    o_parts, refs = refs[:n_col], refs[n_col:]
-    output, grad_in, tabs, acc, ints, scalars, sem = refs
-    blk, share = acc.shape[-1], acc.shape[1]
-    copy = decode_tables(o_parts, 2 * slots * share, ints, scalars, sem)
+    first = min(2, n_col)
+    o_parts, refs = refs[:first] + refs[first + 1 : n_col + 1], refs[n_col + 1 :]
+    output, grad_in, tabs, acc_out, acc_in, scalars, sem = refs
+    blk, share = acc_out.shape[-1], acc_out.shape[1]
+    copy = decode_tables(o_parts, 2 * slots * share, tabs, scalars, sem)
+    acc_out[...] = jnp.zeros(acc_out.shape, f32)
+    acc_in[...] = jnp.zeros(acc_in.shape, f32)
     copy.wait()
-    tabs[...] = ints[...]
-    for first, which, result in ((0, W2_OUT, output), (slots, W1_ROW, grad_in)):
-        acc[...] = jnp.zeros(acc.shape, f32)
+    for first, which, acc, result in ((0, W2_OUT, acc_out, output), (slots, W1_ROW, acc_in, grad_in)):
         for c, ref in enumerate(o_parts):
             for k in range(slots):
                 at = scalars[c * 8, which * slots + k]
@@ -257,27 +271,31 @@
     S = jax.ShapeDtypeStruct
     message = S((slots * rows + 16, blk), bf16)
     wide, narrow = S((slots, rows, blk), f32), S((slots, rows, blk), bf16)
-    p_send, taken = pl.pallas_call(
+    p_send = pl.pallas_call(
         token_kernel,
-        out_shape=(message, narrow),
+        out_shape=message,
         in_specs=[HBM] * 6,
-        out_specs=(VMEM,) * 2,
-        scratch_shapes=[pltpu.VMEM((slots, blk, blk), bf16)]
+        out_specs=HBM,
+        scratch_shapes=[
+            pltpu.VMEM(tokens.shape, bf16),
+            pltpu.VMEM((slots, blk, blk), bf16),
+            pltpu.VMEM((slots * rows + 16, blk), bf16),
+        ]
         + [pltpu.SMEM((slots,), jnp.int32)] * 4
-        + [pltpu.SemaphoreType.DMA((slots + 5,))],
+        + [pltpu.SemaphoreType.DMA((7 + slots,))],
         compiler_params=pltpu.CompilerParams(vmem_limit_bytes=TAKE_LIMIT),
         name="take_tokens",
     )(*tables, tokens, w1)
     p_peers = [send(p_send, "row", d) for d in range(1, n_row)]
-    b_send, cot, p_own, b_own, tab = pl.pallas_call(
+    b_send, taken, cot, p_own, b_own, tab = pl.pallas_call(
         cotangent_kernel,
-        out_shape=(message, narrow, wide, wide, S((4 * slots,), jnp.int32)),
-        in_specs=[SMEM] * 4 + [HBM] + [VMEM] * 3,
-        out_specs=(VMEM,) * 4 + (SMEM,),
-        scratch_shapes=[pltpu.SemaphoreType.DMA((slots,))],
+        out_shape=(message, narrow, narrow, wide, wide, S((4 * slots,), jnp.int32)),
+        in_specs=[SMEM] * 4 + [HBM, HBM] + [VMEM] * 2,
+        out_specs=(VMEM,) * 5 + (SMEM,),
+        scratch_shapes=[pltpu.SemaphoreType.DMA((2, slots))],
         compiler_params=PARAMS,
         name="take_cotangent",
-    )(*tables, grad_out, w1, w2, taken)
+    )(*tables, tokens, grad_out, w1, w2)
     b_peers = [send(b_send, "row", d) for d in range(1, n_row)]
 
     both = [n_tok % 2 == 1 or d % 2 == 0 for d in range(n_tok)]
@@ -326,21 +344,22 @@
     g_parts = exchange(sent[n_col:], "tok")
     o_parts = exchange(sent[:n_col], "col")
 
+    first = min(2, n_col)
     result = S((share, row_blocks * blk), bf16)
     output, grad_in, tabs = pl.pallas_call(
         functools.partial(output_kernel, dims),
         out_shape=(result, result, S((8 * n_col, LANES), jnp.int32)),
-        in_specs=[VMEM] * n_col,
+        in_specs=[VMEM] * first + [ANY] + [VMEM] * (n_col - first),
         out_specs=(VMEM,) * 3,
         scratch_shapes=[
             pltpu.VMEM((row_blocks, share, blk), f32),
-            pltpu.VMEM((8 * n_col, LANES), jnp.int32),
+            pltpu.VMEM((row_blocks, share, blk), f32),
             pltpu.SMEM((8 * n_col, LANES), jnp.int32),
             pltpu.SemaphoreType.DMA,
         ],
         compiler_params=PARAMS,
         name="add_outputs",
-    )(*o_parts)
+    )(*o_parts[:first], g_parts[n_tok // 2], *o_parts[first:])
     summed = S((slots, part, blk), f32)
     gw1, gw2 = pl.pallas_call(
         grad_kernel,
@@ -349,7 +368,7 @@
         out_specs=(VMEM,) * 2,
         compiler_params=PARAMS,
         name="add_grads",
-    )(tabs, *g_parts)
+    )(tabs, *g_parts[::-1])
     return (output, grad_in, gw1.reshape(1, 1, slots, part, blk), gw2.reshape(1, 1, slots, part, blk))
 
 

time: 36.3 us -> 34.8 us (0.959)
  waiting for transfers between devices: 9.32 us -> 6.1 us
  starting transfers between devices: 11.3 us -> 14.4 us
  local copies, waits for them, and re-layouts: 2.58 us -> 1.26 us
    ppermute x8, waiting for transfers between devices: 9.11 us -> 5.96 us  [send(): lax.ppermute(x, axis, [(i, partner(i, d, n)) for i in range(n)])]
    ppermute x8, starting transfers between devices: 9.44 us -> 12.5 us  [send(): lax.ppermute(x, axis, [(i, partner(i, d, n)) for i in range(n)])]
    unnamed x20 -> x16, local copies, waits for them, and re-layouts: 2.58 us -> 1.26 us
  transfers between devices with their start and end apart: 9 -> 9, of which waited for: 7 -> 5; matrix products, arithmetic and copies ran while one was open for 0% -> 0% of each run, Pallas kernels for 18% -> 22%
where the time goes in v7:
time: 34.8 us; the launch traced here: 34.6 us
  starting transfers between devices  14.4 us (41%)
  Pallas kernels  12 us (34%)
  waiting for transfers between devices  6.1 us (18%)
  local copies, waits for them, and re-layouts  1.26 us (4%)
  between operations  0.79 us (2%)
    ppermute x8, starting transfers between devices, send(): lax.ppermute(x, axis, [(i, partner(i, d, n)) for i in range(n)])  12.5 us
    ppermute x8, waiting for transfers between devices, send(): lax.ppermute(x, axis, [(i, partner(i, d, n)) for i in range(n)])  5.96 us
    pallas_call x1, Pallas kernels, shards(): pl.pallas_call(cotangent_kernel, out_shape=(message, narrow, narrow, wide...  3.89 us
    pallas_call x1, Pallas kernels, shards(): pl.pallas_call(token_kernel, out_shape=message, in_specs=[HBM] * 6, out_s...  2.37 us
    ppermute x1, starting transfers between devices, shards(): half = lax.ppermute(half, 'tok', [(i, i ^ 1) for i in range(n_tok)])  1.9 us
    pallas_call x1, Pallas kernels, shards(): pl.pallas_call(functools.partial(output_kernel, dims), out_shape=(result,...  1.89 us
    pallas_call x1, Pallas kernels, shards(): pl.pallas_call(functools.partial(hidden_kernel, dims), out_shape=(narrow,...  1.59 us
    unnamed x16, local copies, waits for them, and re-layouts  1.26 us
  transfers between devices with their start and end apart: 9, of which 5 were waited for; matrix products, arithmetic and copies ran while one was open for 0% of the time, Pallas kernels for 22%

profile of v7, /device:TPU:0, one launch (start us, length us, event | category | flops | bytes accessed | tf_op | source)
XLA Modules:
  0.0 34.6 jit_solution(5231162843870633114)
XLA Ops:
  0.6 0.0 copy-start
  0.6 0.0 copy-start.1
  0.7 0.0 copy-start.3
  0.7 0.0 copy-start.7
  0.7 2.4 %take_tokens.1 = bf16[1040,128]{1,0:T(8,128)(2,1)} custom-call(s32[8]{0:T(128)} %bitcast.13, s32[8]{0:T(128)} %bitcast.15, s32[8]{0:T(128)} %bitcast.17, s32[8]{0:T(128)} %bitcast.19, bf16[128,4096]{1,0:T(8,128)(2,1)} %tokens.3, bf16[8,128,128]{2,1,0:T(8,128)(2,1)} %bitcast.8), custom_call_target="tpu_custom_call" | custom-call | tf_op jit(solution)/shard_map/take_tokens/pallas_call | solution.py:274
  3.1 0.0 copy-start.4
  3.1 0.0 copy-start.5
  3.1 0.0 copy-start.6
  3.1 3.0 %collective-permute-start = (bf16[1040,128]{1,0:T(8,128)(2,1)}, bf16[1040,128]{1,0:T(8,128)(2,1)S(1)}, u32[]{:S(2)}, u32[]{:S(2)}) collective-permute-start(bf16[1040,128]{1,0:T(8,128)(2,1)} %take_tokens.1), channel_id=1, source_target_pairs={{0,4},{4,0},{1,5},{5,1},{2,6},{6,2},{3,7},{7,3},{8,12},{12,8},{9,1... | collective-permute-start | bytes 798728 | tf_op jit(solution)/shard_map/ppermute | solution.py:36
  6.1 0.0 copy-done
  6.1 0.0 copy-done.1
  6.1 0.0 copy-done.3
  6.1 0.0 copy-done.7
  6.1 0.0 copy-done.4
  6.1 0.0 copy-done.5
  6.1 0.0 copy-done.6
  6.1 0.0 copy-start.2
  6.1 1.2 %copy-done.2 = bf16[128,4096]{1,0:T(8,128)(2,1)S(1)} copy-done((bf16[128,4096]{1,0:T(8,128)(2,1)S(1)}, bf16[128,4096]{1,0:T(8,128)(2,1)}, u32[]{:S(2)}) %copy-start.2) | copy-done | bytes 1048600
  7.4 3.9 %take_cotangent.1 = (bf16[1040,128]{1,0:T(8,128)(2,1)S(1)}, bf16[8,128,128]{2,1,0:T(8,128)(2,1)S(1)}, bf16[8,128,128]{2,1,0:T(8,128)(2,1)S(1)}, f32[8,128,128]{2...) custom-call(s32[8]{0:T(128)S(1)} %bitcast.14, s32[8]{0:T(128)S(1)} %bitcast.16, s32[8]{0:T(128)S(1)} %bitcast.18, ...), custom_call_target="tpu_custom_call" | custom-call | tf_op jit(solution)/shard_map/take_cotangent/pallas_call | solution.py:290
  11.3 0.6 %collective-permute-start.1 = (bf16[1040,128]{1,0:T(8,128)(2,1)S(1)}, bf16[1040,128]{1,0:T(8,128)(2,1)S(1)}, u32[]{:S(2)}, u32[]{:S(2)}) collective-permute-start(bf16[1040,128]{1,0:T(8,128)(2,1)S(1)} %get-tuple-element.35), channel_id=1, source_target_pairs={{0,4},{4,0},{1,5},{5,1},{2,6},{6,2},{3,7},{7,3},{8,12},{12,8},{9,1... | collective-permute-start | bytes 798728 | tf_op jit(solution)/shard_map/ppermute | solution.py:36
  11.9 0.8 %collective-permute-done.refs_0_ = bf16[1040,128]{1,0:T(8,128)(2,1)S(1)} collective-permute-done((bf16[1040,128]{1,0:T(8,128)(2,1)}, bf16[1040,128]{1,0:T(8,128)(2,1)S(1)}, u32[]{:S(2)}, u32[]{:S(2)}) %collective-permute-start) | collective-permute-done | bytes 266272 | tf_op jit(solution)/shard_map/ppermute | solution.py:36
  12.7 1.6 %hidden.1 = (bf16[8,128,128]{2,1,0:T(8,128)(2,1)S(1)}, f32[8,128,128]{2,1,0:T(8,128)S(1)}, s32[8,128]{1,0:T(8,128)S(1)}, f32[8,128,128]{2,1,0:T(8,128)S(1)}, bf16[512,128]{1,0:T(8,128)(2,1)S(1)}) custom-call(s32[32]{0:T(128)S(1)} %get-tuple-element.30.tab, f32[8,128,128]{2,1,0:T(8,128)S(1)} %get-tuple-element.31.p_own, ...), custom_call_target="tpu_custom_call" | custom-call | tf_op jit(solution)/shard_map/hidden/pallas_call | solution.py:306
  14.3 1.9 %collective-permute-start.2 = (bf16[512,128]{1,0:T(8,128)(2,1)S(1)}, bf16[512,128]{1,0:T(8,128)(2,1)S(1)}, u32[]{:S(2)}, u32[]{:S(2)}) collective-permute-start(bf16[512,128]{1,0:T(8,128)(2,1)S(1)} %get-tuple-element.42), channel_id=1, source_target_pairs={{0,8},{8,0},{16,24},{24,16},{1,9},{9,1},{17,25},{25,17},{2,10},{10... | collective-permute-start | bytes 393224 | tf_op jit(solution)/shard_map/ppermute | solution.py:321
  16.2 0.3 slope.1
  16.5 2.6 %collective-permute-done.1.refs_0_ = bf16[1040,128]{1,0:T(8,128)(2,1)S(1)} collective-permute-done((bf16[1040,128]{1,0:T(8,128)(2,1)S(1)}, bf16[1040,128]{1,0:T(8,128)(2,1)S(1)}, u32[]{:S(2)}, u32[]{:S(2)}) %collective-permute-start.1) | collective-permute-done | bytes 266272 | tf_op jit(solution)/shard_map/ppermute | solution.py:36
  19.2 0.1 collective-permute-done.2.refs_6_
  19.3 1.2 %back.1 = (bf16[528,128]{1,0:T(8,128)(2,1)S(1)}, bf16[528,128]{1,0:T(8,128)(2,1)S(1)}, bf16[528,128]{1,0:T(8,128)(2,1)S(1)}, bf16[528,128]{1,0:T(8,128)(2,1)S(1)...) custom-call(s32[32]{0:T(128)S(1)} %get-tuple-element.30.tab, ...), custom_call_target="tpu_custom_call" | custom-call | tf_op jit(solution)/shard_map/back/pallas_call | solution.py:331
  20.5 2.9 %collective-permute-start.4 = (bf16[512,128]{1,0:T(8,128)(2,1)S(1)}, bf16[512,128]{1,0:T(8,128)(2,1)S(1)}, u32[]{:S(2)}, u32[]{:S(2)}) collective-permute-start(bf16[512,128]{1,0:T(8,128)(2,1)S(1)} %get-tuple-element.45), channel_id=1, source_target_pairs={{0,16},{8,24},{16,0},{24,8},{1,17},{9,25},{17,1},{25,9},{2,18},{10... | collective-permute-start | bytes 393224 | tf_op jit(solution)/shard_map/ppermute | solution.py:36
  23.4 0.0 collective-permute-start.3
  23.4 1.5 %collective-permute-start.5 = (bf16[528,128]{1,0:T(8,128)(2,1)S(1)}, bf16[528,128]{1,0:T(8,128)(2,1)S(1)}, u32[]{:S(2)}, u32[]{:S(2)}) collective-permute-start(bf16[528,128]{1,0:T(8,128)(2,1)S(1)} %get-tuple-element.46), channel_id=1, source_target_pairs={{0,2},{1,3},{2,0},{3,1},{4,6},{5,7},{6,4},{7,5},{8,10},{9,11},{10,... | collective-permute-start | bytes 405512 | tf_op jit(solution)/shard_map/ppermute | solution.py:36
  25.0 0.3 collective-permute-start.6
  25.3 1.4 %collective-permute-start.7 = (bf16[256,128]{1,0:T(8,128)(2,1)S(1)}, bf16[256,128]{1,0:T(8,128)(2,1)S(1)}, u32[]{:S(2)}, u32[]{:S(2)}) collective-permute-start(bf16[256,128]{1,0:T(8,128)(2,1)S(1)} %get-tuple-element.51), channel_id=1, source_target_pairs={{0,24},{8,16},{16,8},{24,0},{1,25},{9,17},{17,9},{25,1},{2,26},{10... | collective-permute-start | bytes 196616 | tf_op jit(solution)/shard_map/ppermute | solution.py:36
  26.6 1.6 %collective-permute-done.4.refs_2_.refs_1_ = bf16[512,128]{1,0:T(8,128)(2,1)S(1)} collective-permute-done((bf16[512,128]{1,0:T(8,128)(2,1)S(1)}, bf16[512,128]{1,0:T(8,128)(2,1)S(1)}, u32[]{:S(2)}, u32[]{:S(2)}) %collective-permute-start.4) | collective-permute-done | bytes 131104 | tf_op jit(solution)/shard_map/ppermute | solution.py:36
  28.2 2.8 %collective-permute-start.8 = (bf16[256,128]{1,0:T(8,128)(2,1)S(1)}, bf16[256,128]{1,0:T(8,128)(2,1)S(1)}, u32[]{:S(2)}, u32[]{:S(2)}) collective-permute-start(bf16[256,128]{1,0:T(8,128)(2,1)S(1)} %get-tuple-element.52), channel_id=1, source_target_pairs={{0,8},{8,0},{16,24},{24,16},{1,9},{9,1},{17,25},{25,17},{2,10},{10... | collective-permute-start | bytes 196616 | tf_op jit(solution)/shard_map/ppermute | solution.py:36
  31.0 0.0 collective-permute-done.3.refs_1_
  31.0 0.0 collective-permute-done.5.refs_3_
  31.0 0.9 %collective-permute-done.6.refs_4_ = bf16[528,128]{1,0:T(8,128)(2,1)S(1)} collective-permute-done((bf16[528,128]{1,0:T(8,128)(2,1)S(1)}, bf16[528,128]{1,0:T(8,128)(2,1)S(1)}, u32[]{:S(2)}, u32[]{:S(2)}) %collective-permute-start.6) | collective-permute-done | bytes 135200 | tf_op jit(solution)/shard_map/ppermute | solution.py:36
  31.9 1.9 %add_outputs.1 = (bf16[32,4096]{1,0:T(8,128)(2,1)}, bf16[32,4096]{1,0:T(8,128)(2,1)}, s32[32,128]{1,0:T(8,128)S(1)}) custom-call(bf16[528,128]{1,0:T(8,128)(2,1)S(1)} %get-tuple-element.43.refs_0_, bf16[528,128]{1,0:T(8,128)(2,1)S(1)} %collective-permute-done.3.refs_1_, bf16[512,128]{1,0:T(8,128)(2,1)S(1)} %collective-permute-done.4.refs_2_.refs_1_, ...), custom_call_target="tpu_custom_call" | custom-call | tf_op jit(solution)/shard_map/add_outputs/pallas_call | solution.py:349
  33.8 0.0 collective-permute-done.7.refs_0_
  33.9 0.0 collective-permute-done.8.refs_2_
  33.9 0.7 %add_grads.1 = (f32[8,32,128]{2,1,0:T(8,128)}, f32[8,32,128]{2,1,0:T(8,128)}) custom-call(s32[32,128]{1,0:T(8,128)S(1)} %get-tuple-element.50.after, bf16[256,128]{1,0:T(8,128)(2,1)S(1)} %collective-permute-done.7.refs_0_, bf16[512,128]{1,0:T(8,128)(2,1)S(1)} %collective-permute-done.4.refs_2_.refs_1_, bf16[256,128]{1,0:T(8,128)(2,1)S(1)} %collective-permute-done.8.refs_2_, ...), custom_call_target="tpu_custom_call" | custom-call | tf_op jit(solution)/shard_map/add_grads/pallas_call | solution.py:364
Async XLA Ops:
  0.6 5.5 %copy-start = (bf16[128,4096]{1,0:T(8,128)(2,1)S(1)}, bf16[128,4096]{1,0:T(8,128)(2,1)}, u32[]{:S(2)}) copy-start(bf16[128,4096]{1,0:T(8,128)(2,1)} %tokens.3) | copy-start | bytes 3145732
  0.6 5.5 %copy-start.1 = (bf16[1,1,8,128,128]{4,3,2,1,0:T(8,128)(2,1)S(1)}, bf16[1,1,8,128,128]{4,3,2,1,0:T(8,128)(2,1)}, u32[]{:S(2)}) copy-start(bf16[1,1,8,128,128]{4,3,2,1,0:T(8,128)(2,1)} %param.9) | copy-start | bytes 786436
  0.7 5.4 %copy-start.3 = (bf16[1,1,8,128,128]{4,3,2,1,0:T(8,128)(2,1)S(1)}, bf16[1,1,8,128,128]{4,3,2,1,0:T(8,128)(2,1)}, u32[]{:S(2)}) copy-start(bf16[1,1,8,128,128]{4,3,2,1,0:T(8,128)(2,1)} %param.12) | copy-start | bytes 786436
  0.7 5.4 %copy-start.7 = (s32[1,1,8]{2,1,0:T(1,128)S(1)}, s32[1,1,8]{2,1,0:T(1,128)}, u32[]{:S(2)}) copy-start(s32[1,1,8]{2,1,0:T(1,128)} %param.14) | copy-start | bytes 100
  3.1 3.1 %copy-start.4 = (s32[1,1,8]{2,1,0:T(1,128)S(1)}, s32[1,1,8]{2,1,0:T(1,128)}, u32[]{:S(2)}) copy-start(s32[1,1,8]{2,1,0:T(1,128)} %param.10) | copy-start | bytes 100
  3.1 3.1 %copy-start.5 = (s32[1,1,8]{2,1,0:T(1,128)S(1)}, s32[1,1,8]{2,1,0:T(1,128)}, u32[]{:S(2)}) copy-start(s32[1,1,8]{2,1,0:T(1,128)} %param.11) | copy-start | bytes 100
  3.1 3.0 %copy-start.6 = (s32[1,1,8]{2,1,0:T(1,128)S(1)}, s32[1,1,8]{2,1,0:T(1,128)}, u32[]{:S(2)}) copy-start(s32[1,1,8]{2,1,0:T(1,128)} %param.13) | copy-start | bytes 100
  3.1 9.6 %collective-permute-start = (bf16[1040,128]{1,0:T(8,128)(2,1)}, bf16[1040,128]{1,0:T(8,128)(2,1)S(1)}, u32[]{:S(2)}, u32[]{:S(2)}) collective-permute-start(bf16[1040,128]{1,0:T(8,128)(2,1)} %take_tokens.1), channel_id=1, source_target_pairs={{0,4},{4,0},{1,5},{5,1},{2,6},{6,2},{3,7},{7,3},{8,12},{12,8},{9,1... | collective-permute-start | bytes 798728 | tf_op jit(solution)/shard_map/ppermute | solution.py:36
  6.1 1.2 %copy-start.2 = (bf16[128,4096]{1,0:T(8,128)(2,1)S(1)}, bf16[128,4096]{1,0:T(8,128)(2,1)}, u32[]{:S(2)}) copy-start(bf16[128,4096]{1,0:T(8,128)(2,1)} %grad_out.1) | copy-start | bytes 3145732
  11.3 7.9 %collective-permute-start.1 = (bf16[1040,128]{1,0:T(8,128)(2,1)S(1)}, bf16[1040,128]{1,0:T(8,128)(2,1)S(1)}, u32[]{:S(2)}, u32[]{:S(2)}) collective-permute-start(bf16[1040,128]{1,0:T(8,128)(2,1)S(1)} %get-tuple-element.35), channel_id=1, source_target_pairs={{0,4},{4,0},{1,5},{5,1},{2,6},{6,2},{3,7},{7,3},{8,12},{12,8},{9,1... | collective-permute-start | bytes 798728 | tf_op jit(solution)/shard_map/ppermute | solution.py:36
  14.3 5.0 %collective-permute-start.2 = (bf16[512,128]{1,0:T(8,128)(2,1)S(1)}, bf16[512,128]{1,0:T(8,128)(2,1)S(1)}, u32[]{:S(2)}, u32[]{:S(2)}) collective-permute-start(bf16[512,128]{1,0:T(8,128)(2,1)S(1)} %get-tuple-element.42), channel_id=1, source_target_pairs={{0,8},{8,0},{16,24},{24,16},{1,9},{9,1},{17,25},{25,17},{2,10},{10... | collective-permute-start | bytes 393224 | tf_op jit(solution)/shard_map/ppermute | solution.py:321
  20.5 7.7 %collective-permute-start.4 = (bf16[512,128]{1,0:T(8,128)(2,1)S(1)}, bf16[512,128]{1,0:T(8,128)(2,1)S(1)}, u32[]{:S(2)}, u32[]{:S(2)}) collective-permute-start(bf16[512,128]{1,0:T(8,128)(2,1)S(1)} %get-tuple-element.45), channel_id=1, source_target_pairs={{0,16},{8,24},{16,0},{24,8},{1,17},{9,25},{17,1},{25,9},{2,18},{10... | collective-permute-start | bytes 393224 | tf_op jit(solution)/shard_map/ppermute | solution.py:36
  23.4 7.6 %collective-permute-start.3 = (bf16[528,128]{1,0:T(8,128)(2,1)S(1)}, bf16[528,128]{1,0:T(8,128)(2,1)S(1)}, u32[]{:S(2)}, u32[]{:S(2)}) collective-permute-start(bf16[528,128]{1,0:T(8,128)(2,1)S(1)} %get-tuple-element.44), channel_id=1, source_target_pairs={{0,1},{1,0},{2,3},{3,2},{4,5},{5,4},{6,7},{7,6},{8,9},{9,8},{10,11... | collective-permute-start | bytes 405512 | tf_op jit(solution)/shard_map/ppermute | solution.py:36
  23.4 7.6 %collective-permute-start.5 = (bf16[528,128]{1,0:T(8,128)(2,1)S(1)}, bf16[528,128]{1,0:T(8,128)(2,1)S(1)}, u32[]{:S(2)}, u32[]{:S(2)}) collective-permute-start(bf16[528,128]{1,0:T(8,128)(2,1)S(1)} %get-tuple-element.46), channel_id=1, source_target_pairs={{0,2},{1,3},{2,0},{3,1},{4,6},{5,7},{6,4},{7,5},{8,10},{9,11},{10,... | collective-permute-start | bytes 405512 | tf_op jit(solution)/shard_map/ppermute | solution.py:36
  25.0 7.0 %collective-permute-start.6 = (bf16[528,128]{1,0:T(8,128)(2,1)S(1)}, bf16[528,128]{1,0:T(8,128)(2,1)S(1)}, u32[]{:S(2)}, u32[]{:S(2)}) collective-permute-start(bf16[528,128]{1,0:T(8,128)(2,1)S(1)} %get-tuple-element.47), channel_id=1, source_target_pairs={{0,3},{1,2},{2,1},{3,0},{4,7},{5,6},{6,5},{7,4},{8,11},{9,10},{10,... | collective-permute-start | bytes 405512 | tf_op jit(solution)/shard_map/ppermute | solution.py:36
  25.3 8.5 %collective-permute-start.7 = (bf16[256,128]{1,0:T(8,128)(2,1)S(1)}, bf16[256,128]{1,0:T(8,128)(2,1)S(1)}, u32[]{:S(2)}, u32[]{:S(2)}) collective-permute-start(bf16[256,128]{1,0:T(8,128)(2,1)S(1)} %get-tuple-element.51), channel_id=1, source_target_pairs={{0,24},{8,16},{16,8},{24,0},{1,25},{9,17},{17,9},{25,1},{2,26},{10... | collective-permute-start | bytes 196616 | tf_op jit(solution)/shard_map/ppermute | solution.py:36
  28.2 5.7 %collective-permute-start.8 = (bf16[256,128]{1,0:T(8,128)(2,1)S(1)}, bf16[256,128]{1,0:T(8,128)(2,1)S(1)}, u32[]{:S(2)}, u32[]{:S(2)}) collective-permute-start(bf16[256,128]{1,0:T(8,128)(2,1)S(1)} %get-tuple-element.52), channel_id=1, source_target_pairs={{0,8},{8,0},{16,24},{24,16},{1,9},{9,1},{17,25},{25,17},{2,10},{10... | collective-permute-start | bytes 196616 | tf_op jit(solution)/shard_map/ppermute | solution.py:36

commit v8 on v7

v8 whole, which is shorter than its diff:
```python
import functools
import math

import jax
import jax.numpy as jnp
from jax import lax
from jax.experimental import pallas as pl
from jax.experimental.pallas import tpu as pltpu
from jax.sharding import PartitionSpec as P

FF = 32768
LANES = 128
f32 = jnp.float32
bf16 = jnp.bfloat16
VMEM = pl.BlockSpec(memory_space=pltpu.VMEM)
SMEM = pl.BlockSpec(memory_space=pltpu.SMEM)
ANY = pl.BlockSpec(memory_space=pl.ANY)
HBM = pl.BlockSpec(memory_space=pltpu.HBM)
TAKE_LIMIT = 62 * 1024 * 1024
LIMIT = 32 * 1024 * 1024

W1_ROW, W1_COL, W2_HID, W2_OUT = range(4)


def call(kernel, name, limit=LIMIT, **kwargs):
    return pl.pallas_call(
        kernel,
        name=name,
        compiler_params=pltpu.CompilerParams(vmem_limit_bytes=limit),
        cost_estimate=pl.CostEstimate(flops=1 << 25, bytes_accessed=1 << 19, transcendentals=0),
        **kwargs,
    )


def dot(a, b, contract):
    return lax.dot_general(a, b, ((contract[:1], contract[1:]), ((), ())), preferred_element_type=f32)


def cdf(v):
    return 0.5 * (1.0 + lax.erf(v * math.sqrt(0.5)))


def partner(i, d, n):
    return i ^ d if n & (n - 1) == 0 else (i + d) % n


def target(axis, d):
    n = lax.axis_size(axis)
    me = lax.axis_index(axis)
    return jnp.bitwise_xor(me, d) if n & (n - 1) == 0 else lax.rem(me + d, n)


def send(x, axis, d):
    n = lax.axis_size(axis)
    return lax.ppermute(x, axis, [(i, partner(i, d, n)) for i in range(n)]) if d else x


def cut(value, refs, k, axis):
    share = value.shape[0] // len(refs)
    for d, ref in enumerate(refs):
        begin = pl.multiple_of(target(axis, d) * share, share)
        ref[k * share : (k + 1) * share, :] = value[pl.ds(begin, share), :].astype(ref.dtype)


def table_row(tables, slots):
    lane = lax.broadcasted_iota(jnp.int32, (16, LANES), 1)
    row = jnp.zeros((16, LANES), f32)
    for which, table in enumerate(tables):
        for k in range(slots):
            row = jnp.where(lane == which * slots + k, table[k].astype(f32), row)
    return row.astype(bf16)


def decode_tables(refs, rows, ints, scalars, sem):
    for i, ref in enumerate(refs):
        ints[i * 8 : i * 8 + 8] = ref[rows : rows + 16, :].astype(f32)[:8].astype(jnp.int32)
    copy = pltpu.make_async_copy(ints, scalars, sem)
    copy.start()
    return copy


def token_kernel(t0, t1, t2, t3, tokens, w1, message, tokens_v, w_v, sent, c0, c1, c2, c3, sems):
    slots, blk, _ = w_v.shape
    rows = tokens_v.shape[0]
    tables = (c0, c1, c2, c3)
    loads = [pltpu.make_async_copy(t, c, sems.at[i]) for i, (t, c) in enumerate(zip((t0, t1, t2, t3), tables))]
    loads.append(pltpu.make_async_copy(tokens, tokens_v, sems.at[4]))
    loads.append(pltpu.make_async_copy(w1, w_v, sems.at[5]))
    stores = []

    def store(begin, size):
        here = pl.ds(begin, size)
        stores.append(pltpu.make_async_copy(sent.at[here], message.at[here], sems.at[6 + len(stores)]))
        stores[-1].start()

    for c in loads:
        c.start()
    for c in loads[:4]:
        c.wait()
    sent[slots * rows :, :] = table_row(tables, slots)
    store(slots * rows, 16)
    for c in loads[4:]:
        c.wait()
    for k in range(slots):
        here = pl.ds(pl.multiple_of(c0[k] * blk, blk), blk)
        sent[k * rows : (k + 1) * rows, :] = dot(tokens_v[:, here], w_v[k], (1, 0)).astype(bf16)
        store(k * rows, rows)
    for c in stores:
        c.wait()


def first_place(tab, slots, k):
    return tab[4 * slots + k]


def place_of(tab, slots, block):
    return tab[6 * slots + block]


def start_taking(source, table, taken, sems):
    slots, _, blk = taken.shape
    copies = []
    for k in range(slots):
        begin = pl.multiple_of(table[k] * blk, blk)
        copies.append(pltpu.make_async_copy(source.at[:, pl.ds(begin, blk)], taken.at[k], sems.at[k]))
        copies[-1].start()
    return copies


def cotangent_kernel(c0, c1, c2, c3, tokens, grad_out, w1, w2, message, taken, cot, hid, back, tab, sems):
    slots, rows, blk = cot.shape
    copies = start_taking(grad_out, c3, cot, sems.at[0])
    copies_t = start_taking(tokens, c0, taken, sems.at[1])
    for which, table in enumerate((c0, c1, c2, c3)):
        for k in range(slots):
            tab[which * slots + k] = table[k]

    @pl.loop(0, tab.shape[0] - 6 * slots)
    def _(block):
        tab[6 * slots + block] = 2 * slots

    for j in range(2 * slots):
        block = c1[j] if j < slots else c2[j - slots]
        place = jnp.minimum(place_of(tab, slots, block), j)
        tab[6 * slots + block] = place
        tab[4 * slots + j] = place
    hid[...] = jnp.zeros(hid.shape, f32)
    back[...] = jnp.zeros(back.shape, f32)
    message[slots * rows :, :] = jnp.zeros((16, blk), bf16)
    for k in range(slots):
        copies[k].wait()
        value = dot(cot[k], w2[k], (1, 1))
        message[k * rows : (k + 1) * rows, :] = value.astype(bf16)
        at = jnp.minimum(place_of(tab, slots, c2[k]), slots)
        back[at] = back[at] + value
    for k in range(slots):
        copies_t[k].wait()
        at = place_of(tab, slots, c1[k])
        hid[at] = hid[at] + dot(taken[k], w1[k], (1, 0))


def add_peers(acc, own, tab, tables, which, peers, slots):
    places, rows, _ = acc.shape
    for j in range(places):
        acc[j] = own[j]
    for i, ref in enumerate(peers):
        for k in range(slots):
            at = place_of(tab, slots, tables[i * 8, which * slots + k])

            @pl.when(at < places)
            def _():
                acc[at] = acc[at] + ref[k * rows : (k + 1) * rows, :].astype(f32)


def hidden_kernel(dims, tab, own, *refs):
    slots, n_row, n_col, n_tok = dims
    peers, refs = refs[: n_row - 1], refs[n_row - 1 :]
    cot, active, hid, tabs, grad, half, scalars, sem = refs
    part = grad.shape[1] // n_tok
    other = 1 - lax.rem(lax.axis_index("tok"), 2)
    if peers:
        decode_tables(peers, slots * cot.shape[1], tabs, scalars, sem).wait()
    else:
        tabs[...] = jnp.zeros(tabs.shape, jnp.int32)
    add_peers(hid, own, tab, scalars, W1_COL, peers, slots)
    for k in range(slots):
        h = hid[first_place(tab, slots, slots + k)]
        active[k] = (h * cdf(h)).astype(bf16)
        grad[k] = dot(active[k], cot[k], (0, 0))
        for j in range(n_tok // 2):
            begin = pl.multiple_of((2 * j + other) * part, part)
            here = (j * slots + k) * part
            half[here : here + part, :] = grad[k, pl.ds(begin, part), :].astype(bf16)


def slope_kernel(dims, tab, active, hid, w2, out, slope):
    slots = dims[0]
    for k in range(slots):
        out[k] = dot(active[k], w2[k], (1, 0)).astype(bf16)
    for k in range(slots):
        h = hid[first_place(tab, slots, k)]
        slope[k] = cdf(h) + h * jnp.exp(-0.5 * h * h) * (1.0 / math.sqrt(2.0 * math.pi))


def back_kernel(dims, tab, tabs, own, *refs):
    slots, n_row, n_col, n_tok = dims
    peers, refs = refs[: n_row - 1], refs[n_row - 1 :]
    slope, w1, out, taken, grad2, half = refs[:6]
    refs = refs[6:]
    outs, refs = refs[:n_col], refs[n_col:]
    grads, (acc, value, grad) = refs[:n_tok], refs[n_tok:]
    part = grad.shape[1] // n_tok
    paired = n_tok % 2 == 0
    add_peers(acc, own, tab, tabs, W2_HID, peers, slots)
    for k in range(slots):
        g = (acc[first_place(tab, slots, k)] * slope[k]).astype(bf16)
        grad[k] = dot(taken[k], g, (0, 0))
        cut(grad.at[k], grads, k, "tok")
        value[k] = dot(g, w1[k], (1, 1))
        cut(value.at[k], outs, slots + k, "col")
    for k in range(slots):
        cut(out.at[k], outs, k, "col")
    for d in range(0, n_tok, 2 if paired else 1):
        to = target("tok", d)
        begin = pl.multiple_of(to * part, part)
        for k in range(slots):
            total = grad2[k, pl.ds(begin, part), :]
            if paired:
                there = pl.multiple_of((lax.div(to, 2) * slots + k) * part, part)
                total = total + half[pl.ds(there, part), :].astype(f32)
            grads[d][(slots + k) * part : (slots + k + 1) * part, :] = total.astype(bf16)
        spare = grads[d].shape[0] - 2 * slots * part
        grads[d][2 * slots * part :, :] = jnp.zeros((spare, LANES), bf16)
    row = table_row([[tab[which * slots + k] for k in range(slots)] for which in range(4)], slots)
    for ref in outs:
        ref[ref.shape[0] - 16 :, :] = row


def add_shares(parts, result, first):
    part = result.shape[1]
    for k in range(result.shape[0]):
        here = slice((first + k) * part, (first + k + 1) * part)
        result[k] = sum(ref[here, :].astype(f32) for ref in parts)


def output_kernel(dims, *refs):
    slots, n_row, n_col, n_tok = dims
    parts, refs = refs[1 : 1 + n_col], refs[1 + n_col :]
    outputs, tabs, results, (acc_out, acc_in, scalars, sems) = refs[:2], refs[2], refs[3:5], refs[5:]
    blk, share = acc_out.shape[-1], acc_out.shape[1]
    copy = decode_tables(parts, 2 * slots * share, tabs, scalars, sems.at[2])
    acc_out[...] = jnp.zeros(acc_out.shape, f32)
    acc_in[...] = jnp.zeros(acc_in.shape, f32)
    copy.wait()
    for c, ref in enumerate(parts):
        for k in range(slots):
            for first, which, acc in ((0, W2_OUT, acc_out), (slots, W1_ROW, acc_in)):
                at = scalars[c * 8, which * slots + k]
                here = slice((first + k) * share, (first + k + 1) * share)
                acc[at] = acc[at] + ref[here, :].astype(f32)
    stores = []
    for i, acc in enumerate((acc_out, acc_in)):
        for b in range(acc.shape[0]):
            results[i][:, b * blk : (b + 1) * blk] = acc[b].astype(bf16)
        stores.append(pltpu.make_async_copy(results[i], outputs[i], sems.at[i]))
        stores[-1].start()
    for c in stores:
        c.wait()


def grad_kernel(after, *refs):
    del after
    parts, gw1, gw2 = refs[:-2], refs[-2], refs[-1]
    slots, part, _ = gw1.shape
    add_shares(parts, gw1, 0)
    add_shares([ref for ref in parts if ref.shape[0] > slots * part], gw2, slots)


def shards(tokens, w1_blocks, w1_rows, w1_cols, w2_blocks, w2_hidden, w2_outs, grad_out):
    slots, blk = w1_blocks.shape[2], w1_blocks.shape[-1]
    rows = tokens.shape[0]
    n_row, n_col, n_tok = (lax.axis_size(a) for a in ("row", "col", "tok"))
    dims = (slots, n_row, n_col, n_tok)
    row_blocks = tokens.shape[1] // blk
    col_blocks = FF // n_col // blk
    share, part = rows // n_col, blk // n_tok
    w1 = w1_blocks.reshape(slots, blk, blk)
    w2 = w2_blocks.reshape(slots, blk, blk)
    tables = [t.reshape(slots) for t in (w1_rows, w1_cols, w2_hidden, w2_outs)]

    S = jax.ShapeDtypeStruct
    message = S((slots * rows + 16, blk), bf16)
    wide, narrow = S((slots, rows, blk), f32), S((slots, rows, blk), bf16)

    p_send = call(
        token_kernel,
        "take_tokens",
        TAKE_LIMIT,
        out_shape=message,
        in_specs=[HBM] * 6,
        out_specs=HBM,
        scratch_shapes=[
            pltpu.VMEM(tokens.shape, bf16),
            pltpu.VMEM((slots, blk, blk), bf16),
            pltpu.VMEM((slots * rows + 16, blk), bf16),
        ]
        + [pltpu.SMEM((slots,), jnp.int32)] * 4
        + [pltpu.SemaphoreType.DMA((7 + slots,))],
    )(*tables, tokens, w1)
    p_peers = [send(p_send, "row", d) for d in range(1, n_row)]

    b_send, taken, cot, hid, back, tab = call(
        cotangent_kernel,
        "take_cotangent",
        out_shape=(
            message,
            narrow,
            narrow,
            S((2 * slots + 1, rows, blk), f32),
            S((slots + 1, rows, blk), f32),
            S((6 * slots + col_blocks,), jnp.int32),
        ),
        in_specs=[SMEM] * 4 + [HBM, HBM] + [VMEM] * 2,
        out_specs=(VMEM,) * 5 + (SMEM,),
        scratch_shapes=[pltpu.SemaphoreType.DMA((2, slots))],
    )(*tables, tokens, grad_out, w1, w2)
    b_peers = [send(b_send, "row", d) for d in range(1, n_row)]

    outs = (S((2 * slots * share + 16, blk), bf16),) * n_col
    single = S((slots * part, blk), bf16)
    double = S((2 * slots * part + 32, blk), bf16)
    grads = tuple(double if n_tok % 2 == 1 or d % 2 == 0 else single for d in range(n_tok))
    half = S((max(1, n_tok // 2) * slots * part, blk), bf16)
    peer_rows = 8 * max(1, n_row - 1)
    active, hid, peer_tabs, grad2, half = call(
        functools.partial(hidden_kernel, dims),
        "hidden",
        out_shape=(
            narrow,
            S((2 * slots, rows, blk), f32),
            S((peer_rows, LANES), jnp.int32),
            S((slots, blk, blk), f32),
            half,
        ),
        in_specs=[SMEM] + [VMEM] * (n_row + 1),
        out_specs=(VMEM,) * 5,
        scratch_shapes=[pltpu.SMEM((peer_rows, LANES), jnp.int32), pltpu.SemaphoreType.DMA],
    )(tab, hid, *p_peers, cot)
    if n_tok % 2 == 0:
        half = lax.ppermute(half, "tok", [(i, i ^ 1) for i in range(n_tok)])
    out, slope = call(
        functools.partial(slope_kernel, dims),
        "slope",
        out_shape=(narrow, wide),
        in_specs=[SMEM] + [VMEM] * 3,
        out_specs=(VMEM,) * 2,
    )(tab, active, hid, w2)

    sent = call(
        functools.partial(back_kernel, dims),
        "back",
        out_shape=outs + grads,
        in_specs=[SMEM] * 2 + [VMEM] * (n_row + 6),
        out_specs=(VMEM,) * (n_col + n_tok),
        scratch_shapes=[
            pltpu.VMEM((slots, rows, blk), f32),
            pltpu.VMEM((slots, rows, blk), f32),
            pltpu.VMEM((slots, blk, blk), f32),
        ],
    )(tab, peer_tabs, back, *b_peers, slope, w1, out, taken, grad2, half)

    col_parts = [send(sent[d], "col", d) for d in range(n_col)]
    tok_parts = [send(sent[n_col + d], "tok", d) for d in range(n_tok)]

    result = S((share, row_blocks * blk), bf16)
    summed = S((slots, part, blk), f32)
    acc = pltpu.VMEM((row_blocks, share, blk), f32)
    output, grad_in, tabs = call(
        functools.partial(output_kernel, dims),
        "add_outputs",
        out_shape=(result, result, S((8 * n_col, LANES), jnp.int32)),
        in_specs=[ANY] + [VMEM] * n_col,
        out_specs=(HBM, HBM, VMEM),
        scratch_shapes=[pltpu.VMEM(result.shape, bf16)] * 2
        + [acc, acc, pltpu.SMEM((8 * n_col, LANES), jnp.int32), pltpu.SemaphoreType.DMA((3,))],
    )(tok_parts[n_tok // 2], *col_parts)
    gw1, gw2 = call(
        grad_kernel,
        "add_grads",
        out_shape=(summed, summed),
        in_specs=[ANY] + [VMEM] * n_tok,
        out_specs=(VMEM,) * 2,
    )(tabs, *tok_parts[::-1])
    return (output, grad_in, gw1.reshape(1, 1, slots, part, blk), gw2.reshape(1, 1, slots, part, blk))


def solution(mesh):
    placed = (
        P("tok", "row"),
        P("row", "col", None, None, None),
        P("row", "col", None),
        P("row", "col", None),
        P("row", "col", None, None, None),
        P("row", "col", None),
        P("row", "col", None),
        P("tok", "row"),
    )
    return jax.shard_map(
        shards,
        mesh=mesh,
        in_specs=placed,
        out_specs=(
            P(("tok", "col"), "row"),
            P(("tok", "col"), "row"),
            P("row", "col", None, "tok", None),
            P("row", "col", None, "tok", None),
        ),
        check_vma=False,
    )
```

time: 34.8 us -> 35.7 us (1.026)
  starting transfers between devices: 14.4 us -> 10.9 us
  waiting for transfers between devices: 6.1 us -> 9.38 us
  Pallas kernels: 12 us -> 13.2 us
    ppermute x8, starting transfers between devices: 12.5 us -> 9.01 us  [send(): lax.ppermute(x, axis, [(i, partner(i, d, n)) for i in range(n)])]
    ppermute x8, waiting for transfers between devices: 5.96 us -> 9.38 us  [send(): lax.ppermute(x, axis, [(i, partner(i, d, n)) for i in range(n)])]
    pallas_call x7, Pallas kernels: 12 us -> 13.2 us  [the longest x1 4.41 us: shards(): call(cotangent_kernel, 'take_cotangent', out_shape=(message, narrow, narr...]
  transfers between devices with their start and end apart: 9 -> 9, of which waited for: 5 -> 5; matrix products, arithmetic and copies ran while one was open for 0% -> 0% of each run, Pallas kernels for 22% -> 25%
where the time goes in v8:
time: 35.7 us; the launch traced here: 35.5 us
  Pallas kernels  13.2 us (37%)
  starting transfers between devices  10.9 us (31%)
  waiting for transfers between devices  9.38 us (26%)
  local copies, waits for them, and re-layouts  1.25 us (4%)
  between operations  0.8 us (2%)
    ppermute x8, waiting for transfers between devices, send(): lax.ppermute(x, axis, [(i, partner(i, d, n)) for i in range(n)])  9.38 us
    ppermute x8, starting transfers between devices, send(): lax.ppermute(x, axis, [(i, partner(i, d, n)) for i in range(n)])  9.01 us
    pallas_call x1, Pallas kernels, shards(): call(cotangent_kernel, 'take_cotangent', out_shape=(message, narrow, narr...  4.41 us
    pallas_call x1, Pallas kernels, shards(): call(token_kernel, 'take_tokens', TAKE_LIMIT, out_shape=message, in_specs...  2.36 us
    ppermute x1, starting transfers between devices, shards(): half = lax.ppermute(half, 'tok', [(i, i ^ 1) for i in range(n_tok)])  1.9 us
    pallas_call x1, Pallas kernels, shards(): call(functools.partial(output_kernel, dims), 'add_outputs', out_shape=(re...  1.89 us
    pallas_call x1, Pallas kernels, shards(): call(functools.partial(hidden_kernel, dims), 'hidden', out_shape=(narrow,...  1.69 us
    unnamed x16, local copies, waits for them, and re-layouts  1.25 us
  transfers between devices with their start and end apart: 9, of which 5 were waited for; matrix products, arithmetic and copies ran while one was open for 0% of the time, Pallas kernels for 25%

profile of v8, /device:TPU:0, one launch (start us, length us, event | category | flops | bytes accessed | tf_op | source)
XLA Modules:
  0.0 35.5 jit_solution(8643854411115916041)
XLA Ops:
  0.6 0.0 copy-start
  0.6 0.0 copy-start.7
  0.7 0.0 copy-start.6
  0.7 0.0 copy-start.5
  0.7 0.0 copy-start.4
  0.7 0.0 copy-start.1
  0.7 0.0 copy-start.3
  0.7 2.4 %take_tokens.1 = bf16[1040,128]{1,0:T(8,128)(2,1)} custom-call(s32[8]{0:T(128)} %bitcast.13, s32[8]{0:T(128)} %bitcast.15, s32[8]{0:T(128)} %bitcast.17, s32[8]{0:T(128)} %bitcast.19, bf16[128,4096]{1,0:T(8,128)(2,1)} %tokens.3, bf16[8,128,128]{2,1,0:T(8,128)(2,1)} %bitcast.8), custom_call_target="tpu_custom_call" | custom-call | flops 33554432 | bytes 524288 | tf_op jit(solution)/shard_map/take_tokens/pallas_call | solution.py:295
  3.1 3.0 %collective-permute-start = (bf16[1040,128]{1,0:T(8,128)(2,1)}, bf16[1040,128]{1,0:T(8,128)(2,1)S(1)}, u32[]{:S(2)}, u32[]{:S(2)}) collective-permute-start(bf16[1040,128]{1,0:T(8,128)(2,1)} %take_tokens.1), channel_id=1, source_target_pairs={{0,4},{4,0},{1,5},{5,1},{2,6},{6,2},{3,7},{7,3},{8,12},{12,8},{9,1... | collective-permute-start | bytes 798728 | tf_op jit(solution)/shard_map/ppermute | solution.py:55
  6.1 0.0 copy-done
  6.1 0.0 copy-done.7
  6.1 0.0 copy-done.6
  6.1 0.0 copy-done.5
  6.1 0.0 copy-done.4
  6.1 0.0 copy-done.1
  6.1 0.0 copy-done.3
  6.1 0.0 copy-start.2
  6.1 1.2 %copy-done.2 = bf16[128,4096]{1,0:T(8,128)(2,1)S(1)} copy-done((bf16[128,4096]{1,0:T(8,128)(2,1)S(1)}, bf16[128,4096]{1,0:T(8,128)(2,1)}, u32[]{:S(2)}) %copy-start.2) | copy-done | bytes 1048600
  7.3 4.4 %take_cotangent.1 = (bf16[1040,128]{1,0:T(8,128)(2,1)S(1)}, bf16[8,128,128]{2,1,0:T(8,128)(2,1)S(1)}, bf16[8,128,128]{2,1,0:T(8,128)(2,1)S(1)}, f32[17,128,128]{...) custom-call(s32[8]{0:T(128)S(1)} %bitcast.14, s32[8]{0:T(128)S(1)} %bitcast.16, s32[8]{0:T(128)S(1)} %bitcast.18, ...), custom_call_target="tpu_custom_call" | custom-call | flops 33554432 | bytes 524288 | tf_op jit(solution)/shard_map/take_cotangent/pallas_call | solution.py:312
  11.8 0.1 collective-permute-start.1
  11.9 0.8 %collective-permute-done.refs_0_ = bf16[1040,128]{1,0:T(8,128)(2,1)S(1)} collective-permute-done((bf16[1040,128]{1,0:T(8,128)(2,1)}, bf16[1040,128]{1,0:T(8,128)(2,1)S(1)}, u32[]{:S(2)}, u32[]{:S(2)}) %collective-permute-start) | collective-permute-done | bytes 266272 | tf_op jit(solution)/shard_map/ppermute | solution.py:55
  12.7 1.7 %hidden.1 = (bf16[8,128,128]{2,1,0:T(8,128)(2,1)S(1)}, f32[16,128,128]{2,1,0:T(8,128)S(1)}, s32[8,128]{1,0:T(8,128)S(1)}, f32[8,128,128]{2,1,0:T(8,128)S(1)}, bf16[512,128]{1,0:T(8,128)(2,1)S(1)}) custom-call(s32[112]{0:T(128)S(1)} %get-tuple-element.30.tab, f32[17,128,128]{2,1,0:T(8,128)S(1)} %get-tuple-element.31.own, ...), custom_call_target="tpu_custom_call" | custom-call | flops 33554432 | bytes 524288 | tf_op jit(solution)/shard_map/hidden/pallas_call | solution.py:335
  14.4 1.9 %collective-permute-start.2 = (bf16[512,128]{1,0:T(8,128)(2,1)S(1)}, bf16[512,128]{1,0:T(8,128)(2,1)S(1)}, u32[]{:S(2)}, u32[]{:S(2)}) collective-permute-start(bf16[512,128]{1,0:T(8,128)(2,1)S(1)} %get-tuple-element.42), channel_id=1, source_target_pairs={{0,8},{8,0},{16,24},{24,16},{1,9},{9,1},{17,25},{25,17},{2,10},{10... | collective-permute-start | bytes 393224 | tf_op jit(solution)/shard_map/ppermute | solution.py:350
  16.3 0.9 %slope.1 = (bf16[8,128,128]{2,1,0:T(8,128)(2,1)S(1)}, f32[8,128,128]{2,1,0:T(8,128)S(1)}) custom-call(s32[112]{0:T(128)S(1)} %get-tuple-element.30.tab, bf16[8,128,128]{2,1,0:T(8,128)(2,1)S(1)} %get-tuple-element.36.active, f32[16,128,128]{2,1,0:T(8,128)S(1)} %get-tuple-element.37.hid, bf16[8,128,128]{2,1,0:T(8,128)(2,1)S(1)} %bitcast.12), custom_call_target="tpu_custom_call" | custom-call | flops 33554432 | bytes 524288 | tf_op jit(solution)/shard_map/slope/pallas_call | solution.py:351
  17.2 2.5 %collective-permute-done.1.refs_0_ = bf16[1040,128]{1,0:T(8,128)(2,1)S(1)} collective-permute-done((bf16[1040,128]{1,0:T(8,128)(2,1)S(1)}, bf16[1040,128]{1,0:T(8,128)(2,1)S(1)}, u32[]{:S(2)}, u32[]{:S(2)}) %collective-permute-start.1) | collective-permute-done | bytes 266272 | tf_op jit(solution)/shard_map/ppermute | solution.py:55
  19.7 0.0 collective-permute-done.2.refs_6_
  19.7 1.2 %back.1 = (bf16[528,128]{1,0:T(8,128)(2,1)S(1)}, bf16[528,128]{1,0:T(8,128)(2,1)S(1)}, bf16[528,128]{1,0:T(8,128)(2,1)S(1)}, bf16[528,128]{1,0:T(8,128)(2,1)S(1)...) custom-call(s32[112]{0:T(128)S(1)} %get-tuple-element.30.tab, ...), custom_call_target="tpu_custom_call" | custom-call | flops 33554432 | bytes 524288 | tf_op jit(solution)/shard_map/back/pallas_call | solution.py:359
  20.9 0.1 collective-permute-start.4
  21.0 2.7 %collective-permute-start.3 = (bf16[544,128]{1,0:T(8,128)(2,1)S(1)}, bf16[544,128]{1,0:T(8,128)(2,1)S(1)}, u32[]{:S(2)}, u32[]{:S(2)}) collective-permute-start(bf16[544,128]{1,0:T(8,128)(2,1)S(1)} %get-tuple-element.43), channel_id=1, source_target_pairs={{0,16},{8,24},{16,0},{24,8},{1,17},{9,25},{17,1},{25,9},{2,18},{10... | collective-permute-start | bytes 417800 | tf_op jit(solution)/shard_map/ppermute | solution.py:55
  23.6 1.5 %collective-permute-start.5 = (bf16[528,128]{1,0:T(8,128)(2,1)S(1)}, bf16[528,128]{1,0:T(8,128)(2,1)S(1)}, u32[]{:S(2)}, u32[]{:S(2)}) collective-permute-start(bf16[528,128]{1,0:T(8,128)(2,1)S(1)} %get-tuple-element.46), channel_id=1, source_target_pairs={{0,2},{1,3},{2,0},{3,1},{4,6},{5,7},{6,4},{7,5},{8,10},{9,11},{10,... | collective-permute-start | bytes 405512 | tf_op jit(solution)/shard_map/ppermute | solution.py:55
  25.1 0.0 collective-permute-start.6
  25.2 1.3 %collective-permute-start.7 = (bf16[256,128]{1,0:T(8,128)(2,1)S(1)}, bf16[256,128]{1,0:T(8,128)(2,1)S(1)}, u32[]{:S(2)}, u32[]{:S(2)}) collective-permute-start(bf16[256,128]{1,0:T(8,128)(2,1)S(1)} %get-tuple-element.51), channel_id=1, source_target_pairs={{0,24},{8,16},{16,8},{24,0},{1,25},{9,17},{17,9},{25,1},{2,26},{10... | collective-permute-start | bytes 196616 | tf_op jit(solution)/shard_map/ppermute | solution.py:55
  26.5 0.0 collective-permute-done.4.refs_2_
  26.5 0.3 collective-permute-start.8
  26.8 3.3 %collective-permute-done.5.refs_3_ = bf16[528,128]{1,0:T(8,128)(2,1)S(1)} collective-permute-done((bf16[528,128]{1,0:T(8,128)(2,1)S(1)}, bf16[528,128]{1,0:T(8,128)(2,1)S(1)}, u32[]{:S(2)}, u32[]{:S(2)}) %collective-permute-start.5) | collective-permute-done | bytes 135200 | tf_op jit(solution)/shard_map/ppermute | solution.py:55
  30.1 1.3 %collective-permute-done.6.refs_4_ = bf16[528,128]{1,0:T(8,128)(2,1)S(1)} collective-permute-done((bf16[528,128]{1,0:T(8,128)(2,1)S(1)}, bf16[528,128]{1,0:T(8,128)(2,1)S(1)}, u32[]{:S(2)}, u32[]{:S(2)}) %collective-permute-start.6) | collective-permute-done | bytes 135200 | tf_op jit(solution)/shard_map/ppermute | solution.py:55
  31.4 1.4 %collective-permute-done.3.refs_0_.refs_1_ = bf16[544,128]{1,0:T(8,128)(2,1)S(1)} collective-permute-done((bf16[544,128]{1,0:T(8,128)(2,1)S(1)}, bf16[544,128]{1,0:T(8,128)(2,1)S(1)}, u32[]{:S(2)}, u32[]{:S(2)}) %collective-permute-start.3) | collective-permute-done | bytes 139296 | tf_op jit(solution)/shard_map/ppermute | solution.py:55
  32.9 1.9 %add_outputs.1 = (bf16[32,4096]{1,0:T(8,128)(2,1)}, bf16[32,4096]{1,0:T(8,128)(2,1)}, s32[32,128]{1,0:T(8,128)S(1)}) custom-call(bf16[544,128]{1,0:T(8,128)(2,1)S(1)} %collective-permute-done.3.refs_0_.refs_1_, bf16[528,128]{1,0:T(8,128)(2,1)S(1)} %get-tuple-element.44.refs_1_, bf16[528,128]{1,0:T(8,128)(2,1)S(1)} %collective-permute-done.4.refs_2_, ...), custom_call_target="tpu_custom_call" | custom-call | flops 33554432 | bytes 524288 | tf_op jit(solution)/shard_map/add_outputs/pallas_call | solution.py:378
  34.7 0.0 collective-permute-done.7.refs_0_
  34.8 0.0 collective-permute-done.8.refs_2_
  34.8 0.7 %add_grads.1 = (f32[8,32,128]{2,1,0:T(8,128)}, f32[8,32,128]{2,1,0:T(8,128)}) custom-call(s32[32,128]{1,0:T(8,128)S(1)} %get-tuple-element.50.after, bf16[256,128]{1,0:T(8,128)(2,1)S(1)} %collective-permute-done.7.refs_0_, bf16[544,128]{1,0:T(8,128)(2,1)S(1)} %collective-permute-done.3.refs_0_.refs_1_, bf16[256,128]{1,0:T(8,128)(2,1)S(1)} %collective-permute-done.8.refs_2_, ...), custom_call_target="tpu_custom_call" | custom-call | flops 33554432 | bytes 524288 | tf_op jit(solution)/shard_map/add_grads/pallas_call | solution.py:387
Async XLA Ops:
  0.6 5.4 %copy-start = (bf16[128,4096]{1,0:T(8,128)(2,1)S(1)}, bf16[128,4096]{1,0:T(8,128)(2,1)}, u32[]{:S(2)}) copy-start(bf16[128,4096]{1,0:T(8,128)(2,1)} %tokens.3) | copy-start | bytes 3145732
  0.6 5.4 %copy-start.7 = (s32[1,1,8]{2,1,0:T(1,128)S(1)}, s32[1,1,8]{2,1,0:T(1,128)}, u32[]{:S(2)}) copy-start(s32[1,1,8]{2,1,0:T(1,128)} %param.14) | copy-start | bytes 100
  0.7 5.4 %copy-start.6 = (s32[1,1,8]{2,1,0:T(1,128)S(1)}, s32[1,1,8]{2,1,0:T(1,128)}, u32[]{:S(2)}) copy-start(s32[1,1,8]{2,1,0:T(1,128)} %param.13) | copy-start | bytes 100
  0.7 5.4 %copy-start.5 = (s32[1,1,8]{2,1,0:T(1,128)S(1)}, s32[1,1,8]{2,1,0:T(1,128)}, u32[]{:S(2)}) copy-start(s32[1,1,8]{2,1,0:T(1,128)} %param.11) | copy-start | bytes 100
  0.7 5.4 %copy-start.4 = (s32[1,1,8]{2,1,0:T(1,128)S(1)}, s32[1,1,8]{2,1,0:T(1,128)}, u32[]{:S(2)}) copy-start(s32[1,1,8]{2,1,0:T(1,128)} %param.10) | copy-start | bytes 100
  0.7 5.4 %copy-start.1 = (bf16[1,1,8,128,128]{4,3,2,1,0:T(8,128)(2,1)S(1)}, bf16[1,1,8,128,128]{4,3,2,1,0:T(8,128)(2,1)}, u32[]{:S(2)}) copy-start(bf16[1,1,8,128,128]{4,3,2,1,0:T(8,128)(2,1)} %param.9) | copy-start | bytes 786436
  0.7 5.4 %copy-start.3 = (bf16[1,1,8,128,128]{4,3,2,1,0:T(8,128)(2,1)S(1)}, bf16[1,1,8,128,128]{4,3,2,1,0:T(8,128)(2,1)}, u32[]{:S(2)}) copy-start(bf16[1,1,8,128,128]{4,3,2,1,0:T(8,128)(2,1)} %param.12) | copy-start | bytes 786436
  3.1 9.6 %collective-permute-start = (bf16[1040,128]{1,0:T(8,128)(2,1)}, bf16[1040,128]{1,0:T(8,128)(2,1)S(1)}, u32[]{:S(2)}, u32[]{:S(2)}) collective-permute-start(bf16[1040,128]{1,0:T(8,128)(2,1)} %take_tokens.1), channel_id=1, source_target_pairs={{0,4},{4,0},{1,5},{5,1},{2,6},{6,2},{3,7},{7,3},{8,12},{12,8},{9,1... | collective-permute-start | bytes 798728 | tf_op jit(solution)/shard_map/ppermute | solution.py:55
  6.1 1.2 %copy-start.2 = (bf16[128,4096]{1,0:T(8,128)(2,1)S(1)}, bf16[128,4096]{1,0:T(8,128)(2,1)}, u32[]{:S(2)}) copy-start(bf16[128,4096]{1,0:T(8,128)(2,1)} %grad_out.1) | copy-start | bytes 3145732
  11.8 7.9 %collective-permute-start.1 = (bf16[1040,128]{1,0:T(8,128)(2,1)S(1)}, bf16[1040,128]{1,0:T(8,128)(2,1)S(1)}, u32[]{:S(2)}, u32[]{:S(2)}) collective-permute-start(bf16[1040,128]{1,0:T(8,128)(2,1)S(1)} %get-tuple-element.35), channel_id=1, source_target_pairs={{0,4},{4,0},{1,5},{5,1},{2,6},{6,2},{3,7},{7,3},{8,12},{12,8},{9,1... | collective-permute-start | bytes 798728 | tf_op jit(solution)/shard_map/ppermute | solution.py:55
  14.4 5.3 %collective-permute-start.2 = (bf16[512,128]{1,0:T(8,128)(2,1)S(1)}, bf16[512,128]{1,0:T(8,128)(2,1)S(1)}, u32[]{:S(2)}, u32[]{:S(2)}) collective-permute-start(bf16[512,128]{1,0:T(8,128)(2,1)S(1)} %get-tuple-element.42), channel_id=1, source_target_pairs={{0,8},{8,0},{16,24},{24,16},{1,9},{9,1},{17,25},{25,17},{2,10},{10... | collective-permute-start | bytes 393224 | tf_op jit(solution)/shard_map/ppermute | solution.py:350
  20.9 5.6 %collective-permute-start.4 = (bf16[528,128]{1,0:T(8,128)(2,1)S(1)}, bf16[528,128]{1,0:T(8,128)(2,1)S(1)}, u32[]{:S(2)}, u32[]{:S(2)}) collective-permute-start(bf16[528,128]{1,0:T(8,128)(2,1)S(1)} %get-tuple-element.45), channel_id=1, source_target_pairs={{0,1},{1,0},{2,3},{3,2},{4,5},{5,4},{6,7},{7,6},{8,9},{9,8},{10,11... | collective-permute-start | bytes 405512 | tf_op jit(solution)/shard_map/ppermute | solution.py:55
  21.0 11.9 %collective-permute-start.3 = (bf16[544,128]{1,0:T(8,128)(2,1)S(1)}, bf16[544,128]{1,0:T(8,128)(2,1)S(1)}, u32[]{:S(2)}, u32[]{:S(2)}) collective-permute-start(bf16[544,128]{1,0:T(8,128)(2,1)S(1)} %get-tuple-element.43), channel_id=1, source_target_pairs={{0,16},{8,24},{16,0},{24,8},{1,17},{9,25},{17,1},{25,9},{2,18},{10... | collective-permute-start | bytes 417800 | tf_op jit(solution)/shard_map/ppermute | solution.py:55
  23.6 6.4 %collective-permute-start.5 = (bf16[528,128]{1,0:T(8,128)(2,1)S(1)}, bf16[528,128]{1,0:T(8,128)(2,1)S(1)}, u32[]{:S(2)}, u32[]{:S(2)}) collective-permute-start(bf16[528,128]{1,0:T(8,128)(2,1)S(1)} %get-tuple-element.46), channel_id=1, source_target_pairs={{0,2},{1,3},{2,0},{3,1},{4,6},{5,7},{6,4},{7,5},{8,10},{9,11},{10,... | collective-permute-start | bytes 405512 | tf_op jit(solution)/shard_map/ppermute | solution.py:55
  25.1 6.3 %collective-permute-start.6 = (bf16[528,128]{1,0:T(8,128)(2,1)S(1)}, bf16[528,128]{1,0:T(8,128)(2,1)S(1)}, u32[]{:S(2)}, u32[]{:S(2)}) collective-permute-start(bf16[528,128]{1,0:T(8,128)(2,1)S(1)} %get-tuple-element.47), channel_id=1, source_target_pairs={{0,3},{1,2},{2,1},{3,0},{4,7},{5,6},{6,5},{7,4},{8,11},{9,10},{10,... | collective-permute-start | bytes 405512 | tf_op jit(solution)/shard_map/ppermute | solution.py:55
  25.2 9.6 %collective-permute-start.7 = (bf16[256,128]{1,0:T(8,128)(2,1)S(1)}, bf16[256,128]{1,0:T(8,128)(2,1)S(1)}, u32[]{:S(2)}, u32[]{:S(2)}) collective-permute-start(bf16[256,128]{1,0:T(8,128)(2,1)S(1)} %get-tuple-element.51), channel_id=1, source_target_pairs={{0,24},{8,16},{16,8},{24,0},{1,25},{9,17},{17,9},{25,1},{2,26},{10... | collective-permute-start | bytes 196616 | tf_op jit(solution)/shard_map/ppermute | solution.py:55
  26.5 8.2 %collective-permute-start.8 = (bf16[256,128]{1,0:T(8,128)(2,1)S(1)}, bf16[256,128]{1,0:T(8,128)(2,1)S(1)}, u32[]{:S(2)}, u32[]{:S(2)}) collective-permute-start(bf16[256,128]{1,0:T(8,128)(2,1)S(1)} %get-tuple-element.52), channel_id=1, source_target_pairs={{0,8},{8,0},{16,24},{24,16},{1,9},{9,1},{17,25},{25,17},{2,10},{10... | collective-permute-start | bytes 196616 | tf_op jit(solution)/shard_map/ppermute | solution.py:55

commit v9 on v8

--- a/solution.py
+++ b/solution.py
@@ -71,12 +71,8 @@
     return row.astype(bf16)
 
 
-def decode_tables(refs, rows, ints, scalars, sem):
-    for i, ref in enumerate(refs):
-        ints[i * 8 : i * 8 + 8] = ref[rows : rows + 16, :].astype(f32)[:8].astype(jnp.int32)
-    copy = pltpu.make_async_copy(ints, scalars, sem)
-    copy.start()
-    return copy
+def numbers(ref, rows):
+    return ref[rows : rows + 16, :].astype(f32)[:8].astype(jnp.int32)
 
 
 def token_kernel(t0, t1, t2, t3, tokens, w1, message, tokens_v, w_v, sent, c0, c1, c2, c3, sems):
@@ -109,12 +105,14 @@
         c.wait()
 
 
-def first_place(tab, slots, k):
-    return tab[4 * slots + k]
-
-
-def place_of(tab, slots, block):
-    return tab[6 * slots + block]
+def first_places(tab):
+    return tab[:8]
+
+
+def places_of(tab, blocks, slots):
+    place = lax.broadcasted_iota(jnp.int32, (2 * slots, LANES), 0)
+    same = tab[8 : 8 + 2 * slots] == blocks[:1]
+    return jnp.min(jnp.where(same, place, 2 * slots), axis=0, keepdims=True)
 
 
 def start_taking(source, table, taken, sems):
@@ -127,23 +125,27 @@
     return copies
 
 
-def cotangent_kernel(c0, c1, c2, c3, tokens, grad_out, w1, w2, message, taken, cot, hid, back, tab, sems):
+def cotangent_kernel(
+    c0, c1, c2, c3, tokens, grad_out, w1, w2, message, taken, cot, hid, back, tab, row, place_of, sems
+):
     slots, rows, blk = cot.shape
     copies = start_taking(grad_out, c3, cot, sems.at[0])
     copies_t = start_taking(tokens, c0, taken, sems.at[1])
-    for which, table in enumerate((c0, c1, c2, c3)):
-        for k in range(slots):
-            tab[which * slots + k] = table[k]
-
-    @pl.loop(0, tab.shape[0] - 6 * slots)
+
+    @pl.loop(0, place_of.shape[0])
     def _(block):
-        tab[6 * slots + block] = 2 * slots
-
+        place_of[block] = 2 * slots
+
+    lane = lax.broadcasted_iota(jnp.int32, (8, LANES), 1)
+    firsts = jnp.zeros((8, LANES), jnp.int32)
     for j in range(2 * slots):
         block = c1[j] if j < slots else c2[j - slots]
-        place = jnp.minimum(place_of(tab, slots, block), j)
-        tab[6 * slots + block] = place
-        tab[4 * slots + j] = place
+        place = jnp.minimum(place_of[block], j)
+        place_of[block] = place
+        firsts = jnp.where(lane == j, place, firsts)
+        tab[8 + j : 9 + j, :] = jnp.full((1, LANES), block, jnp.int32)
+    tab[:8] = firsts
+    row[...] = table_row((c0, c1, c2, c3), slots)
     hid[...] = jnp.zeros(hid.shape, f32)
     back[...] = jnp.zeros(back.shape, f32)
     message[slots * rows :, :] = jnp.zeros((16, blk), bf16)
@@ -151,23 +153,23 @@
         copies[k].wait()
         value = dot(cot[k], w2[k], (1, 1))
         message[k * rows : (k + 1) * rows, :] = value.astype(bf16)
-        at = jnp.minimum(place_of(tab, slots, c2[k]), slots)
+        at = jnp.minimum(place_of[c2[k]], slots)
         back[at] = back[at] + value
     for k in range(slots):
         copies_t[k].wait()
-        at = place_of(tab, slots, c1[k])
+        at = place_of[c1[k]]
         hid[at] = hid[at] + dot(taken[k], w1[k], (1, 0))
 
 
-def add_peers(acc, own, tab, tables, which, peers, slots):
-    places, rows, _ = acc.shape
-    for j in range(places):
+def add_peers(acc, own, places, which, peers, slots):
+    count, rows, _ = acc.shape
+    for j in range(count):
         acc[j] = own[j]
-    for i, ref in enumerate(peers):
+    for place, ref in zip(places, peers):
         for k in range(slots):
-            at = place_of(tab, slots, tables[i * 8, which * slots + k])
-
-            @pl.when(at < places)
+            at = place[0, which * slots + k]
+
+            @pl.when(at < count)
             def _():
                 acc[at] = acc[at] + ref[k * rows : (k + 1) * rows, :].astype(f32)
 
@@ -175,16 +177,17 @@
 def hidden_kernel(dims, tab, own, *refs):
     slots, n_row, n_col, n_tok = dims
     peers, refs = refs[: n_row - 1], refs[n_row - 1 :]
-    cot, active, hid, tabs, grad, half, scalars, sem = refs
+    cot, active, hid, places, grad, half = refs
     part = grad.shape[1] // n_tok
     other = 1 - lax.rem(lax.axis_index("tok"), 2)
-    if peers:
-        decode_tables(peers, slots * cot.shape[1], tabs, scalars, sem).wait()
-    else:
-        tabs[...] = jnp.zeros(tabs.shape, jnp.int32)
-    add_peers(hid, own, tab, scalars, W1_COL, peers, slots)
-    for k in range(slots):
-        h = hid[first_place(tab, slots, slots + k)]
+    found = [places_of(tab, numbers(ref, slots * cot.shape[1]), slots) for ref in peers]
+    places[...] = jnp.zeros(places.shape, jnp.int32)
+    for i, place in enumerate(found):
+        places[8 * i : 8 * i + 8] = jnp.broadcast_to(place, (8, LANES))
+    add_peers(hid, own, found, W1_COL, peers, slots)
+    firsts = first_places(tab)
+    for k in range(slots):
+        h = hid[firsts[0, slots + k]]
         active[k] = (h * cdf(h)).astype(bf16)
         grad[k] = dot(active[k], cot[k], (0, 0))
         for j in range(n_tok // 2):
@@ -195,14 +198,15 @@
 
 def slope_kernel(dims, tab, active, hid, w2, out, slope):
     slots = dims[0]
+    firsts = first_places(tab)
     for k in range(slots):
         out[k] = dot(active[k], w2[k], (1, 0)).astype(bf16)
     for k in range(slots):
-        h = hid[first_place(tab, slots, k)]
+        h = hid[firsts[0, k]]
         slope[k] = cdf(h) + h * jnp.exp(-0.5 * h * h) * (1.0 / math.sqrt(2.0 * math.pi))
 
 
-def back_kernel(dims, tab, tabs, own, *refs):
+def back_kernel(dims, tab, row, places, own, *refs):
     slots, n_row, n_col, n_tok = dims
     peers, refs = refs[: n_row - 1], refs[n_row - 1 :]
     slope, w1, out, taken, grad2, half = refs[:6]
@@ -211,9 +215,11 @@
     grads, (acc, value, grad) = refs[:n_tok], refs[n_tok:]
     part = grad.shape[1] // n_tok
     paired = n_tok % 2 == 0
-    add_peers(acc, own, tab, tabs, W2_HID, peers, slots)
-    for k in range(slots):
-        g = (acc[first_place(tab, slots, k)] * slope[k]).astype(bf16)
+    found = [places[8 * i : 8 * i + 8] for i in range(len(peers))]
+    add_peers(acc, own, found, W2_HID, peers, slots)
+    firsts = first_places(tab)
+    for k in range(slots):
+        g = (acc[firsts[0, k]] * slope[k]).astype(bf16)
         grad[k] = dot(taken[k], g, (0, 0))
         cut(grad.at[k], grads, k, "tok")
         value[k] = dot(g, w1[k], (1, 1))
@@ -231,9 +237,8 @@
             grads[d][(slots + k) * part : (slots + k + 1) * part, :] = total.astype(bf16)
         spare = grads[d].shape[0] - 2 * slots * part
         grads[d][2 * slots * part :, :] = jnp.zeros((spare, LANES), bf16)
-    row = table_row([[tab[which * slots + k] for k in range(slots)] for which in range(4)], slots)
     for ref in outs:
-        ref[ref.shape[0] - 16 :, :] = row
+        ref[ref.shape[0] - 16 :, :] = row[...]
 
 
 def add_shares(parts, result, first):
@@ -246,16 +251,16 @@
 def output_kernel(dims, *refs):
     slots, n_row, n_col, n_tok = dims
     parts, refs = refs[1 : 1 + n_col], refs[1 + n_col :]
-    outputs, tabs, results, (acc_out, acc_in, scalars, sems) = refs[:2], refs[2], refs[3:5], refs[5:]
+    outputs, last, results, (acc_out, acc_in, sems) = refs[:2], refs[2], refs[3:5], refs[5:]
     blk, share = acc_out.shape[-1], acc_out.shape[1]
-    copy = decode_tables(parts, 2 * slots * share, tabs, scalars, sems.at[2])
     acc_out[...] = jnp.zeros(acc_out.shape, f32)
     acc_in[...] = jnp.zeros(acc_in.shape, f32)
-    copy.wait()
-    for c, ref in enumerate(parts):
+    for ref in parts:
+        blocks = numbers(ref, 2 * slots * share)
+        last[...] = blocks
         for k in range(slots):
             for first, which, acc in ((0, W2_OUT, acc_out), (slots, W1_ROW, acc_in)):
-                at = scalars[c * 8, which * slots + k]
+                at = blocks[0, which * slots + k]
                 here = slice((first + k) * share, (first + k + 1) * share)
                 acc[at] = acc[at] + ref[here, :].astype(f32)
     stores = []
@@ -309,20 +314,21 @@
     )(*tables, tokens, w1)
     p_peers = [send(p_send, "row", d) for d in range(1, n_row)]
 
-    b_send, taken, cot, hid, back, tab = call(
+    b_send, taken, cot, hid, back, tab, row = call(
         cotangent_kernel,
         "take_cotangent",
         out_shape=(
             message,
             narrow,
             narrow,
-            S((2 * slots + 1, rows, blk), f32),
+            S((2 * slots, rows, blk), f32),
             S((slots + 1, rows, blk), f32),
-            S((6 * slots + col_blocks,), jnp.int32),
+            S((8 + 2 * slots, LANES), jnp.int32),
+            S((16, LANES), bf16),
         ),
         in_specs=[SMEM] * 4 + [HBM, HBM] + [VMEM] * 2,
-        out_specs=(VMEM,) * 5 + (SMEM,),
-        scratch_shapes=[pltpu.SemaphoreType.DMA((2, slots))],
+        out_specs=(VMEM,) * 7,
+        scratch_shapes=[pltpu.SMEM((col_blocks,), jnp.int32), pltpu.SemaphoreType.DMA((2, slots))],
     )(*tables, tokens, grad_out, w1, w2)
     b_peers = [send(b_send, "row", d) for d in range(1, n_row)]
 
@@ -332,7 +338,7 @@
     grads = tuple(double if n_tok % 2 == 1 or d % 2 == 0 else single for d in range(n_tok))
     half = S((max(1, n_tok // 2) * slots * part, blk), bf16)
     peer_rows = 8 * max(1, n_row - 1)
-    active, hid, peer_tabs, grad2, half = call(
+    active, hid, places, grad2, half = call(
         functools.partial(hidden_kernel, dims),
         "hidden",
         out_shape=(
@@ -342,9 +348,8 @@
             S((slots, blk, blk), f32),
             half,
         ),
-        in_specs=[SMEM] + [VMEM] * (n_row + 1),
+        in_specs=[VMEM] * (n_row + 2),
         out_specs=(VMEM,) * 5,
-        scratch_shapes=[pltpu.SMEM((peer_rows, LANES), jnp.int32), pltpu.SemaphoreType.DMA],
     )(tab, hid, *p_peers, cot)
     if n_tok % 2 == 0:
         half = lax.ppermute(half, "tok", [(i, i ^ 1) for i in range(n_tok)])
@@ -352,7 +357,7 @@
         functools.partial(slope_kernel, dims),
         "slope",
         out_shape=(narrow, wide),
-        in_specs=[SMEM] + [VMEM] * 3,
+        in_specs=[VMEM] * 4,
         out_specs=(VMEM,) * 2,
     )(tab, active, hid, w2)
 
@@ -360,14 +365,14 @@
         functools.partial(back_kernel, dims),
         "back",
         out_shape=outs + grads,
-        in_specs=[SMEM] * 2 + [VMEM] * (n_row + 6),
+        in_specs=[VMEM] * (n_row + 9),
         out_specs=(VMEM,) * (n_col + n_tok),
         scratch_shapes=[
             pltpu.VMEM((slots, rows, blk), f32),
             pltpu.VMEM((slots, rows, blk), f32),
             pltpu.VMEM((slots, blk, blk), f32),
         ],
-    )(tab, peer_tabs, back, *b_peers, slope, w1, out, taken, grad2, half)
+    )(tab, row, places, back, *b_peers, slope, w1, out, taken, grad2, half)
 
     col_parts = [send(sent[d], "col", d) for d in range(n_col)]
     tok_parts = [send(sent[n_col + d], "tok", d) for d in range(n_tok)]
@@ -375,14 +380,14 @@
     result = S((share, row_blocks * blk), bf16)
     summed = S((slots, part, blk), f32)
     acc = pltpu.VMEM((row_blocks, share, blk), f32)
-    output, grad_in, tabs = call(
+    output, grad_in, last = call(
         functools.partial(output_kernel, dims),
         "add_outputs",
-        out_shape=(result, result, S((8 * n_col, LANES), jnp.int32)),
+        out_shape=(result, result, S((8, LANES), jnp.int32)),
         in_specs=[ANY] + [VMEM] * n_col,
         out_specs=(HBM, HBM, VMEM),
         scratch_shapes=[pltpu.VMEM(result.shape, bf16)] * 2
-        + [acc, acc, pltpu.SMEM((8 * n_col, LANES), jnp.int32), pltpu.SemaphoreType.DMA((3,))],
+        + [acc, acc, pltpu.SemaphoreType.DMA((2,))],
     )(tok_parts[n_tok // 2], *col_parts)
     gw1, gw2 = call(
         grad_kernel,
@@ -390,7 +395,7 @@
         out_shape=(summed, summed),
         in_specs=[ANY] + [VMEM] * n_tok,
         out_specs=(VMEM,) * 2,
-    )(tabs, *tok_parts[::-1])
+    )(last, *tok_parts[::-1])
     return (output, grad_in, gw1.reshape(1, 1, slots, part, blk), gw2.reshape(1, 1, slots, part, blk))
 
 

time: 35.7 us -> 34.6 us (0.969)
  Pallas kernels: 13.2 us -> 11.3 us
  starting transfers between devices: 10.9 us -> 11.5 us
    pallas_call x1, Pallas kernels: 1.89 us -> 1.11 us  [shards(): call(functools.partial(output_kernel, dims), 'add_outputs', out_shape=(re...]
    ppermute x8, starting transfers between devices: 9.01 us -> 9.62 us  [send(): lax.ppermute(x, axis, [(i, partner(i, d, n)) for i in range(n)])]
    pallas_call x1, Pallas kernels: 0.88 us -> 0.37 us  [shards(): call(functools.partial(slope_kernel, dims), 'slope', out_shape=(narrow, w...]
    pallas_call x1, Pallas kernels: 4.41 us -> 3.96 us  [shards(): call(cotangent_kernel, 'take_cotangent', out_shape=(message, narrow, narr...]
  transfers between devices with their start and end apart: 9 -> 9, of which waited for: 5 -> 5; matrix products, arithmetic and copies ran while one was open for 0% -> 0% of each run, Pallas kernels for 25% -> 20%
where the time goes in v9:
time: 34.6 us; the launch traced here: 34.5 us
  starting transfers between devices  11.5 us (33%)
  Pallas kernels  11.3 us (33%)
  waiting for transfers between devices  9.63 us (28%)
  local copies, waits for them, and re-layouts  1.26 us (4%)
  between operations  0.79 us (2%)
    ppermute x8, waiting for transfers between devices, send(): lax.ppermute(x, axis, [(i, partner(i, d, n)) for i in range(n)])  9.62 us
    ppermute x8, starting transfers between devices, send(): lax.ppermute(x, axis, [(i, partner(i, d, n)) for i in range(n)])  9.62 us
    pallas_call x1, Pallas kernels, shards(): call(cotangent_kernel, 'take_cotangent', out_shape=(message, narrow, narr...  3.96 us
    pallas_call x1, Pallas kernels, shards(): call(token_kernel, 'take_tokens', TAKE_LIMIT, out_shape=message, in_specs...  2.37 us
    ppermute x1, starting transfers between devices, shards(): half = lax.ppermute(half, 'tok', [(i, i ^ 1) for i in range(n_tok)])  1.9 us
    pallas_call x1, Pallas kernels, shards(): call(functools.partial(back_kernel, dims), 'back', out_shape=outs + grads...  1.38 us
    pallas_call x1, Pallas kernels, shards(): call(functools.partial(hidden_kernel, dims), 'hidden', out_shape=(narrow,...  1.35 us
    unnamed x16, local copies, waits for them, and re-layouts  1.26 us
  transfers between devices with their start and end apart: 9, of which 5 were waited for; matrix products, arithmetic and copies ran while one was open for 0% of the time, Pallas kernels for 20%

profile of v9, /device:TPU:0, one launch (start us, length us, event | category | flops | bytes accessed | tf_op | source)
XLA Modules:
  0.0 34.5 jit_solution(3615419416685710615)
XLA Ops:
  0.6 0.0 copy-start
  0.6 0.0 copy-start.1
  0.7 0.0 copy-start.3
  0.7 0.0 copy-start.7
  0.7 2.4 %take_tokens.1 = bf16[1040,128]{1,0:T(8,128)(2,1)} custom-call(s32[8]{0:T(128)} %bitcast.13, s32[8]{0:T(128)} %bitcast.15, s32[8]{0:T(128)} %bitcast.17, s32[8]{0:T(128)} %bitcast.19, bf16[128,4096]{1,0:T(8,128)(2,1)} %tokens.3, bf16[8,128,128]{2,1,0:T(8,128)(2,1)} %bitcast.8), custom_call_target="tpu_custom_call" | custom-call | flops 33554432 | bytes 524288 | tf_op jit(solution)/shard_map/take_tokens/pallas_call | solution.py:300
  3.0 0.0 copy-start.4
  3.1 0.0 copy-start.5
  3.1 0.0 copy-start.6
  3.1 3.0 %collective-permute-start = (bf16[1040,128]{1,0:T(8,128)(2,1)}, bf16[1040,128]{1,0:T(8,128)(2,1)S(1)}, u32[]{:S(2)}, u32[]{:S(2)}) collective-permute-start(bf16[1040,128]{1,0:T(8,128)(2,1)} %take_tokens.1), channel_id=1, source_target_pairs={{0,4},{4,0},{1,5},{5,1},{2,6},{6,2},{3,7},{7,3},{8,12},{12,8},{9,1... | collective-permute-start | bytes 798728 | tf_op jit(solution)/shard_map/ppermute | solution.py:55
  6.1 0.0 copy-done
  6.1 0.0 copy-done.1
  6.1 0.0 copy-done.3
  6.1 0.0 copy-done.7
  6.1 0.0 copy-done.4
  6.1 0.0 copy-done.5
  6.1 0.0 copy-done.6
  6.1 0.0 copy-start.2
  6.1 1.2 %copy-done.2 = bf16[128,4096]{1,0:T(8,128)(2,1)S(1)} copy-done((bf16[128,4096]{1,0:T(8,128)(2,1)S(1)}, bf16[128,4096]{1,0:T(8,128)(2,1)}, u32[]{:S(2)}) %copy-start.2) | copy-done | bytes 1048600
  7.4 4.0 %take_cotangent.1 = (bf16[1040,128]{1,0:T(8,128)(2,1)S(1)}, bf16[8,128,128]{2,1,0:T(8,128)(2,1)S(1)}, bf16[8,128,128]{2,1,0:T(8,128)(2,1)S(1)}, f32[16,128,128]{...) custom-call(s32[8]{0:T(128)S(1)} %bitcast.14, s32[8]{0:T(128)S(1)} %bitcast.16, ...), custom_call_target="tpu_custom_call" | custom-call | flops 33554432 | bytes 524288 | tf_op jit(solution)/shard_map/take_cotangent/pallas_call | solution.py:317
  11.3 0.6 %collective-permute-start.1 = (bf16[1040,128]{1,0:T(8,128)(2,1)S(1)}, bf16[1040,128]{1,0:T(8,128)(2,1)S(1)}, u32[]{:S(2)}, u32[]{:S(2)}) collective-permute-start(bf16[1040,128]{1,0:T(8,128)(2,1)S(1)} %get-tuple-element.37), channel_id=1, source_target_pairs={{0,4},{4,0},{1,5},{5,1},{2,6},{6,2},{3,7},{7,3},{8,12},{12,8},{9,1... | collective-permute-start | bytes 798728 | tf_op jit(solution)/shard_map/ppermute | solution.py:55
  11.9 0.8 %collective-permute-done.refs_0_ = bf16[1040,128]{1,0:T(8,128)(2,1)S(1)} collective-permute-done((bf16[1040,128]{1,0:T(8,128)(2,1)}, bf16[1040,128]{1,0:T(8,128)(2,1)S(1)}, u32[]{:S(2)}, u32[]{:S(2)}) %collective-permute-start) | collective-permute-done | bytes 266272 | tf_op jit(solution)/shard_map/ppermute | solution.py:55
  12.7 1.3 %hidden.1 = (bf16[8,128,128]{2,1,0:T(8,128)(2,1)S(1)}, f32[16,128,128]{2,1,0:T(8,128)S(1)}, s32[8,128]{1,0:T(8,128)S(1)}, f32[8,128,128]{2,1,0:T(8,128)S(1)}, bf16[512,128]{1,0:T(8,128)(2,1)S(1)}) custom-call(s32[24,128]{1,0:T(8,128)S(1)} %get-tuple-element.31.tab, f32[16,128,128]{2,1,0:T(8,128)S(1)} %get-tuple-element.33.own, ...), custom_call_target="tpu_custom_call" | custom-call | flops 33554432 | bytes 524288 | tf_op jit(solution)/shard_map/hidden/pallas_call | solution.py:341
  14.0 1.9 %collective-permute-start.2 = (bf16[512,128]{1,0:T(8,128)(2,1)S(1)}, bf16[512,128]{1,0:T(8,128)(2,1)S(1)}, u32[]{:S(2)}, u32[]{:S(2)}) collective-permute-start(bf16[512,128]{1,0:T(8,128)(2,1)S(1)} %get-tuple-element.44), channel_id=1, source_target_pairs={{0,8},{8,0},{16,24},{24,16},{1,9},{9,1},{17,25},{25,17},{2,10},{10... | collective-permute-start | bytes 393224 | tf_op jit(solution)/shard_map/ppermute | solution.py:355
  15.9 0.4 %slope.1 = (bf16[8,128,128]{2,1,0:T(8,128)(2,1)S(1)}, f32[8,128,128]{2,1,0:T(8,128)S(1)}) custom-call(s32[24,128]{1,0:T(8,128)S(1)} %get-tuple-element.31.tab, bf16[8,128,128]{2,1,0:T(8,128)(2,1)S(1)} %get-tuple-element.38.active, f32[16,128,128]{2,1,0:T(8,128)S(1)} %get-tuple-element.39.hid, bf16[8,128,128]{2,1,0:T(8,128)(2,1)S(1)} %bitcast.12), custom_call_target="tpu_custom_call" | custom-call | flops 33554432 | bytes 524288 | tf_op jit(solution)/shard_map/slope/pallas_call | solution.py:356
  16.3 2.9 %collective-permute-done.1.refs_0_ = bf16[1040,128]{1,0:T(8,128)(2,1)S(1)} collective-permute-done((bf16[1040,128]{1,0:T(8,128)(2,1)S(1)}, bf16[1040,128]{1,0:T(8,128)(2,1)S(1)}, u32[]{:S(2)}, u32[]{:S(2)}) %collective-permute-start.1) | collective-permute-done | bytes 266272 | tf_op jit(solution)/shard_map/ppermute | solution.py:55
  19.3 0.0 collective-permute-done.2.refs_6_
  19.3 1.4 %back.1 = (bf16[528,128]{1,0:T(8,128)(2,1)S(1)}, bf16[528,128]{1,0:T(8,128)(2,1)S(1)}, bf16[528,128]{1,0:T(8,128)(2,1)S(1)}, bf16[528,128]{1,0:T(8,128)(2,1)S(1)...) custom-call(s32[24,128]{1,0:T(8,128)S(1)} %get-tuple-element.31.tab,, ...), custom_call_target="tpu_custom_call" | custom-call | flops 33554432 | bytes 524288 | tf_op jit(solution)/shard_map/back/pallas_call | solution.py:364
  20.6 0.1 collective-permute-start.4
  20.7 2.7 %collective-permute-start.3 = (bf16[544,128]{1,0:T(8,128)(2,1)S(1)}, bf16[544,128]{1,0:T(8,128)(2,1)S(1)}, u32[]{:S(2)}, u32[]{:S(2)}) collective-permute-start(bf16[544,128]{1,0:T(8,128)(2,1)S(1)} %get-tuple-element.45), channel_id=1, source_target_pairs={{0,16},{8,24},{16,0},{24,8},{1,17},{9,25},{17,1},{25,9},{2,18},{10... | collective-permute-start | bytes 417800 | tf_op jit(solution)/shard_map/ppermute | solution.py:55
  23.5 1.6 %collective-permute-start.5 = (bf16[528,128]{1,0:T(8,128)(2,1)S(1)}, bf16[528,128]{1,0:T(8,128)(2,1)S(1)}, u32[]{:S(2)}, u32[]{:S(2)}) collective-permute-start(bf16[528,128]{1,0:T(8,128)(2,1)S(1)} %get-tuple-element.48), channel_id=1, source_target_pairs={{0,2},{1,3},{2,0},{3,1},{4,6},{5,7},{6,4},{7,5},{8,10},{9,11},{10,... | collective-permute-start | bytes 405512 | tf_op jit(solution)/shard_map/ppermute | solution.py:55
  25.0 0.0 collective-permute-start.6
  25.0 1.3 %collective-permute-start.7 = (bf16[256,128]{1,0:T(8,128)(2,1)S(1)}, bf16[256,128]{1,0:T(8,128)(2,1)S(1)}, u32[]{:S(2)}, u32[]{:S(2)}) collective-permute-start(bf16[256,128]{1,0:T(8,128)(2,1)S(1)} %get-tuple-element.53), channel_id=1, source_target_pairs={{0,24},{8,16},{16,8},{24,0},{1,25},{9,17},{17,9},{25,1},{2,26},{10... | collective-permute-start | bytes 196616 | tf_op jit(solution)/shard_map/ppermute | solution.py:55
  26.4 0.0 collective-permute-done.4.refs_2_
  26.4 0.3 collective-permute-start.8
  26.7 3.2 %collective-permute-done.5.refs_3_ = bf16[528,128]{1,0:T(8,128)(2,1)S(1)} collective-permute-done((bf16[528,128]{1,0:T(8,128)(2,1)S(1)}, bf16[528,128]{1,0:T(8,128)(2,1)S(1)}, u32[]{:S(2)}, u32[]{:S(2)}) %collective-permute-start.5) | collective-permute-done | bytes 135200 | tf_op jit(solution)/shard_map/ppermute | solution.py:55
  29.9 1.3 %collective-permute-done.6.refs_4_ = bf16[528,128]{1,0:T(8,128)(2,1)S(1)} collective-permute-done((bf16[528,128]{1,0:T(8,128)(2,1)S(1)}, bf16[528,128]{1,0:T(8,128)(2,1)S(1)}, u32[]{:S(2)}, u32[]{:S(2)}) %collective-permute-start.6) | collective-permute-done | bytes 135200 | tf_op jit(solution)/shard_map/ppermute | solution.py:55
  31.2 1.4 %collective-permute-done.3.refs_0_.refs_1_ = bf16[544,128]{1,0:T(8,128)(2,1)S(1)} collective-permute-done((bf16[544,128]{1,0:T(8,128)(2,1)S(1)}, bf16[544,128]{1,0:T(8,128)(2,1)S(1)}, u32[]{:S(2)}, u32[]{:S(2)}) %collective-permute-start.3) | collective-permute-done | bytes 139296 | tf_op jit(solution)/shard_map/ppermute | solution.py:55
  32.6 1.1 %add_outputs.1 = (bf16[32,4096]{1,0:T(8,128)(2,1)}, bf16[32,4096]{1,0:T(8,128)(2,1)}, s32[8,128]{1,0:T(8,128)S(1)}) custom-call(bf16[544,128]{1,0:T(8,128)(2,1)S(1)} %collective-permute-done.3.refs_0_.refs_1_, bf16[528,128]{1,0:T(8,128)(2,1)S(1)} %get-tuple-element.46.refs_1_, bf16[528,128]{1,0:T(8,128)(2,1)S(1)} %collective-permute-done.4.refs_2_, ...), custom_call_target="tpu_custom_call" | custom-call | flops 33554432 | bytes 524288 | tf_op jit(solution)/shard_map/add_outputs/pallas_call | solution.py:383
  33.7 0.0 collective-permute-done.7.refs_0_
  33.7 0.0 collective-permute-done.8.refs_2_
  33.7 0.7 %add_grads.1 = (f32[8,32,128]{2,1,0:T(8,128)}, f32[8,32,128]{2,1,0:T(8,128)}) custom-call(s32[8,128]{1,0:T(8,128)S(1)} %get-tuple-element.52.after, bf16[256,128]{1,0:T(8,128)(2,1)S(1)} %collective-permute-done.7.refs_0_, bf16[544,128]{1,0:T(8,128)(2,1)S(1)} %collective-permute-done.3.refs_0_.refs_1_, bf16[256,128]{1,0:T(8,128)(2,1)S(1)} %collective-permute-done.8.refs_2_, ...), custom_call_target="tpu_custom_call" | custom-call | flops 33554432 | bytes 524288 | tf_op jit(solution)/shard_map/add_grads/pallas_call | solution.py:392
Async XLA Ops:
  0.6 5.5 %copy-start = (bf16[128,4096]{1,0:T(8,128)(2,1)S(1)}, bf16[128,4096]{1,0:T(8,128)(2,1)}, u32[]{:S(2)}) copy-start(bf16[128,4096]{1,0:T(8,128)(2,1)} %tokens.3) | copy-start | bytes 3145732
  0.6 5.5 %copy-start.1 = (bf16[1,1,8,128,128]{4,3,2,1,0:T(8,128)(2,1)S(1)}, bf16[1,1,8,128,128]{4,3,2,1,0:T(8,128)(2,1)}, u32[]{:S(2)}) copy-start(bf16[1,1,8,128,128]{4,3,2,1,0:T(8,128)(2,1)} %param.9) | copy-start | bytes 786436
  0.7 5.4 %copy-start.3 = (bf16[1,1,8,128,128]{4,3,2,1,0:T(8,128)(2,1)S(1)}, bf16[1,1,8,128,128]{4,3,2,1,0:T(8,128)(2,1)}, u32[]{:S(2)}) copy-start(bf16[1,1,8,128,128]{4,3,2,1,0:T(8,128)(2,1)} %param.12) | copy-start | bytes 786436
  0.7 5.4 %copy-start.7 = (s32[1,1,8]{2,1,0:T(1,128)S(1)}, s32[1,1,8]{2,1,0:T(1,128)}, u32[]{:S(2)}) copy-start(s32[1,1,8]{2,1,0:T(1,128)} %param.14) | copy-start | bytes 100
  3.0 3.1 %copy-start.4 = (s32[1,1,8]{2,1,0:T(1,128)S(1)}, s32[1,1,8]{2,1,0:T(1,128)}, u32[]{:S(2)}) copy-start(s32[1,1,8]{2,1,0:T(1,128)} %param.10) | copy-start | bytes 100
  3.1 3.1 %copy-start.5 = (s32[1,1,8]{2,1,0:T(1,128)S(1)}, s32[1,1,8]{2,1,0:T(1,128)}, u32[]{:S(2)}) copy-start(s32[1,1,8]{2,1,0:T(1,128)} %param.11) | copy-start | bytes 100
  3.1 3.1 %copy-start.6 = (s32[1,1,8]{2,1,0:T(1,128)S(1)}, s32[1,1,8]{2,1,0:T(1,128)}, u32[]{:S(2)}) copy-start(s32[1,1,8]{2,1,0:T(1,128)} %param.13) | copy-start | bytes 100
  3.1 9.6 %collective-permute-start = (bf16[1040,128]{1,0:T(8,128)(2,1)}, bf16[1040,128]{1,0:T(8,128)(2,1)S(1)}, u32[]{:S(2)}, u32[]{:S(2)}) collective-permute-start(bf16[1040,128]{1,0:T(8,128)(2,1)} %take_tokens.1), channel_id=1, source_target_pairs={{0,4},{4,0},{1,5},{5,1},{2,6},{6,2},{3,7},{7,3},{8,12},{12,8},{9,1... | collective-permute-start | bytes 798728 | tf_op jit(solution)/shard_map/ppermute | solution.py:55
  6.1 1.2 %copy-start.2 = (bf16[128,4096]{1,0:T(8,128)(2,1)S(1)}, bf16[128,4096]{1,0:T(8,128)(2,1)}, u32[]{:S(2)}) copy-start(bf16[128,4096]{1,0:T(8,128)(2,1)} %grad_out.1) | copy-start | bytes 3145732
  11.3 7.9 %collective-permute-start.1 = (bf16[1040,128]{1,0:T(8,128)(2,1)S(1)}, bf16[1040,128]{1,0:T(8,128)(2,1)S(1)}, u32[]{:S(2)}, u32[]{:S(2)}) collective-permute-start(bf16[1040,128]{1,0:T(8,128)(2,1)S(1)} %get-tuple-element.37), channel_id=1, source_target_pairs={{0,4},{4,0},{1,5},{5,1},{2,6},{6,2},{3,7},{7,3},{8,12},{12,8},{9,1... | collective-permute-start | bytes 798728 | tf_op jit(solution)/shard_map/ppermute | solution.py:55
  14.0 5.2 %collective-permute-start.2 = (bf16[512,128]{1,0:T(8,128)(2,1)S(1)}, bf16[512,128]{1,0:T(8,128)(2,1)S(1)}, u32[]{:S(2)}, u32[]{:S(2)}) collective-permute-start(bf16[512,128]{1,0:T(8,128)(2,1)S(1)} %get-tuple-element.44), channel_id=1, source_target_pairs={{0,8},{8,0},{16,24},{24,16},{1,9},{9,1},{17,25},{25,17},{2,10},{10... | collective-permute-start | bytes 393224 | tf_op jit(solution)/shard_map/ppermute | solution.py:355
  20.6 5.7 %collective-permute-start.4 = (bf16[528,128]{1,0:T(8,128)(2,1)S(1)}, bf16[528,128]{1,0:T(8,128)(2,1)S(1)}, u32[]{:S(2)}, u32[]{:S(2)}) collective-permute-start(bf16[528,128]{1,0:T(8,128)(2,1)S(1)} %get-tuple-element.47), channel_id=1, source_target_pairs={{0,1},{1,0},{2,3},{3,2},{4,5},{5,4},{6,7},{7,6},{8,9},{9,8},{10,11... | collective-permute-start | bytes 405512 | tf_op jit(solution)/shard_map/ppermute | solution.py:55
  20.7 11.9 %collective-permute-start.3 = (bf16[544,128]{1,0:T(8,128)(2,1)S(1)}, bf16[544,128]{1,0:T(8,128)(2,1)S(1)}, u32[]{:S(2)}, u32[]{:S(2)}) collective-permute-start(bf16[544,128]{1,0:T(8,128)(2,1)S(1)} %get-tuple-element.45), channel_id=1, source_target_pairs={{0,16},{8,24},{16,0},{24,8},{1,17},{9,25},{17,1},{25,9},{2,18},{10... | collective-permute-start | bytes 417800 | tf_op jit(solution)/shard_map/ppermute | solution.py:55
  23.5 6.4 %collective-permute-start.5 = (bf16[528,128]{1,0:T(8,128)(2,1)S(1)}, bf16[528,128]{1,0:T(8,128)(2,1)S(1)}, u32[]{:S(2)}, u32[]{:S(2)}) collective-permute-start(bf16[528,128]{1,0:T(8,128)(2,1)S(1)} %get-tuple-element.48), channel_id=1, source_target_pairs={{0,2},{1,3},{2,0},{3,1},{4,6},{5,7},{6,4},{7,5},{8,10},{9,11},{10,... | collective-permute-start | bytes 405512 | tf_op jit(solution)/shard_map/ppermute | solution.py:55
  25.0 6.2 %collective-permute-start.6 = (bf16[528,128]{1,0:T(8,128)(2,1)S(1)}, bf16[528,128]{1,0:T(8,128)(2,1)S(1)}, u32[]{:S(2)}, u32[]{:S(2)}) collective-permute-start(bf16[528,128]{1,0:T(8,128)(2,1)S(1)} %get-tuple-element.49), channel_id=1, source_target_pairs={{0,3},{1,2},{2,1},{3,0},{4,7},{5,6},{6,5},{7,4},{8,11},{9,10},{10,... | collective-permute-start | bytes 405512 | tf_op jit(solution)/shard_map/ppermute | solution.py:55
  25.0 8.7 %collective-permute-start.7 = (bf16[256,128]{1,0:T(8,128)(2,1)S(1)}, bf16[256,128]{1,0:T(8,128)(2,1)S(1)}, u32[]{:S(2)}, u32[]{:S(2)}) collective-permute-start(bf16[256,128]{1,0:T(8,128)(2,1)S(1)} %get-tuple-element.53), channel_id=1, source_target_pairs={{0,24},{8,16},{16,8},{24,0},{1,25},{9,17},{17,9},{25,1},{2,26},{10... | collective-permute-start | bytes 196616 | tf_op jit(solution)/shard_map/ppermute | solution.py:55
  26.4 7.4 %collective-permute-start.8 = (bf16[256,128]{1,0:T(8,128)(2,1)S(1)}, bf16[256,128]{1,0:T(8,128)(2,1)S(1)}, u32[]{:S(2)}, u32[]{:S(2)}) collective-permute-start(bf16[256,128]{1,0:T(8,128)(2,1)S(1)} %get-tuple-element.54), channel_id=1, source_target_pairs={{0,8},{8,0},{16,24},{24,16},{1,9},{9,1},{17,25},{25,17},{2,10},{10... | collective-permute-start | bytes 196616 | tf_op jit(solution)/shard_map/ppermute | solution.py:55

commit v10 on v9

--- a/solution.py
+++ b/solution.py
@@ -126,7 +126,7 @@
 
 
 def cotangent_kernel(
-    c0, c1, c2, c3, tokens, grad_out, w1, w2, message, taken, cot, hid, back, tab, row, place_of, sems
+    c0, c1, c2, c3, tokens, grad_out, w1, w2, message, taken_t, cot, hid, back, tab, row, place_of, taken, sems
 ):
     slots, rows, blk = cot.shape
     copies = start_taking(grad_out, c3, cot, sems.at[0])
@@ -159,15 +159,15 @@
         copies_t[k].wait()
         at = place_of[c1[k]]
         hid[at] = hid[at] + dot(taken[k], w1[k], (1, 0))
-
-
-def add_peers(acc, own, places, which, peers, slots):
+        taken_t[k] = taken[k].T
+
+
+def add_peers(acc, own, numbers_at, peers, slots):
     count, rows, _ = acc.shape
     for j in range(count):
         acc[j] = own[j]
-    for place, ref in zip(places, peers):
-        for k in range(slots):
-            at = place[0, which * slots + k]
+    for numbers_of, ref in zip(numbers_at, peers):
+        for k, at in enumerate(numbers_of):
 
             @pl.when(at < count)
             def _():
@@ -184,10 +184,12 @@
     places[...] = jnp.zeros(places.shape, jnp.int32)
     for i, place in enumerate(found):
         places[8 * i : 8 * i + 8] = jnp.broadcast_to(place, (8, LANES))
-    add_peers(hid, own, found, W1_COL, peers, slots)
+    at = [[place[0, W1_COL * slots + k] for k in range(slots)] for place in found]
     firsts = first_places(tab)
-    for k in range(slots):
-        h = hid[firsts[0, slots + k]]
+    firsts = [firsts[0, slots + k] for k in range(slots)]
+    add_peers(hid, own, at, peers, slots)
+    for k in range(slots):
+        h = hid[firsts[k]]
         active[k] = (h * cdf(h)).astype(bf16)
         grad[k] = dot(active[k], cot[k], (0, 0))
         for j in range(n_tok // 2):
@@ -209,18 +211,20 @@
 def back_kernel(dims, tab, row, places, own, *refs):
     slots, n_row, n_col, n_tok = dims
     peers, refs = refs[: n_row - 1], refs[n_row - 1 :]
-    slope, w1, out, taken, grad2, half = refs[:6]
+    slope, w1, out, taken_t, grad2, half = refs[:6]
     refs = refs[6:]
     outs, refs = refs[:n_col], refs[n_col:]
     grads, (acc, value, grad) = refs[:n_tok], refs[n_tok:]
     part = grad.shape[1] // n_tok
     paired = n_tok % 2 == 0
     found = [places[8 * i : 8 * i + 8] for i in range(len(peers))]
-    add_peers(acc, own, found, W2_HID, peers, slots)
+    at = [[place[0, W2_HID * slots + k] for k in range(slots)] for place in found]
     firsts = first_places(tab)
-    for k in range(slots):
-        g = (acc[firsts[0, k]] * slope[k]).astype(bf16)
-        grad[k] = dot(taken[k], g, (0, 0))
+    firsts = [firsts[0, k] for k in range(slots)]
+    add_peers(acc, own, at, peers, slots)
+    for k in range(slots):
+        g = (acc[firsts[k]] * slope[k]).astype(bf16)
+        grad[k] = dot(taken_t[k], g, (1, 0))
         cut(grad.at[k], grads, k, "tok")
         value[k] = dot(g, w1[k], (1, 1))
         cut(value.at[k], outs, slots + k, "col")
@@ -314,12 +318,12 @@
     )(*tables, tokens, w1)
     p_peers = [send(p_send, "row", d) for d in range(1, n_row)]
 
-    b_send, taken, cot, hid, back, tab, row = call(
+    b_send, taken_t, cot, hid, back, tab, row = call(
         cotangent_kernel,
         "take_cotangent",
         out_shape=(
             message,
-            narrow,
+            S((slots, blk, rows), bf16),
             narrow,
             S((2 * slots, rows, blk), f32),
             S((slots + 1, rows, blk), f32),
@@ -328,7 +332,11 @@
         ),
         in_specs=[SMEM] * 4 + [HBM, HBM] + [VMEM] * 2,
         out_specs=(VMEM,) * 7,
-        scratch_shapes=[pltpu.SMEM((col_blocks,), jnp.int32), pltpu.SemaphoreType.DMA((2, slots))],
+        scratch_shapes=[
+            pltpu.SMEM((col_blocks,), jnp.int32),
+            pltpu.VMEM((slots, rows, blk), bf16),
+            pltpu.SemaphoreType.DMA((2, slots)),
+        ],
     )(*tables, tokens, grad_out, w1, w2)
     b_peers = [send(b_send, "row", d) for d in range(1, n_row)]
 
@@ -372,9 +380,9 @@
             pltpu.VMEM((slots, rows, blk), f32),
             pltpu.VMEM((slots, blk, blk), f32),
         ],
-    )(tab, row, places, back, *b_peers, slope, w1, out, taken, grad2, half)
-
-    col_parts = [send(sent[d], "col", d) for d in range(n_col)]
+    )(tab, row, places, back, *b_peers, slope, w1, out, taken_t, grad2, half)
+
+    col_parts = [send(sent[d], "col", d) for d in [0] + list(range(2, n_col)) + [1][: n_col - 1]]
     tok_parts = [send(sent[n_col + d], "tok", d) for d in range(n_tok)]
 
     result = S((share, row_blocks * blk), bf16)

time: 34.6 us -> 33.4 us (0.965)
  Pallas kernels: 11.3 us -> 9.71 us
  starting transfers between devices: 11.5 us -> 12.1 us
    pallas_call x1, Pallas kernels: 1.35 us -> 0.55 us  [shards(): call(functools.partial(hidden_kernel, dims), 'hidden', out_shape=(narrow,...]
    pallas_call x1, Pallas kernels: 1.38 us -> 0.62 us  [shards(): call(functools.partial(back_kernel, dims), 'back', out_shape=outs + grads...]
    ppermute x8, starting transfers between devices: 9.62 us -> 10.3 us  [send(): lax.ppermute(x, axis, [(i, partner(i, d, n)) for i in range(n)])]
  transfers between devices with their start and end apart: 9 -> 9, of which waited for: 5 -> 4; matrix products, arithmetic and copies ran while one was open for 0% -> 0% of each run, Pallas kernels for 20% -> 18%
where the time goes in v10:
time: 33.4 us; the launch traced here: 33.3 us
  starting transfers between devices  12.1 us (36%)
  Pallas kernels  9.71 us (29%)
  waiting for transfers between devices  9.36 us (28%)
  local copies, waits for them, and re-layouts  1.26 us (4%)
  between operations  0.79 us (2%)
    ppermute x8, starting transfers between devices, send(): lax.ppermute(x, axis, [(i, partner(i, d, n)) for i in range(n)])  10.3 us
    ppermute x8, waiting for transfers between devices, send(): lax.ppermute(x, axis, [(i, partner(i, d, n)) for i in range(n)])  9.35 us
    pallas_call x1, Pallas kernels, shards(): call(cotangent_kernel, 'take_cotangent', out_shape=(message, S((slots, bl...  3.96 us
    pallas_call x1, Pallas kernels, shards(): call(token_kernel, 'take_tokens', TAKE_LIMIT, out_shape=message, in_specs...  2.37 us
    ppermute x1, starting transfers between devices, shards(): half = lax.ppermute(half, 'tok', [(i, i ^ 1) for i in range(n_tok)])  1.89 us
    unnamed x16, local copies, waits for them, and re-layouts  1.26 us
    pallas_call x1, Pallas kernels, shards(): call(functools.partial(output_kernel, dims), 'add_outputs', out_shape=(re...  1.11 us
    pallas_call x1, Pallas kernels, shards(): call(grad_kernel, 'add_grads', out_shape=(summed, summed), in_specs=[ANY]...  0.74 us
  transfers between devices with their start and end apart: 9, of which 4 were waited for; matrix products, arithmetic and copies ran while one was open for 0% of the time, Pallas kernels for 18%

profile of v10, /device:TPU:0, one launch (start us, length us, event | category | flops | bytes accessed | tf_op | source)
XLA Modules:
  0.0 33.3 jit_solution(5932815777404295477)
XLA Ops:
  0.6 0.0 copy-start
  0.6 0.0 copy-start.1
  0.7 0.0 copy-start.3
  0.7 0.0 copy-start.7
  0.7 2.4 %take_tokens.1 = bf16[1040,128]{1,0:T(8,128)(2,1)} custom-call(s32[8]{0:T(128)} %bitcast.13, s32[8]{0:T(128)} %bitcast.15, s32[8]{0:T(128)} %bitcast.17, s32[8]{0:T(128)} %bitcast.19, bf16[128,4096]{1,0:T(8,128)(2,1)} %tokens.3, bf16[8,128,128]{2,1,0:T(8,128)(2,1)} %bitcast.8), custom_call_target="tpu_custom_call" | custom-call | flops 33554432 | bytes 524288 | tf_op jit(solution)/shard_map/take_tokens/pallas_call | solution.py:304
  3.0 0.0 copy-start.4
  3.1 0.0 copy-start.5
  3.1 0.0 copy-start.6
  3.1 3.0 %collective-permute-start = (bf16[1040,128]{1,0:T(8,128)(2,1)}, bf16[1040,128]{1,0:T(8,128)(2,1)S(1)}, u32[]{:S(2)}, u32[]{:S(2)}) collective-permute-start(bf16[1040,128]{1,0:T(8,128)(2,1)} %take_tokens.1), channel_id=1, source_target_pairs={{0,4},{4,0},{1,5},{5,1},{2,6},{6,2},{3,7},{7,3},{8,12},{12,8},{9,1... | collective-permute-start | bytes 798728 | tf_op jit(solution)/shard_map/ppermute | solution.py:55
  6.1 0.0 copy-done
  6.1 0.0 copy-done.1
  6.1 0.0 copy-done.3
  6.1 0.0 copy-done.7
  6.1 0.0 copy-done.4
  6.1 0.0 copy-done.5
  6.1 0.0 copy-done.6
  6.1 0.0 copy-start.2
  6.1 1.2 %copy-done.2 = bf16[128,4096]{1,0:T(8,128)(2,1)S(1)} copy-done((bf16[128,4096]{1,0:T(8,128)(2,1)S(1)}, bf16[128,4096]{1,0:T(8,128)(2,1)}, u32[]{:S(2)}) %copy-start.2) | copy-done | bytes 1048600
  7.4 4.0 %take_cotangent.1 = (bf16[1040,128]{1,0:T(8,128)(2,1)S(1)}, bf16[8,128,128]{2,1,0:T(8,128)(2,1)S(1)}, bf16[8,128,128]{2,1,0:T(8,128)(2,1)S(1)}, f32[16,128,128]{...) custom-call(s32[8]{0:T(128)S(1)} %bitcast.14, s32[8]{0:T(128)S(1)} %bitcast.16, ...), custom_call_target="tpu_custom_call" | custom-call | flops 33554432 | bytes 524288 | tf_op jit(solution)/shard_map/take_cotangent/pallas_call | solution.py:321
  11.3 0.6 %collective-permute-start.1 = (bf16[1040,128]{1,0:T(8,128)(2,1)S(1)}, bf16[1040,128]{1,0:T(8,128)(2,1)S(1)}, u32[]{:S(2)}, u32[]{:S(2)}) collective-permute-start(bf16[1040,128]{1,0:T(8,128)(2,1)S(1)} %get-tuple-element.37), channel_id=1, source_target_pairs={{0,4},{4,0},{1,5},{5,1},{2,6},{6,2},{3,7},{7,3},{8,12},{12,8},{9,1... | collective-permute-start | bytes 798728 | tf_op jit(solution)/shard_map/ppermute | solution.py:55
  11.9 0.8 %collective-permute-done.refs_0_ = bf16[1040,128]{1,0:T(8,128)(2,1)S(1)} collective-permute-done((bf16[1040,128]{1,0:T(8,128)(2,1)}, bf16[1040,128]{1,0:T(8,128)(2,1)S(1)}, u32[]{:S(2)}, u32[]{:S(2)}) %collective-permute-start) | collective-permute-done | bytes 266272 | tf_op jit(solution)/shard_map/ppermute | solution.py:55
  12.7 0.6 %hidden.1 = (bf16[8,128,128]{2,1,0:T(8,128)(2,1)S(1)}, f32[16,128,128]{2,1,0:T(8,128)S(1)}, s32[8,128]{1,0:T(8,128)S(1)}, f32[8,128,128]{2,1,0:T(8,128)S(1)}, bf16[512,128]{1,0:T(8,128)(2,1)S(1)}) custom-call(s32[24,128]{1,0:T(8,128)S(1)} %get-tuple-element.31.tab, f32[16,128,128]{2,1,0:T(8,128)S(1)} %get-tuple-element.33.own, ...), custom_call_target="tpu_custom_call" | custom-call | flops 33554432 | bytes 524288 | tf_op jit(solution)/shard_map/hidden/pallas_call | solution.py:349
  13.3 1.9 %collective-permute-start.2 = (bf16[512,128]{1,0:T(8,128)(2,1)S(1)}, bf16[512,128]{1,0:T(8,128)(2,1)S(1)}, u32[]{:S(2)}, u32[]{:S(2)}) collective-permute-start(bf16[512,128]{1,0:T(8,128)(2,1)S(1)} %get-tuple-element.44), channel_id=1, source_target_pairs={{0,8},{8,0},{16,24},{24,16},{1,9},{9,1},{17,25},{25,17},{2,10},{10... | collective-permute-start | bytes 393224 | tf_op jit(solution)/shard_map/ppermute | solution.py:363
  15.1 0.4 %slope.1 = (bf16[8,128,128]{2,1,0:T(8,128)(2,1)S(1)}, f32[8,128,128]{2,1,0:T(8,128)S(1)}) custom-call(s32[24,128]{1,0:T(8,128)S(1)} %get-tuple-element.31.tab, bf16[8,128,128]{2,1,0:T(8,128)(2,1)S(1)} %get-tuple-element.38.active, f32[16,128,128]{2,1,0:T(8,128)S(1)} %get-tuple-element.39.hid, bf16[8,128,128]{2,1,0:T(8,128)(2,1)S(1)} %bitcast.12), custom_call_target="tpu_custom_call" | custom-call | flops 33554432 | bytes 524288 | tf_op jit(solution)/shard_map/slope/pallas_call | solution.py:364
  15.5 3.7 %collective-permute-done.1.refs_0_ = bf16[1040,128]{1,0:T(8,128)(2,1)S(1)} collective-permute-done((bf16[1040,128]{1,0:T(8,128)(2,1)S(1)}, bf16[1040,128]{1,0:T(8,128)(2,1)S(1)}, u32[]{:S(2)}, u32[]{:S(2)}) %collective-permute-start.1) | collective-permute-done | bytes 266272 | tf_op jit(solution)/shard_map/ppermute | solution.py:55
  19.2 0.0 collective-permute-done.2.refs_6_
  19.3 0.6 %back.1 = (bf16[528,128]{1,0:T(8,128)(2,1)S(1)}, bf16[528,128]{1,0:T(8,128)(2,1)S(1)}, bf16[528,128]{1,0:T(8,128)(2,1)S(1)}, bf16[528,128]{1,0:T(8,128)(2,1)S(1)...) custom-call(s32[24,128]{1,0:T(8,128)S(1)} %get-tuple-element.31.tab,, ...), custom_call_target="tpu_custom_call" | custom-call | flops 33554432 | bytes 524288 | tf_op jit(solution)/shard_map/back/pallas_call | solution.py:372
  19.9 1.6 %collective-permute-start.4 = (bf16[528,128]{1,0:T(8,128)(2,1)S(1)}, bf16[528,128]{1,0:T(8,128)(2,1)S(1)}, u32[]{:S(2)}, u32[]{:S(2)}) collective-permute-start(bf16[528,128]{1,0:T(8,128)(2,1)S(1)} %get-tuple-element.47), channel_id=1, source_target_pairs={{0,2},{1,3},{2,0},{3,1},{4,6},{5,7},{6,4},{7,5},{8,10},{9,11},{10,... | collective-permute-start | bytes 405512 | tf_op jit(solution)/shard_map/ppermute | solution.py:55
  21.5 2.6 %collective-permute-start.3 = (bf16[544,128]{1,0:T(8,128)(2,1)S(1)}, bf16[544,128]{1,0:T(8,128)(2,1)S(1)}, u32[]{:S(2)}, u32[]{:S(2)}) collective-permute-start(bf16[544,128]{1,0:T(8,128)(2,1)S(1)} %get-tuple-element.45), channel_id=1, source_target_pairs={{0,16},{8,24},{16,0},{24,8},{1,17},{9,25},{17,1},{25,9},{2,18},{10... | collective-permute-start | bytes 417800 | tf_op jit(solution)/shard_map/ppermute | solution.py:55
  24.0 0.0 collective-permute-start.5
  24.0 0.6 %collective-permute-start.6 = (bf16[528,128]{1,0:T(8,128)(2,1)S(1)}, bf16[528,128]{1,0:T(8,128)(2,1)S(1)}, u32[]{:S(2)}, u32[]{:S(2)}) collective-permute-start(bf16[528,128]{1,0:T(8,128)(2,1)S(1)} %get-tuple-element.49), channel_id=1, source_target_pairs={{0,1},{1,0},{2,3},{3,2},{4,5},{5,4},{6,7},{7,6},{8,9},{9,8},{10,11... | collective-permute-start | bytes 405512 | tf_op jit(solution)/shard_map/ppermute | solution.py:55
  24.7 1.3 %collective-permute-start.7 = (bf16[256,128]{1,0:T(8,128)(2,1)S(1)}, bf16[256,128]{1,0:T(8,128)(2,1)S(1)}, u32[]{:S(2)}, u32[]{:S(2)}) collective-permute-start(bf16[256,128]{1,0:T(8,128)(2,1)S(1)} %get-tuple-element.53), channel_id=1, source_target_pairs={{0,24},{8,16},{16,8},{24,0},{1,25},{9,17},{17,9},{25,1},{2,26},{10... | collective-permute-start | bytes 196616 | tf_op jit(solution)/shard_map/ppermute | solution.py:55
  26.0 0.0 collective-permute-done.4.refs_2_
  26.0 0.5 %collective-permute-start.8 = (bf16[256,128]{1,0:T(8,128)(2,1)S(1)}, bf16[256,128]{1,0:T(8,128)(2,1)S(1)}, u32[]{:S(2)}, u32[]{:S(2)}) collective-permute-start(bf16[256,128]{1,0:T(8,128)(2,1)S(1)} %get-tuple-element.54), channel_id=1, source_target_pairs={{0,8},{8,0},{16,24},{24,16},{1,9},{9,1},{17,25},{25,17},{2,10},{10... | collective-permute-start | bytes 196616 | tf_op jit(solution)/shard_map/ppermute | solution.py:55
  26.5 2.5 %collective-permute-done.5.refs_3_ = bf16[528,128]{1,0:T(8,128)(2,1)S(1)} collective-permute-done((bf16[528,128]{1,0:T(8,128)(2,1)S(1)}, bf16[528,128]{1,0:T(8,128)(2,1)S(1)}, u32[]{:S(2)}, u32[]{:S(2)}) %collective-permute-start.5) | collective-permute-done | bytes 135200 | tf_op jit(solution)/shard_map/ppermute | solution.py:55
  29.0 0.0 collective-permute-done.6.refs_4_
  29.0 2.4 %collective-permute-done.3.refs_0_.refs_1_ = bf16[544,128]{1,0:T(8,128)(2,1)S(1)} collective-permute-done((bf16[544,128]{1,0:T(8,128)(2,1)S(1)}, bf16[544,128]{1,0:T(8,128)(2,1)S(1)}, u32[]{:S(2)}, u32[]{:S(2)}) %collective-permute-start.3) | collective-permute-done | bytes 139296 | tf_op jit(solution)/shard_map/ppermute | solution.py:55
  31.4 1.1 %add_outputs.1 = (bf16[32,4096]{1,0:T(8,128)(2,1)}, bf16[32,4096]{1,0:T(8,128)(2,1)}, s32[8,128]{1,0:T(8,128)S(1)}) custom-call(bf16[544,128]{1,0:T(8,128)(2,1)S(1)} %collective-permute-done.3.refs_0_.refs_1_, bf16[528,128]{1,0:T(8,128)(2,1)S(1)} %get-tuple-element.46.refs_1_, bf16[528,128]{1,0:T(8,128)(2,1)S(1)} %collective-permute-done.4.refs_2_, ...), custom_call_target="tpu_custom_call" | custom-call | flops 33554432 | bytes 524288 | tf_op jit(solution)/shard_map/add_outputs/pallas_call | solution.py:391
  32.5 0.0 collective-permute-done.7.refs_0_
  32.5 0.0 collective-permute-done.8.refs_2_
  32.5 0.7 %add_grads.1 = (f32[8,32,128]{2,1,0:T(8,128)}, f32[8,32,128]{2,1,0:T(8,128)}) custom-call(s32[8,128]{1,0:T(8,128)S(1)} %get-tuple-element.52.after, bf16[256,128]{1,0:T(8,128)(2,1)S(1)} %collective-permute-done.7.refs_0_, bf16[544,128]{1,0:T(8,128)(2,1)S(1)} %collective-permute-done.3.refs_0_.refs_1_, bf16[256,128]{1,0:T(8,128)(2,1)S(1)} %collective-permute-done.8.refs_2_, ...), custom_call_target="tpu_custom_call" | custom-call | flops 33554432 | bytes 524288 | tf_op jit(solution)/shard_map/add_grads/pallas_call | solution.py:400
Async XLA Ops:
  0.6 5.5 %copy-start = (bf16[128,4096]{1,0:T(8,128)(2,1)S(1)}, bf16[128,4096]{1,0:T(8,128)(2,1)}, u32[]{:S(2)}) copy-start(bf16[128,4096]{1,0:T(8,128)(2,1)} %tokens.3) | copy-start | bytes 3145732
  0.6 5.5 %copy-start.1 = (bf16[1,1,8,128,128]{4,3,2,1,0:T(8,128)(2,1)S(1)}, bf16[1,1,8,128,128]{4,3,2,1,0:T(8,128)(2,1)}, u32[]{:S(2)}) copy-start(bf16[1,1,8,128,128]{4,3,2,1,0:T(8,128)(2,1)} %param.9) | copy-start | bytes 786436
  0.7 5.4 %copy-start.3 = (bf16[1,1,8,128,128]{4,3,2,1,0:T(8,128)(2,1)S(1)}, bf16[1,1,8,128,128]{4,3,2,1,0:T(8,128)(2,1)}, u32[]{:S(2)}) copy-start(bf16[1,1,8,128,128]{4,3,2,1,0:T(8,128)(2,1)} %param.12) | copy-start | bytes 786436
  0.7 5.4 %copy-start.7 = (s32[1,1,8]{2,1,0:T(1,128)S(1)}, s32[1,1,8]{2,1,0:T(1,128)}, u32[]{:S(2)}) copy-start(s32[1,1,8]{2,1,0:T(1,128)} %param.14) | copy-start | bytes 100
  3.0 3.1 %copy-start.4 = (s32[1,1,8]{2,1,0:T(1,128)S(1)}, s32[1,1,8]{2,1,0:T(1,128)}, u32[]{:S(2)}) copy-start(s32[1,1,8]{2,1,0:T(1,128)} %param.10) | copy-start | bytes 100
  3.1 3.1 %copy-start.5 = (s32[1,1,8]{2,1,0:T(1,128)S(1)}, s32[1,1,8]{2,1,0:T(1,128)}, u32[]{:S(2)}) copy-start(s32[1,1,8]{2,1,0:T(1,128)} %param.11) | copy-start | bytes 100
  3.1 3.1 %copy-start.6 = (s32[1,1,8]{2,1,0:T(1,128)S(1)}, s32[1,1,8]{2,1,0:T(1,128)}, u32[]{:S(2)}) copy-start(s32[1,1,8]{2,1,0:T(1,128)} %param.13) | copy-start | bytes 100
  3.1 9.6 %collective-permute-start = (bf16[1040,128]{1,0:T(8,128)(2,1)}, bf16[1040,128]{1,0:T(8,128)(2,1)S(1)}, u32[]{:S(2)}, u32[]{:S(2)}) collective-permute-start(bf16[1040,128]{1,0:T(8,128)(2,1)} %take_tokens.1), channel_id=1, source_target_pairs={{0,4},{4,0},{1,5},{5,1},{2,6},{6,2},{3,7},{7,3},{8,12},{12,8},{9,1... | collective-permute-start | bytes 798728 | tf_op jit(solution)/shard_map/ppermute | solution.py:55
  6.1 1.2 %copy-start.2 = (bf16[128,4096]{1,0:T(8,128)(2,1)S(1)}, bf16[128,4096]{1,0:T(8,128)(2,1)}, u32[]{:S(2)}) copy-start(bf16[128,4096]{1,0:T(8,128)(2,1)} %grad_out.1) | copy-start | bytes 3145732
  11.3 7.9 %collective-permute-start.1 = (bf16[1040,128]{1,0:T(8,128)(2,1)S(1)}, bf16[1040,128]{1,0:T(8,128)(2,1)S(1)}, u32[]{:S(2)}, u32[]{:S(2)}) collective-permute-start(bf16[1040,128]{1,0:T(8,128)(2,1)S(1)} %get-tuple-element.37), channel_id=1, source_target_pairs={{0,4},{4,0},{1,5},{5,1},{2,6},{6,2},{3,7},{7,3},{8,12},{12,8},{9,1... | collective-permute-start | bytes 798728 | tf_op jit(solution)/shard_map/ppermute | solution.py:55
  13.3 6.0 %collective-permute-start.2 = (bf16[512,128]{1,0:T(8,128)(2,1)S(1)}, bf16[512,128]{1,0:T(8,128)(2,1)S(1)}, u32[]{:S(2)}, u32[]{:S(2)}) collective-permute-start(bf16[512,128]{1,0:T(8,128)(2,1)S(1)} %get-tuple-element.44), channel_id=1, source_target_pairs={{0,8},{8,0},{16,24},{24,16},{1,9},{9,1},{17,25},{25,17},{2,10},{10... | collective-permute-start | bytes 393224 | tf_op jit(solution)/shard_map/ppermute | solution.py:363
  19.9 6.1 %collective-permute-start.4 = (bf16[528,128]{1,0:T(8,128)(2,1)S(1)}, bf16[528,128]{1,0:T(8,128)(2,1)S(1)}, u32[]{:S(2)}, u32[]{:S(2)}) collective-permute-start(bf16[528,128]{1,0:T(8,128)(2,1)S(1)} %get-tuple-element.47), channel_id=1, source_target_pairs={{0,2},{1,3},{2,0},{3,1},{4,6},{5,7},{6,4},{7,5},{8,10},{9,11},{10,... | collective-permute-start | bytes 405512 | tf_op jit(solution)/shard_map/ppermute | solution.py:55
  21.5 9.9 %collective-permute-start.3 = (bf16[544,128]{1,0:T(8,128)(2,1)S(1)}, bf16[544,128]{1,0:T(8,128)(2,1)S(1)}, u32[]{:S(2)}, u32[]{:S(2)}) collective-permute-start(bf16[544,128]{1,0:T(8,128)(2,1)S(1)} %get-tuple-element.45), channel_id=1, source_target_pairs={{0,16},{8,24},{16,0},{24,8},{1,17},{9,25},{17,1},{25,9},{2,18},{10... | collective-permute-start | bytes 417800 | tf_op jit(solution)/shard_map/ppermute | solution.py:55
  24.0 4.9 %collective-permute-start.5 = (bf16[528,128]{1,0:T(8,128)(2,1)S(1)}, bf16[528,128]{1,0:T(8,128)(2,1)S(1)}, u32[]{:S(2)}, u32[]{:S(2)}) collective-permute-start(bf16[528,128]{1,0:T(8,128)(2,1)S(1)} %get-tuple-element.48), channel_id=1, source_target_pairs={{0,3},{1,2},{2,1},{3,0},{4,7},{5,6},{6,5},{7,4},{8,11},{9,10},{10,... | collective-permute-start | bytes 405512 | tf_op jit(solution)/shard_map/ppermute | solution.py:55
  24.0 4.9 %collective-permute-start.6 = (bf16[528,128]{1,0:T(8,128)(2,1)S(1)}, bf16[528,128]{1,0:T(8,128)(2,1)S(1)}, u32[]{:S(2)}, u32[]{:S(2)}) collective-permute-start(bf16[528,128]{1,0:T(8,128)(2,1)S(1)} %get-tuple-element.49), channel_id=1, source_target_pairs={{0,1},{1,0},{2,3},{3,2},{4,5},{5,4},{6,7},{7,6},{8,9},{9,8},{10,11... | collective-permute-start | bytes 405512 | tf_op jit(solution)/shard_map/ppermute | solution.py:55
  24.7 7.8 %collective-permute-start.7 = (bf16[256,128]{1,0:T(8,128)(2,1)S(1)}, bf16[256,128]{1,0:T(8,128)(2,1)S(1)}, u32[]{:S(2)}, u32[]{:S(2)}) collective-permute-start(bf16[256,128]{1,0:T(8,128)(2,1)S(1)} %get-tuple-element.53), channel_id=1, source_target_pairs={{0,24},{8,16},{16,8},{24,0},{1,25},{9,17},{17,9},{25,1},{2,26},{10... | collective-permute-start | bytes 196616 | tf_op jit(solution)/shard_map/ppermute | solution.py:55
  26.0 6.5 %collective-permute-start.8 = (bf16[256,128]{1,0:T(8,128)(2,1)S(1)}, bf16[256,128]{1,0:T(8,128)(2,1)S(1)}, u32[]{:S(2)}, u32[]{:S(2)}) collective-permute-start(bf16[256,128]{1,0:T(8,128)(2,1)S(1)} %get-tuple-element.54), channel_id=1, source_target_pairs={{0,8},{8,0},{16,24},{24,16},{1,9},{9,1},{17,25},{25,17},{2,10},{10... | collective-permute-start | bytes 196616 | tf_op jit(solution)/shard_map/ppermute | solution.py:55

commit v11 on v10

--- a/solution.py
+++ b/solution.py
@@ -198,20 +198,24 @@
             half[here : here + part, :] = grad[k, pl.ds(begin, part), :].astype(bf16)
 
 
-def slope_kernel(dims, tab, active, hid, w2, out, slope):
-    slots = dims[0]
+def slope_kernel(dims, tab, row, active, hid, w2, slope, *refs):
+    slots, n_row, n_col, n_tok = dims
+    outs, value = refs[:n_col], refs[n_col]
+    for k in range(slots):
+        value[k] = dot(active[k], w2[k], (1, 0))
+        cut(value.at[k], outs, k, "col")
+    for ref in outs:
+        ref[ref.shape[0] - 16 :, :] = row[...]
     firsts = first_places(tab)
-    for k in range(slots):
-        out[k] = dot(active[k], w2[k], (1, 0)).astype(bf16)
     for k in range(slots):
         h = hid[firsts[0, k]]
         slope[k] = cdf(h) + h * jnp.exp(-0.5 * h * h) * (1.0 / math.sqrt(2.0 * math.pi))
 
 
-def back_kernel(dims, tab, row, places, own, *refs):
+def back_kernel(dims, tab, places, own, *refs):
     slots, n_row, n_col, n_tok = dims
     peers, refs = refs[: n_row - 1], refs[n_row - 1 :]
-    slope, w1, out, taken_t, grad2, half = refs[:6]
+    slope, w1, near, taken_t, grad2, half = refs[:6]
     refs = refs[6:]
     outs, refs = refs[:n_col], refs[n_col:]
     grads, (acc, value, grad) = refs[:n_tok], refs[n_tok:]
@@ -227,9 +231,9 @@
         grad[k] = dot(taken_t[k], g, (1, 0))
         cut(grad.at[k], grads, k, "tok")
         value[k] = dot(g, w1[k], (1, 1))
-        cut(value.at[k], outs, slots + k, "col")
-    for k in range(slots):
-        cut(out.at[k], outs, k, "col")
+        cut(value.at[k], outs, k, "col")
+    if n_col > 1:
+        outs[1][outs[0].shape[0] :, :] = near[...]
     for d in range(0, n_tok, 2 if paired else 1):
         to = target("tok", d)
         begin = pl.multiple_of(to * part, part)
@@ -241,8 +245,10 @@
             grads[d][(slots + k) * part : (slots + k + 1) * part, :] = total.astype(bf16)
         spare = grads[d].shape[0] - 2 * slots * part
         grads[d][2 * slots * part :, :] = jnp.zeros((spare, LANES), bf16)
-    for ref in outs:
-        ref[ref.shape[0] - 16 :, :] = row[...]
+
+
+def pass_kernel(share, *refs):
+    refs[-1][...] = share[...]
 
 
 def add_shares(parts, result, first):
@@ -252,20 +258,34 @@
         result[k] = sum(ref[here, :].astype(f32) for ref in parts)
 
 
+def halves(refs, count):
+    refs = list(refs)
+    second, first = refs[:count], refs[count:]
+    if len(refs) % 2 == 1:
+        joined = refs[-1]
+        rows = refs[count].shape[0]
+        first = refs[count:-1] + [joined.at[:rows]]
+        second = second + [joined.at[rows:]]
+    return second, first
+
+
 def output_kernel(dims, *refs):
     slots, n_row, n_col, n_tok = dims
-    parts, refs = refs[1 : 1 + n_col], refs[1 + n_col :]
+    alone = max(1, n_col - 1)
+    count = 2 * alone + (n_col > 1)
+    outs, backs = halves(refs[:count], alone)
+    refs = refs[count:]
     outputs, last, results, (acc_out, acc_in, sems) = refs[:2], refs[2], refs[3:5], refs[5:]
     blk, share = acc_out.shape[-1], acc_out.shape[1]
     acc_out[...] = jnp.zeros(acc_out.shape, f32)
     acc_in[...] = jnp.zeros(acc_in.shape, f32)
-    for ref in parts:
-        blocks = numbers(ref, 2 * slots * share)
+    for out, back in zip(outs, backs):
+        blocks = numbers(out, slots * share)
         last[...] = blocks
         for k in range(slots):
-            for first, which, acc in ((0, W2_OUT, acc_out), (slots, W1_ROW, acc_in)):
+            here = slice(k * share, (k + 1) * share)
+            for ref, which, acc in ((out, W2_OUT, acc_out), (back, W1_ROW, acc_in)):
                 at = blocks[0, which * slots + k]
-                here = slice((first + k) * share, (first + k + 1) * share)
                 acc[at] = acc[at] + ref[here, :].astype(f32)
     stores = []
     for i, acc in enumerate((acc_out, acc_in)):
@@ -283,6 +303,10 @@
     slots, part, _ = gw1.shape
     add_shares(parts, gw1, 0)
     add_shares([ref for ref in parts if ref.shape[0] > slots * part], gw2, slots)
+
+
+def alone(n):
+    return [0] + list(range(2, n))
 
 
 def shards(tokens, w1_blocks, w1_rows, w1_cols, w2_blocks, w2_hidden, w2_outs, grad_out):
@@ -340,7 +364,6 @@
     )(*tables, tokens, grad_out, w1, w2)
     b_peers = [send(b_send, "row", d) for d in range(1, n_row)]
 
-    outs = (S((2 * slots * share + 16, blk), bf16),) * n_col
     single = S((slots * part, blk), bf16)
     double = S((2 * slots * part + 32, blk), bf16)
     grads = tuple(double if n_tok % 2 == 1 or d % 2 == 0 else single for d in range(n_tok))
@@ -361,29 +384,43 @@
     )(tab, hid, *p_peers, cot)
     if n_tok % 2 == 0:
         half = lax.ppermute(half, "tok", [(i, i ^ 1) for i in range(n_tok)])
-    out, slope = call(
+    out_share, back_share = S((slots * share + 16, blk), bf16), S((slots * share, blk), bf16)
+    slope, *o_sent = call(
         functools.partial(slope_kernel, dims),
         "slope",
-        out_shape=(narrow, wide),
-        in_specs=[VMEM] * 4,
-        out_specs=(VMEM,) * 2,
-    )(tab, active, hid, w2)
-
+        out_shape=(wide,) + (out_share,) * n_col,
+        in_specs=[VMEM] * 5,
+        out_specs=(VMEM,) * (1 + n_col),
+        scratch_shapes=[pltpu.VMEM((slots, rows, blk), f32)],
+    )(tab, row, active, hid, w2)
+    o_parts = [send(o_sent[d], "col", d) for d in alone(n_col)]
+
+    outs = [back_share] * n_col
+    if n_col > 1:
+        outs[1] = S((2 * slots * share + 16, blk), bf16)
     sent = call(
         functools.partial(back_kernel, dims),
         "back",
-        out_shape=outs + grads,
-        in_specs=[VMEM] * (n_row + 9),
+        out_shape=(*outs, *grads),
+        in_specs=[VMEM] * (n_row + 8),
         out_specs=(VMEM,) * (n_col + n_tok),
         scratch_shapes=[
             pltpu.VMEM((slots, rows, blk), f32),
             pltpu.VMEM((slots, rows, blk), f32),
             pltpu.VMEM((slots, blk, blk), f32),
         ],
-    )(tab, row, places, back, *b_peers, slope, w1, out, taken_t, grad2, half)
-
-    col_parts = [send(sent[d], "col", d) for d in [0] + list(range(2, n_col)) + [1][: n_col - 1]]
-    tok_parts = [send(sent[n_col + d], "tok", d) for d in range(n_tok)]
+    )(tab, places, back, *b_peers, slope, w1, o_sent[min(1, n_col - 1)], taken_t, grad2, half)
+    i_sent, g_sent = list(sent[:n_col]), list(sent[n_col:])
+    if n_col > 2:
+        i_sent[2] = call(
+            pass_kernel,
+            "pass_share",
+            out_shape=back_share,
+            in_specs=[VMEM] + [ANY] * len(o_parts[1:]),
+            out_specs=VMEM,
+        )(i_sent[2], *o_parts[1:])
+    i_parts = [send(i_sent[d], "col", d) for d in alone(n_col) + [1][: n_col - 1]]
+    tok_parts = [send(g_sent[d], "tok", d) for d in range(n_tok)]
 
     result = S((share, row_blocks * blk), bf16)
     summed = S((slots, part, blk), f32)
@@ -392,11 +429,11 @@
         functools.partial(output_kernel, dims),
         "add_outputs",
         out_shape=(result, result, S((8, LANES), jnp.int32)),
-        in_specs=[ANY] + [VMEM] * n_col,
+        in_specs=[VMEM] * len(o_parts + i_parts),
         out_specs=(HBM, HBM, VMEM),
         scratch_shapes=[pltpu.VMEM(result.shape, bf16)] * 2
         + [acc, acc, pltpu.SemaphoreType.DMA((2,))],
-    )(tok_parts[n_tok // 2], *col_parts)
+    )(*o_parts, *i_parts)
     gw1, gw2 = call(
         grad_kernel,
         "add_grads",

time: 33.4 us -> 33 us (0.988)
  waiting for transfers between devices: 9.36 us -> 6.47 us
  starting transfers between devices: 12.1 us -> 14.6 us
    ppermute x8 -> x10, waiting for transfers between devices: 9.35 us -> 6.47 us  [send(): lax.ppermute(x, axis, [(i, partner(i, d, n)) for i in range(n)])]
    ppermute x8 -> x10, starting transfers between devices: 10.3 us -> 12.7 us  [send(): lax.ppermute(x, axis, [(i, partner(i, d, n)) for i in range(n)])]
    pallas_call x2 -> x3, Pallas kernels: 0.98 us -> 1.01 us  [the longest x1 0.62 us: shards(): call(functools.partial(back_kernel, dims), 'back', out_shape=(*outs, *gra...]
  transfers between devices with their start and end apart: 9 -> 11, of which waited for: 4 -> 5; matrix products, arithmetic and copies ran while one was open for 0% -> 0% of each run, Pallas kernels for 18% -> 20%
where the time goes in v11:
time: 33 us; the launch traced here: 32.8 us
  starting transfers between devices  14.6 us (44%)
  Pallas kernels  9.73 us (29%)
  waiting for transfers between devices  6.47 us (20%)
  local copies, waits for them, and re-layouts  1.26 us (4%)
  between operations  0.79 us (2%)
    ppermute x10, starting transfers between devices, send(): lax.ppermute(x, axis, [(i, partner(i, d, n)) for i in range(n)])  12.7 us
    ppermute x10, waiting for transfers between devices, send(): lax.ppermute(x, axis, [(i, partner(i, d, n)) for i in range(n)])  6.47 us
    pallas_call x1, Pallas kernels, shards(): call(cotangent_kernel, 'take_cotangent', out_shape=(message, S((slots, bl...  3.96 us
    pallas_call x1, Pallas kernels, shards(): call(token_kernel, 'take_tokens', TAKE_LIMIT, out_shape=message, in_specs...  2.39 us
    ppermute x1, starting transfers between devices, shards(): half = lax.ppermute(half, 'tok', [(i, i ^ 1) for i in range(n_tok)])  1.89 us
    unnamed x16, local copies, waits for them, and re-layouts  1.26 us
    pallas_call x1, Pallas kernels, shards(): call(functools.partial(output_kernel, dims), 'add_outputs', out_shape=(re...  1.1 us
    pallas_call x1, Pallas kernels, shards(): call(grad_kernel, 'add_grads', out_shape=(summed, summed), in_specs=[ANY]...  0.74 us
  transfers between devices with their start and end apart: 11, of which 5 were waited for; matrix products, arithmetic and copies ran while one was open for 0% of the time, Pallas kernels for 20%

profile of v11, /device:TPU:0, one launch (start us, length us, event | category | flops | bytes accessed | tf_op | source)
XLA Modules:
  0.0 32.8 jit_solution(4139547308990663728)
XLA Ops:
  0.6 0.0 copy-start
  0.6 0.0 copy-start.1
  0.7 0.0 copy-start.2
  0.7 0.0 copy-start.7
  0.7 2.4 %take_tokens.1 = bf16[1040,128]{1,0:T(8,128)(2,1)} custom-call(s32[8]{0:T(128)} %bitcast.13, s32[8]{0:T(128)} %bitcast.15, s32[8]{0:T(128)} %bitcast.17, s32[8]{0:T(128)} %bitcast.19, bf16[128,4096]{1,0:T(8,128)(2,1)} %tokens.3, bf16[8,128,128]{2,1,0:T(8,128)(2,1)} %bitcast.8), custom_call_target="tpu_custom_call" | custom-call | flops 33554432 | bytes 524288 | tf_op jit(solution)/shard_map/take_tokens/pallas_call | solution.py:328
  3.1 0.0 copy-start.4
  3.1 0.0 copy-start.5
  3.1 0.0 copy-start.6
  3.1 3.0 %collective-permute-start = (bf16[1040,128]{1,0:T(8,128)(2,1)}, bf16[1040,128]{1,0:T(8,128)(2,1)S(1)}, u32[]{:S(2)}, u32[]{:S(2)}) collective-permute-start(bf16[1040,128]{1,0:T(8,128)(2,1)} %take_tokens.1), channel_id=1, source_target_pairs={{0,4},{4,0},{1,5},{5,1},{2,6},{6,2},{3,7},{7,3},{8,12},{12,8},{9,1... | collective-permute-start | bytes 798728 | tf_op jit(solution)/shard_map/ppermute | solution.py:55
  6.1 0.0 copy-done
  6.1 0.0 copy-done.1
  6.1 0.0 copy-done.2
  6.1 0.0 copy-done.7
  6.1 0.0 copy-done.4
  6.1 0.0 copy-done.5
  6.2 0.0 copy-done.6
  6.2 0.0 copy-start.3
  6.2 1.2 %copy-done.3 = bf16[128,4096]{1,0:T(8,128)(2,1)S(1)} copy-done((bf16[128,4096]{1,0:T(8,128)(2,1)S(1)}, bf16[128,4096]{1,0:T(8,128)(2,1)}, u32[]{:S(2)}) %copy-start.3) | copy-done | bytes 1048600
  7.4 4.0 %take_cotangent.1 = (bf16[1040,128]{1,0:T(8,128)(2,1)S(1)}, bf16[8,128,128]{2,1,0:T(8,128)(2,1)S(1)}, bf16[8,128,128]{2,1,0:T(8,128)(2,1)S(1)}, f32[16,128,128]{...) custom-call(s32[8]{0:T(128)S(1)} %bitcast.14, s32[8]{0:T(128)S(1)} %bitcast.16, ...), custom_call_target="tpu_custom_call" | custom-call | flops 33554432 | bytes 524288 | tf_op jit(solution)/shard_map/take_cotangent/pallas_call | solution.py:345
  11.4 0.6 %collective-permute-start.3 = (bf16[1040,128]{1,0:T(8,128)(2,1)S(1)}, bf16[1040,128]{1,0:T(8,128)(2,1)S(1)}, u32[]{:S(2)}, u32[]{:S(2)}) collective-permute-start(bf16[1040,128]{1,0:T(8,128)(2,1)S(1)} %get-tuple-element.45), channel_id=1, source_target_pairs={{0,4},{4,0},{1,5},{5,1},{2,6},{6,2},{3,7},{7,3},{8,12},{12,8},{9,1... | collective-permute-start | bytes 798728 | tf_op jit(solution)/shard_map/ppermute | solution.py:55
  12.0 0.8 %collective-permute-done.refs_0_ = bf16[1040,128]{1,0:T(8,128)(2,1)S(1)} collective-permute-done((bf16[1040,128]{1,0:T(8,128)(2,1)}, bf16[1040,128]{1,0:T(8,128)(2,1)S(1)}, u32[]{:S(2)}, u32[]{:S(2)}) %collective-permute-start) | collective-permute-done | bytes 266272 | tf_op jit(solution)/shard_map/ppermute | solution.py:55
  12.7 0.5 %hidden.1 = (bf16[8,128,128]{2,1,0:T(8,128)(2,1)S(1)}, f32[16,128,128]{2,1,0:T(8,128)S(1)}, s32[8,128]{1,0:T(8,128)S(1)}, f32[8,128,128]{2,1,0:T(8,128)S(1)}, bf16[512,128]{1,0:T(8,128)(2,1)S(1)}) custom-call(s32[24,128]{1,0:T(8,128)S(1)} %get-tuple-element.34.tab, f32[16,128,128]{2,1,0:T(8,128)S(1)} %get-tuple-element.36.own, ...), custom_call_target="tpu_custom_call" | custom-call | flops 33554432 | bytes 524288 | tf_op jit(solution)/shard_map/hidden/pallas_call | solution.py:372
  13.3 1.9 %collective-permute-start.4 = (bf16[512,128]{1,0:T(8,128)(2,1)S(1)}, bf16[512,128]{1,0:T(8,128)(2,1)S(1)}, u32[]{:S(2)}, u32[]{:S(2)}) collective-permute-start(bf16[512,128]{1,0:T(8,128)(2,1)S(1)} %get-tuple-element.50), channel_id=1, source_target_pairs={{0,8},{8,0},{16,24},{24,16},{1,9},{9,1},{17,25},{25,17},{2,10},{10... | collective-permute-start | bytes 393224 | tf_op jit(solution)/shard_map/ppermute | solution.py:386
  15.1 0.4 %slope.1 = (f32[8,128,128]{2,1,0:T(8,128)S(1)}, bf16[272,128]{1,0:T(8,128)(2,1)S(1)}, bf16[272,128]{1,0:T(8,128)(2,1)S(1)}, bf16[272,128]{1,0:T(8,128)(2,1)S(1)}, bf16[272,128]{1,0:T(8,128)(2,1)S(1)}) custom-call(s32[24,128]{1,0:T(8,128)S(1)} %get-tuple-element.34.tab, bf16[16,128]{1,0:T(8,128)(2,1)S(1)} %get-tuple-element.35.row, ...), custom_call_target="tpu_custom_call" | custom-call | flops 33554432 | bytes 524288 | tf_op jit(solution)/shard_map/slope/pallas_call | solution.py:388
  15.5 1.6 %collective-permute-start.1 = (bf16[272,128]{1,0:T(8,128)(2,1)S(1)}, bf16[272,128]{1,0:T(8,128)(2,1)S(1)}, u32[]{:S(2)}, u32[]{:S(2)}) collective-permute-start(bf16[272,128]{1,0:T(8,128)(2,1)S(1)} %get-tuple-element.41), channel_id=1, source_target_pairs={{0,2},{1,3},{2,0},{3,1},{4,6},{5,7},{6,4},{7,5},{8,10},{9,11},{10,... | collective-permute-start | bytes 208904 | tf_op jit(solution)/shard_map/ppermute | solution.py:55
  17.1 0.0 collective-permute-start.2
  17.1 2.1 %collective-permute-done.3.refs_0_ = bf16[1040,128]{1,0:T(8,128)(2,1)S(1)} collective-permute-done((bf16[1040,128]{1,0:T(8,128)(2,1)S(1)}, bf16[1040,128]{1,0:T(8,128)(2,1)S(1)}, u32[]{:S(2)}, u32[]{:S(2)}) %collective-permute-start.3) | collective-permute-done | bytes 266272 | tf_op jit(solution)/shard_map/ppermute | solution.py:55
  19.3 0.0 collective-permute-done.4.refs_6_
  19.3 0.6 %back.1 = (bf16[256,128]{1,0:T(8,128)(2,1)S(1)}, bf16[528,128]{1,0:T(8,128)(2,1)S(1)}, bf16[256,128]{1,0:T(8,128)(2,1)S(1)}, bf16[256,128]{1,0:T(8,128)(2,1)S(1)...) custom-call(s32[24,128]{1,0:T(8,128)S(1)} %get-tuple-element.34.tab,, ...), custom_call_target="tpu_custom_call" | custom-call | flops 33554432 | bytes 524288 | tf_op jit(solution)/shard_map/back/pallas_call | solution.py:401
  19.9 2.7 %collective-permute-start.9 = (bf16[544,128]{1,0:T(8,128)(2,1)S(1)}, bf16[544,128]{1,0:T(8,128)(2,1)S(1)}, u32[]{:S(2)}, u32[]{:S(2)}) collective-permute-start(bf16[544,128]{1,0:T(8,128)(2,1)S(1)} %get-tuple-element.59), channel_id=1, source_target_pairs={{0,16},{8,24},{16,0},{24,8},{1,17},{9,25},{17,1},{25,9},{2,18},{10... | collective-permute-start | bytes 417800 | tf_op jit(solution)/shard_map/ppermute | solution.py:55
  22.6 0.0 collective-permute-start.7
  22.6 0.0 collective-permute-done.1.refs_0_.refs_1_
  22.6 0.0 collective-permute-done.2.refs_1_.refs_2_
  22.6 1.6 %collective-permute-start.5 = (bf16[256,128]{1,0:T(8,128)(2,1)S(1)}, bf16[256,128]{1,0:T(8,128)(2,1)S(1)}, u32[]{:S(2)}, u32[]{:S(2)}) collective-permute-start(bf16[256,128]{1,0:T(8,128)(2,1)S(1)} %pass_share.1), channel_id=1, source_target_pairs={{0,2},{1,3},{2,0},{3,1},{4,6},{5,7},{6,4},{7,5},{8,10},{9,11},{10,... | collective-permute-start | bytes 196616 | tf_op jit(solution)/shard_map/ppermute | solution.py:55
  24.2 0.3 collective-permute-start.6
  24.5 1.3 %collective-permute-start.8 = (bf16[256,128]{1,0:T(8,128)(2,1)S(1)}, bf16[256,128]{1,0:T(8,128)(2,1)S(1)}, u32[]{:S(2)}, u32[]{:S(2)}) collective-permute-start(bf16[256,128]{1,0:T(8,128)(2,1)S(1)} %get-tuple-element.58), channel_id=1, source_target_pairs={{0,24},{8,16},{16,8},{24,0},{1,25},{9,17},{17,9},{25,1},{2,26},{10... | collective-permute-start | bytes 196616 | tf_op jit(solution)/shard_map/ppermute | solution.py:55
  25.9 1.3 %collective-permute-done.5.refs_4_ = bf16[256,128]{1,0:T(8,128)(2,1)S(1)} collective-permute-done((bf16[256,128]{1,0:T(8,128)(2,1)S(1)}, bf16[256,128]{1,0:T(8,128)(2,1)S(1)}, u32[]{:S(2)}, u32[]{:S(2)}) %collective-permute-start.5) | collective-permute-done | bytes 65568 | tf_op jit(solution)/shard_map/ppermute | solution.py:55
  27.2 1.6 %collective-permute-start.10 = (bf16[256,128]{1,0:T(8,128)(2,1)S(1)}, bf16[256,128]{1,0:T(8,128)(2,1)S(1)}, u32[]{:S(2)}, u32[]{:S(2)}) collective-permute-start(bf16[256,128]{1,0:T(8,128)(2,1)S(1)} %get-tuple-element.60), channel_id=1, source_target_pairs={{0,8},{8,0},{16,24},{24,16},{1,9},{9,1},{17,25},{25,17},{2,10},{10... | collective-permute-start | bytes 196616 | tf_op jit(solution)/shard_map/ppermute | solution.py:55
  28.7 0.0 collective-permute-done.6.refs_5_
  28.7 0.0 collective-permute-done.7.refs_6_
  28.7 1.1 %add_outputs.1 = (bf16[32,4096]{1,0:T(8,128)(2,1)}, bf16[32,4096]{1,0:T(8,128)(2,1)}, s32[8,128]{1,0:T(8,128)S(1)}) custom-call(bf16[272,128]{1,0:T(8,128)(2,1)S(1)} %get-tuple-element.40.refs_0_, bf16[272,128]{1,0:T(8,128)(2,1)S(1)} %collective-permute-done.1.refs_0_.refs_1_, bf16[272,128]{1,0:T(8,128)(2,1)S(1)} %collective-permute-done.2.refs_1_.refs_2_, ...), custom_call_target="tpu_custom_call" | custom-call | flops 33554432 | bytes 524288 | tf_op jit(solution)/shard_map/add_outputs/pallas_call | solution.py:428
  29.8 1.4 %collective-permute-done.8.refs_0_ = bf16[256,128]{1,0:T(8,128)(2,1)S(1)} collective-permute-done((bf16[256,128]{1,0:T(8,128)(2,1)S(1)}, bf16[256,128]{1,0:T(8,128)(2,1)S(1)}, u32[]{:S(2)}, u32[]{:S(2)}) %collective-permute-start.8) | collective-permute-done | bytes 65568 | tf_op jit(solution)/shard_map/ppermute | solution.py:55
  31.2 0.9 %collective-permute-done.10.refs_2_ = bf16[256,128]{1,0:T(8,128)(2,1)S(1)} collective-permute-done((bf16[256,128]{1,0:T(8,128)(2,1)S(1)}, bf16[256,128]{1,0:T(8,128)(2,1)S(1)}, u32[]{:S(2)}, u32[]{:S(2)}) %collective-permute-start.10) | collective-permute-done | bytes 65568 | tf_op jit(solution)/shard_map/ppermute | solution.py:55
  32.1 0.0 collective-permute-done.9.refs_1_
  32.1 0.7 %add_grads.1 = (f32[8,32,128]{2,1,0:T(8,128)}, f32[8,32,128]{2,1,0:T(8,128)}) custom-call(s32[8,128]{1,0:T(8,128)S(1)} %get-tuple-element.57.after, bf16[256,128]{1,0:T(8,128)(2,1)S(1)} %collective-permute-done.8.refs_0_, bf16[544,128]{1,0:T(8,128)(2,1)S(1)} %collective-permute-done.9.refs_1_, bf16[256,128]{1,0:T(8,128)(2,1)S(1)} %collective-permute-done.10.refs_2_, ...), custom_call_target="tpu_custom_call" | custom-call | flops 33554432 | bytes 524288 | tf_op jit(solution)/shard_map/add_grads/pallas_call | solution.py:437
  (1 shorter events, 0.0 us)
Async XLA Ops:
  0.6 5.5 %copy-start = (bf16[128,4096]{1,0:T(8,128)(2,1)S(1)}, bf16[128,4096]{1,0:T(8,128)(2,1)}, u32[]{:S(2)}) copy-start(bf16[128,4096]{1,0:T(8,128)(2,1)} %tokens.3) | copy-start | bytes 3145732
  0.6 5.5 %copy-start.1 = (bf16[1,1,8,128,128]{4,3,2,1,0:T(8,128)(2,1)S(1)}, bf16[1,1,8,128,128]{4,3,2,1,0:T(8,128)(2,1)}, u32[]{:S(2)}) copy-start(bf16[1,1,8,128,128]{4,3,2,1,0:T(8,128)(2,1)} %param.9) | copy-start | bytes 786436
  0.7 5.5 %copy-start.2 = (bf16[1,1,8,128,128]{4,3,2,1,0:T(8,128)(2,1)S(1)}, bf16[1,1,8,128,128]{4,3,2,1,0:T(8,128)(2,1)}, u32[]{:S(2)}) copy-start(bf16[1,1,8,128,128]{4,3,2,1,0:T(8,128)(2,1)} %param.12) | copy-start | bytes 786436
  0.7 5.5 %copy-start.7 = (s32[1,1,8]{2,1,0:T(1,128)S(1)}, s32[1,1,8]{2,1,0:T(1,128)}, u32[]{:S(2)}) copy-start(s32[1,1,8]{2,1,0:T(1,128)} %param.14) | copy-start | bytes 100
  3.1 3.1 %copy-start.4 = (s32[1,1,8]{2,1,0:T(1,128)S(1)}, s32[1,1,8]{2,1,0:T(1,128)}, u32[]{:S(2)}) copy-start(s32[1,1,8]{2,1,0:T(1,128)} %param.10) | copy-start | bytes 100
  3.1 3.1 %copy-start.5 = (s32[1,1,8]{2,1,0:T(1,128)S(1)}, s32[1,1,8]{2,1,0:T(1,128)}, u32[]{:S(2)}) copy-start(s32[1,1,8]{2,1,0:T(1,128)} %param.11) | copy-start | bytes 100
  3.1 3.1 %copy-start.6 = (s32[1,1,8]{2,1,0:T(1,128)S(1)}, s32[1,1,8]{2,1,0:T(1,128)}, u32[]{:S(2)}) copy-start(s32[1,1,8]{2,1,0:T(1,128)} %param.13) | copy-start | bytes 100
  3.1 9.6 %collective-permute-start = (bf16[1040,128]{1,0:T(8,128)(2,1)}, bf16[1040,128]{1,0:T(8,128)(2,1)S(1)}, u32[]{:S(2)}, u32[]{:S(2)}) collective-permute-start(bf16[1040,128]{1,0:T(8,128)(2,1)} %take_tokens.1), channel_id=1, source_target_pairs={{0,4},{4,0},{1,5},{5,1},{2,6},{6,2},{3,7},{7,3},{8,12},{12,8},{9,1... | collective-permute-start | bytes 798728 | tf_op jit(solution)/shard_map/ppermute | solution.py:55
  6.2 1.2 %copy-start.3 = (bf16[128,4096]{1,0:T(8,128)(2,1)S(1)}, bf16[128,4096]{1,0:T(8,128)(2,1)}, u32[]{:S(2)}) copy-start(bf16[128,4096]{1,0:T(8,128)(2,1)} %grad_out.1) | copy-start | bytes 3145732
  11.4 7.9 %collective-permute-start.3 = (bf16[1040,128]{1,0:T(8,128)(2,1)S(1)}, bf16[1040,128]{1,0:T(8,128)(2,1)S(1)}, u32[]{:S(2)}, u32[]{:S(2)}) collective-permute-start(bf16[1040,128]{1,0:T(8,128)(2,1)S(1)} %get-tuple-element.45), channel_id=1, source_target_pairs={{0,4},{4,0},{1,5},{5,1},{2,6},{6,2},{3,7},{7,3},{8,12},{12,8},{9,1... | collective-permute-start | bytes 798728 | tf_op jit(solution)/shard_map/ppermute | solution.py:55
  13.3 6.0 %collective-permute-start.4 = (bf16[512,128]{1,0:T(8,128)(2,1)S(1)}, bf16[512,128]{1,0:T(8,128)(2,1)S(1)}, u32[]{:S(2)}, u32[]{:S(2)}) collective-permute-start(bf16[512,128]{1,0:T(8,128)(2,1)S(1)} %get-tuple-element.50), channel_id=1, source_target_pairs={{0,8},{8,0},{16,24},{24,16},{1,9},{9,1},{17,25},{25,17},{2,10},{10... | collective-permute-start | bytes 393224 | tf_op jit(solution)/shard_map/ppermute | solution.py:386
  15.5 7.0 %collective-permute-start.1 = (bf16[272,128]{1,0:T(8,128)(2,1)S(1)}, bf16[272,128]{1,0:T(8,128)(2,1)S(1)}, u32[]{:S(2)}, u32[]{:S(2)}) collective-permute-start(bf16[272,128]{1,0:T(8,128)(2,1)S(1)} %get-tuple-element.41), channel_id=1, source_target_pairs={{0,2},{1,3},{2,0},{3,1},{4,6},{5,7},{6,4},{7,5},{8,10},{9,11},{10,... | collective-permute-start | bytes 208904 | tf_op jit(solution)/shard_map/ppermute | solution.py:55
  17.1 5.4 %collective-permute-start.2 = (bf16[272,128]{1,0:T(8,128)(2,1)S(1)}, bf16[272,128]{1,0:T(8,128)(2,1)S(1)}, u32[]{:S(2)}, u32[]{:S(2)}) collective-permute-start(bf16[272,128]{1,0:T(8,128)(2,1)S(1)} %get-tuple-element.42), channel_id=1, source_target_pairs={{0,3},{1,2},{2,1},{3,0},{4,7},{5,6},{6,5},{7,4},{8,11},{9,10},{10,... | collective-permute-start | bytes 208904 | tf_op jit(solution)/shard_map/ppermute | solution.py:55
  19.9 12.2 %collective-permute-start.9 = (bf16[544,128]{1,0:T(8,128)(2,1)S(1)}, bf16[544,128]{1,0:T(8,128)(2,1)S(1)}, u32[]{:S(2)}, u32[]{:S(2)}) collective-permute-start(bf16[544,128]{1,0:T(8,128)(2,1)S(1)} %get-tuple-element.59), channel_id=1, source_target_pairs={{0,16},{8,24},{16,0},{24,8},{1,17},{9,25},{17,1},{25,9},{2,18},{10... | collective-permute-start | bytes 417800 | tf_op jit(solution)/shard_map/ppermute | solution.py:55
  22.6 6.2 %collective-permute-start.7 = (bf16[528,128]{1,0:T(8,128)(2,1)S(1)}, bf16[528,128]{1,0:T(8,128)(2,1)S(1)}, u32[]{:S(2)}, u32[]{:S(2)}) collective-permute-start(bf16[528,128]{1,0:T(8,128)(2,1)S(1)} %get-tuple-element.54), channel_id=1, source_target_pairs={{0,1},{1,0},{2,3},{3,2},{4,5},{5,4},{6,7},{7,6},{8,9},{9,8},{10,11... | collective-permute-start | bytes 405512 | tf_op jit(solution)/shard_map/ppermute | solution.py:55
  22.6 4.6 %collective-permute-start.5 = (bf16[256,128]{1,0:T(8,128)(2,1)S(1)}, bf16[256,128]{1,0:T(8,128)(2,1)S(1)}, u32[]{:S(2)}, u32[]{:S(2)}) collective-permute-start(bf16[256,128]{1,0:T(8,128)(2,1)S(1)} %pass_share.1), channel_id=1, source_target_pairs={{0,2},{1,3},{2,0},{3,1},{4,6},{5,7},{6,4},{7,5},{8,10},{9,11},{10,... | collective-permute-start | bytes 196616 | tf_op jit(solution)/shard_map/ppermute | solution.py:55
  24.2 4.6 %collective-permute-start.6 = (bf16[256,128]{1,0:T(8,128)(2,1)S(1)}, bf16[256,128]{1,0:T(8,128)(2,1)S(1)}, u32[]{:S(2)}, u32[]{:S(2)}) collective-permute-start(bf16[256,128]{1,0:T(8,128)(2,1)S(1)} %get-tuple-element.53), channel_id=1, source_target_pairs={{0,3},{1,2},{2,1},{3,0},{4,7},{5,6},{6,5},{7,4},{8,11},{9,10},{10,... | collective-permute-start | bytes 196616 | tf_op jit(solution)/shard_map/ppermute | solution.py:55
  24.5 6.7 %collective-permute-start.8 = (bf16[256,128]{1,0:T(8,128)(2,1)S(1)}, bf16[256,128]{1,0:T(8,128)(2,1)S(1)}, u32[]{:S(2)}, u32[]{:S(2)}) collective-permute-start(bf16[256,128]{1,0:T(8,128)(2,1)S(1)} %get-tuple-element.58), channel_id=1, source_target_pairs={{0,24},{8,16},{16,8},{24,0},{1,25},{9,17},{17,9},{25,1},{2,26},{10... | collective-permute-start | bytes 196616 | tf_op jit(solution)/shard_map/ppermute | solution.py:55
  27.2 4.9 %collective-permute-start.10 = (bf16[256,128]{1,0:T(8,128)(2,1)S(1)}, bf16[256,128]{1,0:T(8,128)(2,1)S(1)}, u32[]{:S(2)}, u32[]{:S(2)}) collective-permute-start(bf16[256,128]{1,0:T(8,128)(2,1)S(1)} %get-tuple-element.60), channel_id=1, source_target_pairs={{0,8},{8,0},{16,24},{24,16},{1,9},{9,1},{17,25},{25,17},{2,10},{10... | collective-permute-start | bytes 196616 | tf_op jit(solution)/shard_map/ppermute | solution.py:55

commit v12 on v11

--- a/solution.py
+++ b/solution.py
@@ -148,7 +148,6 @@
     row[...] = table_row((c0, c1, c2, c3), slots)
     hid[...] = jnp.zeros(hid.shape, f32)
     back[...] = jnp.zeros(back.shape, f32)
-    message[slots * rows :, :] = jnp.zeros((16, blk), bf16)
     for k in range(slots):
         copies[k].wait()
         value = dot(cot[k], w2[k], (1, 1))
@@ -258,22 +257,17 @@
         result[k] = sum(ref[here, :].astype(f32) for ref in parts)
 
 
-def halves(refs, count):
-    refs = list(refs)
-    second, first = refs[:count], refs[count:]
-    if len(refs) % 2 == 1:
-        joined = refs[-1]
-        rows = refs[count].shape[0]
-        first = refs[count:-1] + [joined.at[:rows]]
-        second = second + [joined.at[rows:]]
-    return second, first
+def halves(refs):
+    joined, refs = list(refs[: len(refs) % 2]), list(refs[len(refs) % 2 :])
+    count = len(refs) // 2
+    rows = refs[count].shape[0]
+    return refs[:count] + [j.at[rows:] for j in joined], refs[count:] + [j.at[:rows] for j in joined]
 
 
 def output_kernel(dims, *refs):
     slots, n_row, n_col, n_tok = dims
-    alone = max(1, n_col - 1)
-    count = 2 * alone + (n_col > 1)
-    outs, backs = halves(refs[:count], alone)
+    count = max(2, 2 * n_col - 1)
+    outs, backs = halves(refs[:count])
     refs = refs[count:]
     outputs, last, results, (acc_out, acc_in, sems) = refs[:2], refs[2], refs[3:5], refs[5:]
     blk, share = acc_out.shape[-1], acc_out.shape[1]
@@ -346,7 +340,7 @@
         cotangent_kernel,
         "take_cotangent",
         out_shape=(
-            message,
+            S((slots * rows, blk), bf16),
             S((slots, blk, rows), bf16),
             narrow,
             S((2 * slots, rows, blk), f32),
@@ -419,7 +413,8 @@
             in_specs=[VMEM] + [ANY] * len(o_parts[1:]),
             out_specs=VMEM,
         )(i_sent[2], *o_parts[1:])
-    i_parts = [send(i_sent[d], "col", d) for d in alone(n_col) + [1][: n_col - 1]]
+    i_parts = [send(i_sent[d], "col", d) for d in alone(n_col)]
+    joined = [send(i_sent[1], "col", 1)] if n_col > 1 else []
     tok_parts = [send(g_sent[d], "tok", d) for d in range(n_tok)]
 
     result = S((share, row_blocks * blk), bf16)
@@ -429,11 +424,11 @@
         functools.partial(output_kernel, dims),
         "add_outputs",
         out_shape=(result, result, S((8, LANES), jnp.int32)),
-        in_specs=[VMEM] * len(o_parts + i_parts),
+        in_specs=[VMEM] * len(joined + o_parts + i_parts),
         out_specs=(HBM, HBM, VMEM),
         scratch_shapes=[pltpu.VMEM(result.shape, bf16)] * 2
         + [acc, acc, pltpu.SemaphoreType.DMA((2,))],
-    )(*o_parts, *i_parts)
+    )(*joined, *o_parts, *i_parts)
     gw1, gw2 = call(
         grad_kernel,
         "add_grads",

time: 33 us -> 32.7 us (level)
  waiting for transfers between devices: 6.47 us -> 5.92 us
    ppermute x10, waiting for transfers between devices: 6.47 us -> 5.92 us  [send(): lax.ppermute(x, axis, [(i, partner(i, d, n)) for i in range(n)])]
  transfers between devices with their start and end apart: 11 -> 11, of which waited for: 5 -> 6; matrix products, arithmetic and copies ran while one was open for 0% -> 0% of each run, Pallas kernels for 20% -> 20%
where the time goes in v12:
time: 32.7 us; the launch traced here: 32.6 us
  starting transfers between devices  14.9 us (46%)
  Pallas kernels  9.72 us (30%)
  waiting for transfers between devices  5.92 us (18%)
  local copies, waits for them, and re-layouts  1.26 us (4%)
  between operations  0.78 us (2%)
    ppermute x10, starting transfers between devices, send(): lax.ppermute(x, axis, [(i, partner(i, d, n)) for i in range(n)])  13 us
    ppermute x10, waiting for transfers between devices, send(): lax.ppermute(x, axis, [(i, partner(i, d, n)) for i in range(n)])  5.92 us
    pallas_call x1, Pallas kernels, shards(): call(cotangent_kernel, 'take_cotangent', out_shape=(S((slots * rows, blk)...  3.96 us
    pallas_call x1, Pallas kernels, shards(): call(token_kernel, 'take_tokens', TAKE_LIMIT, out_shape=message, in_specs...  2.4 us
    ppermute x1, starting transfers between devices, shards(): half = lax.ppermute(half, 'tok', [(i, i ^ 1) for i in range(n_tok)])  1.89 us
    unnamed x16, local copies, waits for them, and re-layouts  1.26 us
    pallas_call x1, Pallas kernels, shards(): call(functools.partial(output_kernel, dims), 'add_outputs', out_shape=(re...  1.09 us
    pallas_call x1, Pallas kernels, shards(): call(grad_kernel, 'add_grads', out_shape=(summed, summed), in_specs=[ANY]...  0.74 us
  transfers between devices with their start and end apart: 11, of which 6 were waited for; matrix products, arithmetic and copies ran while one was open for 0% of the time, Pallas kernels for 20%

profile of v12, /device:TPU:0, one launch (start us, length us, event | category | flops | bytes accessed | tf_op | source)
XLA Modules:
  0.0 32.6 jit_solution(10963269084220968244)
XLA Ops:
  0.6 0.0 copy-start
  0.6 0.0 copy-start.1
  0.7 0.0 copy-start.2
  0.7 0.0 copy-start.7
  0.7 2.4 %take_tokens.1 = bf16[1040,128]{1,0:T(8,128)(2,1)} custom-call(s32[8]{0:T(128)} %bitcast.13, s32[8]{0:T(128)} %bitcast.15, s32[8]{0:T(128)} %bitcast.17, s32[8]{0:T(128)} %bitcast.19, bf16[128,4096]{1,0:T(8,128)(2,1)} %tokens.3, bf16[8,128,128]{2,1,0:T(8,128)(2,1)} %bitcast.8), custom_call_target="tpu_custom_call" | custom-call | flops 33554432 | bytes 524288 | tf_op jit(solution)/shard_map/take_tokens/pallas_call | solution.py:322
  3.1 0.0 copy-start.4
  3.1 0.0 copy-start.5
  3.1 0.0 copy-start.6
  3.1 3.0 %collective-permute-start = (bf16[1040,128]{1,0:T(8,128)(2,1)}, bf16[1040,128]{1,0:T(8,128)(2,1)S(1)}, u32[]{:S(2)}, u32[]{:S(2)}) collective-permute-start(bf16[1040,128]{1,0:T(8,128)(2,1)} %take_tokens.1), channel_id=1, source_target_pairs={{0,4},{4,0},{1,5},{5,1},{2,6},{6,2},{3,7},{7,3},{8,12},{12,8},{9,1... | collective-permute-start | bytes 798728 | tf_op jit(solution)/shard_map/ppermute | solution.py:55
  6.1 0.0 copy-done
  6.1 0.0 copy-done.1
  6.1 0.0 copy-done.2
  6.1 0.0 copy-done.7
  6.1 0.0 copy-done.4
  6.1 0.0 copy-done.5
  6.1 0.0 copy-done.6
  6.2 0.0 copy-start.3
  6.2 1.2 %copy-done.3 = bf16[128,4096]{1,0:T(8,128)(2,1)S(1)} copy-done((bf16[128,4096]{1,0:T(8,128)(2,1)S(1)}, bf16[128,4096]{1,0:T(8,128)(2,1)}, u32[]{:S(2)}) %copy-start.3) | copy-done | bytes 1048600
  7.4 4.0 %take_cotangent.1 = (bf16[1024,128]{1,0:T(8,128)(2,1)S(1)}, bf16[8,128,128]{2,1,0:T(8,128)(2,1)S(1)}, bf16[8,128,128]{2,1,0:T(8,128)(2,1)S(1)}, f32[16,128,128]{...) custom-call(s32[8]{0:T(128)S(1)} %bitcast.14, s32[8]{0:T(128)S(1)} %bitcast.16, ...), custom_call_target="tpu_custom_call" | custom-call | flops 33554432 | bytes 524288 | tf_op jit(solution)/shard_map/take_cotangent/pallas_call | solution.py:339
  11.4 0.6 %collective-permute-start.1 = (bf16[1024,128]{1,0:T(8,128)(2,1)S(1)}, bf16[1024,128]{1,0:T(8,128)(2,1)S(1)}, u32[]{:S(2)}, u32[]{:S(2)}) collective-permute-start(bf16[1024,128]{1,0:T(8,128)(2,1)S(1)} %get-tuple-element.39), channel_id=1, source_target_pairs={{0,4},{4,0},{1,5},{5,1},{2,6},{6,2},{3,7},{7,3},{8,12},{12,8},{9,1... | collective-permute-start | bytes 786440 | tf_op jit(solution)/shard_map/ppermute | solution.py:55
  12.0 0.8 %collective-permute-done.refs_0_ = bf16[1040,128]{1,0:T(8,128)(2,1)S(1)} collective-permute-done((bf16[1040,128]{1,0:T(8,128)(2,1)}, bf16[1040,128]{1,0:T(8,128)(2,1)S(1)}, u32[]{:S(2)}, u32[]{:S(2)}) %collective-permute-start) | collective-permute-done | bytes 266272 | tf_op jit(solution)/shard_map/ppermute | solution.py:55
  12.7 0.5 %hidden.1 = (bf16[8,128,128]{2,1,0:T(8,128)(2,1)S(1)}, f32[16,128,128]{2,1,0:T(8,128)S(1)}, s32[8,128]{1,0:T(8,128)S(1)}, f32[8,128,128]{2,1,0:T(8,128)S(1)}, bf16[512,128]{1,0:T(8,128)(2,1)S(1)}) custom-call(s32[24,128]{1,0:T(8,128)S(1)} %get-tuple-element.34.tab, f32[16,128,128]{2,1,0:T(8,128)S(1)} %get-tuple-element.35.own, ...), custom_call_target="tpu_custom_call" | custom-call | flops 33554432 | bytes 524288 | tf_op jit(solution)/shard_map/hidden/pallas_call | solution.py:366
  13.3 1.9 %collective-permute-start.2 = (bf16[512,128]{1,0:T(8,128)(2,1)S(1)}, bf16[512,128]{1,0:T(8,128)(2,1)S(1)}, u32[]{:S(2)}, u32[]{:S(2)}) collective-permute-start(bf16[512,128]{1,0:T(8,128)(2,1)S(1)} %get-tuple-element.47), channel_id=1, source_target_pairs={{0,8},{8,0},{16,24},{24,16},{1,9},{9,1},{17,25},{25,17},{2,10},{10... | collective-permute-start | bytes 393224 | tf_op jit(solution)/shard_map/ppermute | solution.py:380
  15.2 0.4 %slope.1 = (f32[8,128,128]{2,1,0:T(8,128)S(1)}, bf16[272,128]{1,0:T(8,128)(2,1)S(1)}, bf16[272,128]{1,0:T(8,128)(2,1)S(1)}, bf16[272,128]{1,0:T(8,128)(2,1)S(1)}, bf16[272,128]{1,0:T(8,128)(2,1)S(1)}) custom-call(s32[24,128]{1,0:T(8,128)S(1)} %get-tuple-element.34.tab, bf16[16,128]{1,0:T(8,128)(2,1)S(1)} %get-tuple-element.40.row, ...), custom_call_target="tpu_custom_call" | custom-call | flops 33554432 | bytes 524288 | tf_op jit(solution)/shard_map/slope/pallas_call | solution.py:382
  15.6 1.6 %collective-permute-start.4 = (bf16[272,128]{1,0:T(8,128)(2,1)S(1)}, bf16[272,128]{1,0:T(8,128)(2,1)S(1)}, u32[]{:S(2)}, u32[]{:S(2)}) collective-permute-start(bf16[272,128]{1,0:T(8,128)(2,1)S(1)} %get-tuple-element.50), channel_id=1, source_target_pairs={{0,2},{1,3},{2,0},{3,1},{4,6},{5,7},{6,4},{7,5},{8,10},{9,11},{10,... | collective-permute-start | bytes 208904 | tf_op jit(solution)/shard_map/ppermute | solution.py:55
  17.1 0.0 collective-permute-start.5
  17.1 2.1 %collective-permute-done.1.refs_0_ = bf16[1024,128]{1,0:T(8,128)(2,1)S(1)} collective-permute-done((bf16[1024,128]{1,0:T(8,128)(2,1)S(1)}, bf16[1024,128]{1,0:T(8,128)(2,1)S(1)}, u32[]{:S(2)}, u32[]{:S(2)}) %collective-permute-start.1) | collective-permute-done | bytes 262176 | tf_op jit(solution)/shard_map/ppermute | solution.py:55
  19.2 0.0 collective-permute-done.2.refs_6_
  19.2 0.6 %back.1 = (bf16[256,128]{1,0:T(8,128)(2,1)S(1)}, bf16[528,128]{1,0:T(8,128)(2,1)S(1)}, bf16[256,128]{1,0:T(8,128)(2,1)S(1)}, bf16[256,128]{1,0:T(8,128)(2,1)S(1)...) custom-call(s32[24,128]{1,0:T(8,128)S(1)} %get-tuple-element.34.tab,, ...), custom_call_target="tpu_custom_call" | custom-call | flops 33554432 | bytes 524288 | tf_op jit(solution)/shard_map/back/pallas_call | solution.py:395
  19.8 2.7 %collective-permute-start.9 = (bf16[544,128]{1,0:T(8,128)(2,1)S(1)}, bf16[544,128]{1,0:T(8,128)(2,1)S(1)}, u32[]{:S(2)}, u32[]{:S(2)}) collective-permute-start(bf16[544,128]{1,0:T(8,128)(2,1)S(1)} %get-tuple-element.59), channel_id=1, source_target_pairs={{0,16},{8,24},{16,0},{24,8},{1,17},{9,25},{17,1},{25,9},{2,18},{10... | collective-permute-start | bytes 417800 | tf_op jit(solution)/shard_map/ppermute | solution.py:55
  22.5 0.0 collective-permute-start.3
  22.5 1.6 %collective-permute-start.7 = (bf16[256,128]{1,0:T(8,128)(2,1)S(1)}, bf16[256,128]{1,0:T(8,128)(2,1)S(1)}, u32[]{:S(2)}, u32[]{:S(2)}) collective-permute-start(bf16[256,128]{1,0:T(8,128)(2,1)S(1)} %get-tuple-element.54), channel_id=1, source_target_pairs={{0,3},{1,2},{2,1},{3,0},{4,7},{5,6},{6,5},{7,4},{8,11},{9,10},{10,... | collective-permute-start | bytes 196616 | tf_op jit(solution)/shard_map/ppermute | solution.py:55
  24.1 0.0 collective-permute-done.4.refs_0_.refs_2_
  24.1 0.0 collective-permute-done.5.refs_1_.refs_3_
  24.1 0.6 %collective-permute-start.6 = (bf16[256,128]{1,0:T(8,128)(2,1)S(1)}, bf16[256,128]{1,0:T(8,128)(2,1)S(1)}, u32[]{:S(2)}, u32[]{:S(2)}) collective-permute-start(bf16[256,128]{1,0:T(8,128)(2,1)S(1)} %pass_share.1), channel_id=1, source_target_pairs={{0,2},{1,3},{2,0},{3,1},{4,6},{5,7},{6,4},{7,5},{8,10},{9,11},{10,... | collective-permute-start | bytes 196616 | tf_op jit(solution)/shard_map/ppermute | solution.py:55
  24.7 1.3 %collective-permute-start.8 = (bf16[256,128]{1,0:T(8,128)(2,1)S(1)}, bf16[256,128]{1,0:T(8,128)(2,1)S(1)}, u32[]{:S(2)}, u32[]{:S(2)}) collective-permute-start(bf16[256,128]{1,0:T(8,128)(2,1)S(1)} %get-tuple-element.58), channel_id=1, source_target_pairs={{0,24},{8,16},{16,8},{24,0},{1,25},{9,17},{17,9},{25,1},{2,26},{10... | collective-permute-start | bytes 196616 | tf_op jit(solution)/shard_map/ppermute | solution.py:55
  26.0 0.5 %collective-permute-done.7.refs_6_ = bf16[256,128]{1,0:T(8,128)(2,1)S(1)} collective-permute-done((bf16[256,128]{1,0:T(8,128)(2,1)S(1)}, bf16[256,128]{1,0:T(8,128)(2,1)S(1)}, u32[]{:S(2)}, u32[]{:S(2)}) %collective-permute-start.7) | collective-permute-done | bytes 65568 | tf_op jit(solution)/shard_map/ppermute | solution.py:55
  26.5 1.6 %collective-permute-start.10 = (bf16[256,128]{1,0:T(8,128)(2,1)S(1)}, bf16[256,128]{1,0:T(8,128)(2,1)S(1)}, u32[]{:S(2)}, u32[]{:S(2)}) collective-permute-start(bf16[256,128]{1,0:T(8,128)(2,1)S(1)} %get-tuple-element.60), channel_id=1, source_target_pairs={{0,8},{8,0},{16,24},{24,16},{1,9},{9,1},{17,25},{25,17},{2,10},{10... | collective-permute-start | bytes 196616 | tf_op jit(solution)/shard_map/ppermute | solution.py:55
  28.1 0.3 collective-permute-done.6.refs_5_
  28.4 0.0 collective-permute-done.3.refs_0_
  28.5 1.1 %add_outputs.1 = (bf16[32,4096]{1,0:T(8,128)(2,1)}, bf16[32,4096]{1,0:T(8,128)(2,1)}, s32[8,128]{1,0:T(8,128)S(1)}) custom-call(bf16[528,128]{1,0:T(8,128)(2,1)S(1)} %collective-permute-done.3.refs_0_, bf16[272,128]{1,0:T(8,128)(2,1)S(1)} %get-tuple-element.49.refs_1_, bf16[272,128]{1,0:T(8,128)(2,1)S(1)} %collective-permute-done.4.refs_0_.refs_2_, ...), custom_call_target="tpu_custom_call" | custom-call | flops 33554432 | bytes 524288 | tf_op jit(solution)/shard_map/add_outputs/pallas_call | solution.py:423
  29.6 1.5 %collective-permute-done.8.refs_0_ = bf16[256,128]{1,0:T(8,128)(2,1)S(1)} collective-permute-done((bf16[256,128]{1,0:T(8,128)(2,1)S(1)}, bf16[256,128]{1,0:T(8,128)(2,1)S(1)}, u32[]{:S(2)}, u32[]{:S(2)}) %collective-permute-start.8) | collective-permute-done | bytes 65568 | tf_op jit(solution)/shard_map/ppermute | solution.py:55
  31.0 0.8 %collective-permute-done.10.refs_2_ = bf16[256,128]{1,0:T(8,128)(2,1)S(1)} collective-permute-done((bf16[256,128]{1,0:T(8,128)(2,1)S(1)}, bf16[256,128]{1,0:T(8,128)(2,1)S(1)}, u32[]{:S(2)}, u32[]{:S(2)}) %collective-permute-start.10) | collective-permute-done | bytes 65568 | tf_op jit(solution)/shard_map/ppermute | solution.py:55
  31.8 0.0 collective-permute-done.9.refs_1_
  31.8 0.7 %add_grads.1 = (f32[8,32,128]{2,1,0:T(8,128)}, f32[8,32,128]{2,1,0:T(8,128)}) custom-call(s32[8,128]{1,0:T(8,128)S(1)} %get-tuple-element.57.after, bf16[256,128]{1,0:T(8,128)(2,1)S(1)} %collective-permute-done.8.refs_0_, bf16[544,128]{1,0:T(8,128)(2,1)S(1)} %collective-permute-done.9.refs_1_, bf16[256,128]{1,0:T(8,128)(2,1)S(1)} %collective-permute-done.10.refs_2_, ...), custom_call_target="tpu_custom_call" | custom-call | flops 33554432 | bytes 524288 | tf_op jit(solution)/shard_map/add_grads/pallas_call | solution.py:432
  (1 shorter events, 0.0 us)
Async XLA Ops:
  0.6 5.5 %copy-start = (bf16[128,4096]{1,0:T(8,128)(2,1)S(1)}, bf16[128,4096]{1,0:T(8,128)(2,1)}, u32[]{:S(2)}) copy-start(bf16[128,4096]{1,0:T(8,128)(2,1)} %tokens.3) | copy-start | bytes 3145732
  0.6 5.5 %copy-start.1 = (bf16[1,1,8,128,128]{4,3,2,1,0:T(8,128)(2,1)S(1)}, bf16[1,1,8,128,128]{4,3,2,1,0:T(8,128)(2,1)}, u32[]{:S(2)}) copy-start(bf16[1,1,8,128,128]{4,3,2,1,0:T(8,128)(2,1)} %param.9) | copy-start | bytes 786436
  0.7 5.5 %copy-start.2 = (bf16[1,1,8,128,128]{4,3,2,1,0:T(8,128)(2,1)S(1)}, bf16[1,1,8,128,128]{4,3,2,1,0:T(8,128)(2,1)}, u32[]{:S(2)}) copy-start(bf16[1,1,8,128,128]{4,3,2,1,0:T(8,128)(2,1)} %param.12) | copy-start | bytes 786436
  0.7 5.5 %copy-start.7 = (s32[1,1,8]{2,1,0:T(1,128)S(1)}, s32[1,1,8]{2,1,0:T(1,128)}, u32[]{:S(2)}) copy-start(s32[1,1,8]{2,1,0:T(1,128)} %param.14) | copy-start | bytes 100
  3.1 3.1 %copy-start.4 = (s32[1,1,8]{2,1,0:T(1,128)S(1)}, s32[1,1,8]{2,1,0:T(1,128)}, u32[]{:S(2)}) copy-start(s32[1,1,8]{2,1,0:T(1,128)} %param.10) | copy-start | bytes 100
  3.1 3.1 %copy-start.5 = (s32[1,1,8]{2,1,0:T(1,128)S(1)}, s32[1,1,8]{2,1,0:T(1,128)}, u32[]{:S(2)}) copy-start(s32[1,1,8]{2,1,0:T(1,128)} %param.11) | copy-start | bytes 100
  3.1 3.1 %copy-start.6 = (s32[1,1,8]{2,1,0:T(1,128)S(1)}, s32[1,1,8]{2,1,0:T(1,128)}, u32[]{:S(2)}) copy-start(s32[1,1,8]{2,1,0:T(1,128)} %param.13) | copy-start | bytes 100
  3.1 9.6 %collective-permute-start = (bf16[1040,128]{1,0:T(8,128)(2,1)}, bf16[1040,128]{1,0:T(8,128)(2,1)S(1)}, u32[]{:S(2)}, u32[]{:S(2)}) collective-permute-start(bf16[1040,128]{1,0:T(8,128)(2,1)} %take_tokens.1), channel_id=1, source_target_pairs={{0,4},{4,0},{1,5},{5,1},{2,6},{6,2},{3,7},{7,3},{8,12},{12,8},{9,1... | collective-permute-start | bytes 798728 | tf_op jit(solution)/shard_map/ppermute | solution.py:55
  6.2 1.2 %copy-start.3 = (bf16[128,4096]{1,0:T(8,128)(2,1)S(1)}, bf16[128,4096]{1,0:T(8,128)(2,1)}, u32[]{:S(2)}) copy-start(bf16[128,4096]{1,0:T(8,128)(2,1)} %grad_out.1) | copy-start | bytes 3145732
  11.4 7.8 %collective-permute-start.1 = (bf16[1024,128]{1,0:T(8,128)(2,1)S(1)}, bf16[1024,128]{1,0:T(8,128)(2,1)S(1)}, u32[]{:S(2)}, u32[]{:S(2)}) collective-permute-start(bf16[1024,128]{1,0:T(8,128)(2,1)S(1)} %get-tuple-element.39), channel_id=1, source_target_pairs={{0,4},{4,0},{1,5},{5,1},{2,6},{6,2},{3,7},{7,3},{8,12},{12,8},{9,1... | collective-permute-start | bytes 786440 | tf_op jit(solution)/shard_map/ppermute | solution.py:55
  13.3 5.9 %collective-permute-start.2 = (bf16[512,128]{1,0:T(8,128)(2,1)S(1)}, bf16[512,128]{1,0:T(8,128)(2,1)S(1)}, u32[]{:S(2)}, u32[]{:S(2)}) collective-permute-start(bf16[512,128]{1,0:T(8,128)(2,1)S(1)} %get-tuple-element.47), channel_id=1, source_target_pairs={{0,8},{8,0},{16,24},{24,16},{1,9},{9,1},{17,25},{25,17},{2,10},{10... | collective-permute-start | bytes 393224 | tf_op jit(solution)/shard_map/ppermute | solution.py:380
  15.6 8.6 %collective-permute-start.4 = (bf16[272,128]{1,0:T(8,128)(2,1)S(1)}, bf16[272,128]{1,0:T(8,128)(2,1)S(1)}, u32[]{:S(2)}, u32[]{:S(2)}) collective-permute-start(bf16[272,128]{1,0:T(8,128)(2,1)S(1)} %get-tuple-element.50), channel_id=1, source_target_pairs={{0,2},{1,3},{2,0},{3,1},{4,6},{5,7},{6,4},{7,5},{8,10},{9,11},{10,... | collective-permute-start | bytes 208904 | tf_op jit(solution)/shard_map/ppermute | solution.py:55
  17.1 7.0 %collective-permute-start.5 = (bf16[272,128]{1,0:T(8,128)(2,1)S(1)}, bf16[272,128]{1,0:T(8,128)(2,1)S(1)}, u32[]{:S(2)}, u32[]{:S(2)}) collective-permute-start(bf16[272,128]{1,0:T(8,128)(2,1)S(1)} %get-tuple-element.51), channel_id=1, source_target_pairs={{0,3},{1,2},{2,1},{3,0},{4,7},{5,6},{6,5},{7,4},{8,11},{9,10},{10,... | collective-permute-start | bytes 208904 | tf_op jit(solution)/shard_map/ppermute | solution.py:55
  19.8 12.0 %collective-permute-start.9 = (bf16[544,128]{1,0:T(8,128)(2,1)S(1)}, bf16[544,128]{1,0:T(8,128)(2,1)S(1)}, u32[]{:S(2)}, u32[]{:S(2)}) collective-permute-start(bf16[544,128]{1,0:T(8,128)(2,1)S(1)} %get-tuple-element.59), channel_id=1, source_target_pairs={{0,16},{8,24},{16,0},{24,8},{1,17},{9,25},{17,1},{25,9},{2,18},{10... | collective-permute-start | bytes 417800 | tf_op jit(solution)/shard_map/ppermute | solution.py:55
  22.5 6.0 %collective-permute-start.3 = (bf16[528,128]{1,0:T(8,128)(2,1)S(1)}, bf16[528,128]{1,0:T(8,128)(2,1)S(1)}, u32[]{:S(2)}, u32[]{:S(2)}) collective-permute-start(bf16[528,128]{1,0:T(8,128)(2,1)S(1)} %get-tuple-element.48), channel_id=1, source_target_pairs={{0,1},{1,0},{2,3},{3,2},{4,5},{5,4},{6,7},{7,6},{8,9},{9,8},{10,11... | collective-permute-start | bytes 405512 | tf_op jit(solution)/shard_map/ppermute | solution.py:55
  22.5 4.1 %collective-permute-start.7 = (bf16[256,128]{1,0:T(8,128)(2,1)S(1)}, bf16[256,128]{1,0:T(8,128)(2,1)S(1)}, u32[]{:S(2)}, u32[]{:S(2)}) collective-permute-start(bf16[256,128]{1,0:T(8,128)(2,1)S(1)} %get-tuple-element.54), channel_id=1, source_target_pairs={{0,3},{1,2},{2,1},{3,0},{4,7},{5,6},{6,5},{7,4},{8,11},{9,10},{10,... | collective-permute-start | bytes 196616 | tf_op jit(solution)/shard_map/ppermute | solution.py:55
  24.1 4.3 %collective-permute-start.6 = (bf16[256,128]{1,0:T(8,128)(2,1)S(1)}, bf16[256,128]{1,0:T(8,128)(2,1)S(1)}, u32[]{:S(2)}, u32[]{:S(2)}) collective-permute-start(bf16[256,128]{1,0:T(8,128)(2,1)S(1)} %pass_share.1), channel_id=1, source_target_pairs={{0,2},{1,3},{2,0},{3,1},{4,6},{5,7},{6,4},{7,5},{8,10},{9,11},{10,... | collective-permute-start | bytes 196616 | tf_op jit(solution)/shard_map/ppermute | solution.py:55
  24.7 6.3 %collective-permute-start.8 = (bf16[256,128]{1,0:T(8,128)(2,1)S(1)}, bf16[256,128]{1,0:T(8,128)(2,1)S(1)}, u32[]{:S(2)}, u32[]{:S(2)}) collective-permute-start(bf16[256,128]{1,0:T(8,128)(2,1)S(1)} %get-tuple-element.58), channel_id=1, source_target_pairs={{0,24},{8,16},{16,8},{24,0},{1,25},{9,17},{17,9},{25,1},{2,26},{10... | collective-permute-start | bytes 196616 | tf_op jit(solution)/shard_map/ppermute | solution.py:55
  26.5 5.3 %collective-permute-start.10 = (bf16[256,128]{1,0:T(8,128)(2,1)S(1)}, bf16[256,128]{1,0:T(8,128)(2,1)S(1)}, u32[]{:S(2)}, u32[]{:S(2)}) collective-permute-start(bf16[256,128]{1,0:T(8,128)(2,1)S(1)} %get-tuple-element.60), channel_id=1, source_target_pairs={{0,8},{8,0},{16,24},{24,16},{1,9},{9,1},{17,25},{25,17},{2,10},{10... | collective-permute-start | bytes 196616 | tf_op jit(solution)/shard_map/ppermute | solution.py:55

commit v13 on v12

--- a/solution.py
+++ b/solution.py
@@ -177,8 +177,8 @@
     slots, n_row, n_col, n_tok = dims
     peers, refs = refs[: n_row - 1], refs[n_row - 1 :]
     cot, active, hid, places, grad, half = refs
-    part = grad.shape[1] // n_tok
-    other = 1 - lax.rem(lax.axis_index("tok"), 2)
+    rows = half.shape[0] // slots
+    begin = pl.multiple_of((1 - lax.div(lax.axis_index("tok"), max(1, n_tok // 2))) * rows, rows)
     found = [places_of(tab, numbers(ref, slots * cot.shape[1]), slots) for ref in peers]
     places[...] = jnp.zeros(places.shape, jnp.int32)
     for i, place in enumerate(found):
@@ -191,10 +191,8 @@
         h = hid[firsts[k]]
         active[k] = (h * cdf(h)).astype(bf16)
         grad[k] = dot(active[k], cot[k], (0, 0))
-        for j in range(n_tok // 2):
-            begin = pl.multiple_of((2 * j + other) * part, part)
-            here = (j * slots + k) * part
-            half[here : here + part, :] = grad[k, pl.ds(begin, part), :].astype(bf16)
+        if n_tok > 1:
+            half[k * rows : (k + 1) * rows, :] = grad[k, pl.ds(begin, rows), :].astype(bf16)
 
 
 def slope_kernel(dims, tab, row, active, hid, w2, slope, *refs):
@@ -214,12 +212,10 @@
 def back_kernel(dims, tab, places, own, *refs):
     slots, n_row, n_col, n_tok = dims
     peers, refs = refs[: n_row - 1], refs[n_row - 1 :]
-    slope, w1, near, taken_t, grad2, half = refs[:6]
-    refs = refs[6:]
+    slope, w1, near, taken_t = refs[:4]
+    refs = refs[4:]
     outs, refs = refs[:n_col], refs[n_col:]
     grads, (acc, value, grad) = refs[:n_tok], refs[n_tok:]
-    part = grad.shape[1] // n_tok
-    paired = n_tok % 2 == 0
     found = [places[8 * i : 8 * i + 8] for i in range(len(peers))]
     at = [[place[0, W2_HID * slots + k] for k in range(slots)] for place in found]
     firsts = first_places(tab)
@@ -233,21 +229,28 @@
         cut(value.at[k], outs, k, "col")
     if n_col > 1:
         outs[1][outs[0].shape[0] :, :] = near[...]
-    for d in range(0, n_tok, 2 if paired else 1):
+    for ref in grads:
+        rows = slots * grad.shape[1] // n_tok
+        if ref.shape[0] > rows:
+            ref[rows:, :] = jnp.zeros((ref.shape[0] - rows, LANES), bf16)
+
+
+def join_kernel(dims, grad2, half, *refs):
+    slots, n_row, n_col, n_tok = dims
+    side = max(1, n_tok // 2)
+    part = grad2.shape[1] // n_tok
+    shares, joined = refs[:side], refs[-side:]
+    for d in range(side):
         to = target("tok", d)
         begin = pl.multiple_of(to * part, part)
+        size = shares[d].shape[0]
+        joined[d][:size, :] = shares[d][...]
         for k in range(slots):
             total = grad2[k, pl.ds(begin, part), :]
-            if paired:
-                there = pl.multiple_of((lax.div(to, 2) * slots + k) * part, part)
+            if n_tok > 1:
+                there = pl.multiple_of(k * side * part + lax.rem(to, side) * part, part)
                 total = total + half[pl.ds(there, part), :].astype(f32)
-            grads[d][(slots + k) * part : (slots + k + 1) * part, :] = total.astype(bf16)
-        spare = grads[d].shape[0] - 2 * slots * part
-        grads[d][2 * slots * part :, :] = jnp.zeros((spare, LANES), bf16)
-
-
-def pass_kernel(share, *refs):
-    refs[-1][...] = share[...]
+            joined[d][size + k * part : size + (k + 1) * part, :] = total.astype(bf16)
 
 
 def add_shares(parts, result, first):
@@ -264,24 +267,25 @@
     return refs[:count] + [j.at[rows:] for j in joined], refs[count:] + [j.at[:rows] for j in joined]
 
 
-def output_kernel(dims, *refs):
+def output_kernel(dims, sum1, sum2, *refs):
     slots, n_row, n_col, n_tok = dims
     count = max(2, 2 * n_col - 1)
     outs, backs = halves(refs[:count])
     refs = refs[count:]
-    outputs, last, results, (acc_out, acc_in, sems) = refs[:2], refs[2], refs[3:5], refs[5:]
+    outputs, gw1, gw2, results, (acc_out, acc_in, sems) = refs[:2], refs[2], refs[3], refs[4:6], refs[6:]
     blk, share = acc_out.shape[-1], acc_out.shape[1]
+    stores = [pltpu.make_async_copy(sum1, gw1, sems.at[2]), pltpu.make_async_copy(sum2, gw2, sems.at[3])]
+    for c in stores:
+        c.start()
     acc_out[...] = jnp.zeros(acc_out.shape, f32)
     acc_in[...] = jnp.zeros(acc_in.shape, f32)
     for out, back in zip(outs, backs):
         blocks = numbers(out, slots * share)
-        last[...] = blocks
         for k in range(slots):
             here = slice(k * share, (k + 1) * share)
             for ref, which, acc in ((out, W2_OUT, acc_out), (back, W1_ROW, acc_in)):
                 at = blocks[0, which * slots + k]
                 acc[at] = acc[at] + ref[here, :].astype(f32)
-    stores = []
     for i, acc in enumerate((acc_out, acc_in)):
         for b in range(acc.shape[0]):
             results[i][:, b * blk : (b + 1) * blk] = acc[b].astype(bf16)
@@ -291,12 +295,11 @@
         c.wait()
 
 
-def grad_kernel(after, *refs):
-    del after
+def grad_kernel(*refs):
     parts, gw1, gw2 = refs[:-2], refs[-2], refs[-1]
     slots, part, _ = gw1.shape
     add_shares(parts, gw1, 0)
-    add_shares([ref for ref in parts if ref.shape[0] > slots * part], gw2, slots)
+    add_shares([ref for ref in parts if ref.shape[0] == 2 * slots * part], gw2, slots)
 
 
 def alone(n):
@@ -359,9 +362,10 @@
     b_peers = [send(b_send, "row", d) for d in range(1, n_row)]
 
     single = S((slots * part, blk), bf16)
-    double = S((2 * slots * part + 32, blk), bf16)
-    grads = tuple(double if n_tok % 2 == 1 or d % 2 == 0 else single for d in range(n_tok))
-    half = S((max(1, n_tok // 2) * slots * part, blk), bf16)
+    side = max(1, n_tok // 2)
+    across = S((slots * part + 32, blk), bf16)
+    grads = tuple(single if d < side else across for d in range(n_tok))
+    half = S((slots * side * part, blk), bf16)
     peer_rows = 8 * max(1, n_row - 1)
     active, hid, places, grad2, half = call(
         functools.partial(hidden_kernel, dims),
@@ -376,8 +380,8 @@
         in_specs=[VMEM] * (n_row + 2),
         out_specs=(VMEM,) * 5,
     )(tab, hid, *p_peers, cot)
-    if n_tok % 2 == 0:
-        half = lax.ppermute(half, "tok", [(i, i ^ 1) for i in range(n_tok)])
+    if n_tok > 1:
+        half = lax.ppermute(half, "tok", [(i, (i + side) % n_tok) for i in range(n_tok)])
     out_share, back_share = S((slots * share + 16, blk), bf16), S((slots * share, blk), bf16)
     slope, *o_sent = call(
         functools.partial(slope_kernel, dims),
@@ -396,23 +400,23 @@
         functools.partial(back_kernel, dims),
         "back",
         out_shape=(*outs, *grads),
-        in_specs=[VMEM] * (n_row + 8),
+        in_specs=[VMEM] * (n_row + 6),
         out_specs=(VMEM,) * (n_col + n_tok),
         scratch_shapes=[
             pltpu.VMEM((slots, rows, blk), f32),
             pltpu.VMEM((slots, rows, blk), f32),
             pltpu.VMEM((slots, blk, blk), f32),
         ],
-    )(tab, places, back, *b_peers, slope, w1, o_sent[min(1, n_col - 1)], taken_t, grad2, half)
+    )(tab, places, back, *b_peers, slope, w1, o_sent[min(1, n_col - 1)], taken_t)
     i_sent, g_sent = list(sent[:n_col]), list(sent[n_col:])
-    if n_col > 2:
-        i_sent[2] = call(
-            pass_kernel,
-            "pass_share",
-            out_shape=back_share,
-            in_specs=[VMEM] + [ANY] * len(o_parts[1:]),
-            out_specs=VMEM,
-        )(i_sent[2], *o_parts[1:])
+    early = o_parts[1:]
+    g_sent[:side] = call(
+        functools.partial(join_kernel, dims),
+        "join_shares",
+        out_shape=(S((2 * slots * part, blk), bf16),) * side,
+        in_specs=[VMEM] * (2 + side) + [ANY] * len(early),
+        out_specs=(VMEM,) * side,
+    )(grad2, half, *g_sent[:side], *early)
     i_parts = [send(i_sent[d], "col", d) for d in alone(n_col)]
     joined = [send(i_sent[1], "col", 1)] if n_col > 1 else []
     tok_parts = [send(g_sent[d], "tok", d) for d in range(n_tok)]
@@ -420,22 +424,23 @@
     result = S((share, row_blocks * blk), bf16)
     summed = S((slots, part, blk), f32)
     acc = pltpu.VMEM((row_blocks, share, blk), f32)
-    output, grad_in, last = call(
-        functools.partial(output_kernel, dims),
-        "add_outputs",
-        out_shape=(result, result, S((8, LANES), jnp.int32)),
-        in_specs=[VMEM] * len(joined + o_parts + i_parts),
-        out_specs=(HBM, HBM, VMEM),
-        scratch_shapes=[pltpu.VMEM(result.shape, bf16)] * 2
-        + [acc, acc, pltpu.SemaphoreType.DMA((2,))],
-    )(*joined, *o_parts, *i_parts)
-    gw1, gw2 = call(
+    summed = S((slots, part, blk), f32)
+    sums = call(
         grad_kernel,
         "add_grads",
         out_shape=(summed, summed),
-        in_specs=[ANY] + [VMEM] * n_tok,
+        in_specs=[VMEM] * n_tok,
         out_specs=(VMEM,) * 2,
-    )(last, *tok_parts[::-1])
+    )(*tok_parts[::-1])
+    output, grad_in, gw1, gw2 = call(
+        functools.partial(output_kernel, dims),
+        "add_outputs",
+        out_shape=(result, result, summed, summed),
+        in_specs=[VMEM] * len([*sums, *joined, *o_parts, *i_parts]),
+        out_specs=(HBM,) * 4,
+        scratch_shapes=[pltpu.VMEM(result.shape, bf16)] * 2
+        + [acc, acc, pltpu.SemaphoreType.DMA((4,))],
+    )(*sums, *joined, *o_parts, *i_parts)
     return (output, grad_in, gw1.reshape(1, 1, slots, part, blk), gw2.reshape(1, 1, slots, part, blk))
 
 

time: 32.7 us -> 33.2 us (1.015)
  starting transfers between devices: 14.9 us -> 16.1 us
  Pallas kernels: 9.72 us -> 9.04 us
    ppermute x1, starting transfers between devices: 1.89 us -> 2.9 us  [shards(): lax.ppermute(half, 'tok', [(i, (i + side) % n_tok) for i in range(n_tok)])]
    pallas_call x2, Pallas kernels: 0.74 us -> 0.09 us  [the longest x1 0.05 us: shards(): call(grad_kernel, 'add_grads', out_shape=(summed, summed), in_specs=[VMEM...]
  transfers between devices with their start and end apart: 11 -> 11, of which waited for: 6 -> 4; matrix products, arithmetic and copies ran while one was open for 0% -> 0% of each run, Pallas kernels for 20% -> 17%
where the time goes in v13:
time: 33.2 us; the launch traced here: 33 us
  starting transfers between devices  16.1 us (48%)
  Pallas kernels  9.04 us (27%)
  waiting for transfers between devices  5.88 us (18%)
  local copies, waits for them, and re-layouts  1.26 us (4%)
  between operations  0.79 us (2%)
    ppermute x10, starting transfers between devices, send(): lax.ppermute(x, axis, [(i, partner(i, d, n)) for i in range(n)])  13.2 us
    ppermute x10, waiting for transfers between devices, send(): lax.ppermute(x, axis, [(i, partner(i, d, n)) for i in range(n)])  5.88 us
    pallas_call x1, Pallas kernels, shards(): call(cotangent_kernel, 'take_cotangent', out_shape=(S((slots * rows, blk)...  3.97 us
    ppermute x1, starting transfers between devices, shards(): lax.ppermute(half, 'tok', [(i, (i + side) % n_tok) for i in range(n_tok)])  2.9 us
    pallas_call x1, Pallas kernels, shards(): call(token_kernel, 'take_tokens', TAKE_LIMIT, out_shape=message, in_specs...  2.38 us
    unnamed x16, local copies, waits for them, and re-layouts  1.26 us
    pallas_call x1, Pallas kernels, shards(): call(functools.partial(output_kernel, dims), 'add_outputs', out_shape=(re...  1.12 us
  transfers between devices with their start and end apart: 11, of which 4 were waited for; matrix products, arithmetic and copies ran while one was open for 0% of the time, Pallas kernels for 17%

profile of v13, /device:TPU:0, one launch (start us, length us, event | category | flops | bytes accessed | tf_op | source)
XLA Modules:
  0.0 33.0 jit_solution(910448170219802582)
XLA Ops:
  0.6 0.0 copy-start
  0.6 0.0 copy-start.1
  0.7 0.0 copy-start.2
  0.7 0.0 copy-start.7
  0.7 2.4 %take_tokens.1 = bf16[1040,128]{1,0:T(8,128)(2,1)} custom-call(s32[8]{0:T(128)} %bitcast.13, s32[8]{0:T(128)} %bitcast.15, s32[8]{0:T(128)} %bitcast.17, s32[8]{0:T(128)} %bitcast.19, bf16[128,4096]{1,0:T(8,128)(2,1)} %tokens.3, bf16[8,128,128]{2,1,0:T(8,128)(2,1)} %bitcast.8), custom_call_target="tpu_custom_call" | custom-call | flops 33554432 | bytes 524288 | tf_op jit(solution)/shard_map/take_tokens/pallas_call | solution.py:325
  3.1 0.0 copy-start.4
  3.1 0.0 copy-start.5
  3.1 0.0 copy-start.6
  3.1 3.0 %collective-permute-start = (bf16[1040,128]{1,0:T(8,128)(2,1)}, bf16[1040,128]{1,0:T(8,128)(2,1)S(1)}, u32[]{:S(2)}, u32[]{:S(2)}) collective-permute-start(bf16[1040,128]{1,0:T(8,128)(2,1)} %take_tokens.1), channel_id=1, source_target_pairs={{0,4},{4,0},{1,5},{5,1},{2,6},{6,2},{3,7},{7,3},{8,12},{12,8},{9,1... | collective-permute-start | bytes 798728 | tf_op jit(solution)/shard_map/ppermute | solution.py:55
  6.1 0.0 copy-done
  6.1 0.0 copy-done.1
  6.1 0.0 copy-done.2
  6.1 0.0 copy-done.7
  6.1 0.0 copy-done.4
  6.1 0.0 copy-done.5
  6.1 0.0 copy-done.6
  6.1 0.0 copy-start.3
  6.2 1.2 %copy-done.3 = bf16[128,4096]{1,0:T(8,128)(2,1)S(1)} copy-done((bf16[128,4096]{1,0:T(8,128)(2,1)S(1)}, bf16[128,4096]{1,0:T(8,128)(2,1)}, u32[]{:S(2)}) %copy-start.3) | copy-done | bytes 1048600
  7.4 4.0 %take_cotangent.1 = (bf16[1024,128]{1,0:T(8,128)(2,1)S(1)}, bf16[8,128,128]{2,1,0:T(8,128)(2,1)S(1)}, bf16[8,128,128]{2,1,0:T(8,128)(2,1)S(1)}, f32[16,128,128]{...) custom-call(s32[8]{0:T(128)S(1)} %bitcast.14, s32[8]{0:T(128)S(1)} %bitcast.16, ...), custom_call_target="tpu_custom_call" | custom-call | flops 33554432 | bytes 524288 | tf_op jit(solution)/shard_map/take_cotangent/pallas_call | solution.py:342
  11.3 0.6 %collective-permute-start.1 = (bf16[1024,128]{1,0:T(8,128)(2,1)S(1)}, bf16[1024,128]{1,0:T(8,128)(2,1)S(1)}, u32[]{:S(2)}, u32[]{:S(2)}) collective-permute-start(bf16[1024,128]{1,0:T(8,128)(2,1)S(1)} %get-tuple-element.42), channel_id=1, source_target_pairs={{0,4},{4,0},{1,5},{5,1},{2,6},{6,2},{3,7},{7,3},{8,12},{12,8},{9,1... | collective-permute-start | bytes 786440 | tf_op jit(solution)/shard_map/ppermute | solution.py:55
  12.0 0.7 %collective-permute-done.refs_0_ = bf16[1040,128]{1,0:T(8,128)(2,1)S(1)} collective-permute-done((bf16[1040,128]{1,0:T(8,128)(2,1)}, bf16[1040,128]{1,0:T(8,128)(2,1)S(1)}, u32[]{:S(2)}, u32[]{:S(2)}) %collective-permute-start) | collective-permute-done | bytes 266272 | tf_op jit(solution)/shard_map/ppermute | solution.py:55
  12.7 0.5 %hidden.1 = (bf16[8,128,128]{2,1,0:T(8,128)(2,1)S(1)}, f32[16,128,128]{2,1,0:T(8,128)S(1)}, s32[8,128]{1,0:T(8,128)S(1)}, f32[8,128,128]{2,1,0:T(8,128)S(1)}, bf16[512,128]{1,0:T(8,128)(2,1)S(1)}) custom-call(s32[24,128]{1,0:T(8,128)S(1)} %get-tuple-element.37.tab, f32[16,128,128]{2,1,0:T(8,128)S(1)} %get-tuple-element.38.own, ...), custom_call_target="tpu_custom_call" | custom-call | flops 33554432 | bytes 524288 | tf_op jit(solution)/shard_map/hidden/pallas_call | solution.py:370
  13.2 2.9 %collective-permute-start.4 = (bf16[512,128]{1,0:T(8,128)(2,1)S(1)}, bf16[512,128]{1,0:T(8,128)(2,1)S(1)}, u32[]{:S(2)}, u32[]{:S(2)}) collective-permute-start(bf16[512,128]{1,0:T(8,128)(2,1)S(1)} %get-tuple-element.52), channel_id=1, source_target_pairs={{0,16},{8,24},{16,0},{24,8},{1,17},{9,25},{17,1},{25,9},{2,18},{10... | collective-permute-start | bytes 393224 | tf_op jit(solution)/shard_map/ppermute | solution.py:384
  16.1 0.4 %slope.1 = (f32[8,128,128]{2,1,0:T(8,128)S(1)}, bf16[272,128]{1,0:T(8,128)(2,1)S(1)}, bf16[272,128]{1,0:T(8,128)(2,1)S(1)}, bf16[272,128]{1,0:T(8,128)(2,1)S(1)}, bf16[272,128]{1,0:T(8,128)(2,1)S(1)}) custom-call(s32[24,128]{1,0:T(8,128)S(1)} %get-tuple-element.37.tab, bf16[16,128]{1,0:T(8,128)(2,1)S(1)} %get-tuple-element.43.row, ...), custom_call_target="tpu_custom_call" | custom-call | flops 33554432 | bytes 524288 | tf_op jit(solution)/shard_map/slope/pallas_call | solution.py:386
  16.5 1.6 %collective-permute-start.5 = (bf16[272,128]{1,0:T(8,128)(2,1)S(1)}, bf16[272,128]{1,0:T(8,128)(2,1)S(1)}, u32[]{:S(2)}, u32[]{:S(2)}) collective-permute-start(bf16[272,128]{1,0:T(8,128)(2,1)S(1)} %get-tuple-element.55), channel_id=1, source_target_pairs={{0,2},{1,3},{2,0},{3,1},{4,6},{5,7},{6,4},{7,5},{8,10},{9,11},{10,... | collective-permute-start | bytes 208904 | tf_op jit(solution)/shard_map/ppermute | solution.py:55
  18.1 0.0 collective-permute-start.6
  18.1 1.0 %collective-permute-done.1.refs_0_ = bf16[1024,128]{1,0:T(8,128)(2,1)S(1)} collective-permute-done((bf16[1024,128]{1,0:T(8,128)(2,1)S(1)}, bf16[1024,128]{1,0:T(8,128)(2,1)S(1)}, u32[]{:S(2)}, u32[]{:S(2)}) %collective-permute-start.1) | collective-permute-done | bytes 262176 | tf_op jit(solution)/shard_map/ppermute | solution.py:55
  19.2 0.6 %back.1 = (bf16[256,128]{1,0:T(8,128)(2,1)S(1)}, bf16[528,128]{1,0:T(8,128)(2,1)S(1)}, bf16[256,128]{1,0:T(8,128)(2,1)S(1)}, bf16[256,128]{1,0:T(8,128)(2,1)S(1)...) custom-call(s32[24,128]{1,0:T(8,128)S(1)} %get-tuple-element.37.tab,, ...), custom_call_target="tpu_custom_call" | custom-call | flops 33554432 | bytes 524288 | tf_op jit(solution)/shard_map/back/pallas_call | solution.py:399
  19.8 3.7 %collective-permute-start.2 = (bf16[288,128]{1,0:T(8,128)(2,1)S(1)}, bf16[288,128]{1,0:T(8,128)(2,1)S(1)}, u32[]{:S(2)}, u32[]{:S(2)}) collective-permute-start(bf16[288,128]{1,0:T(8,128)(2,1)S(1)} %get-tuple-element.49), channel_id=1, source_target_pairs={{0,24},{8,16},{16,8},{24,0},{1,25},{9,17},{17,9},{25,1},{2,26},{10... | collective-permute-start | bytes 221192 | tf_op jit(solution)/shard_map/ppermute | solution.py:55
  23.4 0.0 collective-permute-start.8
  23.4 0.0 collective-permute-done.5.refs_2_
  23.5 0.0 collective-permute-done.6.refs_3_
  23.5 0.0 collective-permute-done.4.half
  23.5 0.6 %collective-permute-start.7 = (bf16[512,128]{1,0:T(8,128)(2,1)S(1)}, bf16[512,128]{1,0:T(8,128)(2,1)S(1)}, u32[]{:S(2)}, u32[]{:S(2)}) collective-permute-start(bf16[512,128]{1,0:T(8,128)(2,1)S(1)} %get-tuple-element.57), channel_id=1, source_target_pairs={{0,8},{8,0},{16,24},{24,16},{1,9},{9,1},{17,25},{25,17},{2,10},{10... | collective-permute-start | bytes 393224 | tf_op jit(solution)/shard_map/ppermute | solution.py:55
  24.1 2.1 %collective-permute-start.3 = (bf16[288,128]{1,0:T(8,128)(2,1)S(1)}, bf16[288,128]{1,0:T(8,128)(2,1)S(1)}, u32[]{:S(2)}, u32[]{:S(2)}) collective-permute-start(bf16[288,128]{1,0:T(8,128)(2,1)S(1)} %get-tuple-element.50), channel_id=1, source_target_pairs={{0,16},{8,24},{16,0},{24,8},{1,17},{9,25},{17,1},{25,9},{2,18},{10... | collective-permute-start | bytes 221192 | tf_op jit(solution)/shard_map/ppermute | solution.py:55
  26.2 1.5 %collective-permute-start.9 = (bf16[256,128]{1,0:T(8,128)(2,1)S(1)}, bf16[256,128]{1,0:T(8,128)(2,1)S(1)}, u32[]{:S(2)}, u32[]{:S(2)}) collective-permute-start(bf16[256,128]{1,0:T(8,128)(2,1)S(1)} %get-tuple-element.64), channel_id=1, source_target_pairs={{0,2},{1,3},{2,0},{3,1},{4,6},{5,7},{6,4},{7,5},{8,10},{9,11},{10,... | collective-permute-start | bytes 196616 | tf_op jit(solution)/shard_map/ppermute | solution.py:55
  27.8 0.0 collective-permute-done.2.refs_0_
  27.8 0.0 collective-permute-start.10
  27.8 3.3 %collective-permute-done.3.refs_1_ = bf16[288,128]{1,0:T(8,128)(2,1)S(1)} collective-permute-done((bf16[288,128]{1,0:T(8,128)(2,1)S(1)}, bf16[288,128]{1,0:T(8,128)(2,1)S(1)}, u32[]{:S(2)}, u32[]{:S(2)}) %collective-permute-start.3) | collective-permute-done | bytes 73760 | tf_op jit(solution)/shard_map/ppermute | solution.py:55
  31.0 0.0 collective-permute-done.7.refs_2_
  31.1 0.0 collective-permute-done.9.refs_5_
  31.1 0.8 %collective-permute-done.10.refs_6_ = bf16[256,128]{1,0:T(8,128)(2,1)S(1)} collective-permute-done((bf16[256,128]{1,0:T(8,128)(2,1)S(1)}, bf16[256,128]{1,0:T(8,128)(2,1)S(1)}, u32[]{:S(2)}, u32[]{:S(2)}) %collective-permute-start.10) | collective-permute-done | bytes 65568 | tf_op jit(solution)/shard_map/ppermute | solution.py:55
  31.9 0.0 collective-permute-done.8.refs_0_
  31.9 1.1 %add_outputs.1 = (bf16[32,4096]{1,0:T(8,128)(2,1)}, bf16[32,4096]{1,0:T(8,128)(2,1)}, f32[8,32,128]{2,1,0:T(8,128)}, f32[8,32,128]{2,1,0:T(8,128)}) custom-call(f32[8,32,128]{2,1,0:T(8,128)S(1)} %get-tuple-element.59.sum1, f32[8,32,128]{2,1,0:T(8,128)S(1)} %get-tuple-element.60.sum2, bf16[528,128]{1,0:T(8,128)(2,1)S(1)} %collective-permute-done.8.refs_0_, ...), custom_call_target="tpu_custom_call" | custom-call | flops 33554432 | bytes 524288 | tf_op jit(solution)/shard_map/add_outputs/pallas_call | solution.py:435
  (2 shorter events, 0.1 us)
Async XLA Ops:
  0.6 5.5 %copy-start = (bf16[128,4096]{1,0:T(8,128)(2,1)S(1)}, bf16[128,4096]{1,0:T(8,128)(2,1)}, u32[]{:S(2)}) copy-start(bf16[128,4096]{1,0:T(8,128)(2,1)} %tokens.3) | copy-start | bytes 3145732
  0.6 5.5 %copy-start.1 = (bf16[1,1,8,128,128]{4,3,2,1,0:T(8,128)(2,1)S(1)}, bf16[1,1,8,128,128]{4,3,2,1,0:T(8,128)(2,1)}, u32[]{:S(2)}) copy-start(bf16[1,1,8,128,128]{4,3,2,1,0:T(8,128)(2,1)} %param.9) | copy-start | bytes 786436
  0.7 5.5 %copy-start.2 = (bf16[1,1,8,128,128]{4,3,2,1,0:T(8,128)(2,1)S(1)}, bf16[1,1,8,128,128]{4,3,2,1,0:T(8,128)(2,1)}, u32[]{:S(2)}) copy-start(bf16[1,1,8,128,128]{4,3,2,1,0:T(8,128)(2,1)} %param.12) | copy-start | bytes 786436
  0.7 5.4 %copy-start.7 = (s32[1,1,8]{2,1,0:T(1,128)S(1)}, s32[1,1,8]{2,1,0:T(1,128)}, u32[]{:S(2)}) copy-start(s32[1,1,8]{2,1,0:T(1,128)} %param.14) | copy-start | bytes 100
  3.1 3.1 %copy-start.4 = (s32[1,1,8]{2,1,0:T(1,128)S(1)}, s32[1,1,8]{2,1,0:T(1,128)}, u32[]{:S(2)}) copy-start(s32[1,1,8]{2,1,0:T(1,128)} %param.10) | copy-start | bytes 100
  3.1 3.1 %copy-start.5 = (s32[1,1,8]{2,1,0:T(1,128)S(1)}, s32[1,1,8]{2,1,0:T(1,128)}, u32[]{:S(2)}) copy-start(s32[1,1,8]{2,1,0:T(1,128)} %param.11) | copy-start | bytes 100
  3.1 3.1 %copy-start.6 = (s32[1,1,8]{2,1,0:T(1,128)S(1)}, s32[1,1,8]{2,1,0:T(1,128)}, u32[]{:S(2)}) copy-start(s32[1,1,8]{2,1,0:T(1,128)} %param.13) | copy-start | bytes 100
  3.1 9.6 %collective-permute-start = (bf16[1040,128]{1,0:T(8,128)(2,1)}, bf16[1040,128]{1,0:T(8,128)(2,1)S(1)}, u32[]{:S(2)}, u32[]{:S(2)}) collective-permute-start(bf16[1040,128]{1,0:T(8,128)(2,1)} %take_tokens.1), channel_id=1, source_target_pairs={{0,4},{4,0},{1,5},{5,1},{2,6},{6,2},{3,7},{7,3},{8,12},{12,8},{9,1... | collective-permute-start | bytes 798728 | tf_op jit(solution)/shard_map/ppermute | solution.py:55
  6.1 1.2 %copy-start.3 = (bf16[128,4096]{1,0:T(8,128)(2,1)S(1)}, bf16[128,4096]{1,0:T(8,128)(2,1)}, u32[]{:S(2)}) copy-start(bf16[128,4096]{1,0:T(8,128)(2,1)} %grad_out.1) | copy-start | bytes 3145732
  11.3 7.8 %collective-permute-start.1 = (bf16[1024,128]{1,0:T(8,128)(2,1)S(1)}, bf16[1024,128]{1,0:T(8,128)(2,1)S(1)}, u32[]{:S(2)}, u32[]{:S(2)}) collective-permute-start(bf16[1024,128]{1,0:T(8,128)(2,1)S(1)} %get-tuple-element.42), channel_id=1, source_target_pairs={{0,4},{4,0},{1,5},{5,1},{2,6},{6,2},{3,7},{7,3},{8,12},{12,8},{9,1... | collective-permute-start | bytes 786440 | tf_op jit(solution)/shard_map/ppermute | solution.py:55
  13.2 10.2 %collective-permute-start.4 = (bf16[512,128]{1,0:T(8,128)(2,1)S(1)}, bf16[512,128]{1,0:T(8,128)(2,1)S(1)}, u32[]{:S(2)}, u32[]{:S(2)}) collective-permute-start(bf16[512,128]{1,0:T(8,128)(2,1)S(1)} %get-tuple-element.52), channel_id=1, source_target_pairs={{0,16},{8,24},{16,0},{24,8},{1,17},{9,25},{17,1},{25,9},{2,18},{10... | collective-permute-start | bytes 393224 | tf_op jit(solution)/shard_map/ppermute | solution.py:384
  16.5 6.9 %collective-permute-start.5 = (bf16[272,128]{1,0:T(8,128)(2,1)S(1)}, bf16[272,128]{1,0:T(8,128)(2,1)S(1)}, u32[]{:S(2)}, u32[]{:S(2)}) collective-permute-start(bf16[272,128]{1,0:T(8,128)(2,1)S(1)} %get-tuple-element.55), channel_id=1, source_target_pairs={{0,2},{1,3},{2,0},{3,1},{4,6},{5,7},{6,4},{7,5},{8,10},{9,11},{10,... | collective-permute-start | bytes 208904 | tf_op jit(solution)/shard_map/ppermute | solution.py:55
  18.1 5.3 %collective-permute-start.6 = (bf16[272,128]{1,0:T(8,128)(2,1)S(1)}, bf16[272,128]{1,0:T(8,128)(2,1)S(1)}, u32[]{:S(2)}, u32[]{:S(2)}) collective-permute-start(bf16[272,128]{1,0:T(8,128)(2,1)S(1)} %get-tuple-element.56), channel_id=1, source_target_pairs={{0,3},{1,2},{2,1},{3,0},{4,7},{5,6},{6,5},{7,4},{8,11},{9,10},{10,... | collective-permute-start | bytes 208904 | tf_op jit(solution)/shard_map/ppermute | solution.py:55
  19.8 8.0 %collective-permute-start.2 = (bf16[288,128]{1,0:T(8,128)(2,1)S(1)}, bf16[288,128]{1,0:T(8,128)(2,1)S(1)}, u32[]{:S(2)}, u32[]{:S(2)}) collective-permute-start(bf16[288,128]{1,0:T(8,128)(2,1)S(1)} %get-tuple-element.49), channel_id=1, source_target_pairs={{0,24},{8,16},{16,8},{24,0},{1,25},{9,17},{17,9},{25,1},{2,26},{10... | collective-permute-start | bytes 221192 | tf_op jit(solution)/shard_map/ppermute | solution.py:55
  23.4 8.5 %collective-permute-start.8 = (bf16[528,128]{1,0:T(8,128)(2,1)S(1)}, bf16[528,128]{1,0:T(8,128)(2,1)S(1)}, u32[]{:S(2)}, u32[]{:S(2)}) collective-permute-start(bf16[528,128]{1,0:T(8,128)(2,1)S(1)} %get-tuple-element.61), channel_id=1, source_target_pairs={{0,1},{1,0},{2,3},{3,2},{4,5},{5,4},{6,7},{7,6},{8,9},{9,8},{10,11... | collective-permute-start | bytes 405512 | tf_op jit(solution)/shard_map/ppermute | solution.py:55
  23.5 7.5 %collective-permute-start.7 = (bf16[512,128]{1,0:T(8,128)(2,1)S(1)}, bf16[512,128]{1,0:T(8,128)(2,1)S(1)}, u32[]{:S(2)}, u32[]{:S(2)}) collective-permute-start(bf16[512,128]{1,0:T(8,128)(2,1)S(1)} %get-tuple-element.57), channel_id=1, source_target_pairs={{0,8},{8,0},{16,24},{24,16},{1,9},{9,1},{17,25},{25,17},{2,10},{10... | collective-permute-start | bytes 393224 | tf_op jit(solution)/shard_map/ppermute | solution.py:55
  24.1 6.9 %collective-permute-start.3 = (bf16[288,128]{1,0:T(8,128)(2,1)S(1)}, bf16[288,128]{1,0:T(8,128)(2,1)S(1)}, u32[]{:S(2)}, u32[]{:S(2)}) collective-permute-start(bf16[288,128]{1,0:T(8,128)(2,1)S(1)} %get-tuple-element.50), channel_id=1, source_target_pairs={{0,16},{8,24},{16,0},{24,8},{1,17},{9,25},{17,1},{25,9},{2,18},{10... | collective-permute-start | bytes 221192 | tf_op jit(solution)/shard_map/ppermute | solution.py:55
  26.2 4.9 %collective-permute-start.9 = (bf16[256,128]{1,0:T(8,128)(2,1)S(1)}, bf16[256,128]{1,0:T(8,128)(2,1)S(1)}, u32[]{:S(2)}, u32[]{:S(2)}) collective-permute-start(bf16[256,128]{1,0:T(8,128)(2,1)S(1)} %get-tuple-element.64), channel_id=1, source_target_pairs={{0,2},{1,3},{2,0},{3,1},{4,6},{5,7},{6,4},{7,5},{8,10},{9,11},{10,... | collective-permute-start | bytes 196616 | tf_op jit(solution)/shard_map/ppermute | solution.py:55
  27.8 4.1 %collective-permute-start.10 = (bf16[256,128]{1,0:T(8,128)(2,1)S(1)}, bf16[256,128]{1,0:T(8,128)(2,1)S(1)}, u32[]{:S(2)}, u32[]{:S(2)}) collective-permute-start(bf16[256,128]{1,0:T(8,128)(2,1)S(1)} %get-tuple-element.65), channel_id=1, source_target_pairs={{0,3},{1,2},{2,1},{3,0},{4,7},{5,6},{6,5},{7,4},{8,11},{9,10},{10,... | collective-permute-start | bytes 196616 | tf_op jit(solution)/shard_map/ppermute | solution.py:55

commit v14 on v13

--- a/solution.py
+++ b/solution.py
@@ -212,8 +212,8 @@
 def back_kernel(dims, tab, places, own, *refs):
     slots, n_row, n_col, n_tok = dims
     peers, refs = refs[: n_row - 1], refs[n_row - 1 :]
-    slope, w1, near, taken_t = refs[:4]
-    refs = refs[4:]
+    slope, w1, taken_t = refs[:3]
+    refs = refs[3:]
     outs, refs = refs[:n_col], refs[n_col:]
     grads, (acc, value, grad) = refs[:n_tok], refs[n_tok:]
     found = [places[8 * i : 8 * i + 8] for i in range(len(peers))]
@@ -227,8 +227,6 @@
         cut(grad.at[k], grads, k, "tok")
         value[k] = dot(g, w1[k], (1, 1))
         cut(value.at[k], outs, k, "col")
-    if n_col > 1:
-        outs[1][outs[0].shape[0] :, :] = near[...]
     for ref in grads:
         rows = slots * grad.shape[1] // n_tok
         if ref.shape[0] > rows:
@@ -260,18 +258,9 @@
         result[k] = sum(ref[here, :].astype(f32) for ref in parts)
 
 
-def halves(refs):
-    joined, refs = list(refs[: len(refs) % 2]), list(refs[len(refs) % 2 :])
-    count = len(refs) // 2
-    rows = refs[count].shape[0]
-    return refs[:count] + [j.at[rows:] for j in joined], refs[count:] + [j.at[:rows] for j in joined]
-
-
 def output_kernel(dims, sum1, sum2, *refs):
     slots, n_row, n_col, n_tok = dims
-    count = max(2, 2 * n_col - 1)
-    outs, backs = halves(refs[:count])
-    refs = refs[count:]
+    outs, backs, refs = refs[:n_col], refs[n_col : 2 * n_col], refs[2 * n_col :]
     outputs, gw1, gw2, results, (acc_out, acc_in, sems) = refs[:2], refs[2], refs[3], refs[4:6], refs[6:]
     blk, share = acc_out.shape[-1], acc_out.shape[1]
     stores = [pltpu.make_async_copy(sum1, gw1, sems.at[2]), pltpu.make_async_copy(sum2, gw2, sems.at[3])]
@@ -302,8 +291,8 @@
     add_shares([ref for ref in parts if ref.shape[0] == 2 * slots * part], gw2, slots)
 
 
-def alone(n):
-    return [0] + list(range(2, n))
+def near_last(n):
+    return [0] + list(range(2, n)) + [1][: n - 1]
 
 
 def shards(tokens, w1_blocks, w1_rows, w1_cols, w2_blocks, w2_hidden, w2_outs, grad_out):
@@ -391,23 +380,20 @@
         out_specs=(VMEM,) * (1 + n_col),
         scratch_shapes=[pltpu.VMEM((slots, rows, blk), f32)],
     )(tab, row, active, hid, w2)
-    o_parts = [send(o_sent[d], "col", d) for d in alone(n_col)]
-
-    outs = [back_share] * n_col
-    if n_col > 1:
-        outs[1] = S((2 * slots * share + 16, blk), bf16)
+    o_parts = [send(o_sent[d], "col", d) for d in near_last(n_col)]
+
     sent = call(
         functools.partial(back_kernel, dims),
         "back",
-        out_shape=(*outs, *grads),
-        in_specs=[VMEM] * (n_row + 6),
+        out_shape=(back_share,) * n_col + grads,
+        in_specs=[VMEM] * (n_row + 5),
         out_specs=(VMEM,) * (n_col + n_tok),
         scratch_shapes=[
             pltpu.VMEM((slots, rows, blk), f32),
             pltpu.VMEM((slots, rows, blk), f32),
             pltpu.VMEM((slots, blk, blk), f32),
         ],
-    )(tab, places, back, *b_peers, slope, w1, o_sent[min(1, n_col - 1)], taken_t)
+    )(tab, places, back, *b_peers, slope, w1, taken_t)
     i_sent, g_sent = list(sent[:n_col]), list(sent[n_col:])
     early = o_parts[1:]
     g_sent[:side] = call(
@@ -417,8 +403,7 @@
         in_specs=[VMEM] * (2 + side) + [ANY] * len(early),
         out_specs=(VMEM,) * side,
     )(grad2, half, *g_sent[:side], *early)
-    i_parts = [send(i_sent[d], "col", d) for d in alone(n_col)]
-    joined = [send(i_sent[1], "col", 1)] if n_col > 1 else []
+    i_parts = [send(i_sent[d], "col", d) for d in near_last(n_col)]
     tok_parts = [send(g_sent[d], "tok", d) for d in range(n_tok)]
 
     result = S((share, row_blocks * blk), bf16)
@@ -431,16 +416,16 @@
         out_shape=(summed, summed),
         in_specs=[VMEM] * n_tok,
         out_specs=(VMEM,) * 2,
-    )(*tok_parts[::-1])
+    )(*tok_parts[:1], *tok_parts[2:], *tok_parts[1:2])
     output, grad_in, gw1, gw2 = call(
         functools.partial(output_kernel, dims),
         "add_outputs",
         out_shape=(result, result, summed, summed),
-        in_specs=[VMEM] * len([*sums, *joined, *o_parts, *i_parts]),
+        in_specs=[VMEM] * len([*sums, *o_parts, *i_parts]),
         out_specs=(HBM,) * 4,
         scratch_shapes=[pltpu.VMEM(result.shape, bf16)] * 2
         + [acc, acc, pltpu.SemaphoreType.DMA((4,))],
-    )(*sums, *joined, *o_parts, *i_parts)
+    )(*sums, *o_parts, *i_parts)
     return (output, grad_in, gw1.reshape(1, 1, slots, part, blk), gw2.reshape(1, 1, slots, part, blk))
 
 

time: 33.2 us -> 32.3 us (0.973)
  waiting for transfers between devices: 5.88 us -> 4.68 us
    ppermute x10 -> x11, waiting for transfers between devices: 5.88 us -> 4.67 us  [send(): lax.ppermute(x, axis, [(i, partner(i, d, n)) for i in range(n)])]
    ppermute x10 -> x11, starting transfers between devices: 13.2 us -> 13.4 us  [send(): lax.ppermute(x, axis, [(i, partner(i, d, n)) for i in range(n)])]
  transfers between devices with their start and end apart: 11 -> 12, of which waited for: 4 -> 4; matrix products, arithmetic and copies ran while one was open for 0% -> 0% of each run, Pallas kernels for 17% -> 17%
where the time goes in v14:
time: 32.3 us; the launch traced here: 32.1 us
  starting transfers between devices  16.3 us (50%)
  Pallas kernels  9.05 us (28%)
  waiting for transfers between devices  4.68 us (14%)
  local copies, waits for them, and re-layouts  1.26 us (4%)
  between operations  0.79 us (2%)
    ppermute x11, starting transfers between devices, send(): lax.ppermute(x, axis, [(i, partner(i, d, n)) for i in range(n)])  13.4 us
    ppermute x11, waiting for transfers between devices, send(): lax.ppermute(x, axis, [(i, partner(i, d, n)) for i in range(n)])  4.67 us
    pallas_call x1, Pallas kernels, shards(): call(cotangent_kernel, 'take_cotangent', out_shape=(S((slots * rows, blk)...  3.96 us
    ppermute x1, starting transfers between devices, shards(): lax.ppermute(half, 'tok', [(i, (i + side) % n_tok) for i in range(n_tok)])  2.9 us
    pallas_call x1, Pallas kernels, shards(): call(token_kernel, 'take_tokens', TAKE_LIMIT, out_shape=message, in_specs...  2.38 us
    unnamed x16, local copies, waits for them, and re-layouts  1.26 us
    pallas_call x1, Pallas kernels, shards(): call(functools.partial(output_kernel, dims), 'add_outputs', out_shape=(re...  1.12 us
  transfers between devices with their start and end apart: 12, of which 4 were waited for; matrix products, arithmetic and copies ran while one was open for 0% of the time, Pallas kernels for 17%

profile of v14, /device:TPU:0, one launch (start us, length us, event | category | flops | bytes accessed | tf_op | source)
XLA Modules:
  0.0 32.1 jit_solution(14770170495440694180)
XLA Ops:
  0.6 0.0 copy-start
  0.6 0.0 copy-start.1
  0.7 0.0 copy-start.2
  0.7 0.0 copy-start.7
  0.7 2.4 %take_tokens.1 = bf16[1040,128]{1,0:T(8,128)(2,1)} custom-call(s32[8]{0:T(128)} %bitcast.13, s32[8]{0:T(128)} %bitcast.15, s32[8]{0:T(128)} %bitcast.17, s32[8]{0:T(128)} %bitcast.19, bf16[128,4096]{1,0:T(8,128)(2,1)} %tokens.3, bf16[8,128,128]{2,1,0:T(8,128)(2,1)} %bitcast.8), custom_call_target="tpu_custom_call" | custom-call | flops 33554432 | bytes 524288 | tf_op jit(solution)/shard_map/take_tokens/pallas_call | solution.py:314
  3.1 0.0 copy-start.4
  3.1 0.0 copy-start.5
  3.1 0.0 copy-start.6
  3.1 3.0 %collective-permute-start = (bf16[1040,128]{1,0:T(8,128)(2,1)}, bf16[1040,128]{1,0:T(8,128)(2,1)S(1)}, u32[]{:S(2)}, u32[]{:S(2)}) collective-permute-start(bf16[1040,128]{1,0:T(8,128)(2,1)} %take_tokens.1), channel_id=1, source_target_pairs={{0,4},{4,0},{1,5},{5,1},{2,6},{6,2},{3,7},{7,3},{8,12},{12,8},{9,1... | collective-permute-start | bytes 798728 | tf_op jit(solution)/shard_map/ppermute | solution.py:55
  6.1 0.0 copy-done
  6.1 0.0 copy-done.1
  6.1 0.0 copy-done.2
  6.1 0.0 copy-done.7
  6.1 0.0 copy-done.4
  6.1 0.0 copy-done.5
  6.1 0.0 copy-done.6
  6.1 0.0 copy-start.3
  6.2 1.2 %copy-done.3 = bf16[128,4096]{1,0:T(8,128)(2,1)S(1)} copy-done((bf16[128,4096]{1,0:T(8,128)(2,1)S(1)}, bf16[128,4096]{1,0:T(8,128)(2,1)}, u32[]{:S(2)}) %copy-start.3) | copy-done | bytes 1048600
  7.4 4.0 %take_cotangent.1 = (bf16[1024,128]{1,0:T(8,128)(2,1)S(1)}, bf16[8,128,128]{2,1,0:T(8,128)(2,1)S(1)}, bf16[8,128,128]{2,1,0:T(8,128)(2,1)S(1)}, f32[16,128,128]{...) custom-call(s32[8]{0:T(128)S(1)} %bitcast.14, s32[8]{0:T(128)S(1)} %bitcast.16, ...), custom_call_target="tpu_custom_call" | custom-call | flops 33554432 | bytes 524288 | tf_op jit(solution)/shard_map/take_cotangent/pallas_call | solution.py:331
  11.3 0.6 %collective-permute-start.2 = (bf16[1024,128]{1,0:T(8,128)(2,1)S(1)}, bf16[1024,128]{1,0:T(8,128)(2,1)S(1)}, u32[]{:S(2)}, u32[]{:S(2)}) collective-permute-start(bf16[1024,128]{1,0:T(8,128)(2,1)S(1)} %get-tuple-element.44), channel_id=1, source_target_pairs={{0,4},{4,0},{1,5},{5,1},{2,6},{6,2},{3,7},{7,3},{8,12},{12,8},{9,1... | collective-permute-start | bytes 786440 | tf_op jit(solution)/shard_map/ppermute | solution.py:55
  11.9 0.8 %collective-permute-done.refs_0_ = bf16[1040,128]{1,0:T(8,128)(2,1)S(1)} collective-permute-done((bf16[1040,128]{1,0:T(8,128)(2,1)}, bf16[1040,128]{1,0:T(8,128)(2,1)S(1)}, u32[]{:S(2)}, u32[]{:S(2)}) %collective-permute-start) | collective-permute-done | bytes 266272 | tf_op jit(solution)/shard_map/ppermute | solution.py:55
  12.7 0.5 %hidden.1 = (bf16[8,128,128]{2,1,0:T(8,128)(2,1)S(1)}, f32[16,128,128]{2,1,0:T(8,128)S(1)}, s32[8,128]{1,0:T(8,128)S(1)}, f32[8,128,128]{2,1,0:T(8,128)S(1)}, bf16[512,128]{1,0:T(8,128)(2,1)S(1)}) custom-call(s32[24,128]{1,0:T(8,128)S(1)} %get-tuple-element.37.tab, f32[16,128,128]{2,1,0:T(8,128)S(1)} %get-tuple-element.38.own, ...), custom_call_target="tpu_custom_call" | custom-call | flops 33554432 | bytes 524288 | tf_op jit(solution)/shard_map/hidden/pallas_call | solution.py:359
  13.2 2.9 %collective-permute-start.1 = (bf16[512,128]{1,0:T(8,128)(2,1)S(1)}, bf16[512,128]{1,0:T(8,128)(2,1)S(1)}, u32[]{:S(2)}, u32[]{:S(2)}) collective-permute-start(bf16[512,128]{1,0:T(8,128)(2,1)S(1)} %get-tuple-element.41), channel_id=1, source_target_pairs={{0,16},{8,24},{16,0},{24,8},{1,17},{9,25},{17,1},{25,9},{2,18},{10... | collective-permute-start | bytes 393224 | tf_op jit(solution)/shard_map/ppermute | solution.py:373
  16.1 0.4 %slope.1 = (f32[8,128,128]{2,1,0:T(8,128)S(1)}, bf16[272,128]{1,0:T(8,128)(2,1)S(1)}, bf16[272,128]{1,0:T(8,128)(2,1)S(1)}, bf16[272,128]{1,0:T(8,128)(2,1)S(1)}, bf16[272,128]{1,0:T(8,128)(2,1)S(1)}) custom-call(s32[24,128]{1,0:T(8,128)S(1)} %get-tuple-element.37.tab, bf16[16,128]{1,0:T(8,128)(2,1)S(1)} %get-tuple-element.45.row, ...), custom_call_target="tpu_custom_call" | custom-call | flops 33554432 | bytes 524288 | tf_op jit(solution)/shard_map/slope/pallas_call | solution.py:375
  16.5 1.6 %collective-permute-start.3 = (bf16[272,128]{1,0:T(8,128)(2,1)S(1)}, bf16[272,128]{1,0:T(8,128)(2,1)S(1)}, u32[]{:S(2)}, u32[]{:S(2)}) collective-permute-start(bf16[272,128]{1,0:T(8,128)(2,1)S(1)} %get-tuple-element.52), channel_id=1, source_target_pairs={{0,2},{1,3},{2,0},{3,1},{4,6},{5,7},{6,4},{7,5},{8,10},{9,11},{10,... | collective-permute-start | bytes 208904 | tf_op jit(solution)/shard_map/ppermute | solution.py:55
  18.1 0.0 collective-permute-start.4
  18.1 0.6 %collective-permute-start.5 = (bf16[272,128]{1,0:T(8,128)(2,1)S(1)}, bf16[272,128]{1,0:T(8,128)(2,1)S(1)}, u32[]{:S(2)}, u32[]{:S(2)}) collective-permute-start(bf16[272,128]{1,0:T(8,128)(2,1)S(1)} %get-tuple-element.54), channel_id=1, source_target_pairs={{0,1},{1,0},{2,3},{3,2},{4,5},{5,4},{6,7},{7,6},{8,9},{9,8},{10,11... | collective-permute-start | bytes 208904 | tf_op jit(solution)/shard_map/ppermute | solution.py:55
  18.7 0.4 %collective-permute-done.2.refs_0_ = bf16[1024,128]{1,0:T(8,128)(2,1)S(1)} collective-permute-done((bf16[1024,128]{1,0:T(8,128)(2,1)S(1)}, bf16[1024,128]{1,0:T(8,128)(2,1)S(1)}, u32[]{:S(2)}, u32[]{:S(2)}) %collective-permute-start.2) | collective-permute-done | bytes 262176 | tf_op jit(solution)/shard_map/ppermute | solution.py:55
  19.2 0.6 %back.1 = (bf16[256,128]{1,0:T(8,128)(2,1)S(1)}, bf16[256,128]{1,0:T(8,128)(2,1)S(1)}, bf16[256,128]{1,0:T(8,128)(2,1)S(1)}, bf16[256,128]{1,0:T(8,128)(2,1)S(1)...) custom-call(s32[24,128]{1,0:T(8,128)S(1)} %get-tuple-element.37.tab,, ...), custom_call_target="tpu_custom_call" | custom-call | flops 33554432 | bytes 524288 | tf_op jit(solution)/shard_map/back/pallas_call | solution.py:385
  19.8 2.6 %collective-permute-start.6 = (bf16[288,128]{1,0:T(8,128)(2,1)S(1)}, bf16[288,128]{1,0:T(8,128)(2,1)S(1)}, u32[]{:S(2)}, u32[]{:S(2)}) collective-permute-start(bf16[288,128]{1,0:T(8,128)(2,1)S(1)} %get-tuple-element.56), channel_id=1, source_target_pairs={{0,16},{8,24},{16,0},{24,8},{1,17},{9,25},{17,1},{25,9},{2,18},{10... | collective-permute-start | bytes 221192 | tf_op jit(solution)/shard_map/ppermute | solution.py:55
  22.4 0.0 collective-permute-done.3.refs_2_.refs_1_
  22.4 0.0 collective-permute-done.4.refs_3_.refs_2_
  22.4 0.0 collective-permute-done.5.refs_4_.refs_3_
  22.4 0.0 collective-permute-done.1.half
  22.5 1.6 %collective-permute-start.8 = (bf16[512,128]{1,0:T(8,128)(2,1)S(1)}, bf16[512,128]{1,0:T(8,128)(2,1)S(1)}, u32[]{:S(2)}, u32[]{:S(2)}) collective-permute-start(bf16[512,128]{1,0:T(8,128)(2,1)S(1)} %get-tuple-element.58), channel_id=1, source_target_pairs={{0,8},{8,0},{16,24},{24,16},{1,9},{9,1},{17,25},{25,17},{2,10},{10... | collective-permute-start | bytes 393224 | tf_op jit(solution)/shard_map/ppermute | solution.py:55
  24.1 1.1 %collective-permute-start.7 = (bf16[288,128]{1,0:T(8,128)(2,1)S(1)}, bf16[288,128]{1,0:T(8,128)(2,1)S(1)}, u32[]{:S(2)}, u32[]{:S(2)}) collective-permute-start(bf16[288,128]{1,0:T(8,128)(2,1)S(1)} %get-tuple-element.57), channel_id=1, source_target_pairs={{0,24},{8,16},{16,8},{24,0},{1,25},{9,17},{17,9},{25,1},{2,26},{10... | collective-permute-start | bytes 221192 | tf_op jit(solution)/shard_map/ppermute | solution.py:55
  25.3 1.5 %collective-permute-start.9 = (bf16[256,128]{1,0:T(8,128)(2,1)S(1)}, bf16[256,128]{1,0:T(8,128)(2,1)S(1)}, u32[]{:S(2)}, u32[]{:S(2)}) collective-permute-start(bf16[256,128]{1,0:T(8,128)(2,1)S(1)} %get-tuple-element.63), channel_id=1, source_target_pairs={{0,2},{1,3},{2,0},{3,1},{4,6},{5,7},{6,4},{7,5},{8,10},{9,11},{10,... | collective-permute-start | bytes 196616 | tf_op jit(solution)/shard_map/ppermute | solution.py:55
  26.8 0.0 collective-permute-start.10
  26.8 0.0 collective-permute-done.6.refs_1_
  26.8 0.6 %collective-permute-start.11 = (bf16[256,128]{1,0:T(8,128)(2,1)S(1)}, bf16[256,128]{1,0:T(8,128)(2,1)S(1)}, u32[]{:S(2)}, u32[]{:S(2)}) collective-permute-start(bf16[256,128]{1,0:T(8,128)(2,1)S(1)} %get-tuple-element.65), channel_id=1, source_target_pairs={{0,1},{1,0},{2,3},{3,2},{4,5},{5,4},{6,7},{7,6},{8,9},{9,8},{10,11... | collective-permute-start | bytes 196616 | tf_op jit(solution)/shard_map/ppermute | solution.py:55
  27.4 3.1 %collective-permute-done.7.refs_2_ = bf16[288,128]{1,0:T(8,128)(2,1)S(1)} collective-permute-done((bf16[288,128]{1,0:T(8,128)(2,1)S(1)}, bf16[288,128]{1,0:T(8,128)(2,1)S(1)}, u32[]{:S(2)}, u32[]{:S(2)}) %collective-permute-start.7) | collective-permute-done | bytes 73760 | tf_op jit(solution)/shard_map/ppermute | solution.py:55
  30.5 0.0 collective-permute-done.8.refs_3_
  30.5 0.0 collective-permute-done.9.refs_5_
  30.6 0.4 %collective-permute-done.10.refs_6_ = bf16[256,128]{1,0:T(8,128)(2,1)S(1)} collective-permute-done((bf16[256,128]{1,0:T(8,128)(2,1)S(1)}, bf16[256,128]{1,0:T(8,128)(2,1)S(1)}, u32[]{:S(2)}, u32[]{:S(2)}) %collective-permute-start.10) | collective-permute-done | bytes 65568 | tf_op jit(solution)/shard_map/ppermute | solution.py:55
  31.0 0.0 collective-permute-done.11.refs_7_
  31.0 1.1 %add_outputs.1 = (bf16[32,4096]{1,0:T(8,128)(2,1)}, bf16[32,4096]{1,0:T(8,128)(2,1)}, f32[8,32,128]{2,1,0:T(8,128)}, f32[8,32,128]{2,1,0:T(8,128)}) custom-call(f32[8,32,128]{2,1,0:T(8,128)S(1)} %get-tuple-element.59.sum1, f32[8,32,128]{2,1,0:T(8,128)S(1)} %get-tuple-element.60.sum2, bf16[272,128]{1,0:T(8,128)(2,1)S(1)} %get-tuple-element.61.refs_0_, ...), custom_call_target="tpu_custom_call" | custom-call | flops 33554432 | bytes 524288 | tf_op jit(solution)/shard_map/add_outputs/pallas_call | solution.py:420
  (2 shorter events, 0.1 us)
Async XLA Ops:
  0.6 5.5 %copy-start = (bf16[128,4096]{1,0:T(8,128)(2,1)S(1)}, bf16[128,4096]{1,0:T(8,128)(2,1)}, u32[]{:S(2)}) copy-start(bf16[128,4096]{1,0:T(8,128)(2,1)} %tokens.3) | copy-start | bytes 3145732
  0.6 5.5 %copy-start.1 = (bf16[1,1,8,128,128]{4,3,2,1,0:T(8,128)(2,1)S(1)}, bf16[1,1,8,128,128]{4,3,2,1,0:T(8,128)(2,1)}, u32[]{:S(2)}) copy-start(bf16[1,1,8,128,128]{4,3,2,1,0:T(8,128)(2,1)} %param.9) | copy-start | bytes 786436
  0.7 5.5 %copy-start.2 = (bf16[1,1,8,128,128]{4,3,2,1,0:T(8,128)(2,1)S(1)}, bf16[1,1,8,128,128]{4,3,2,1,0:T(8,128)(2,1)}, u32[]{:S(2)}) copy-start(bf16[1,1,8,128,128]{4,3,2,1,0:T(8,128)(2,1)} %param.12) | copy-start | bytes 786436
  0.7 5.4 %copy-start.7 = (s32[1,1,8]{2,1,0:T(1,128)S(1)}, s32[1,1,8]{2,1,0:T(1,128)}, u32[]{:S(2)}) copy-start(s32[1,1,8]{2,1,0:T(1,128)} %param.14) | copy-start | bytes 100
  3.1 3.1 %copy-start.4 = (s32[1,1,8]{2,1,0:T(1,128)S(1)}, s32[1,1,8]{2,1,0:T(1,128)}, u32[]{:S(2)}) copy-start(s32[1,1,8]{2,1,0:T(1,128)} %param.10) | copy-start | bytes 100
  3.1 3.1 %copy-start.5 = (s32[1,1,8]{2,1,0:T(1,128)S(1)}, s32[1,1,8]{2,1,0:T(1,128)}, u32[]{:S(2)}) copy-start(s32[1,1,8]{2,1,0:T(1,128)} %param.11) | copy-start | bytes 100
  3.1 3.1 %copy-start.6 = (s32[1,1,8]{2,1,0:T(1,128)S(1)}, s32[1,1,8]{2,1,0:T(1,128)}, u32[]{:S(2)}) copy-start(s32[1,1,8]{2,1,0:T(1,128)} %param.13) | copy-start | bytes 100
  3.1 9.6 %collective-permute-start = (bf16[1040,128]{1,0:T(8,128)(2,1)}, bf16[1040,128]{1,0:T(8,128)(2,1)S(1)}, u32[]{:S(2)}, u32[]{:S(2)}) collective-permute-start(bf16[1040,128]{1,0:T(8,128)(2,1)} %take_tokens.1), channel_id=1, source_target_pairs={{0,4},{4,0},{1,5},{5,1},{2,6},{6,2},{3,7},{7,3},{8,12},{12,8},{9,1... | collective-permute-start | bytes 798728 | tf_op jit(solution)/shard_map/ppermute | solution.py:55
  6.1 1.2 %copy-start.3 = (bf16[128,4096]{1,0:T(8,128)(2,1)S(1)}, bf16[128,4096]{1,0:T(8,128)(2,1)}, u32[]{:S(2)}) copy-start(bf16[128,4096]{1,0:T(8,128)(2,1)} %grad_out.1) | copy-start | bytes 3145732
  11.3 7.8 %collective-permute-start.2 = (bf16[1024,128]{1,0:T(8,128)(2,1)S(1)}, bf16[1024,128]{1,0:T(8,128)(2,1)S(1)}, u32[]{:S(2)}, u32[]{:S(2)}) collective-permute-start(bf16[1024,128]{1,0:T(8,128)(2,1)S(1)} %get-tuple-element.44), channel_id=1, source_target_pairs={{0,4},{4,0},{1,5},{5,1},{2,6},{6,2},{3,7},{7,3},{8,12},{12,8},{9,1... | collective-permute-start | bytes 786440 | tf_op jit(solution)/shard_map/ppermute | solution.py:55
  13.2 9.2 %collective-permute-start.1 = (bf16[512,128]{1,0:T(8,128)(2,1)S(1)}, bf16[512,128]{1,0:T(8,128)(2,1)S(1)}, u32[]{:S(2)}, u32[]{:S(2)}) collective-permute-start(bf16[512,128]{1,0:T(8,128)(2,1)S(1)} %get-tuple-element.41), channel_id=1, source_target_pairs={{0,16},{8,24},{16,0},{24,8},{1,17},{9,25},{17,1},{25,9},{2,18},{10... | collective-permute-start | bytes 393224 | tf_op jit(solution)/shard_map/ppermute | solution.py:373
  16.5 5.9 %collective-permute-start.3 = (bf16[272,128]{1,0:T(8,128)(2,1)S(1)}, bf16[272,128]{1,0:T(8,128)(2,1)S(1)}, u32[]{:S(2)}, u32[]{:S(2)}) collective-permute-start(bf16[272,128]{1,0:T(8,128)(2,1)S(1)} %get-tuple-element.52), channel_id=1, source_target_pairs={{0,2},{1,3},{2,0},{3,1},{4,6},{5,7},{6,4},{7,5},{8,10},{9,11},{10,... | collective-permute-start | bytes 208904 | tf_op jit(solution)/shard_map/ppermute | solution.py:55
  18.1 4.3 %collective-permute-start.4 = (bf16[272,128]{1,0:T(8,128)(2,1)S(1)}, bf16[272,128]{1,0:T(8,128)(2,1)S(1)}, u32[]{:S(2)}, u32[]{:S(2)}) collective-permute-start(bf16[272,128]{1,0:T(8,128)(2,1)S(1)} %get-tuple-element.53), channel_id=1, source_target_pairs={{0,3},{1,2},{2,1},{3,0},{4,7},{5,6},{6,5},{7,4},{8,11},{9,10},{10,... | collective-permute-start | bytes 208904 | tf_op jit(solution)/shard_map/ppermute | solution.py:55
  18.1 4.3 %collective-permute-start.5 = (bf16[272,128]{1,0:T(8,128)(2,1)S(1)}, bf16[272,128]{1,0:T(8,128)(2,1)S(1)}, u32[]{:S(2)}, u32[]{:S(2)}) collective-permute-start(bf16[272,128]{1,0:T(8,128)(2,1)S(1)} %get-tuple-element.54), channel_id=1, source_target_pairs={{0,1},{1,0},{2,3},{3,2},{4,5},{5,4},{6,7},{7,6},{8,9},{9,8},{10,11... | collective-permute-start | bytes 208904 | tf_op jit(solution)/shard_map/ppermute | solution.py:55
  19.8 7.0 %collective-permute-start.6 = (bf16[288,128]{1,0:T(8,128)(2,1)S(1)}, bf16[288,128]{1,0:T(8,128)(2,1)S(1)}, u32[]{:S(2)}, u32[]{:S(2)}) collective-permute-start(bf16[288,128]{1,0:T(8,128)(2,1)S(1)} %get-tuple-element.56), channel_id=1, source_target_pairs={{0,16},{8,24},{16,0},{24,8},{1,17},{9,25},{17,1},{25,9},{2,18},{10... | collective-permute-start | bytes 221192 | tf_op jit(solution)/shard_map/ppermute | solution.py:55
  22.5 8.0 %collective-permute-start.8 = (bf16[512,128]{1,0:T(8,128)(2,1)S(1)}, bf16[512,128]{1,0:T(8,128)(2,1)S(1)}, u32[]{:S(2)}, u32[]{:S(2)}) collective-permute-start(bf16[512,128]{1,0:T(8,128)(2,1)S(1)} %get-tuple-element.58), channel_id=1, source_target_pairs={{0,8},{8,0},{16,24},{24,16},{1,9},{9,1},{17,25},{25,17},{2,10},{10... | collective-permute-start | bytes 393224 | tf_op jit(solution)/shard_map/ppermute | solution.py:55
  24.1 6.3 %collective-permute-start.7 = (bf16[288,128]{1,0:T(8,128)(2,1)S(1)}, bf16[288,128]{1,0:T(8,128)(2,1)S(1)}, u32[]{:S(2)}, u32[]{:S(2)}) collective-permute-start(bf16[288,128]{1,0:T(8,128)(2,1)S(1)} %get-tuple-element.57), channel_id=1, source_target_pairs={{0,24},{8,16},{16,8},{24,0},{1,25},{9,17},{17,9},{25,1},{2,26},{10... | collective-permute-start | bytes 221192 | tf_op jit(solution)/shard_map/ppermute | solution.py:55
  25.3 5.3 %collective-permute-start.9 = (bf16[256,128]{1,0:T(8,128)(2,1)S(1)}, bf16[256,128]{1,0:T(8,128)(2,1)S(1)}, u32[]{:S(2)}, u32[]{:S(2)}) collective-permute-start(bf16[256,128]{1,0:T(8,128)(2,1)S(1)} %get-tuple-element.63), channel_id=1, source_target_pairs={{0,2},{1,3},{2,0},{3,1},{4,6},{5,7},{6,4},{7,5},{8,10},{9,11},{10,... | collective-permute-start | bytes 196616 | tf_op jit(solution)/shard_map/ppermute | solution.py:55
  26.8 4.1 %collective-permute-start.10 = (bf16[256,128]{1,0:T(8,128)(2,1)S(1)}, bf16[256,128]{1,0:T(8,128)(2,1)S(1)}, u32[]{:S(2)}, u32[]{:S(2)}) collective-permute-start(bf16[256,128]{1,0:T(8,128)(2,1)S(1)} %get-tuple-element.64), channel_id=1, source_target_pairs={{0,3},{1,2},{2,1},{3,0},{4,7},{5,6},{6,5},{7,4},{8,11},{9,10},{10,... | collective-permute-start | bytes 196616 | tf_op jit(solution)/shard_map/ppermute | solution.py:55
  26.8 4.1 %collective-permute-start.11 = (bf16[256,128]{1,0:T(8,128)(2,1)S(1)}, bf16[256,128]{1,0:T(8,128)(2,1)S(1)}, u32[]{:S(2)}, u32[]{:S(2)}) collective-permute-start(bf16[256,128]{1,0:T(8,128)(2,1)S(1)} %get-tuple-element.65), channel_id=1, source_target_pairs={{0,1},{1,0},{2,3},{3,2},{4,5},{5,4},{6,7},{7,6},{8,9},{9,8},{10,11... | collective-permute-start | bytes 196616 | tf_op jit(solution)/shard_map/ppermute | solution.py:55

commit v15 on v14

--- a/solution.py
+++ b/solution.py
@@ -258,28 +258,48 @@
         result[k] = sum(ref[here, :].astype(f32) for ref in parts)
 
 
-def output_kernel(dims, sum1, sum2, *refs):
+def place_shares(shares, tables, acc):
+    slots = len(tables[0])
+    share = acc.shape[1]
+    acc[...] = jnp.zeros(acc.shape, f32)
+    for ref, table in zip(shares, tables):
+        for k in range(slots):
+            acc[table[k]] = acc[table[k]] + ref[k * share : (k + 1) * share, :].astype(f32)
+
+
+def store_rows(acc, result, output, sem):
+    blk = acc.shape[-1]
+    for b in range(acc.shape[0]):
+        result[:, b * blk : (b + 1) * blk] = acc[b].astype(bf16)
+    copy = pltpu.make_async_copy(result, output, sem)
+    copy.start()
+    return copy
+
+
+def tables_of(parts, rows, which, slots):
+    return [[table[0, which * slots + k] for k in range(slots)] for table in [numbers(ref, rows) for ref in parts]]
+
+
+def output_kernel(dims, *refs):
+    slots, n_row, n_col, n_tok = dims
+    parts, (output, last, result, acc, sem) = refs[:n_col], refs[n_col:]
+    rows = slots * acc.shape[1]
+    last[...] = jnp.zeros(last.shape, jnp.int32)
+    place_shares(parts, tables_of(parts, rows, W2_OUT, slots), acc)
+    store_rows(acc, result, output, sem).wait()
+
+
+def input_kernel(dims, after, sum1, sum2, *refs):
+    del after
     slots, n_row, n_col, n_tok = dims
     outs, backs, refs = refs[:n_col], refs[n_col : 2 * n_col], refs[2 * n_col :]
-    outputs, gw1, gw2, results, (acc_out, acc_in, sems) = refs[:2], refs[2], refs[3], refs[4:6], refs[6:]
-    blk, share = acc_out.shape[-1], acc_out.shape[1]
-    stores = [pltpu.make_async_copy(sum1, gw1, sems.at[2]), pltpu.make_async_copy(sum2, gw2, sems.at[3])]
+    grad_in, gw1, gw2, result, acc, sems = refs
+    stores = [pltpu.make_async_copy(sum1, gw1, sems.at[0]), pltpu.make_async_copy(sum2, gw2, sems.at[1])]
     for c in stores:
         c.start()
-    acc_out[...] = jnp.zeros(acc_out.shape, f32)
-    acc_in[...] = jnp.zeros(acc_in.shape, f32)
-    for out, back in zip(outs, backs):
-        blocks = numbers(out, slots * share)
-        for k in range(slots):
-            here = slice(k * share, (k + 1) * share)
-            for ref, which, acc in ((out, W2_OUT, acc_out), (back, W1_ROW, acc_in)):
-                at = blocks[0, which * slots + k]
-                acc[at] = acc[at] + ref[here, :].astype(f32)
-    for i, acc in enumerate((acc_out, acc_in)):
-        for b in range(acc.shape[0]):
-            results[i][:, b * blk : (b + 1) * blk] = acc[b].astype(bf16)
-        stores.append(pltpu.make_async_copy(results[i], outputs[i], sems.at[i]))
-        stores[-1].start()
+    rows = slots * acc.shape[1]
+    place_shares(backs, tables_of(outs, rows, W1_ROW, slots), acc)
+    stores.append(store_rows(acc, result, grad_in, sems.at[2]))
     for c in stores:
         c.wait()
 
@@ -352,8 +372,8 @@
 
     single = S((slots * part, blk), bf16)
     side = max(1, n_tok // 2)
-    across = S((slots * part + 32, blk), bf16)
-    grads = tuple(single if d < side else across for d in range(n_tok))
+    spare = [16, 16]
+    grads = tuple(single if d < side else S((slots * part + spare[d % 2], blk), bf16) for d in range(n_tok))
     half = S((slots * side * part, blk), bf16)
     peer_rows = 8 * max(1, n_row - 1)
     active, hid, places, grad2, half = call(
@@ -417,15 +437,22 @@
         in_specs=[VMEM] * n_tok,
         out_specs=(VMEM,) * 2,
     )(*tok_parts[:1], *tok_parts[2:], *tok_parts[1:2])
-    output, grad_in, gw1, gw2 = call(
+    output, last = call(
         functools.partial(output_kernel, dims),
         "add_outputs",
-        out_shape=(result, result, summed, summed),
-        in_specs=[VMEM] * len([*sums, *o_parts, *i_parts]),
-        out_specs=(HBM,) * 4,
-        scratch_shapes=[pltpu.VMEM(result.shape, bf16)] * 2
-        + [acc, acc, pltpu.SemaphoreType.DMA((4,))],
-    )(*sums, *o_parts, *i_parts)
+        out_shape=(result, S((8, LANES), jnp.int32)),
+        in_specs=[VMEM] * n_col,
+        out_specs=(HBM, VMEM),
+        scratch_shapes=[pltpu.VMEM(result.shape, bf16), acc, pltpu.SemaphoreType.DMA],
+    )(*o_parts)
+    grad_in, gw1, gw2 = call(
+        functools.partial(input_kernel, dims),
+        "add_inputs",
+        out_shape=(result, summed, summed),
+        in_specs=[ANY] + [VMEM] * len([*sums, *o_parts, *i_parts]),
+        out_specs=(HBM,) * 3,
+        scratch_shapes=[pltpu.VMEM(result.shape, bf16), acc, pltpu.SemaphoreType.DMA((3,))],
+    )(last, *sums, *o_parts, *i_parts)
     return (output, grad_in, gw1.reshape(1, 1, slots, part, blk), gw2.reshape(1, 1, slots, part, blk))
 
 

time: 32.3 us -> 32.1 us (level)
  waiting for transfers between devices: 4.68 us -> 3.69 us
  Pallas kernels: 9.05 us -> 9.86 us
    ppermute x11, waiting for transfers between devices: 4.67 us -> 3.69 us  [send(): lax.ppermute(x, axis, [(i, partner(i, d, n)) for i in range(n)])]
    pallas_call x0 -> x1, Pallas kernels: none -> 0.98 us  [shards(): call(functools.partial(input_kernel, dims), 'add_inputs', out_shape=(resu...]
  transfers between devices with their start and end apart: 12 -> 12, of which waited for: 4 -> 4; matrix products, arithmetic and copies ran while one was open for 0% -> 0% of each run, Pallas kernels for 17% -> 20%
where the time goes in v15:
time: 32.1 us; the launch traced here: 31.9 us
  starting transfers between devices  16.3 us (51%)
  Pallas kernels  9.86 us (31%)
  waiting for transfers between devices  3.69 us (11%)
  local copies, waits for them, and re-layouts  1.26 us (4%)
  between operations  0.8 us (2%)
    ppermute x11, starting transfers between devices, send(): lax.ppermute(x, axis, [(i, partner(i, d, n)) for i in range(n)])  13.4 us
    pallas_call x1, Pallas kernels, shards(): call(cotangent_kernel, 'take_cotangent', out_shape=(S((slots * rows, blk)...  3.96 us
    ppermute x11, waiting for transfers between devices, send(): lax.ppermute(x, axis, [(i, partner(i, d, n)) for i in range(n)])  3.69 us
    ppermute x1, starting transfers between devices, shards(): lax.ppermute(half, 'tok', [(i, (i + side) % n_tok) for i in range(n_tok)])  2.9 us
    pallas_call x1, Pallas kernels, shards(): call(token_kernel, 'take_tokens', TAKE_LIMIT, out_shape=message, in_specs...  2.37 us
    unnamed x16, local copies, waits for them, and re-layouts  1.26 us
    pallas_call x1, Pallas kernels, shards(): call(functools.partial(input_kernel, dims), 'add_inputs', out_shape=(resu...  0.98 us
    pallas_call x1, Pallas kernels, shards(): call(functools.partial(output_kernel, dims), 'add_outputs', out_shape=(re...  0.96 us
  transfers between devices with their start and end apart: 12, of which 4 were waited for; matrix products, arithmetic and copies ran while one was open for 0% of the time, Pallas kernels for 20%

profile of v15, /device:TPU:0, one launch (start us, length us, event | category | flops | bytes accessed | tf_op | source)
XLA Modules:
  0.0 31.9 jit_solution(8090798440055060157)
XLA Ops:
  0.6 0.0 copy-start
  0.6 0.0 copy-start.1
  0.7 0.0 copy-start.2
  0.7 0.0 copy-start.7
  0.7 2.4 %take_tokens.1 = bf16[1040,128]{1,0:T(8,128)(2,1)} custom-call(s32[8]{0:T(128)} %bitcast.13, s32[8]{0:T(128)} %bitcast.15, s32[8]{0:T(128)} %bitcast.17, s32[8]{0:T(128)} %bitcast.19, bf16[128,4096]{1,0:T(8,128)(2,1)} %tokens.3, bf16[8,128,128]{2,1,0:T(8,128)(2,1)} %bitcast.8), custom_call_target="tpu_custom_call" | custom-call | flops 33554432 | bytes 524288 | tf_op jit(solution)/shard_map/take_tokens/pallas_call | solution.py:334
  3.0 0.0 copy-start.4
  3.1 0.0 copy-start.5
  3.1 0.0 copy-start.6
  3.1 3.0 %collective-permute-start = (bf16[1040,128]{1,0:T(8,128)(2,1)}, bf16[1040,128]{1,0:T(8,128)(2,1)S(1)}, u32[]{:S(2)}, u32[]{:S(2)}) collective-permute-start(bf16[1040,128]{1,0:T(8,128)(2,1)} %take_tokens.1), channel_id=1, source_target_pairs={{0,4},{4,0},{1,5},{5,1},{2,6},{6,2},{3,7},{7,3},{8,12},{12,8},{9,1... | collective-permute-start | bytes 798728 | tf_op jit(solution)/shard_map/ppermute | solution.py:55
  6.1 0.0 copy-done
  6.1 0.0 copy-done.1
  6.1 0.0 copy-done.2
  6.1 0.0 copy-done.7
  6.1 0.0 copy-done.4
  6.1 0.0 copy-done.5
  6.1 0.0 copy-done.6
  6.1 0.0 copy-start.3
  6.1 1.2 %copy-done.3 = bf16[128,4096]{1,0:T(8,128)(2,1)S(1)} copy-done((bf16[128,4096]{1,0:T(8,128)(2,1)S(1)}, bf16[128,4096]{1,0:T(8,128)(2,1)}, u32[]{:S(2)}) %copy-start.3) | copy-done | bytes 1048600
  7.4 4.0 %take_cotangent.1 = (bf16[1024,128]{1,0:T(8,128)(2,1)S(1)}, bf16[8,128,128]{2,1,0:T(8,128)(2,1)S(1)}, bf16[8,128,128]{2,1,0:T(8,128)(2,1)S(1)}, f32[16,128,128]{...) custom-call(s32[8]{0:T(128)S(1)} %bitcast.14, s32[8]{0:T(128)S(1)} %bitcast.16, ...), custom_call_target="tpu_custom_call" | custom-call | flops 33554432 | bytes 524288 | tf_op jit(solution)/shard_map/take_cotangent/pallas_call | solution.py:351
  11.3 0.6 %collective-permute-start.5 = (bf16[1024,128]{1,0:T(8,128)(2,1)S(1)}, bf16[1024,128]{1,0:T(8,128)(2,1)S(1)}, u32[]{:S(2)}, u32[]{:S(2)}) collective-permute-start(bf16[1024,128]{1,0:T(8,128)(2,1)S(1)} %get-tuple-element.54), channel_id=1, source_target_pairs={{0,4},{4,0},{1,5},{5,1},{2,6},{6,2},{3,7},{7,3},{8,12},{12,8},{9,1... | collective-permute-start | bytes 786440 | tf_op jit(solution)/shard_map/ppermute | solution.py:55
  11.9 0.8 %collective-permute-done.refs_0_ = bf16[1040,128]{1,0:T(8,128)(2,1)S(1)} collective-permute-done((bf16[1040,128]{1,0:T(8,128)(2,1)}, bf16[1040,128]{1,0:T(8,128)(2,1)S(1)}, u32[]{:S(2)}, u32[]{:S(2)}) %collective-permute-start) | collective-permute-done | bytes 266272 | tf_op jit(solution)/shard_map/ppermute | solution.py:55
  12.7 0.5 %hidden.1 = (bf16[8,128,128]{2,1,0:T(8,128)(2,1)S(1)}, f32[16,128,128]{2,1,0:T(8,128)S(1)}, s32[8,128]{1,0:T(8,128)S(1)}, f32[8,128,128]{2,1,0:T(8,128)S(1)}, bf16[512,128]{1,0:T(8,128)(2,1)S(1)}) custom-call(s32[24,128]{1,0:T(8,128)S(1)} %get-tuple-element.38.tab, f32[16,128,128]{2,1,0:T(8,128)S(1)} %get-tuple-element.40.own, ...), custom_call_target="tpu_custom_call" | custom-call | flops 33554432 | bytes 524288 | tf_op jit(solution)/shard_map/hidden/pallas_call | solution.py:379
  13.2 2.9 %collective-permute-start.4 = (bf16[512,128]{1,0:T(8,128)(2,1)S(1)}, bf16[512,128]{1,0:T(8,128)(2,1)S(1)}, u32[]{:S(2)}, u32[]{:S(2)}) collective-permute-start(bf16[512,128]{1,0:T(8,128)(2,1)S(1)} %get-tuple-element.51), channel_id=1, source_target_pairs={{0,16},{8,24},{16,0},{24,8},{1,17},{9,25},{17,1},{25,9},{2,18},{10... | collective-permute-start | bytes 393224 | tf_op jit(solution)/shard_map/ppermute | solution.py:393
  16.1 0.4 %slope.1 = (f32[8,128,128]{2,1,0:T(8,128)S(1)}, bf16[272,128]{1,0:T(8,128)(2,1)S(1)}, bf16[272,128]{1,0:T(8,128)(2,1)S(1)}, bf16[272,128]{1,0:T(8,128)(2,1)S(1)}, bf16[272,128]{1,0:T(8,128)(2,1)S(1)}) custom-call(s32[24,128]{1,0:T(8,128)S(1)} %get-tuple-element.38.tab, bf16[16,128]{1,0:T(8,128)(2,1)S(1)} %get-tuple-element.39.row, ...), custom_call_target="tpu_custom_call" | custom-call | flops 33554432 | bytes 524288 | tf_op jit(solution)/shard_map/slope/pallas_call | solution.py:395
  16.5 1.6 %collective-permute-start.1 = (bf16[272,128]{1,0:T(8,128)(2,1)S(1)}, bf16[272,128]{1,0:T(8,128)(2,1)S(1)}, u32[]{:S(2)}, u32[]{:S(2)}) collective-permute-start(bf16[272,128]{1,0:T(8,128)(2,1)S(1)} %get-tuple-element.45), channel_id=1, source_target_pairs={{0,2},{1,3},{2,0},{3,1},{4,6},{5,7},{6,4},{7,5},{8,10},{9,11},{10,... | collective-permute-start | bytes 208904 | tf_op jit(solution)/shard_map/ppermute | solution.py:55
  18.1 0.0 collective-permute-start.2
  18.1 0.6 %collective-permute-start.3 = (bf16[272,128]{1,0:T(8,128)(2,1)S(1)}, bf16[272,128]{1,0:T(8,128)(2,1)S(1)}, u32[]{:S(2)}, u32[]{:S(2)}) collective-permute-start(bf16[272,128]{1,0:T(8,128)(2,1)S(1)} %get-tuple-element.47), channel_id=1, source_target_pairs={{0,1},{1,0},{2,3},{3,2},{4,5},{5,4},{6,7},{7,6},{8,9},{9,8},{10,11... | collective-permute-start | bytes 208904 | tf_op jit(solution)/shard_map/ppermute | solution.py:55
  18.7 0.4 %collective-permute-done.5.refs_0_ = bf16[1024,128]{1,0:T(8,128)(2,1)S(1)} collective-permute-done((bf16[1024,128]{1,0:T(8,128)(2,1)S(1)}, bf16[1024,128]{1,0:T(8,128)(2,1)S(1)}, u32[]{:S(2)}, u32[]{:S(2)}) %collective-permute-start.5) | collective-permute-done | bytes 262176 | tf_op jit(solution)/shard_map/ppermute | solution.py:55
  19.2 0.6 %back.1 = (bf16[256,128]{1,0:T(8,128)(2,1)S(1)}, bf16[256,128]{1,0:T(8,128)(2,1)S(1)}, bf16[256,128]{1,0:T(8,128)(2,1)S(1)}, bf16[256,128]{1,0:T(8,128)(2,1)S(1)...) custom-call(s32[24,128]{1,0:T(8,128)S(1)} %get-tuple-element.38.tab,, ...), custom_call_target="tpu_custom_call" | custom-call | flops 33554432 | bytes 524288 | tf_op jit(solution)/shard_map/back/pallas_call | solution.py:405
  19.7 2.7 %collective-permute-start.6 = (bf16[272,128]{1,0:T(8,128)(2,1)S(1)}, bf16[272,128]{1,0:T(8,128)(2,1)S(1)}, u32[]{:S(2)}, u32[]{:S(2)}) collective-permute-start(bf16[272,128]{1,0:T(8,128)(2,1)S(1)} %get-tuple-element.60), channel_id=1, source_target_pairs={{0,16},{8,24},{16,0},{24,8},{1,17},{9,25},{17,1},{25,9},{2,18},{10... | collective-permute-start | bytes 208904 | tf_op jit(solution)/shard_map/ppermute | solution.py:55
  22.4 0.0 collective-permute-done.1.refs_1_.refs_2_
  22.4 0.0 collective-permute-done.2.refs_2_.refs_3_
  22.4 0.0 collective-permute-done.3.refs_3_.refs_4_
  22.4 0.0 collective-permute-done.4.half
  22.5 1.6 %collective-permute-start.8 = (bf16[512,128]{1,0:T(8,128)(2,1)S(1)}, bf16[512,128]{1,0:T(8,128)(2,1)S(1)}, u32[]{:S(2)}, u32[]{:S(2)}) collective-permute-start(bf16[512,128]{1,0:T(8,128)(2,1)S(1)} %get-tuple-element.62), channel_id=1, source_target_pairs={{0,8},{8,0},{16,24},{24,16},{1,9},{9,1},{17,25},{25,17},{2,10},{10... | collective-permute-start | bytes 393224 | tf_op jit(solution)/shard_map/ppermute | solution.py:55
  24.1 1.1 %collective-permute-start.7 = (bf16[272,128]{1,0:T(8,128)(2,1)S(1)}, bf16[272,128]{1,0:T(8,128)(2,1)S(1)}, u32[]{:S(2)}, u32[]{:S(2)}) collective-permute-start(bf16[272,128]{1,0:T(8,128)(2,1)S(1)} %get-tuple-element.61), channel_id=1, source_target_pairs={{0,24},{8,16},{16,8},{24,0},{1,25},{9,17},{17,9},{25,1},{2,26},{10... | collective-permute-start | bytes 208904 | tf_op jit(solution)/shard_map/ppermute | solution.py:55
  25.3 1.5 %collective-permute-start.9 = (bf16[256,128]{1,0:T(8,128)(2,1)S(1)}, bf16[256,128]{1,0:T(8,128)(2,1)S(1)}, u32[]{:S(2)}, u32[]{:S(2)}) collective-permute-start(bf16[256,128]{1,0:T(8,128)(2,1)S(1)} %get-tuple-element.66), channel_id=1, source_target_pairs={{0,2},{1,3},{2,0},{3,1},{4,6},{5,7},{6,4},{7,5},{8,10},{9,11},{10,... | collective-permute-start | bytes 196616 | tf_op jit(solution)/shard_map/ppermute | solution.py:55
  26.8 0.0 collective-permute-start.10
  26.8 0.0 collective-permute-done.6.refs_1_
  26.8 0.6 %collective-permute-start.11 = (bf16[256,128]{1,0:T(8,128)(2,1)S(1)}, bf16[256,128]{1,0:T(8,128)(2,1)S(1)}, u32[]{:S(2)}, u32[]{:S(2)}) collective-permute-start(bf16[256,128]{1,0:T(8,128)(2,1)S(1)} %get-tuple-element.68), channel_id=1, source_target_pairs={{0,1},{1,0},{2,3},{3,2},{4,5},{5,4},{6,7},{7,6},{8,9},{9,8},{10,11... | collective-permute-start | bytes 196616 | tf_op jit(solution)/shard_map/ppermute | solution.py:55
  27.4 1.0 %add_outputs.1 = (bf16[32,4096]{1,0:T(8,128)(2,1)}, s32[8,128]{1,0:T(8,128)S(1)}) custom-call(bf16[272,128]{1,0:T(8,128)(2,1)S(1)} %get-tuple-element.44.refs_0_, bf16[272,128]{1,0:T(8,128)(2,1)S(1)} %collective-permute-done.1.refs_1_.refs_2_, bf16[272,128]{1,0:T(8,128)(2,1)S(1)} %collective-permute-done.2.refs_2_.refs_3_, ...), custom_call_target="tpu_custom_call" | custom-call | flops 33554432 | bytes 524288 | tf_op jit(solution)/shard_map/add_outputs/pallas_call | solution.py:440
  28.4 1.9 %collective-permute-done.7.refs_2_ = bf16[272,128]{1,0:T(8,128)(2,1)S(1)} collective-permute-done((bf16[272,128]{1,0:T(8,128)(2,1)S(1)}, bf16[272,128]{1,0:T(8,128)(2,1)S(1)}, u32[]{:S(2)}, u32[]{:S(2)}) %collective-permute-start.7) | collective-permute-done | bytes 69664 | tf_op jit(solution)/shard_map/ppermute | solution.py:55
  30.3 0.0 collective-permute-done.8.refs_3_
  30.3 0.1 add_grads.1
  30.4 0.0 collective-permute-done.9.refs_5_
  30.4 0.5 %collective-permute-done.10.refs_6_ = bf16[256,128]{1,0:T(8,128)(2,1)S(1)} collective-permute-done((bf16[256,128]{1,0:T(8,128)(2,1)S(1)}, bf16[256,128]{1,0:T(8,128)(2,1)S(1)}, u32[]{:S(2)}, u32[]{:S(2)}) %collective-permute-start.10) | collective-permute-done | bytes 65568 | tf_op jit(solution)/shard_map/ppermute | solution.py:55
  30.9 0.0 collective-permute-done.11.refs_7_
  30.9 1.0 %add_inputs.1 = (bf16[32,4096]{1,0:T(8,128)(2,1)}, f32[8,32,128]{2,1,0:T(8,128)}, f32[8,32,128]{2,1,0:T(8,128)}) custom-call(s32[8,128]{1,0:T(8,128)S(1)} %get-tuple-element.49.after, f32[8,32,128]{2,1,0:T(8,128)S(1)} %get-tuple-element.63.sum1, f32[8,32,128]{2,1,0:T(8,128)S(1)} %get-tuple-element.64.sum2, bf16[272,128]{1,0:T(8,128)(2,1)S(1)} %get-tuple-element.44.refs_0_, ...), custom_call_target="tpu_custom_call" | custom-call | flops 33554432 | bytes 524288 | tf_op jit(solution)/shard_map/add_inputs/pallas_call | solution.py:448
  (1 shorter events, 0.0 us)
Async XLA Ops:
  0.6 5.5 %copy-start = (bf16[128,4096]{1,0:T(8,128)(2,1)S(1)}, bf16[128,4096]{1,0:T(8,128)(2,1)}, u32[]{:S(2)}) copy-start(bf16[128,4096]{1,0:T(8,128)(2,1)} %tokens.3) | copy-start | bytes 3145732
  0.6 5.5 %copy-start.1 = (bf16[1,1,8,128,128]{4,3,2,1,0:T(8,128)(2,1)S(1)}, bf16[1,1,8,128,128]{4,3,2,1,0:T(8,128)(2,1)}, u32[]{:S(2)}) copy-start(bf16[1,1,8,128,128]{4,3,2,1,0:T(8,128)(2,1)} %param.9) | copy-start | bytes 786436
  0.7 5.4 %copy-start.2 = (bf16[1,1,8,128,128]{4,3,2,1,0:T(8,128)(2,1)S(1)}, bf16[1,1,8,128,128]{4,3,2,1,0:T(8,128)(2,1)}, u32[]{:S(2)}) copy-start(bf16[1,1,8,128,128]{4,3,2,1,0:T(8,128)(2,1)} %param.12) | copy-start | bytes 786436
  0.7 5.4 %copy-start.7 = (s32[1,1,8]{2,1,0:T(1,128)S(1)}, s32[1,1,8]{2,1,0:T(1,128)}, u32[]{:S(2)}) copy-start(s32[1,1,8]{2,1,0:T(1,128)} %param.14) | copy-start | bytes 100
  3.0 3.1 %copy-start.4 = (s32[1,1,8]{2,1,0:T(1,128)S(1)}, s32[1,1,8]{2,1,0:T(1,128)}, u32[]{:S(2)}) copy-start(s32[1,1,8]{2,1,0:T(1,128)} %param.10) | copy-start | bytes 100
  3.1 3.1 %copy-start.5 = (s32[1,1,8]{2,1,0:T(1,128)S(1)}, s32[1,1,8]{2,1,0:T(1,128)}, u32[]{:S(2)}) copy-start(s32[1,1,8]{2,1,0:T(1,128)} %param.11) | copy-start | bytes 100
  3.1 3.1 %copy-start.6 = (s32[1,1,8]{2,1,0:T(1,128)S(1)}, s32[1,1,8]{2,1,0:T(1,128)}, u32[]{:S(2)}) copy-start(s32[1,1,8]{2,1,0:T(1,128)} %param.13) | copy-start | bytes 100
  3.1 9.6 %collective-permute-start = (bf16[1040,128]{1,0:T(8,128)(2,1)}, bf16[1040,128]{1,0:T(8,128)(2,1)S(1)}, u32[]{:S(2)}, u32[]{:S(2)}) collective-permute-start(bf16[1040,128]{1,0:T(8,128)(2,1)} %take_tokens.1), channel_id=1, source_target_pairs={{0,4},{4,0},{1,5},{5,1},{2,6},{6,2},{3,7},{7,3},{8,12},{12,8},{9,1... | collective-permute-start | bytes 798728 | tf_op jit(solution)/shard_map/ppermute | solution.py:55
  6.1 1.2 %copy-start.3 = (bf16[128,4096]{1,0:T(8,128)(2,1)S(1)}, bf16[128,4096]{1,0:T(8,128)(2,1)}, u32[]{:S(2)}) copy-start(bf16[128,4096]{1,0:T(8,128)(2,1)} %grad_out.1) | copy-start | bytes 3145732
  11.3 7.8 %collective-permute-start.5 = (bf16[1024,128]{1,0:T(8,128)(2,1)S(1)}, bf16[1024,128]{1,0:T(8,128)(2,1)S(1)}, u32[]{:S(2)}, u32[]{:S(2)}) collective-permute-start(bf16[1024,128]{1,0:T(8,128)(2,1)S(1)} %get-tuple-element.54), channel_id=1, source_target_pairs={{0,4},{4,0},{1,5},{5,1},{2,6},{6,2},{3,7},{7,3},{8,12},{12,8},{9,1... | collective-permute-start | bytes 786440 | tf_op jit(solution)/shard_map/ppermute | solution.py:55
  13.2 9.2 %collective-permute-start.4 = (bf16[512,128]{1,0:T(8,128)(2,1)S(1)}, bf16[512,128]{1,0:T(8,128)(2,1)S(1)}, u32[]{:S(2)}, u32[]{:S(2)}) collective-permute-start(bf16[512,128]{1,0:T(8,128)(2,1)S(1)} %get-tuple-element.51), channel_id=1, source_target_pairs={{0,16},{8,24},{16,0},{24,8},{1,17},{9,25},{17,1},{25,9},{2,18},{10... | collective-permute-start | bytes 393224 | tf_op jit(solution)/shard_map/ppermute | solution.py:393
  16.5 5.9 %collective-permute-start.1 = (bf16[272,128]{1,0:T(8,128)(2,1)S(1)}, bf16[272,128]{1,0:T(8,128)(2,1)S(1)}, u32[]{:S(2)}, u32[]{:S(2)}) collective-permute-start(bf16[272,128]{1,0:T(8,128)(2,1)S(1)} %get-tuple-element.45), channel_id=1, source_target_pairs={{0,2},{1,3},{2,0},{3,1},{4,6},{5,7},{6,4},{7,5},{8,10},{9,11},{10,... | collective-permute-start | bytes 208904 | tf_op jit(solution)/shard_map/ppermute | solution.py:55
  18.1 4.3 %collective-permute-start.2 = (bf16[272,128]{1,0:T(8,128)(2,1)S(1)}, bf16[272,128]{1,0:T(8,128)(2,1)S(1)}, u32[]{:S(2)}, u32[]{:S(2)}) collective-permute-start(bf16[272,128]{1,0:T(8,128)(2,1)S(1)} %get-tuple-element.46), channel_id=1, source_target_pairs={{0,3},{1,2},{2,1},{3,0},{4,7},{5,6},{6,5},{7,4},{8,11},{9,10},{10,... | collective-permute-start | bytes 208904 | tf_op jit(solution)/shard_map/ppermute | solution.py:55
  18.1 4.3 %collective-permute-start.3 = (bf16[272,128]{1,0:T(8,128)(2,1)S(1)}, bf16[272,128]{1,0:T(8,128)(2,1)S(1)}, u32[]{:S(2)}, u32[]{:S(2)}) collective-permute-start(bf16[272,128]{1,0:T(8,128)(2,1)S(1)} %get-tuple-element.47), channel_id=1, source_target_pairs={{0,1},{1,0},{2,3},{3,2},{4,5},{5,4},{6,7},{7,6},{8,9},{9,8},{10,11... | collective-permute-start | bytes 208904 | tf_op jit(solution)/shard_map/ppermute | solution.py:55
  19.7 7.1 %collective-permute-start.6 = (bf16[272,128]{1,0:T(8,128)(2,1)S(1)}, bf16[272,128]{1,0:T(8,128)(2,1)S(1)}, u32[]{:S(2)}, u32[]{:S(2)}) collective-permute-start(bf16[272,128]{1,0:T(8,128)(2,1)S(1)} %get-tuple-element.60), channel_id=1, source_target_pairs={{0,16},{8,24},{16,0},{24,8},{1,17},{9,25},{17,1},{25,9},{2,18},{10... | collective-permute-start | bytes 208904 | tf_op jit(solution)/shard_map/ppermute | solution.py:55
  22.5 7.9 %collective-permute-start.8 = (bf16[512,128]{1,0:T(8,128)(2,1)S(1)}, bf16[512,128]{1,0:T(8,128)(2,1)S(1)}, u32[]{:S(2)}, u32[]{:S(2)}) collective-permute-start(bf16[512,128]{1,0:T(8,128)(2,1)S(1)} %get-tuple-element.62), channel_id=1, source_target_pairs={{0,8},{8,0},{16,24},{24,16},{1,9},{9,1},{17,25},{25,17},{2,10},{10... | collective-permute-start | bytes 393224 | tf_op jit(solution)/shard_map/ppermute | solution.py:55
  24.1 6.2 %collective-permute-start.7 = (bf16[272,128]{1,0:T(8,128)(2,1)S(1)}, bf16[272,128]{1,0:T(8,128)(2,1)S(1)}, u32[]{:S(2)}, u32[]{:S(2)}) collective-permute-start(bf16[272,128]{1,0:T(8,128)(2,1)S(1)} %get-tuple-element.61), channel_id=1, source_target_pairs={{0,24},{8,16},{16,8},{24,0},{1,25},{9,17},{17,9},{25,1},{2,26},{10... | collective-permute-start | bytes 208904 | tf_op jit(solution)/shard_map/ppermute | solution.py:55
  25.3 5.1 %collective-permute-start.9 = (bf16[256,128]{1,0:T(8,128)(2,1)S(1)}, bf16[256,128]{1,0:T(8,128)(2,1)S(1)}, u32[]{:S(2)}, u32[]{:S(2)}) collective-permute-start(bf16[256,128]{1,0:T(8,128)(2,1)S(1)} %get-tuple-element.66), channel_id=1, source_target_pairs={{0,2},{1,3},{2,0},{3,1},{4,6},{5,7},{6,4},{7,5},{8,10},{9,11},{10,... | collective-permute-start | bytes 196616 | tf_op jit(solution)/shard_map/ppermute | solution.py:55
  26.8 4.1 %collective-permute-start.10 = (bf16[256,128]{1,0:T(8,128)(2,1)S(1)}, bf16[256,128]{1,0:T(8,128)(2,1)S(1)}, u32[]{:S(2)}, u32[]{:S(2)}) collective-permute-start(bf16[256,128]{1,0:T(8,128)(2,1)S(1)} %get-tuple-element.67), channel_id=1, source_target_pairs={{0,3},{1,2},{2,1},{3,0},{4,7},{5,6},{6,5},{7,4},{8,11},{9,10},{10,... | collective-permute-start | bytes 196616 | tf_op jit(solution)/shard_map/ppermute | solution.py:55
  26.8 4.1 %collective-permute-start.11 = (bf16[256,128]{1,0:T(8,128)(2,1)S(1)}, bf16[256,128]{1,0:T(8,128)(2,1)S(1)}, u32[]{:S(2)}, u32[]{:S(2)}) collective-permute-start(bf16[256,128]{1,0:T(8,128)(2,1)S(1)} %get-tuple-element.68), channel_id=1, source_target_pairs={{0,1},{1,0},{2,3},{3,2},{4,5},{5,4},{6,7},{7,6},{8,9},{9,8},{10,11... | collective-permute-start | bytes 196616 | tf_op jit(solution)/shard_map/ppermute | solution.py:55

commit v16 on v15

--- a/solution.py
+++ b/solution.py
@@ -227,35 +227,27 @@
         cut(grad.at[k], grads, k, "tok")
         value[k] = dot(g, w1[k], (1, 1))
         cut(value.at[k], outs, k, "col")
-    for ref in grads:
-        rows = slots * grad.shape[1] // n_tok
-        if ref.shape[0] > rows:
-            ref[rows:, :] = jnp.zeros((ref.shape[0] - rows, LANES), bf16)
-
-
-def join_kernel(dims, grad2, half, *refs):
+
+
+def pair_kernel(dims, grad2, half, *refs):
     slots, n_row, n_col, n_tok = dims
     side = max(1, n_tok // 2)
     part = grad2.shape[1] // n_tok
-    shares, joined = refs[:side], refs[-side:]
-    for d in range(side):
+    for d, ref in enumerate(refs[-side:]):
         to = target("tok", d)
         begin = pl.multiple_of(to * part, part)
-        size = shares[d].shape[0]
-        joined[d][:size, :] = shares[d][...]
         for k in range(slots):
             total = grad2[k, pl.ds(begin, part), :]
             if n_tok > 1:
                 there = pl.multiple_of(k * side * part + lax.rem(to, side) * part, part)
                 total = total + half[pl.ds(there, part), :].astype(f32)
-            joined[d][size + k * part : size + (k + 1) * part, :] = total.astype(bf16)
-
-
-def add_shares(parts, result, first):
+            ref[k * part : (k + 1) * part, :] = total.astype(bf16)
+
+
+def add_shares(parts, result):
     part = result.shape[1]
     for k in range(result.shape[0]):
-        here = slice((first + k) * part, (first + k + 1) * part)
-        result[k] = sum(ref[here, :].astype(f32) for ref in parts)
+        result[k] = sum(ref[k * part : (k + 1) * part, :].astype(f32) for ref in parts)
 
 
 def place_shares(shares, tables, acc):
@@ -282,7 +274,7 @@
 
 def output_kernel(dims, *refs):
     slots, n_row, n_col, n_tok = dims
-    parts, (output, last, result, acc, sem) = refs[:n_col], refs[n_col:]
+    parts, (output, last, result, acc, sem) = refs[:n_col], refs[n_col + 1 :]
     rows = slots * acc.shape[1]
     last[...] = jnp.zeros(last.shape, jnp.int32)
     place_shares(parts, tables_of(parts, rows, W2_OUT, slots), acc)
@@ -304,11 +296,9 @@
         c.wait()
 
 
-def grad_kernel(*refs):
-    parts, gw1, gw2 = refs[:-2], refs[-2], refs[-1]
-    slots, part, _ = gw1.shape
-    add_shares(parts, gw1, 0)
-    add_shares([ref for ref in parts if ref.shape[0] == 2 * slots * part], gw2, slots)
+def grad_kernel(side, *refs):
+    add_shares(refs[:side], refs[-1])
+    add_shares(refs[side:-2], refs[-2])
 
 
 def near_last(n):
@@ -372,8 +362,7 @@
 
     single = S((slots * part, blk), bf16)
     side = max(1, n_tok // 2)
-    spare = [16, 16]
-    grads = tuple(single if d < side else S((slots * part + spare[d % 2], blk), bf16) for d in range(n_tok))
+    grads = (single,) * n_tok
     half = S((slots * side * part, blk), bf16)
     peer_rows = 8 * max(1, n_row - 1)
     active, hid, places, grad2, half = call(
@@ -416,35 +405,36 @@
     )(tab, places, back, *b_peers, slope, w1, taken_t)
     i_sent, g_sent = list(sent[:n_col]), list(sent[n_col:])
     early = o_parts[1:]
-    g_sent[:side] = call(
-        functools.partial(join_kernel, dims),
-        "join_shares",
-        out_shape=(S((2 * slots * part, blk), bf16),) * side,
-        in_specs=[VMEM] * (2 + side) + [ANY] * len(early),
+    g2_sent = call(
+        functools.partial(pair_kernel, dims),
+        "add_pairs",
+        out_shape=(single,) * side,
+        in_specs=[VMEM] * 2 + [ANY] * len(early),
         out_specs=(VMEM,) * side,
-    )(grad2, half, *g_sent[:side], *early)
+    )(grad2, half, *early)
     i_parts = [send(i_sent[d], "col", d) for d in near_last(n_col)]
     tok_parts = [send(g_sent[d], "tok", d) for d in range(n_tok)]
+    g2_parts = [send(g2_sent[d], "tok", d) for d in range(side)]
 
     result = S((share, row_blocks * blk), bf16)
     summed = S((slots, part, blk), f32)
     acc = pltpu.VMEM((row_blocks, share, blk), f32)
     summed = S((slots, part, blk), f32)
     sums = call(
-        grad_kernel,
+        functools.partial(grad_kernel, side),
         "add_grads",
         out_shape=(summed, summed),
-        in_specs=[VMEM] * n_tok,
+        in_specs=[VMEM] * (side + n_tok),
         out_specs=(VMEM,) * 2,
-    )(*tok_parts[:1], *tok_parts[2:], *tok_parts[1:2])
+    )(*g2_parts, *tok_parts[:1], *tok_parts[2:], *tok_parts[1:2])
     output, last = call(
         functools.partial(output_kernel, dims),
         "add_outputs",
         out_shape=(result, S((8, LANES), jnp.int32)),
-        in_specs=[VMEM] * n_col,
+        in_specs=[VMEM] * n_col + [ANY] * 1,
         out_specs=(HBM, VMEM),
         scratch_shapes=[pltpu.VMEM(result.shape, bf16), acc, pltpu.SemaphoreType.DMA],
-    )(*o_parts)
+    )(*o_parts, i_parts[1])
     grad_in, gw1, gw2 = call(
         functools.partial(input_kernel, dims),
         "add_inputs",

time: 32.1 us -> 32.7 us (1.019)
  starting transfers between devices: 16.3 us -> 17 us
    ppermute x11 -> x12, starting transfers between devices: 13.4 us -> 14.1 us  [send(): lax.ppermute(x, axis, [(i, partner(i, d, n)) for i in range(n)])]
    ppermute x11 -> x12, waiting for transfers between devices: 3.69 us -> 3.62 us  [send(): lax.ppermute(x, axis, [(i, partner(i, d, n)) for i in range(n)])]
  transfers between devices with their start and end apart: 12 -> 13, of which waited for: 4 -> 7; matrix products, arithmetic and copies ran while one was open for 0% -> 0% of each run, Pallas kernels for 20% -> 20%
where the time goes in v16:
time: 32.7 us; the launch traced here: 32.5 us
  starting transfers between devices  17 us (52%)
  Pallas kernels  9.87 us (30%)
  waiting for transfers between devices  3.62 us (11%)
  local copies, waits for them, and re-layouts  1.26 us (4%)
  between operations  0.78 us (2%)
    ppermute x12, starting transfers between devices, send(): lax.ppermute(x, axis, [(i, partner(i, d, n)) for i in range(n)])  14.1 us
    pallas_call x1, Pallas kernels, shards(): call(cotangent_kernel, 'take_cotangent', out_shape=(S((slots * rows, blk)...  3.96 us
    ppermute x12, waiting for transfers between devices, send(): lax.ppermute(x, axis, [(i, partner(i, d, n)) for i in range(n)])  3.62 us
    ppermute x1, starting transfers between devices, shards(): lax.ppermute(half, 'tok', [(i, (i + side) % n_tok) for i in range(n_tok)])  2.9 us
    pallas_call x1, Pallas kernels, shards(): call(token_kernel, 'take_tokens', TAKE_LIMIT, out_shape=message, in_specs...  2.39 us
    unnamed x16, local copies, waits for them, and re-layouts  1.26 us
    pallas_call x1, Pallas kernels, shards(): call(functools.partial(input_kernel, dims), 'add_inputs', out_shape=(resu...  0.98 us
    pallas_call x1, Pallas kernels, shards(): call(functools.partial(output_kernel, dims), 'add_outputs', out_shape=(re...  0.96 us
  transfers between devices with their start and end apart: 13, of which 7 were waited for; matrix products, arithmetic and copies ran while one was open for 0% of the time, Pallas kernels for 20%

profile of v16, /device:TPU:0, one launch (start us, length us, event | category | flops | bytes accessed | tf_op | source)
XLA Modules:
  0.0 32.5 jit_solution(8358884048501154545)
XLA Ops:
  0.6 0.0 copy-start
  0.6 0.0 copy-start.1
  0.7 0.0 copy-start.2
  0.7 0.0 copy-start.7
  0.7 2.4 %take_tokens.1 = bf16[1040,128]{1,0:T(8,128)(2,1)} custom-call(s32[8]{0:T(128)} %bitcast.13, s32[8]{0:T(128)} %bitcast.15, s32[8]{0:T(128)} %bitcast.17, s32[8]{0:T(128)} %bitcast.19, bf16[128,4096]{1,0:T(8,128)(2,1)} %tokens.3, bf16[8,128,128]{2,1,0:T(8,128)(2,1)} %bitcast.8), custom_call_target="tpu_custom_call" | custom-call | flops 33554432 | bytes 524288 | tf_op jit(solution)/shard_map/take_tokens/pallas_call | solution.py:324
  3.1 0.0 copy-start.4
  3.1 0.0 copy-start.5
  3.1 0.0 copy-start.6
  3.1 3.0 %collective-permute-start = (bf16[1040,128]{1,0:T(8,128)(2,1)}, bf16[1040,128]{1,0:T(8,128)(2,1)S(1)}, u32[]{:S(2)}, u32[]{:S(2)}) collective-permute-start(bf16[1040,128]{1,0:T(8,128)(2,1)} %take_tokens.1), channel_id=1, source_target_pairs={{0,4},{4,0},{1,5},{5,1},{2,6},{6,2},{3,7},{7,3},{8,12},{12,8},{9,1... | collective-permute-start | bytes 798728 | tf_op jit(solution)/shard_map/ppermute | solution.py:55
  6.1 0.0 copy-done
  6.1 0.0 copy-done.1
  6.1 0.0 copy-done.2
  6.1 0.0 copy-done.4
  6.1 0.0 copy-done.5
  6.1 0.0 copy-done.6
  6.1 0.0 copy-start.3
  6.2 1.2 %copy-done.3 = bf16[128,4096]{1,0:T(8,128)(2,1)S(1)} copy-done((bf16[128,4096]{1,0:T(8,128)(2,1)S(1)}, bf16[128,4096]{1,0:T(8,128)(2,1)}, u32[]{:S(2)}) %copy-start.3) | copy-done | bytes 1048600
  7.4 4.0 %take_cotangent.1 = (bf16[1024,128]{1,0:T(8,128)(2,1)S(1)}, bf16[8,128,128]{2,1,0:T(8,128)(2,1)S(1)}, bf16[8,128,128]{2,1,0:T(8,128)(2,1)S(1)}, f32[16,128,128]{...) custom-call(s32[8]{0:T(128)S(1)} %bitcast.14, s32[8]{0:T(128)S(1)} %bitcast.16, ...), custom_call_target="tpu_custom_call" | custom-call | flops 33554432 | bytes 524288 | tf_op jit(solution)/shard_map/take_cotangent/pallas_call | solution.py:341
  11.3 0.6 %collective-permute-start.4 = (bf16[1024,128]{1,0:T(8,128)(2,1)S(1)}, bf16[1024,128]{1,0:T(8,128)(2,1)S(1)}, u32[]{:S(2)}, u32[]{:S(2)}) collective-permute-start(bf16[1024,128]{1,0:T(8,128)(2,1)S(1)} %get-tuple-element.50), channel_id=1, source_target_pairs={{0,4},{4,0},{1,5},{5,1},{2,6},{6,2},{3,7},{7,3},{8,12},{12,8},{9,1... | collective-permute-start | bytes 786440 | tf_op jit(solution)/shard_map/ppermute | solution.py:55
  12.0 0.8 %collective-permute-done.refs_0_ = bf16[1040,128]{1,0:T(8,128)(2,1)S(1)} collective-permute-done((bf16[1040,128]{1,0:T(8,128)(2,1)}, bf16[1040,128]{1,0:T(8,128)(2,1)S(1)}, u32[]{:S(2)}, u32[]{:S(2)}) %collective-permute-start) | collective-permute-done | bytes 266272 | tf_op jit(solution)/shard_map/ppermute | solution.py:55
  12.7 0.5 %hidden.1 = (bf16[8,128,128]{2,1,0:T(8,128)(2,1)S(1)}, f32[16,128,128]{2,1,0:T(8,128)S(1)}, s32[8,128]{1,0:T(8,128)S(1)}, f32[8,128,128]{2,1,0:T(8,128)S(1)}, bf16[512,128]{1,0:T(8,128)(2,1)S(1)}) custom-call(s32[24,128]{1,0:T(8,128)S(1)} %get-tuple-element.38.tab, f32[16,128,128]{2,1,0:T(8,128)S(1)} %get-tuple-element.40.own, ...), custom_call_target="tpu_custom_call" | custom-call | flops 33554432 | bytes 524288 | tf_op jit(solution)/shard_map/hidden/pallas_call | solution.py:368
  13.2 2.9 %collective-permute-start.6 = (bf16[512,128]{1,0:T(8,128)(2,1)S(1)}, bf16[512,128]{1,0:T(8,128)(2,1)S(1)}, u32[]{:S(2)}, u32[]{:S(2)}) collective-permute-start(bf16[512,128]{1,0:T(8,128)(2,1)S(1)} %get-tuple-element.57), channel_id=1, source_target_pairs={{0,16},{8,24},{16,0},{24,8},{1,17},{9,25},{17,1},{25,9},{2,18},{10... | collective-permute-start | bytes 393224 | tf_op jit(solution)/shard_map/ppermute | solution.py:382
  16.1 0.4 %slope.1 = (f32[8,128,128]{2,1,0:T(8,128)S(1)}, bf16[272,128]{1,0:T(8,128)(2,1)S(1)}, bf16[272,128]{1,0:T(8,128)(2,1)S(1)}, bf16[272,128]{1,0:T(8,128)(2,1)S(1)}, bf16[272,128]{1,0:T(8,128)(2,1)S(1)}) custom-call(s32[24,128]{1,0:T(8,128)S(1)} %get-tuple-element.38.tab, bf16[16,128]{1,0:T(8,128)(2,1)S(1)} %get-tuple-element.39.row, ...), custom_call_target="tpu_custom_call" | custom-call | flops 33554432 | bytes 524288 | tf_op jit(solution)/shard_map/slope/pallas_call | solution.py:384
  16.5 1.6 %collective-permute-start.1 = (bf16[272,128]{1,0:T(8,128)(2,1)S(1)}, bf16[272,128]{1,0:T(8,128)(2,1)S(1)}, u32[]{:S(2)}, u32[]{:S(2)}) collective-permute-start(bf16[272,128]{1,0:T(8,128)(2,1)S(1)} %get-tuple-element.45), channel_id=1, source_target_pairs={{0,2},{1,3},{2,0},{3,1},{4,6},{5,7},{6,4},{7,5},{8,10},{9,11},{10,... | collective-permute-start | bytes 208904 | tf_op jit(solution)/shard_map/ppermute | solution.py:55
  18.1 0.0 collective-permute-start.2
  18.1 0.6 %collective-permute-start.3 = (bf16[272,128]{1,0:T(8,128)(2,1)S(1)}, bf16[272,128]{1,0:T(8,128)(2,1)S(1)}, u32[]{:S(2)}, u32[]{:S(2)}) collective-permute-start(bf16[272,128]{1,0:T(8,128)(2,1)S(1)} %get-tuple-element.47), channel_id=1, source_target_pairs={{0,1},{1,0},{2,3},{3,2},{4,5},{5,4},{6,7},{7,6},{8,9},{9,8},{10,11... | collective-permute-start | bytes 208904 | tf_op jit(solution)/shard_map/ppermute | solution.py:55
  18.7 0.4 %collective-permute-done.4.refs_0_ = bf16[1024,128]{1,0:T(8,128)(2,1)S(1)} collective-permute-done((bf16[1024,128]{1,0:T(8,128)(2,1)S(1)}, bf16[1024,128]{1,0:T(8,128)(2,1)S(1)}, u32[]{:S(2)}, u32[]{:S(2)}) %collective-permute-start.4) | collective-permute-done | bytes 262176 | tf_op jit(solution)/shard_map/ppermute | solution.py:55
  19.2 0.6 %back.1 = (bf16[256,128]{1,0:T(8,128)(2,1)S(1)}, bf16[256,128]{1,0:T(8,128)(2,1)S(1)}, bf16[256,128]{1,0:T(8,128)(2,1)S(1)}, bf16[256,128]{1,0:T(8,128)(2,1)S(1)...) custom-call(s32[24,128]{1,0:T(8,128)S(1)} %get-tuple-element.38.tab,, ...), custom_call_target="tpu_custom_call" | custom-call | flops 33554432 | bytes 524288 | tf_op jit(solution)/shard_map/back/pallas_call | solution.py:394
  19.8 1.6 %collective-permute-start.5 = (bf16[256,128]{1,0:T(8,128)(2,1)S(1)}, bf16[256,128]{1,0:T(8,128)(2,1)S(1)}, u32[]{:S(2)}, u32[]{:S(2)}) collective-permute-start(bf16[256,128]{1,0:T(8,128)(2,1)S(1)} %get-tuple-element.53), channel_id=1, source_target_pairs={{0,2},{1,3},{2,0},{3,1},{4,6},{5,7},{6,4},{7,5},{8,10},{9,11},{10,... | collective-permute-start | bytes 196616 | tf_op jit(solution)/shard_map/ppermute | solution.py:55
  21.4 0.0 collective-permute-done.1.refs_1_.refs_0_
  21.4 2.6 %collective-permute-start.8 = (bf16[256,128]{1,0:T(8,128)(2,1)S(1)}, bf16[256,128]{1,0:T(8,128)(2,1)S(1)}, u32[]{:S(2)}, u32[]{:S(2)}) collective-permute-start(bf16[256,128]{1,0:T(8,128)(2,1)S(1)} %get-tuple-element.61), channel_id=1, source_target_pairs={{0,16},{8,24},{16,0},{24,8},{1,17},{9,25},{17,1},{25,9},{2,18},{10... | collective-permute-start | bytes 196616 | tf_op jit(solution)/shard_map/ppermute | solution.py:55
  24.0 0.0 collective-permute-done.2.refs_2_.refs_1_
  24.0 1.3 %collective-permute-start.9 = (bf16[256,128]{1,0:T(8,128)(2,1)S(1)}, bf16[256,128]{1,0:T(8,128)(2,1)S(1)}, u32[]{:S(2)}, u32[]{:S(2)}) collective-permute-start(bf16[256,128]{1,0:T(8,128)(2,1)S(1)} %get-tuple-element.62), channel_id=1, source_target_pairs={{0,24},{8,16},{16,8},{24,0},{1,25},{9,17},{17,9},{25,1},{2,26},{10... | collective-permute-start | bytes 196616 | tf_op jit(solution)/shard_map/ppermute | solution.py:55
  25.3 0.0 collective-permute-done.3.refs_3_.refs_2_
  25.3 0.3 collective-permute-start.10
  25.6 0.0 collective-permute-done.6.half
  25.7 1.8 %collective-permute-start.7 = (bf16[256,128]{1,0:T(8,128)(2,1)S(1)}, bf16[256,128]{1,0:T(8,128)(2,1)S(1)}, u32[]{:S(2)}, u32[]{:S(2)}) collective-permute-start(bf16[256,128]{1,0:T(8,128)(2,1)S(1)} %get-tuple-element.59), channel_id=1, source_target_pairs={{0,8},{8,0},{16,24},{24,16},{1,9},{9,1},{17,25},{25,17},{2,10},{10... | collective-permute-start | bytes 196616 | tf_op jit(solution)/shard_map/ppermute | solution.py:55
  27.4 0.0 collective-permute-done.5.refs_4_.refs_5_
  27.5 0.0 collective-permute-start.11
  27.5 1.2 %collective-permute-done.8.refs_3_ = bf16[256,128]{1,0:T(8,128)(2,1)S(1)} collective-permute-done((bf16[256,128]{1,0:T(8,128)(2,1)S(1)}, bf16[256,128]{1,0:T(8,128)(2,1)S(1)}, u32[]{:S(2)}, u32[]{:S(2)}) %collective-permute-start.8) | collective-permute-done | bytes 65568 | tf_op jit(solution)/shard_map/ppermute | solution.py:55
  28.6 0.7 %collective-permute-start.12 = (bf16[256,128]{1,0:T(8,128)(2,1)S(1)}, bf16[256,128]{1,0:T(8,128)(2,1)S(1)}, u32[]{:S(2)}, u32[]{:S(2)}) collective-permute-start(bf16[256,128]{1,0:T(8,128)(2,1)S(1)} %get-tuple-element.68), channel_id=1, source_target_pairs={{0,1},{1,0},{2,3},{3,2},{4,5},{5,4},{6,7},{7,6},{8,9},{9,8},{10,11... | collective-permute-start | bytes 196616 | tf_op jit(solution)/shard_map/ppermute | solution.py:55
  29.3 1.0 %add_outputs.1 = (bf16[32,4096]{1,0:T(8,128)(2,1)}, s32[8,128]{1,0:T(8,128)S(1)}) custom-call(bf16[272,128]{1,0:T(8,128)(2,1)S(1)} %get-tuple-element.44.refs_0_, bf16[272,128]{1,0:T(8,128)(2,1)S(1)} %collective-permute-done.1.refs_1_.refs_0_, bf16[272,128]{1,0:T(8,128)(2,1)S(1)} %collective-permute-done.2.refs_2_.refs_1_, ...), custom_call_target="tpu_custom_call" | custom-call | flops 33554432 | bytes 524288 | tf_op jit(solution)/shard_map/add_outputs/pallas_call | solution.py:430
  30.3 0.1 collective-permute-done.9.refs_4_
  30.4 0.1 collective-permute-done.10.refs_5_
  30.4 0.7 %collective-permute-done.7.refs_1_ = bf16[256,128]{1,0:T(8,128)(2,1)S(1)} collective-permute-done((bf16[256,128]{1,0:T(8,128)(2,1)S(1)}, bf16[256,128]{1,0:T(8,128)(2,1)S(1)}, u32[]{:S(2)}, u32[]{:S(2)}) %collective-permute-start.7) | collective-permute-done | bytes 65568 | tf_op jit(solution)/shard_map/ppermute | solution.py:55
  31.2 0.4 %collective-permute-done.11.refs_6_ = bf16[256,128]{1,0:T(8,128)(2,1)S(1)} collective-permute-done((bf16[256,128]{1,0:T(8,128)(2,1)S(1)}, bf16[256,128]{1,0:T(8,128)(2,1)S(1)}, u32[]{:S(2)}, u32[]{:S(2)}) %collective-permute-start.11) | collective-permute-done | bytes 65568 | tf_op jit(solution)/shard_map/ppermute | solution.py:55
  31.6 0.0 collective-permute-done.12.refs_7_
  31.6 1.0 %add_inputs.1 = (bf16[32,4096]{1,0:T(8,128)(2,1)}, f32[8,32,128]{2,1,0:T(8,128)}, f32[8,32,128]{2,1,0:T(8,128)}) custom-call(s32[8,128]{1,0:T(8,128)S(1)} %get-tuple-element.55.after, f32[8,32,128]{2,1,0:T(8,128)S(1)} %get-tuple-element.64.sum1, f32[8,32,128]{2,1,0:T(8,128)S(1)} %get-tuple-element.65.sum2, bf16[272,128]{1,0:T(8,128)(2,1)S(1)} %get-tuple-element.44.refs_0_, ...), custom_call_target="tpu_custom_call" | custom-call | flops 33554432 | bytes 524288 | tf_op jit(solution)/shard_map/add_inputs/pallas_call | solution.py:438
  (3 shorter events, 0.1 us)
Async XLA Ops:
  0.6 5.5 %copy-start = (bf16[128,4096]{1,0:T(8,128)(2,1)S(1)}, bf16[128,4096]{1,0:T(8,128)(2,1)}, u32[]{:S(2)}) copy-start(bf16[128,4096]{1,0:T(8,128)(2,1)} %tokens.3) | copy-start | bytes 3145732
  0.6 5.5 %copy-start.1 = (bf16[1,1,8,128,128]{4,3,2,1,0:T(8,128)(2,1)S(1)}, bf16[1,1,8,128,128]{4,3,2,1,0:T(8,128)(2,1)}, u32[]{:S(2)}) copy-start(bf16[1,1,8,128,128]{4,3,2,1,0:T(8,128)(2,1)} %param.9) | copy-start | bytes 786436
  0.7 5.5 %copy-start.2 = (bf16[1,1,8,128,128]{4,3,2,1,0:T(8,128)(2,1)S(1)}, bf16[1,1,8,128,128]{4,3,2,1,0:T(8,128)(2,1)}, u32[]{:S(2)}) copy-start(bf16[1,1,8,128,128]{4,3,2,1,0:T(8,128)(2,1)} %param.12) | copy-start | bytes 786436
  0.7 5.5 %copy-start.7 = (s32[1,1,8]{2,1,0:T(1,128)S(1)}, s32[1,1,8]{2,1,0:T(1,128)}, u32[]{:S(2)}) copy-start(s32[1,1,8]{2,1,0:T(1,128)} %param.14) | copy-start | bytes 100
  3.1 3.1 %copy-start.4 = (s32[1,1,8]{2,1,0:T(1,128)S(1)}, s32[1,1,8]{2,1,0:T(1,128)}, u32[]{:S(2)}) copy-start(s32[1,1,8]{2,1,0:T(1,128)} %param.10) | copy-start | bytes 100
  3.1 3.1 %copy-start.5 = (s32[1,1,8]{2,1,0:T(1,128)S(1)}, s32[1,1,8]{2,1,0:T(1,128)}, u32[]{:S(2)}) copy-start(s32[1,1,8]{2,1,0:T(1,128)} %param.11) | copy-start | bytes 100
  3.1 3.1 %copy-start.6 = (s32[1,1,8]{2,1,0:T(1,128)S(1)}, s32[1,1,8]{2,1,0:T(1,128)}, u32[]{:S(2)}) copy-start(s32[1,1,8]{2,1,0:T(1,128)} %param.13) | copy-start | bytes 100
  3.1 9.6 %collective-permute-start = (bf16[1040,128]{1,0:T(8,128)(2,1)}, bf16[1040,128]{1,0:T(8,128)(2,1)S(1)}, u32[]{:S(2)}, u32[]{:S(2)}) collective-permute-start(bf16[1040,128]{1,0:T(8,128)(2,1)} %take_tokens.1), channel_id=1, source_target_pairs={{0,4},{4,0},{1,5},{5,1},{2,6},{6,2},{3,7},{7,3},{8,12},{12,8},{9,1... | collective-permute-start | bytes 798728 | tf_op jit(solution)/shard_map/ppermute | solution.py:55
  6.1 1.2 %copy-start.3 = (bf16[128,4096]{1,0:T(8,128)(2,1)S(1)}, bf16[128,4096]{1,0:T(8,128)(2,1)}, u32[]{:S(2)}) copy-start(bf16[128,4096]{1,0:T(8,128)(2,1)} %grad_out.1) | copy-start | bytes 3145732
  11.3 7.8 %collective-permute-start.4 = (bf16[1024,128]{1,0:T(8,128)(2,1)S(1)}, bf16[1024,128]{1,0:T(8,128)(2,1)S(1)}, u32[]{:S(2)}, u32[]{:S(2)}) collective-permute-start(bf16[1024,128]{1,0:T(8,128)(2,1)S(1)} %get-tuple-element.50), channel_id=1, source_target_pairs={{0,4},{4,0},{1,5},{5,1},{2,6},{6,2},{3,7},{7,3},{8,12},{12,8},{9,1... | collective-permute-start | bytes 786440 | tf_op jit(solution)/shard_map/ppermute | solution.py:55
  13.2 12.4 %collective-permute-start.6 = (bf16[512,128]{1,0:T(8,128)(2,1)S(1)}, bf16[512,128]{1,0:T(8,128)(2,1)S(1)}, u32[]{:S(2)}, u32[]{:S(2)}) collective-permute-start(bf16[512,128]{1,0:T(8,128)(2,1)S(1)} %get-tuple-element.57), channel_id=1, source_target_pairs={{0,16},{8,24},{16,0},{24,8},{1,17},{9,25},{17,1},{25,9},{2,18},{10... | collective-permute-start | bytes 393224 | tf_op jit(solution)/shard_map/ppermute | solution.py:382
  16.5 4.8 %collective-permute-start.1 = (bf16[272,128]{1,0:T(8,128)(2,1)S(1)}, bf16[272,128]{1,0:T(8,128)(2,1)S(1)}, u32[]{:S(2)}, u32[]{:S(2)}) collective-permute-start(bf16[272,128]{1,0:T(8,128)(2,1)S(1)} %get-tuple-element.45), channel_id=1, source_target_pairs={{0,2},{1,3},{2,0},{3,1},{4,6},{5,7},{6,4},{7,5},{8,10},{9,11},{10,... | collective-permute-start | bytes 208904 | tf_op jit(solution)/shard_map/ppermute | solution.py:55
  18.1 5.8 %collective-permute-start.2 = (bf16[272,128]{1,0:T(8,128)(2,1)S(1)}, bf16[272,128]{1,0:T(8,128)(2,1)S(1)}, u32[]{:S(2)}, u32[]{:S(2)}) collective-permute-start(bf16[272,128]{1,0:T(8,128)(2,1)S(1)} %get-tuple-element.46), channel_id=1, source_target_pairs={{0,3},{1,2},{2,1},{3,0},{4,7},{5,6},{6,5},{7,4},{8,11},{9,10},{10,... | collective-permute-start | bytes 208904 | tf_op jit(solution)/shard_map/ppermute | solution.py:55
  18.1 7.2 %collective-permute-start.3 = (bf16[272,128]{1,0:T(8,128)(2,1)S(1)}, bf16[272,128]{1,0:T(8,128)(2,1)S(1)}, u32[]{:S(2)}, u32[]{:S(2)}) collective-permute-start(bf16[272,128]{1,0:T(8,128)(2,1)S(1)} %get-tuple-element.47), channel_id=1, source_target_pairs={{0,1},{1,0},{2,3},{3,2},{4,5},{5,4},{6,7},{7,6},{8,9},{9,8},{10,11... | collective-permute-start | bytes 208904 | tf_op jit(solution)/shard_map/ppermute | solution.py:55
  19.8 7.7 %collective-permute-start.5 = (bf16[256,128]{1,0:T(8,128)(2,1)S(1)}, bf16[256,128]{1,0:T(8,128)(2,1)S(1)}, u32[]{:S(2)}, u32[]{:S(2)}) collective-permute-start(bf16[256,128]{1,0:T(8,128)(2,1)S(1)} %get-tuple-element.53), channel_id=1, source_target_pairs={{0,2},{1,3},{2,0},{3,1},{4,6},{5,7},{6,4},{7,5},{8,10},{9,11},{10,... | collective-permute-start | bytes 196616 | tf_op jit(solution)/shard_map/ppermute | solution.py:55
  21.4 7.3 %collective-permute-start.8 = (bf16[256,128]{1,0:T(8,128)(2,1)S(1)}, bf16[256,128]{1,0:T(8,128)(2,1)S(1)}, u32[]{:S(2)}, u32[]{:S(2)}) collective-permute-start(bf16[256,128]{1,0:T(8,128)(2,1)S(1)} %get-tuple-element.61), channel_id=1, source_target_pairs={{0,16},{8,24},{16,0},{24,8},{1,17},{9,25},{17,1},{25,9},{2,18},{10... | collective-permute-start | bytes 196616 | tf_op jit(solution)/shard_map/ppermute | solution.py:55
  24.0 6.4 %collective-permute-start.9 = (bf16[256,128]{1,0:T(8,128)(2,1)S(1)}, bf16[256,128]{1,0:T(8,128)(2,1)S(1)}, u32[]{:S(2)}, u32[]{:S(2)}) collective-permute-start(bf16[256,128]{1,0:T(8,128)(2,1)S(1)} %get-tuple-element.62), channel_id=1, source_target_pairs={{0,24},{8,16},{16,8},{24,0},{1,25},{9,17},{17,9},{25,1},{2,26},{10... | collective-permute-start | bytes 196616 | tf_op jit(solution)/shard_map/ppermute | solution.py:55
  25.3 5.1 %collective-permute-start.10 = (bf16[256,128]{1,0:T(8,128)(2,1)S(1)}, bf16[256,128]{1,0:T(8,128)(2,1)S(1)}, u32[]{:S(2)}, u32[]{:S(2)}) collective-permute-start(bf16[256,128]{1,0:T(8,128)(2,1)S(1)} %get-tuple-element.63), channel_id=1, source_target_pairs={{0,8},{8,0},{16,24},{24,16},{1,9},{9,1},{17,25},{25,17},{2,10},{10... | collective-permute-start | bytes 196616 | tf_op jit(solution)/shard_map/ppermute | solution.py:55
  25.7 5.5 %collective-permute-start.7 = (bf16[256,128]{1,0:T(8,128)(2,1)S(1)}, bf16[256,128]{1,0:T(8,128)(2,1)S(1)}, u32[]{:S(2)}, u32[]{:S(2)}) collective-permute-start(bf16[256,128]{1,0:T(8,128)(2,1)S(1)} %get-tuple-element.59), channel_id=1, source_target_pairs={{0,8},{8,0},{16,24},{24,16},{1,9},{9,1},{17,25},{25,17},{2,10},{10... | collective-permute-start | bytes 196616 | tf_op jit(solution)/shard_map/ppermute | solution.py:55
  27.5 4.1 %collective-permute-start.11 = (bf16[256,128]{1,0:T(8,128)(2,1)S(1)}, bf16[256,128]{1,0:T(8,128)(2,1)S(1)}, u32[]{:S(2)}, u32[]{:S(2)}) collective-permute-start(bf16[256,128]{1,0:T(8,128)(2,1)S(1)} %get-tuple-element.67), channel_id=1, source_target_pairs={{0,3},{1,2},{2,1},{3,0},{4,7},{5,6},{6,5},{7,4},{8,11},{9,10},{10,... | collective-permute-start | bytes 196616 | tf_op jit(solution)/shard_map/ppermute | solution.py:55
  28.6 2.9 %collective-permute-start.12 = (bf16[256,128]{1,0:T(8,128)(2,1)S(1)}, bf16[256,128]{1,0:T(8,128)(2,1)S(1)}, u32[]{:S(2)}, u32[]{:S(2)}) collective-permute-start(bf16[256,128]{1,0:T(8,128)(2,1)S(1)} %get-tuple-element.68), channel_id=1, source_target_pairs={{0,1},{1,0},{2,3},{3,2},{4,5},{5,4},{6,7},{7,6},{8,9},{9,8},{10,11... | collective-permute-start | bytes 196616 | tf_op jit(solution)/shard_map/ppermute | solution.py:55

commit v17 on v16

--- a/solution.py
+++ b/solution.py
@@ -274,7 +274,7 @@
 
 def output_kernel(dims, *refs):
     slots, n_row, n_col, n_tok = dims
-    parts, (output, last, result, acc, sem) = refs[:n_col], refs[n_col + 1 :]
+    parts, (output, last, result, acc, sem) = refs[:n_col], refs[-5:]
     rows = slots * acc.shape[1]
     last[...] = jnp.zeros(last.shape, jnp.int32)
     place_shares(parts, tables_of(parts, rows, W2_OUT, slots), acc)
@@ -427,14 +427,15 @@
         in_specs=[VMEM] * (side + n_tok),
         out_specs=(VMEM,) * 2,
     )(*g2_parts, *tok_parts[:1], *tok_parts[2:], *tok_parts[1:2])
+    ahead = tok_parts[2:3] + i_parts[1:3]
     output, last = call(
         functools.partial(output_kernel, dims),
         "add_outputs",
         out_shape=(result, S((8, LANES), jnp.int32)),
-        in_specs=[VMEM] * n_col + [ANY] * 1,
+        in_specs=[VMEM] * n_col + [ANY] * len(ahead),
         out_specs=(HBM, VMEM),
         scratch_shapes=[pltpu.VMEM(result.shape, bf16), acc, pltpu.SemaphoreType.DMA],
-    )(*o_parts, i_parts[1])
+    )(*o_parts, *ahead)
     grad_in, gw1, gw2 = call(
         functools.partial(input_kernel, dims),
         "add_inputs",

time: 32.7 us -> 33.7 us (1.031)
  waiting for transfers between devices: 3.62 us -> 5.16 us
  starting transfers between devices: 17 us -> 16.4 us
    ppermute x12, waiting for transfers between devices: 3.62 us -> 5.16 us  [send(): lax.ppermute(x, axis, [(i, partner(i, d, n)) for i in range(n)])]
    ppermute x12, starting transfers between devices: 14.1 us -> 13.5 us  [send(): lax.ppermute(x, axis, [(i, partner(i, d, n)) for i in range(n)])]
  transfers between devices with their start and end apart: 13 -> 13, of which waited for: 7 -> 6; matrix products, arithmetic and copies ran while one was open for 0% -> 0% of each run, Pallas kernels for 20% -> 19%
where the time goes in v17:
time: 33.7 us; the launch traced here: 33.5 us
  starting transfers between devices  16.4 us (49%)
  Pallas kernels  9.88 us (29%)
  waiting for transfers between devices  5.16 us (15%)
  local copies, waits for them, and re-layouts  1.26 us (4%)
  between operations  0.8 us (2%)
    ppermute x12, starting transfers between devices, send(): lax.ppermute(x, axis, [(i, partner(i, d, n)) for i in range(n)])  13.5 us
    ppermute x12, waiting for transfers between devices, send(): lax.ppermute(x, axis, [(i, partner(i, d, n)) for i in range(n)])  5.16 us
    pallas_call x1, Pallas kernels, shards(): call(cotangent_kernel, 'take_cotangent', out_shape=(S((slots * rows, blk)...  3.96 us
    ppermute x1, starting transfers between devices, shards(): lax.ppermute(half, 'tok', [(i, (i + side) % n_tok) for i in range(n_tok)])  2.9 us
    pallas_call x1, Pallas kernels, shards(): call(token_kernel, 'take_tokens', TAKE_LIMIT, out_shape=message, in_specs...  2.39 us
    unnamed x16, local copies, waits for them, and re-layouts  1.26 us
    pallas_call x1, Pallas kernels, shards(): call(functools.partial(input_kernel, dims), 'add_inputs', out_shape=(resu...  0.98 us
    pallas_call x1, Pallas kernels, shards(): call(functools.partial(output_kernel, dims), 'add_outputs', out_shape=(re...  0.96 us
  transfers between devices with their start and end apart: 13, of which 6 were waited for; matrix products, arithmetic and copies ran while one was open for 0% of the time, Pallas kernels for 19%

profile of v17, /device:TPU:0, one launch (start us, length us, event | category | flops | bytes accessed | tf_op | source)
XLA Modules:
  0.0 33.5 jit_solution(3595938840625948543)
XLA Ops:
  0.6 0.0 copy-start
  0.6 0.0 copy-start.1
  0.7 0.0 copy-start.2
  0.7 0.0 copy-start.7
  0.7 2.4 %take_tokens.1 = bf16[1040,128]{1,0:T(8,128)(2,1)} custom-call(s32[8]{0:T(128)} %bitcast.13, s32[8]{0:T(128)} %bitcast.15, s32[8]{0:T(128)} %bitcast.17, s32[8]{0:T(128)} %bitcast.19, bf16[128,4096]{1,0:T(8,128)(2,1)} %tokens.3, bf16[8,128,128]{2,1,0:T(8,128)(2,1)} %bitcast.8), custom_call_target="tpu_custom_call" | custom-call | flops 33554432 | bytes 524288 | tf_op jit(solution)/shard_map/take_tokens/pallas_call | solution.py:324
  3.1 0.0 copy-start.4
  3.1 0.0 copy-start.5
  3.1 0.0 copy-start.6
  3.1 3.0 %collective-permute-start = (bf16[1040,128]{1,0:T(8,128)(2,1)}, bf16[1040,128]{1,0:T(8,128)(2,1)S(1)}, u32[]{:S(2)}, u32[]{:S(2)}) collective-permute-start(bf16[1040,128]{1,0:T(8,128)(2,1)} %take_tokens.1), channel_id=1, source_target_pairs={{0,4},{4,0},{1,5},{5,1},{2,6},{6,2},{3,7},{7,3},{8,12},{12,8},{9,1... | collective-permute-start | bytes 798728 | tf_op jit(solution)/shard_map/ppermute | solution.py:55
  6.1 0.0 copy-done
  6.1 0.0 copy-done.1
  6.1 0.0 copy-done.2
  6.1 0.0 copy-done.7
  6.1 0.0 copy-done.4
  6.1 0.0 copy-done.5
  6.2 0.0 copy-start.3
  6.2 1.2 %copy-done.3 = bf16[128,4096]{1,0:T(8,128)(2,1)S(1)} copy-done((bf16[128,4096]{1,0:T(8,128)(2,1)S(1)}, bf16[128,4096]{1,0:T(8,128)(2,1)}, u32[]{:S(2)}) %copy-start.3) | copy-done | bytes 1048600
  7.4 4.0 %take_cotangent.1 = (bf16[1024,128]{1,0:T(8,128)(2,1)S(1)}, bf16[8,128,128]{2,1,0:T(8,128)(2,1)S(1)}, bf16[8,128,128]{2,1,0:T(8,128)(2,1)S(1)}, f32[16,128,128]{...) custom-call(s32[8]{0:T(128)S(1)} %bitcast.14, s32[8]{0:T(128)S(1)} %bitcast.16, ...), custom_call_target="tpu_custom_call" | custom-call | flops 33554432 | bytes 524288 | tf_op jit(solution)/shard_map/take_cotangent/pallas_call | solution.py:341
  11.3 0.6 %collective-permute-start.4 = (bf16[1024,128]{1,0:T(8,128)(2,1)S(1)}, bf16[1024,128]{1,0:T(8,128)(2,1)S(1)}, u32[]{:S(2)}, u32[]{:S(2)}) collective-permute-start(bf16[1024,128]{1,0:T(8,128)(2,1)S(1)} %get-tuple-element.50), channel_id=1, source_target_pairs={{0,4},{4,0},{1,5},{5,1},{2,6},{6,2},{3,7},{7,3},{8,12},{12,8},{9,1... | collective-permute-start | bytes 786440 | tf_op jit(solution)/shard_map/ppermute | solution.py:55
  12.0 0.8 %collective-permute-done.refs_0_ = bf16[1040,128]{1,0:T(8,128)(2,1)S(1)} collective-permute-done((bf16[1040,128]{1,0:T(8,128)(2,1)}, bf16[1040,128]{1,0:T(8,128)(2,1)S(1)}, u32[]{:S(2)}, u32[]{:S(2)}) %collective-permute-start) | collective-permute-done | bytes 266272 | tf_op jit(solution)/shard_map/ppermute | solution.py:55
  12.7 0.5 %hidden.1 = (bf16[8,128,128]{2,1,0:T(8,128)(2,1)S(1)}, f32[16,128,128]{2,1,0:T(8,128)S(1)}, s32[8,128]{1,0:T(8,128)S(1)}, f32[8,128,128]{2,1,0:T(8,128)S(1)}, bf16[512,128]{1,0:T(8,128)(2,1)S(1)}) custom-call(s32[24,128]{1,0:T(8,128)S(1)} %get-tuple-element.38.tab, f32[16,128,128]{2,1,0:T(8,128)S(1)} %get-tuple-element.40.own, ...), custom_call_target="tpu_custom_call" | custom-call | flops 33554432 | bytes 524288 | tf_op jit(solution)/shard_map/hidden/pallas_call | solution.py:368
  13.2 2.9 %collective-permute-start.8 = (bf16[512,128]{1,0:T(8,128)(2,1)S(1)}, bf16[512,128]{1,0:T(8,128)(2,1)S(1)}, u32[]{:S(2)}, u32[]{:S(2)}) collective-permute-start(bf16[512,128]{1,0:T(8,128)(2,1)S(1)} %get-tuple-element.59), channel_id=1, source_target_pairs={{0,16},{8,24},{16,0},{24,8},{1,17},{9,25},{17,1},{25,9},{2,18},{10... | collective-permute-start | bytes 393224 | tf_op jit(solution)/shard_map/ppermute | solution.py:382
  16.2 0.4 %slope.1 = (f32[8,128,128]{2,1,0:T(8,128)S(1)}, bf16[272,128]{1,0:T(8,128)(2,1)S(1)}, bf16[272,128]{1,0:T(8,128)(2,1)S(1)}, bf16[272,128]{1,0:T(8,128)(2,1)S(1)}, bf16[272,128]{1,0:T(8,128)(2,1)S(1)}) custom-call(s32[24,128]{1,0:T(8,128)S(1)} %get-tuple-element.38.tab, bf16[16,128]{1,0:T(8,128)(2,1)S(1)} %get-tuple-element.39.row, ...), custom_call_target="tpu_custom_call" | custom-call | flops 33554432 | bytes 524288 | tf_op jit(solution)/shard_map/slope/pallas_call | solution.py:384
  16.5 1.6 %collective-permute-start.1 = (bf16[272,128]{1,0:T(8,128)(2,1)S(1)}, bf16[272,128]{1,0:T(8,128)(2,1)S(1)}, u32[]{:S(2)}, u32[]{:S(2)}) collective-permute-start(bf16[272,128]{1,0:T(8,128)(2,1)S(1)} %get-tuple-element.45), channel_id=1, source_target_pairs={{0,2},{1,3},{2,0},{3,1},{4,6},{5,7},{6,4},{7,5},{8,10},{9,11},{10,... | collective-permute-start | bytes 208904 | tf_op jit(solution)/shard_map/ppermute | solution.py:55
  18.1 0.0 collective-permute-start.2
  18.1 0.6 %collective-permute-start.3 = (bf16[272,128]{1,0:T(8,128)(2,1)S(1)}, bf16[272,128]{1,0:T(8,128)(2,1)S(1)}, u32[]{:S(2)}, u32[]{:S(2)}) collective-permute-start(bf16[272,128]{1,0:T(8,128)(2,1)S(1)} %get-tuple-element.47), channel_id=1, source_target_pairs={{0,1},{1,0},{2,3},{3,2},{4,5},{5,4},{6,7},{7,6},{8,9},{9,8},{10,11... | collective-permute-start | bytes 208904 | tf_op jit(solution)/shard_map/ppermute | solution.py:55
  18.8 0.4 %collective-permute-done.4.refs_0_ = bf16[1024,128]{1,0:T(8,128)(2,1)S(1)} collective-permute-done((bf16[1024,128]{1,0:T(8,128)(2,1)S(1)}, bf16[1024,128]{1,0:T(8,128)(2,1)S(1)}, u32[]{:S(2)}, u32[]{:S(2)}) %collective-permute-start.4) | collective-permute-done | bytes 262176 | tf_op jit(solution)/shard_map/ppermute | solution.py:55
  19.2 0.6 %back.1 = (bf16[256,128]{1,0:T(8,128)(2,1)S(1)}, bf16[256,128]{1,0:T(8,128)(2,1)S(1)}, bf16[256,128]{1,0:T(8,128)(2,1)S(1)}, bf16[256,128]{1,0:T(8,128)(2,1)S(1)...) custom-call(s32[24,128]{1,0:T(8,128)S(1)} %get-tuple-element.38.tab,, ...), custom_call_target="tpu_custom_call" | custom-call | flops 33554432 | bytes 524288 | tf_op jit(solution)/shard_map/back/pallas_call | solution.py:394
  19.8 2.7 %collective-permute-start.5 = (bf16[256,128]{1,0:T(8,128)(2,1)S(1)}, bf16[256,128]{1,0:T(8,128)(2,1)S(1)}, u32[]{:S(2)}, u32[]{:S(2)}) collective-permute-start(bf16[256,128]{1,0:T(8,128)(2,1)S(1)} %get-tuple-element.53), channel_id=1, source_target_pairs={{0,16},{8,24},{16,0},{24,8},{1,17},{9,25},{17,1},{25,9},{2,18},{10... | collective-permute-start | bytes 196616 | tf_op jit(solution)/shard_map/ppermute | solution.py:55
  22.4 0.0 collective-permute-done.1.refs_1_.refs_0_
  22.4 1.5 %collective-permute-start.6 = (bf16[256,128]{1,0:T(8,128)(2,1)S(1)}, bf16[256,128]{1,0:T(8,128)(2,1)S(1)}, u32[]{:S(2)}, u32[]{:S(2)}) collective-permute-start(bf16[256,128]{1,0:T(8,128)(2,1)S(1)} %get-tuple-element.54), channel_id=1, source_target_pairs={{0,2},{1,3},{2,0},{3,1},{4,6},{5,7},{6,4},{7,5},{8,10},{9,11},{10,... | collective-permute-start | bytes 196616 | tf_op jit(solution)/shard_map/ppermute | solution.py:55
  24.0 0.0 collective-permute-done.2.refs_2_.refs_1_
  24.0 0.0 collective-permute-start.7
  24.0 0.0 collective-permute-done.3.refs_3_.refs_2_
  24.0 1.4 %collective-permute-start.10 = (bf16[256,128]{1,0:T(8,128)(2,1)S(1)}, bf16[256,128]{1,0:T(8,128)(2,1)S(1)}, u32[]{:S(2)}, u32[]{:S(2)}) collective-permute-start(bf16[256,128]{1,0:T(8,128)(2,1)S(1)} %get-tuple-element.63), channel_id=1, source_target_pairs={{0,24},{8,16},{16,8},{24,0},{1,25},{9,17},{17,9},{25,1},{2,26},{10... | collective-permute-start | bytes 196616 | tf_op jit(solution)/shard_map/ppermute | solution.py:55
  25.4 0.0 collective-permute-done.8.half
  25.4 0.3 collective-permute-start.11
  25.7 0.0 collective-permute-done.5.refs_4_.refs_3_
  25.8 1.8 %collective-permute-start.9 = (bf16[256,128]{1,0:T(8,128)(2,1)S(1)}, bf16[256,128]{1,0:T(8,128)(2,1)S(1)}, u32[]{:S(2)}, u32[]{:S(2)}) collective-permute-start(bf16[256,128]{1,0:T(8,128)(2,1)S(1)} %get-tuple-element.61), channel_id=1, source_target_pairs={{0,8},{8,0},{16,24},{24,16},{1,9},{9,1},{17,25},{25,17},{2,10},{10... | collective-permute-start | bytes 196616 | tf_op jit(solution)/shard_map/ppermute | solution.py:55
  27.5 0.0 collective-permute-done.6.refs_5_
  27.5 0.0 collective-permute-start.12
  27.5 0.6 %collective-permute-done.7.refs_6_ = bf16[256,128]{1,0:T(8,128)(2,1)S(1)} collective-permute-done((bf16[256,128]{1,0:T(8,128)(2,1)S(1)}, bf16[256,128]{1,0:T(8,128)(2,1)S(1)}, u32[]{:S(2)}, u32[]{:S(2)}) %collective-permute-start.7) | collective-permute-done | bytes 65568 | tf_op jit(solution)/shard_map/ppermute | solution.py:55
  28.1 1.0 %add_outputs.1 = (bf16[32,4096]{1,0:T(8,128)(2,1)}, s32[8,128]{1,0:T(8,128)S(1)}) custom-call(bf16[272,128]{1,0:T(8,128)(2,1)S(1)} %get-tuple-element.44.refs_0_, bf16[272,128]{1,0:T(8,128)(2,1)S(1)} %collective-permute-done.1.refs_1_.refs_0_, bf16[272,128]{1,0:T(8,128)(2,1)S(1)} %collective-permute-done.2.refs_2_.refs_1_, ...), custom_call_target="tpu_custom_call" | custom-call | flops 33554432 | bytes 524288 | tf_op jit(solution)/shard_map/add_outputs/pallas_call | solution.py:431
  29.1 1.7 %collective-permute-done.10.refs_4_ = bf16[256,128]{1,0:T(8,128)(2,1)S(1)} collective-permute-done((bf16[256,128]{1,0:T(8,128)(2,1)S(1)}, bf16[256,128]{1,0:T(8,128)(2,1)S(1)}, u32[]{:S(2)}, u32[]{:S(2)}) %collective-permute-start.10) | collective-permute-done | bytes 65568 | tf_op jit(solution)/shard_map/ppermute | solution.py:55
  30.8 0.9 %collective-permute-done.11.refs_5_ = bf16[256,128]{1,0:T(8,128)(2,1)S(1)} collective-permute-done((bf16[256,128]{1,0:T(8,128)(2,1)S(1)}, bf16[256,128]{1,0:T(8,128)(2,1)S(1)}, u32[]{:S(2)}, u32[]{:S(2)}) %collective-permute-start.11) | collective-permute-done | bytes 65568 | tf_op jit(solution)/shard_map/ppermute | solution.py:55
  31.7 0.7 %collective-permute-done.9.refs_1_ = bf16[256,128]{1,0:T(8,128)(2,1)S(1)} collective-permute-done((bf16[256,128]{1,0:T(8,128)(2,1)S(1)}, bf16[256,128]{1,0:T(8,128)(2,1)S(1)}, u32[]{:S(2)}, u32[]{:S(2)}) %collective-permute-start.9) | collective-permute-done | bytes 65568 | tf_op jit(solution)/shard_map/ppermute | solution.py:55
  32.5 0.0 collective-permute-done.12.refs_7_
  32.5 1.0 %add_inputs.1 = (bf16[32,4096]{1,0:T(8,128)(2,1)}, f32[8,32,128]{2,1,0:T(8,128)}, f32[8,32,128]{2,1,0:T(8,128)}) custom-call(s32[8,128]{1,0:T(8,128)S(1)} %get-tuple-element.57.after, f32[8,32,128]{2,1,0:T(8,128)S(1)} %get-tuple-element.65.sum1, f32[8,32,128]{2,1,0:T(8,128)S(1)} %get-tuple-element.66.sum2, bf16[272,128]{1,0:T(8,128)(2,1)S(1)} %get-tuple-element.44.refs_0_, ...), custom_call_target="tpu_custom_call" | custom-call | flops 33554432 | bytes 524288 | tf_op jit(solution)/shard_map/add_inputs/pallas_call | solution.py:439
  (3 shorter events, 0.1 us)
Async XLA Ops:
  0.6 5.5 %copy-start = (bf16[128,4096]{1,0:T(8,128)(2,1)S(1)}, bf16[128,4096]{1,0:T(8,128)(2,1)}, u32[]{:S(2)}) copy-start(bf16[128,4096]{1,0:T(8,128)(2,1)} %tokens.3) | copy-start | bytes 3145732
  0.6 5.5 %copy-start.1 = (bf16[1,1,8,128,128]{4,3,2,1,0:T(8,128)(2,1)S(1)}, bf16[1,1,8,128,128]{4,3,2,1,0:T(8,128)(2,1)}, u32[]{:S(2)}) copy-start(bf16[1,1,8,128,128]{4,3,2,1,0:T(8,128)(2,1)} %param.9) | copy-start | bytes 786436
  0.7 5.5 %copy-start.2 = (bf16[1,1,8,128,128]{4,3,2,1,0:T(8,128)(2,1)S(1)}, bf16[1,1,8,128,128]{4,3,2,1,0:T(8,128)(2,1)}, u32[]{:S(2)}) copy-start(bf16[1,1,8,128,128]{4,3,2,1,0:T(8,128)(2,1)} %param.12) | copy-start | bytes 786436
  0.7 5.5 %copy-start.7 = (s32[1,1,8]{2,1,0:T(1,128)S(1)}, s32[1,1,8]{2,1,0:T(1,128)}, u32[]{:S(2)}) copy-start(s32[1,1,8]{2,1,0:T(1,128)} %param.14) | copy-start | bytes 100
  3.1 3.1 %copy-start.4 = (s32[1,1,8]{2,1,0:T(1,128)S(1)}, s32[1,1,8]{2,1,0:T(1,128)}, u32[]{:S(2)}) copy-start(s32[1,1,8]{2,1,0:T(1,128)} %param.10) | copy-start | bytes 100
  3.1 3.1 %copy-start.5 = (s32[1,1,8]{2,1,0:T(1,128)S(1)}, s32[1,1,8]{2,1,0:T(1,128)}, u32[]{:S(2)}) copy-start(s32[1,1,8]{2,1,0:T(1,128)} %param.11) | copy-start | bytes 100
  3.1 3.1 %copy-start.6 = (s32[1,1,8]{2,1,0:T(1,128)S(1)}, s32[1,1,8]{2,1,0:T(1,128)}, u32[]{:S(2)}) copy-start(s32[1,1,8]{2,1,0:T(1,128)} %param.13) | copy-start | bytes 100
  3.1 9.6 %collective-permute-start = (bf16[1040,128]{1,0:T(8,128)(2,1)}, bf16[1040,128]{1,0:T(8,128)(2,1)S(1)}, u32[]{:S(2)}, u32[]{:S(2)}) collective-permute-start(bf16[1040,128]{1,0:T(8,128)(2,1)} %take_tokens.1), channel_id=1, source_target_pairs={{0,4},{4,0},{1,5},{5,1},{2,6},{6,2},{3,7},{7,3},{8,12},{12,8},{9,1... | collective-permute-start | bytes 798728 | tf_op jit(solution)/shard_map/ppermute | solution.py:55
  6.2 1.2 %copy-start.3 = (bf16[128,4096]{1,0:T(8,128)(2,1)S(1)}, bf16[128,4096]{1,0:T(8,128)(2,1)}, u32[]{:S(2)}) copy-start(bf16[128,4096]{1,0:T(8,128)(2,1)} %grad_out.1) | copy-start | bytes 3145732
  11.3 7.8 %collective-permute-start.4 = (bf16[1024,128]{1,0:T(8,128)(2,1)S(1)}, bf16[1024,128]{1,0:T(8,128)(2,1)S(1)}, u32[]{:S(2)}, u32[]{:S(2)}) collective-permute-start(bf16[1024,128]{1,0:T(8,128)(2,1)S(1)} %get-tuple-element.50), channel_id=1, source_target_pairs={{0,4},{4,0},{1,5},{5,1},{2,6},{6,2},{3,7},{7,3},{8,12},{12,8},{9,1... | collective-permute-start | bytes 786440 | tf_op jit(solution)/shard_map/ppermute | solution.py:55
  13.2 12.1 %collective-permute-start.8 = (bf16[512,128]{1,0:T(8,128)(2,1)S(1)}, bf16[512,128]{1,0:T(8,128)(2,1)S(1)}, u32[]{:S(2)}, u32[]{:S(2)}) collective-permute-start(bf16[512,128]{1,0:T(8,128)(2,1)S(1)} %get-tuple-element.59), channel_id=1, source_target_pairs={{0,16},{8,24},{16,0},{24,8},{1,17},{9,25},{17,1},{25,9},{2,18},{10... | collective-permute-start | bytes 393224 | tf_op jit(solution)/shard_map/ppermute | solution.py:382
  16.5 5.9 %collective-permute-start.1 = (bf16[272,128]{1,0:T(8,128)(2,1)S(1)}, bf16[272,128]{1,0:T(8,128)(2,1)S(1)}, u32[]{:S(2)}, u32[]{:S(2)}) collective-permute-start(bf16[272,128]{1,0:T(8,128)(2,1)S(1)} %get-tuple-element.45), channel_id=1, source_target_pairs={{0,2},{1,3},{2,0},{3,1},{4,6},{5,7},{6,4},{7,5},{8,10},{9,11},{10,... | collective-permute-start | bytes 208904 | tf_op jit(solution)/shard_map/ppermute | solution.py:55
  18.1 5.8 %collective-permute-start.2 = (bf16[272,128]{1,0:T(8,128)(2,1)S(1)}, bf16[272,128]{1,0:T(8,128)(2,1)S(1)}, u32[]{:S(2)}, u32[]{:S(2)}) collective-permute-start(bf16[272,128]{1,0:T(8,128)(2,1)S(1)} %get-tuple-element.46), channel_id=1, source_target_pairs={{0,3},{1,2},{2,1},{3,0},{4,7},{5,6},{6,5},{7,4},{8,11},{9,10},{10,... | collective-permute-start | bytes 208904 | tf_op jit(solution)/shard_map/ppermute | solution.py:55
  18.1 5.8 %collective-permute-start.3 = (bf16[272,128]{1,0:T(8,128)(2,1)S(1)}, bf16[272,128]{1,0:T(8,128)(2,1)S(1)}, u32[]{:S(2)}, u32[]{:S(2)}) collective-permute-start(bf16[272,128]{1,0:T(8,128)(2,1)S(1)} %get-tuple-element.47), channel_id=1, source_target_pairs={{0,1},{1,0},{2,3},{3,2},{4,5},{5,4},{6,7},{7,6},{8,9},{9,8},{10,11... | collective-permute-start | bytes 208904 | tf_op jit(solution)/shard_map/ppermute | solution.py:55
  19.8 6.0 %collective-permute-start.5 = (bf16[256,128]{1,0:T(8,128)(2,1)S(1)}, bf16[256,128]{1,0:T(8,128)(2,1)S(1)}, u32[]{:S(2)}, u32[]{:S(2)}) collective-permute-start(bf16[256,128]{1,0:T(8,128)(2,1)S(1)} %get-tuple-element.53), channel_id=1, source_target_pairs={{0,16},{8,24},{16,0},{24,8},{1,17},{9,25},{17,1},{25,9},{2,18},{10... | collective-permute-start | bytes 196616 | tf_op jit(solution)/shard_map/ppermute | solution.py:55
  22.4 5.1 %collective-permute-start.6 = (bf16[256,128]{1,0:T(8,128)(2,1)S(1)}, bf16[256,128]{1,0:T(8,128)(2,1)S(1)}, u32[]{:S(2)}, u32[]{:S(2)}) collective-permute-start(bf16[256,128]{1,0:T(8,128)(2,1)S(1)} %get-tuple-element.54), channel_id=1, source_target_pairs={{0,2},{1,3},{2,0},{3,1},{4,6},{5,7},{6,4},{7,5},{8,10},{9,11},{10,... | collective-permute-start | bytes 196616 | tf_op jit(solution)/shard_map/ppermute | solution.py:55
  24.0 4.1 %collective-permute-start.7 = (bf16[256,128]{1,0:T(8,128)(2,1)S(1)}, bf16[256,128]{1,0:T(8,128)(2,1)S(1)}, u32[]{:S(2)}, u32[]{:S(2)}) collective-permute-start(bf16[256,128]{1,0:T(8,128)(2,1)S(1)} %get-tuple-element.55), channel_id=1, source_target_pairs={{0,3},{1,2},{2,1},{3,0},{4,7},{5,6},{6,5},{7,4},{8,11},{9,10},{10,... | collective-permute-start | bytes 196616 | tf_op jit(solution)/shard_map/ppermute | solution.py:55
  24.0 6.8 %collective-permute-start.10 = (bf16[256,128]{1,0:T(8,128)(2,1)S(1)}, bf16[256,128]{1,0:T(8,128)(2,1)S(1)}, u32[]{:S(2)}, u32[]{:S(2)}) collective-permute-start(bf16[256,128]{1,0:T(8,128)(2,1)S(1)} %get-tuple-element.63), channel_id=1, source_target_pairs={{0,24},{8,16},{16,8},{24,0},{1,25},{9,17},{17,9},{25,1},{2,26},{10... | collective-permute-start | bytes 196616 | tf_op jit(solution)/shard_map/ppermute | solution.py:55
  25.4 6.3 %collective-permute-start.11 = (bf16[256,128]{1,0:T(8,128)(2,1)S(1)}, bf16[256,128]{1,0:T(8,128)(2,1)S(1)}, u32[]{:S(2)}, u32[]{:S(2)}) collective-permute-start(bf16[256,128]{1,0:T(8,128)(2,1)S(1)} %get-tuple-element.64), channel_id=1, source_target_pairs={{0,8},{8,0},{16,24},{24,16},{1,9},{9,1},{17,25},{25,17},{2,10},{10... | collective-permute-start | bytes 196616 | tf_op jit(solution)/shard_map/ppermute | solution.py:55
  25.8 6.7 %collective-permute-start.9 = (bf16[256,128]{1,0:T(8,128)(2,1)S(1)}, bf16[256,128]{1,0:T(8,128)(2,1)S(1)}, u32[]{:S(2)}, u32[]{:S(2)}) collective-permute-start(bf16[256,128]{1,0:T(8,128)(2,1)S(1)} %get-tuple-element.61), channel_id=1, source_target_pairs={{0,8},{8,0},{16,24},{24,16},{1,9},{9,1},{17,25},{25,17},{2,10},{10... | collective-permute-start | bytes 196616 | tf_op jit(solution)/shard_map/ppermute | solution.py:55
  27.5 5.0 %collective-permute-start.12 = (bf16[256,128]{1,0:T(8,128)(2,1)S(1)}, bf16[256,128]{1,0:T(8,128)(2,1)S(1)}, u32[]{:S(2)}, u32[]{:S(2)}) collective-permute-start(bf16[256,128]{1,0:T(8,128)(2,1)S(1)} %get-tuple-element.68), channel_id=1, source_target_pairs={{0,1},{1,0},{2,3},{3,2},{4,5},{5,4},{6,7},{7,6},{8,9},{9,8},{10,11... | collective-permute-start | bytes 196616 | tf_op jit(solution)/shard_map/ppermute | solution.py:55

commit v18 on v15

--- a/solution.py
+++ b/solution.py
@@ -436,7 +436,7 @@
         out_shape=(summed, summed),
         in_specs=[VMEM] * n_tok,
         out_specs=(VMEM,) * 2,
-    )(*tok_parts[:1], *tok_parts[2:], *tok_parts[1:2])
+    )(*tok_parts[::-1])
     output, last = call(
         functools.partial(output_kernel, dims),
         "add_outputs",

time: 32.1 us -> 33.1 us (1.031)
  starting transfers between devices: 16.3 us -> 17.3 us
    ppermute x11, starting transfers between devices: 13.4 us -> 14.4 us  [send(): lax.ppermute(x, axis, [(i, partner(i, d, n)) for i in range(n)])]
  transfers between devices with their start and end apart: 12 -> 12, of which waited for: 4 -> 6; matrix products, arithmetic and copies ran while one was open for 0% -> 0% of each run, Pallas kernels for 20% -> 20%
where the time goes in v18:
time: 33.1 us; the launch traced here: 32.9 us
  starting transfers between devices  17.3 us (52%)
  Pallas kernels  9.87 us (30%)
  waiting for transfers between devices  3.71 us (11%)
  local copies, waits for them, and re-layouts  1.26 us (4%)
  between operations  0.79 us (2%)
    ppermute x11, starting transfers between devices, send(): lax.ppermute(x, axis, [(i, partner(i, d, n)) for i in range(n)])  14.4 us
    pallas_call x1, Pallas kernels, shards(): call(cotangent_kernel, 'take_cotangent', out_shape=(S((slots * rows, blk)...  3.96 us
    ppermute x11, waiting for transfers between devices, send(): lax.ppermute(x, axis, [(i, partner(i, d, n)) for i in range(n)])  3.71 us
    ppermute x1, starting transfers between devices, shards(): lax.ppermute(half, 'tok', [(i, (i + side) % n_tok) for i in range(n_tok)])  2.9 us
    pallas_call x1, Pallas kernels, shards(): call(token_kernel, 'take_tokens', TAKE_LIMIT, out_shape=message, in_specs...  2.38 us
    unnamed x16, local copies, waits for them, and re-layouts  1.26 us
    pallas_call x1, Pallas kernels, shards(): call(functools.partial(input_kernel, dims), 'add_inputs', out_shape=(resu...  0.98 us
    pallas_call x1, Pallas kernels, shards(): call(functools.partial(output_kernel, dims), 'add_outputs', out_shape=(re...  0.96 us
  transfers between devices with their start and end apart: 12, of which 6 were waited for; matrix products, arithmetic and copies ran while one was open for 0% of the time, Pallas kernels for 20%

profile of v18, /device:TPU:0, one launch (start us, length us, event | category | flops | bytes accessed | tf_op | source)
XLA Modules:
  0.0 32.9 jit_solution(12591295619817756872)
XLA Ops:
  0.6 0.0 copy-start
  0.6 0.0 copy-start.1
  0.7 0.0 copy-start.2
  0.7 0.0 copy-start.7
  0.7 2.4 %take_tokens.1 = bf16[1040,128]{1,0:T(8,128)(2,1)} custom-call(s32[8]{0:T(128)} %bitcast.13, s32[8]{0:T(128)} %bitcast.15, s32[8]{0:T(128)} %bitcast.17, s32[8]{0:T(128)} %bitcast.19, bf16[128,4096]{1,0:T(8,128)(2,1)} %tokens.3, bf16[8,128,128]{2,1,0:T(8,128)(2,1)} %bitcast.8), custom_call_target="tpu_custom_call" | custom-call | flops 33554432 | bytes 524288 | tf_op jit(solution)/shard_map/take_tokens/pallas_call | solution.py:334
  3.1 0.0 copy-start.4
  3.1 0.0 copy-start.5
  3.1 0.0 copy-start.6
  3.1 3.0 %collective-permute-start = (bf16[1040,128]{1,0:T(8,128)(2,1)}, bf16[1040,128]{1,0:T(8,128)(2,1)S(1)}, u32[]{:S(2)}, u32[]{:S(2)}) collective-permute-start(bf16[1040,128]{1,0:T(8,128)(2,1)} %take_tokens.1), channel_id=1, source_target_pairs={{0,4},{4,0},{1,5},{5,1},{2,6},{6,2},{3,7},{7,3},{8,12},{12,8},{9,1... | collective-permute-start | bytes 798728 | tf_op jit(solution)/shard_map/ppermute | solution.py:55
  6.1 0.0 copy-done
  6.1 0.0 copy-done.1
  6.1 0.0 copy-done.2
  6.1 0.0 copy-done.7
  6.1 0.0 copy-done.4
  6.1 0.0 copy-done.5
  6.1 0.0 copy-done.6
  6.1 0.0 copy-start.3
  6.1 1.2 %copy-done.3 = bf16[128,4096]{1,0:T(8,128)(2,1)S(1)} copy-done((bf16[128,4096]{1,0:T(8,128)(2,1)S(1)}, bf16[128,4096]{1,0:T(8,128)(2,1)}, u32[]{:S(2)}) %copy-start.3) | copy-done | bytes 1048600
  7.4 4.0 %take_cotangent.1 = (bf16[1024,128]{1,0:T(8,128)(2,1)S(1)}, bf16[8,128,128]{2,1,0:T(8,128)(2,1)S(1)}, bf16[8,128,128]{2,1,0:T(8,128)(2,1)S(1)}, f32[16,128,128]{...) custom-call(s32[8]{0:T(128)S(1)} %bitcast.14, s32[8]{0:T(128)S(1)} %bitcast.16, ...), custom_call_target="tpu_custom_call" | custom-call | flops 33554432 | bytes 524288 | tf_op jit(solution)/shard_map/take_cotangent/pallas_call | solution.py:351
  11.3 0.6 %collective-permute-start.4 = (bf16[1024,128]{1,0:T(8,128)(2,1)S(1)}, bf16[1024,128]{1,0:T(8,128)(2,1)S(1)}, u32[]{:S(2)}, u32[]{:S(2)}) collective-permute-start(bf16[1024,128]{1,0:T(8,128)(2,1)S(1)} %get-tuple-element.52), channel_id=1, source_target_pairs={{0,4},{4,0},{1,5},{5,1},{2,6},{6,2},{3,7},{7,3},{8,12},{12,8},{9,1... | collective-permute-start | bytes 786440 | tf_op jit(solution)/shard_map/ppermute | solution.py:55
  11.9 0.8 %collective-permute-done.refs_0_ = bf16[1040,128]{1,0:T(8,128)(2,1)S(1)} collective-permute-done((bf16[1040,128]{1,0:T(8,128)(2,1)}, bf16[1040,128]{1,0:T(8,128)(2,1)S(1)}, u32[]{:S(2)}, u32[]{:S(2)}) %collective-permute-start) | collective-permute-done | bytes 266272 | tf_op jit(solution)/shard_map/ppermute | solution.py:55
  12.7 0.5 %hidden.1 = (bf16[8,128,128]{2,1,0:T(8,128)(2,1)S(1)}, f32[16,128,128]{2,1,0:T(8,128)S(1)}, s32[8,128]{1,0:T(8,128)S(1)}, f32[8,128,128]{2,1,0:T(8,128)S(1)}, bf16[512,128]{1,0:T(8,128)(2,1)S(1)}) custom-call(s32[24,128]{1,0:T(8,128)S(1)} %get-tuple-element.38.tab, f32[16,128,128]{2,1,0:T(8,128)S(1)} %get-tuple-element.40.own, ...), custom_call_target="tpu_custom_call" | custom-call | flops 33554432 | bytes 524288 | tf_op jit(solution)/shard_map/hidden/pallas_call | solution.py:379
  13.2 2.9 %collective-permute-start.7 = (bf16[512,128]{1,0:T(8,128)(2,1)S(1)}, bf16[512,128]{1,0:T(8,128)(2,1)S(1)}, u32[]{:S(2)}, u32[]{:S(2)}) collective-permute-start(bf16[512,128]{1,0:T(8,128)(2,1)S(1)} %get-tuple-element.58), channel_id=1, source_target_pairs={{0,16},{8,24},{16,0},{24,8},{1,17},{9,25},{17,1},{25,9},{2,18},{10... | collective-permute-start | bytes 393224 | tf_op jit(solution)/shard_map/ppermute | solution.py:393
  16.1 0.4 %slope.1 = (f32[8,128,128]{2,1,0:T(8,128)S(1)}, bf16[272,128]{1,0:T(8,128)(2,1)S(1)}, bf16[272,128]{1,0:T(8,128)(2,1)S(1)}, bf16[272,128]{1,0:T(8,128)(2,1)S(1)}, bf16[272,128]{1,0:T(8,128)(2,1)S(1)}) custom-call(s32[24,128]{1,0:T(8,128)S(1)} %get-tuple-element.38.tab, bf16[16,128]{1,0:T(8,128)(2,1)S(1)} %get-tuple-element.39.row, ...), custom_call_target="tpu_custom_call" | custom-call | flops 33554432 | bytes 524288 | tf_op jit(solution)/shard_map/slope/pallas_call | solution.py:395
  16.5 1.6 %collective-permute-start.1 = (bf16[272,128]{1,0:T(8,128)(2,1)S(1)}, bf16[272,128]{1,0:T(8,128)(2,1)S(1)}, u32[]{:S(2)}, u32[]{:S(2)}) collective-permute-start(bf16[272,128]{1,0:T(8,128)(2,1)S(1)} %get-tuple-element.45), channel_id=1, source_target_pairs={{0,2},{1,3},{2,0},{3,1},{4,6},{5,7},{6,4},{7,5},{8,10},{9,11},{10,... | collective-permute-start | bytes 208904 | tf_op jit(solution)/shard_map/ppermute | solution.py:55
  18.1 0.0 collective-permute-start.2
  18.1 0.6 %collective-permute-start.3 = (bf16[272,128]{1,0:T(8,128)(2,1)S(1)}, bf16[272,128]{1,0:T(8,128)(2,1)S(1)}, u32[]{:S(2)}, u32[]{:S(2)}) collective-permute-start(bf16[272,128]{1,0:T(8,128)(2,1)S(1)} %get-tuple-element.47), channel_id=1, source_target_pairs={{0,1},{1,0},{2,3},{3,2},{4,5},{5,4},{6,7},{7,6},{8,9},{9,8},{10,11... | collective-permute-start | bytes 208904 | tf_op jit(solution)/shard_map/ppermute | solution.py:55
  18.7 0.4 %collective-permute-done.4.refs_0_ = bf16[1024,128]{1,0:T(8,128)(2,1)S(1)} collective-permute-done((bf16[1024,128]{1,0:T(8,128)(2,1)S(1)}, bf16[1024,128]{1,0:T(8,128)(2,1)S(1)}, u32[]{:S(2)}, u32[]{:S(2)}) %collective-permute-start.4) | collective-permute-done | bytes 262176 | tf_op jit(solution)/shard_map/ppermute | solution.py:55
  19.2 0.6 %back.1 = (bf16[256,128]{1,0:T(8,128)(2,1)S(1)}, bf16[256,128]{1,0:T(8,128)(2,1)S(1)}, bf16[256,128]{1,0:T(8,128)(2,1)S(1)}, bf16[256,128]{1,0:T(8,128)(2,1)S(1)...) custom-call(s32[24,128]{1,0:T(8,128)S(1)} %get-tuple-element.38.tab,, ...), custom_call_target="tpu_custom_call" | custom-call | flops 33554432 | bytes 524288 | tf_op jit(solution)/shard_map/back/pallas_call | solution.py:405
  19.8 3.7 %collective-permute-start.5 = (bf16[272,128]{1,0:T(8,128)(2,1)S(1)}, bf16[272,128]{1,0:T(8,128)(2,1)S(1)}, u32[]{:S(2)}, u32[]{:S(2)}) collective-permute-start(bf16[272,128]{1,0:T(8,128)(2,1)S(1)} %get-tuple-element.55), channel_id=1, source_target_pairs={{0,24},{8,16},{16,8},{24,0},{1,25},{9,17},{17,9},{25,1},{2,26},{10... | collective-permute-start | bytes 208904 | tf_op jit(solution)/shard_map/ppermute | solution.py:55
  23.4 0.0 collective-permute-done.1.refs_1_.refs_2_
  23.4 0.0 collective-permute-done.2.refs_2_.refs_3_
  23.4 0.0 collective-permute-done.3.refs_3_.refs_4_
  23.4 0.0 collective-permute-done.7.half
  23.5 0.6 %collective-permute-start.8 = (bf16[512,128]{1,0:T(8,128)(2,1)S(1)}, bf16[512,128]{1,0:T(8,128)(2,1)S(1)}, u32[]{:S(2)}, u32[]{:S(2)}) collective-permute-start(bf16[512,128]{1,0:T(8,128)(2,1)S(1)} %get-tuple-element.61), channel_id=1, source_target_pairs={{0,8},{8,0},{16,24},{24,16},{1,9},{9,1},{17,25},{25,17},{2,10},{10... | collective-permute-start | bytes 393224 | tf_op jit(solution)/shard_map/ppermute | solution.py:55
  24.1 2.2 %collective-permute-start.6 = (bf16[272,128]{1,0:T(8,128)(2,1)S(1)}, bf16[272,128]{1,0:T(8,128)(2,1)S(1)}, u32[]{:S(2)}, u32[]{:S(2)}) collective-permute-start(bf16[272,128]{1,0:T(8,128)(2,1)S(1)} %get-tuple-element.56), channel_id=1, source_target_pairs={{0,16},{8,24},{16,0},{24,8},{1,17},{9,25},{17,1},{25,9},{2,18},{10... | collective-permute-start | bytes 208904 | tf_op jit(solution)/shard_map/ppermute | solution.py:55
  26.3 1.5 %collective-permute-start.9 = (bf16[256,128]{1,0:T(8,128)(2,1)S(1)}, bf16[256,128]{1,0:T(8,128)(2,1)S(1)}, u32[]{:S(2)}, u32[]{:S(2)}) collective-permute-start(bf16[256,128]{1,0:T(8,128)(2,1)S(1)} %get-tuple-element.66), channel_id=1, source_target_pairs={{0,2},{1,3},{2,0},{3,1},{4,6},{5,7},{6,4},{7,5},{8,10},{9,11},{10,... | collective-permute-start | bytes 196616 | tf_op jit(solution)/shard_map/ppermute | solution.py:55
  27.7 0.0 collective-permute-start.10
  27.7 0.0 collective-permute-done.5.refs_0_
  27.7 0.7 %collective-permute-start.11 = (bf16[256,128]{1,0:T(8,128)(2,1)S(1)}, bf16[256,128]{1,0:T(8,128)(2,1)S(1)}, u32[]{:S(2)}, u32[]{:S(2)}) collective-permute-start(bf16[256,128]{1,0:T(8,128)(2,1)S(1)} %get-tuple-element.68), channel_id=1, source_target_pairs={{0,1},{1,0},{2,3},{3,2},{4,5},{5,4},{6,7},{7,6},{8,9},{9,8},{10,11... | collective-permute-start | bytes 196616 | tf_op jit(solution)/shard_map/ppermute | solution.py:55
  28.4 1.0 %add_outputs.1 = (bf16[32,4096]{1,0:T(8,128)(2,1)}, s32[8,128]{1,0:T(8,128)S(1)}) custom-call(bf16[272,128]{1,0:T(8,128)(2,1)S(1)} %get-tuple-element.44.refs_0_, bf16[272,128]{1,0:T(8,128)(2,1)S(1)} %collective-permute-done.1.refs_1_.refs_2_, bf16[272,128]{1,0:T(8,128)(2,1)S(1)} %collective-permute-done.2.refs_2_.refs_3_, ...), custom_call_target="tpu_custom_call" | custom-call | flops 33554432 | bytes 524288 | tf_op jit(solution)/shard_map/add_outputs/pallas_call | solution.py:440
  29.4 0.1 collective-permute-done.6.refs_1_
  29.5 0.5 %collective-permute-done.8.refs_2_ = bf16[512,128]{1,0:T(8,128)(2,1)S(1)} collective-permute-done((bf16[512,128]{1,0:T(8,128)(2,1)S(1)}, bf16[512,128]{1,0:T(8,128)(2,1)S(1)}, u32[]{:S(2)}, u32[]{:S(2)}) %collective-permute-start.8) | collective-permute-done | bytes 131104 | tf_op jit(solution)/shard_map/ppermute | solution.py:55
  30.1 0.5 %collective-permute-done.9.refs_5_ = bf16[256,128]{1,0:T(8,128)(2,1)S(1)} collective-permute-done((bf16[256,128]{1,0:T(8,128)(2,1)S(1)}, bf16[256,128]{1,0:T(8,128)(2,1)S(1)}, u32[]{:S(2)}, u32[]{:S(2)}) %collective-permute-start.9) | collective-permute-done | bytes 65568 | tf_op jit(solution)/shard_map/ppermute | solution.py:55
  30.5 1.4 %collective-permute-done.10.refs_6_ = bf16[256,128]{1,0:T(8,128)(2,1)S(1)} collective-permute-done((bf16[256,128]{1,0:T(8,128)(2,1)S(1)}, bf16[256,128]{1,0:T(8,128)(2,1)S(1)}, u32[]{:S(2)}, u32[]{:S(2)}) %collective-permute-start.10) | collective-permute-done | bytes 65568 | tf_op jit(solution)/shard_map/ppermute | solution.py:55
  31.9 0.0 collective-permute-done.11.refs_7_
  32.0 1.0 %add_inputs.1 = (bf16[32,4096]{1,0:T(8,128)(2,1)}, f32[8,32,128]{2,1,0:T(8,128)}, f32[8,32,128]{2,1,0:T(8,128)}) custom-call(s32[8,128]{1,0:T(8,128)S(1)} %get-tuple-element.49.after, f32[8,32,128]{2,1,0:T(8,128)S(1)} %get-tuple-element.63.sum1, f32[8,32,128]{2,1,0:T(8,128)S(1)} %get-tuple-element.64.sum2, bf16[272,128]{1,0:T(8,128)(2,1)S(1)} %get-tuple-element.44.refs_0_, ...), custom_call_target="tpu_custom_call" | custom-call | flops 33554432 | bytes 524288 | tf_op jit(solution)/shard_map/add_inputs/pallas_call | solution.py:448
  (2 shorter events, 0.1 us)
Async XLA Ops:
  0.6 5.5 %copy-start = (bf16[128,4096]{1,0:T(8,128)(2,1)S(1)}, bf16[128,4096]{1,0:T(8,128)(2,1)}, u32[]{:S(2)}) copy-start(bf16[128,4096]{1,0:T(8,128)(2,1)} %tokens.3) | copy-start | bytes 3145732
  0.6 5.5 %copy-start.1 = (bf16[1,1,8,128,128]{4,3,2,1,0:T(8,128)(2,1)S(1)}, bf16[1,1,8,128,128]{4,3,2,1,0:T(8,128)(2,1)}, u32[]{:S(2)}) copy-start(bf16[1,1,8,128,128]{4,3,2,1,0:T(8,128)(2,1)} %param.9) | copy-start | bytes 786436
  0.7 5.4 %copy-start.2 = (bf16[1,1,8,128,128]{4,3,2,1,0:T(8,128)(2,1)S(1)}, bf16[1,1,8,128,128]{4,3,2,1,0:T(8,128)(2,1)}, u32[]{:S(2)}) copy-start(bf16[1,1,8,128,128]{4,3,2,1,0:T(8,128)(2,1)} %param.12) | copy-start | bytes 786436
  0.7 5.4 %copy-start.7 = (s32[1,1,8]{2,1,0:T(1,128)S(1)}, s32[1,1,8]{2,1,0:T(1,128)}, u32[]{:S(2)}) copy-start(s32[1,1,8]{2,1,0:T(1,128)} %param.14) | copy-start | bytes 100
  3.1 3.0 %copy-start.4 = (s32[1,1,8]{2,1,0:T(1,128)S(1)}, s32[1,1,8]{2,1,0:T(1,128)}, u32[]{:S(2)}) copy-start(s32[1,1,8]{2,1,0:T(1,128)} %param.10) | copy-start | bytes 100
  3.1 3.0 %copy-start.5 = (s32[1,1,8]{2,1,0:T(1,128)S(1)}, s32[1,1,8]{2,1,0:T(1,128)}, u32[]{:S(2)}) copy-start(s32[1,1,8]{2,1,0:T(1,128)} %param.11) | copy-start | bytes 100
  3.1 3.0 %copy-start.6 = (s32[1,1,8]{2,1,0:T(1,128)S(1)}, s32[1,1,8]{2,1,0:T(1,128)}, u32[]{:S(2)}) copy-start(s32[1,1,8]{2,1,0:T(1,128)} %param.13) | copy-start | bytes 100
  3.1 9.6 %collective-permute-start = (bf16[1040,128]{1,0:T(8,128)(2,1)}, bf16[1040,128]{1,0:T(8,128)(2,1)S(1)}, u32[]{:S(2)}, u32[]{:S(2)}) collective-permute-start(bf16[1040,128]{1,0:T(8,128)(2,1)} %take_tokens.1), channel_id=1, source_target_pairs={{0,4},{4,0},{1,5},{5,1},{2,6},{6,2},{3,7},{7,3},{8,12},{12,8},{9,1... | collective-permute-start | bytes 798728 | tf_op jit(solution)/shard_map/ppermute | solution.py:55
  6.1 1.2 %copy-start.3 = (bf16[128,4096]{1,0:T(8,128)(2,1)S(1)}, bf16[128,4096]{1,0:T(8,128)(2,1)}, u32[]{:S(2)}) copy-start(bf16[128,4096]{1,0:T(8,128)(2,1)} %grad_out.1) | copy-start | bytes 3145732
  11.3 7.8 %collective-permute-start.4 = (bf16[1024,128]{1,0:T(8,128)(2,1)S(1)}, bf16[1024,128]{1,0:T(8,128)(2,1)S(1)}, u32[]{:S(2)}, u32[]{:S(2)}) collective-permute-start(bf16[1024,128]{1,0:T(8,128)(2,1)S(1)} %get-tuple-element.52), channel_id=1, source_target_pairs={{0,4},{4,0},{1,5},{5,1},{2,6},{6,2},{3,7},{7,3},{8,12},{12,8},{9,1... | collective-permute-start | bytes 786440 | tf_op jit(solution)/shard_map/ppermute | solution.py:55
  13.2 10.2 %collective-permute-start.7 = (bf16[512,128]{1,0:T(8,128)(2,1)S(1)}, bf16[512,128]{1,0:T(8,128)(2,1)S(1)}, u32[]{:S(2)}, u32[]{:S(2)}) collective-permute-start(bf16[512,128]{1,0:T(8,128)(2,1)S(1)} %get-tuple-element.58), channel_id=1, source_target_pairs={{0,16},{8,24},{16,0},{24,8},{1,17},{9,25},{17,1},{25,9},{2,18},{10... | collective-permute-start | bytes 393224 | tf_op jit(solution)/shard_map/ppermute | solution.py:393
  16.5 6.9 %collective-permute-start.1 = (bf16[272,128]{1,0:T(8,128)(2,1)S(1)}, bf16[272,128]{1,0:T(8,128)(2,1)S(1)}, u32[]{:S(2)}, u32[]{:S(2)}) collective-permute-start(bf16[272,128]{1,0:T(8,128)(2,1)S(1)} %get-tuple-element.45), channel_id=1, source_target_pairs={{0,2},{1,3},{2,0},{3,1},{4,6},{5,7},{6,4},{7,5},{8,10},{9,11},{10,... | collective-permute-start | bytes 208904 | tf_op jit(solution)/shard_map/ppermute | solution.py:55
  18.1 5.3 %collective-permute-start.2 = (bf16[272,128]{1,0:T(8,128)(2,1)S(1)}, bf16[272,128]{1,0:T(8,128)(2,1)S(1)}, u32[]{:S(2)}, u32[]{:S(2)}) collective-permute-start(bf16[272,128]{1,0:T(8,128)(2,1)S(1)} %get-tuple-element.46), channel_id=1, source_target_pairs={{0,3},{1,2},{2,1},{3,0},{4,7},{5,6},{6,5},{7,4},{8,11},{9,10},{10,... | collective-permute-start | bytes 208904 | tf_op jit(solution)/shard_map/ppermute | solution.py:55
  18.1 5.3 %collective-permute-start.3 = (bf16[272,128]{1,0:T(8,128)(2,1)S(1)}, bf16[272,128]{1,0:T(8,128)(2,1)S(1)}, u32[]{:S(2)}, u32[]{:S(2)}) collective-permute-start(bf16[272,128]{1,0:T(8,128)(2,1)S(1)} %get-tuple-element.47), channel_id=1, source_target_pairs={{0,1},{1,0},{2,3},{3,2},{4,5},{5,4},{6,7},{7,6},{8,9},{9,8},{10,11... | collective-permute-start | bytes 208904 | tf_op jit(solution)/shard_map/ppermute | solution.py:55
  19.8 8.0 %collective-permute-start.5 = (bf16[272,128]{1,0:T(8,128)(2,1)S(1)}, bf16[272,128]{1,0:T(8,128)(2,1)S(1)}, u32[]{:S(2)}, u32[]{:S(2)}) collective-permute-start(bf16[272,128]{1,0:T(8,128)(2,1)S(1)} %get-tuple-element.55), channel_id=1, source_target_pairs={{0,24},{8,16},{16,8},{24,0},{1,25},{9,17},{17,9},{25,1},{2,26},{10... | collective-permute-start | bytes 208904 | tf_op jit(solution)/shard_map/ppermute | solution.py:55
  23.5 6.5 %collective-permute-start.8 = (bf16[512,128]{1,0:T(8,128)(2,1)S(1)}, bf16[512,128]{1,0:T(8,128)(2,1)S(1)}, u32[]{:S(2)}, u32[]{:S(2)}) collective-permute-start(bf16[512,128]{1,0:T(8,128)(2,1)S(1)} %get-tuple-element.61), channel_id=1, source_target_pairs={{0,8},{8,0},{16,24},{24,16},{1,9},{9,1},{17,25},{25,17},{2,10},{10... | collective-permute-start | bytes 393224 | tf_op jit(solution)/shard_map/ppermute | solution.py:55
  24.1 5.4 %collective-permute-start.6 = (bf16[272,128]{1,0:T(8,128)(2,1)S(1)}, bf16[272,128]{1,0:T(8,128)(2,1)S(1)}, u32[]{:S(2)}, u32[]{:S(2)}) collective-permute-start(bf16[272,128]{1,0:T(8,128)(2,1)S(1)} %get-tuple-element.56), channel_id=1, source_target_pairs={{0,16},{8,24},{16,0},{24,8},{1,17},{9,25},{17,1},{25,9},{2,18},{10... | collective-permute-start | bytes 208904 | tf_op jit(solution)/shard_map/ppermute | solution.py:55
  26.3 4.3 %collective-permute-start.9 = (bf16[256,128]{1,0:T(8,128)(2,1)S(1)}, bf16[256,128]{1,0:T(8,128)(2,1)S(1)}, u32[]{:S(2)}, u32[]{:S(2)}) collective-permute-start(bf16[256,128]{1,0:T(8,128)(2,1)S(1)} %get-tuple-element.66), channel_id=1, source_target_pairs={{0,2},{1,3},{2,0},{3,1},{4,6},{5,7},{6,4},{7,5},{8,10},{9,11},{10,... | collective-permute-start | bytes 196616 | tf_op jit(solution)/shard_map/ppermute | solution.py:55
  27.7 4.2 %collective-permute-start.10 = (bf16[256,128]{1,0:T(8,128)(2,1)S(1)}, bf16[256,128]{1,0:T(8,128)(2,1)S(1)}, u32[]{:S(2)}, u32[]{:S(2)}) collective-permute-start(bf16[256,128]{1,0:T(8,128)(2,1)S(1)} %get-tuple-element.67), channel_id=1, source_target_pairs={{0,3},{1,2},{2,1},{3,0},{4,7},{5,6},{6,5},{7,4},{8,11},{9,10},{10,... | collective-permute-start | bytes 196616 | tf_op jit(solution)/shard_map/ppermute | solution.py:55
  27.7 4.2 %collective-permute-start.11 = (bf16[256,128]{1,0:T(8,128)(2,1)S(1)}, bf16[256,128]{1,0:T(8,128)(2,1)S(1)}, u32[]{:S(2)}, u32[]{:S(2)}) collective-permute-start(bf16[256,128]{1,0:T(8,128)(2,1)S(1)} %get-tuple-element.68), channel_id=1, source_target_pairs={{0,1},{1,0},{2,3},{3,2},{4,5},{5,4},{6,7},{7,6},{8,9},{9,8},{10,11... | collective-permute-start | bytes 196616 | tf_op jit(solution)/shard_map/ppermute | solution.py:55

commit v19 on v15

--- a/solution.py
+++ b/solution.py
@@ -312,7 +312,7 @@
 
 
 def near_last(n):
-    return [0] + list(range(2, n)) + [1][: n - 1]
+    return [0] + list(range(n - 1, 1, -1)) + [1][: n - 1]
 
 
 def shards(tokens, w1_blocks, w1_rows, w1_cols, w2_blocks, w2_hidden, w2_outs, grad_out):

time: 32.1 us -> 32.2 us (level)
  waiting for transfers between devices: 3.69 us -> 4.52 us
  starting transfers between devices: 16.3 us -> 15.6 us
    ppermute x11, waiting for transfers between devices: 3.69 us -> 4.52 us  [send(): lax.ppermute(x, axis, [(i, partner(i, d, n)) for i in range(n)])]
    ppermute x11, starting transfers between devices: 13.4 us -> 12.7 us  [send(): lax.ppermute(x, axis, [(i, partner(i, d, n)) for i in range(n)])]
  transfers between devices with their start and end apart: 12 -> 12, of which waited for: 4 -> 5; matrix products, arithmetic and copies ran while one was open for 0% -> 0% of each run, Pallas kernels for 20% -> 20%
where the time goes in v19:
time: 32.2 us; the launch traced here: 32.1 us
  starting transfers between devices  15.6 us (48%)
  Pallas kernels  9.86 us (31%)
  waiting for transfers between devices  4.52 us (14%)
  local copies, waits for them, and re-layouts  1.26 us (4%)
  between operations  0.8 us (2%)
    ppermute x11, starting transfers between devices, send(): lax.ppermute(x, axis, [(i, partner(i, d, n)) for i in range(n)])  12.7 us
    ppermute x11, waiting for transfers between devices, send(): lax.ppermute(x, axis, [(i, partner(i, d, n)) for i in range(n)])  4.52 us
    pallas_call x1, Pallas kernels, shards(): call(cotangent_kernel, 'take_cotangent', out_shape=(S((slots * rows, blk)...  3.96 us
    ppermute x1, starting transfers between devices, shards(): lax.ppermute(half, 'tok', [(i, (i + side) % n_tok) for i in range(n_tok)])  2.9 us
    pallas_call x1, Pallas kernels, shards(): call(token_kernel, 'take_tokens', TAKE_LIMIT, out_shape=message, in_specs...  2.37 us
    unnamed x16, local copies, waits for them, and re-layouts  1.26 us
    pallas_call x1, Pallas kernels, shards(): call(functools.partial(input_kernel, dims), 'add_inputs', out_shape=(resu...  0.98 us
    pallas_call x1, Pallas kernels, shards(): call(functools.partial(output_kernel, dims), 'add_outputs', out_shape=(re...  0.97 us
  transfers between devices with their start and end apart: 12, of which 5 were waited for; matrix products, arithmetic and copies ran while one was open for 0% of the time, Pallas kernels for 20%

profile of v19, /device:TPU:0, one launch (start us, length us, event | category | flops | bytes accessed | tf_op | source)
XLA Modules:
  0.0 32.1 jit_solution(8197254029330578672)
XLA Ops:
  0.6 0.0 copy-start
  0.6 0.0 copy-start.1
  0.7 0.0 copy-start.2
  0.7 0.0 copy-start.7
  0.7 2.4 %take_tokens.1 = bf16[1040,128]{1,0:T(8,128)(2,1)} custom-call(s32[8]{0:T(128)} %bitcast.13, s32[8]{0:T(128)} %bitcast.15, s32[8]{0:T(128)} %bitcast.17, s32[8]{0:T(128)} %bitcast.19, bf16[128,4096]{1,0:T(8,128)(2,1)} %tokens.3, bf16[8,128,128]{2,1,0:T(8,128)(2,1)} %bitcast.8), custom_call_target="tpu_custom_call" | custom-call | flops 33554432 | bytes 524288 | tf_op jit(solution)/shard_map/take_tokens/pallas_call | solution.py:334
  3.0 0.0 copy-start.4
  3.1 0.0 copy-start.5
  3.1 0.0 copy-start.6
  3.1 3.0 %collective-permute-start = (bf16[1040,128]{1,0:T(8,128)(2,1)}, bf16[1040,128]{1,0:T(8,128)(2,1)S(1)}, u32[]{:S(2)}, u32[]{:S(2)}) collective-permute-start(bf16[1040,128]{1,0:T(8,128)(2,1)} %take_tokens.1), channel_id=1, source_target_pairs={{0,4},{4,0},{1,5},{5,1},{2,6},{6,2},{3,7},{7,3},{8,12},{12,8},{9,1... | collective-permute-start | bytes 798728 | tf_op jit(solution)/shard_map/ppermute | solution.py:55
  6.1 0.0 copy-done
  6.1 0.0 copy-done.1
  6.1 0.0 copy-done.2
  6.1 0.0 copy-done.7
  6.1 0.0 copy-done.4
  6.1 0.0 copy-done.5
  6.1 0.0 copy-done.6
  6.1 0.0 copy-start.3
  6.1 1.2 %copy-done.3 = bf16[128,4096]{1,0:T(8,128)(2,1)S(1)} copy-done((bf16[128,4096]{1,0:T(8,128)(2,1)S(1)}, bf16[128,4096]{1,0:T(8,128)(2,1)}, u32[]{:S(2)}) %copy-start.3) | copy-done | bytes 1048600
  7.4 4.0 %take_cotangent.1 = (bf16[1024,128]{1,0:T(8,128)(2,1)S(1)}, bf16[8,128,128]{2,1,0:T(8,128)(2,1)S(1)}, bf16[8,128,128]{2,1,0:T(8,128)(2,1)S(1)}, f32[16,128,128]{...) custom-call(s32[8]{0:T(128)S(1)} %bitcast.14, s32[8]{0:T(128)S(1)} %bitcast.16, ...), custom_call_target="tpu_custom_call" | custom-call | flops 33554432 | bytes 524288 | tf_op jit(solution)/shard_map/take_cotangent/pallas_call | solution.py:351
  11.3 0.6 %collective-permute-start.5 = (bf16[1024,128]{1,0:T(8,128)(2,1)S(1)}, bf16[1024,128]{1,0:T(8,128)(2,1)S(1)}, u32[]{:S(2)}, u32[]{:S(2)}) collective-permute-start(bf16[1024,128]{1,0:T(8,128)(2,1)S(1)} %get-tuple-element.54), channel_id=1, source_target_pairs={{0,4},{4,0},{1,5},{5,1},{2,6},{6,2},{3,7},{7,3},{8,12},{12,8},{9,1... | collective-permute-start | bytes 786440 | tf_op jit(solution)/shard_map/ppermute | solution.py:55
  11.9 0.8 %collective-permute-done.refs_0_ = bf16[1040,128]{1,0:T(8,128)(2,1)S(1)} collective-permute-done((bf16[1040,128]{1,0:T(8,128)(2,1)}, bf16[1040,128]{1,0:T(8,128)(2,1)S(1)}, u32[]{:S(2)}, u32[]{:S(2)}) %collective-permute-start) | collective-permute-done | bytes 266272 | tf_op jit(solution)/shard_map/ppermute | solution.py:55
  12.7 0.5 %hidden.1 = (bf16[8,128,128]{2,1,0:T(8,128)(2,1)S(1)}, f32[16,128,128]{2,1,0:T(8,128)S(1)}, s32[8,128]{1,0:T(8,128)S(1)}, f32[8,128,128]{2,1,0:T(8,128)S(1)}, bf16[512,128]{1,0:T(8,128)(2,1)S(1)}) custom-call(s32[24,128]{1,0:T(8,128)S(1)} %get-tuple-element.38.tab, f32[16,128,128]{2,1,0:T(8,128)S(1)} %get-tuple-element.40.own, ...), custom_call_target="tpu_custom_call" | custom-call | flops 33554432 | bytes 524288 | tf_op jit(solution)/shard_map/hidden/pallas_call | solution.py:379
  13.2 2.9 %collective-permute-start.4 = (bf16[512,128]{1,0:T(8,128)(2,1)S(1)}, bf16[512,128]{1,0:T(8,128)(2,1)S(1)}, u32[]{:S(2)}, u32[]{:S(2)}) collective-permute-start(bf16[512,128]{1,0:T(8,128)(2,1)S(1)} %get-tuple-element.51), channel_id=1, source_target_pairs={{0,16},{8,24},{16,0},{24,8},{1,17},{9,25},{17,1},{25,9},{2,18},{10... | collective-permute-start | bytes 393224 | tf_op jit(solution)/shard_map/ppermute | solution.py:393
  16.1 0.4 %slope.1 = (f32[8,128,128]{2,1,0:T(8,128)S(1)}, bf16[272,128]{1,0:T(8,128)(2,1)S(1)}, bf16[272,128]{1,0:T(8,128)(2,1)S(1)}, bf16[272,128]{1,0:T(8,128)(2,1)S(1)}, bf16[272,128]{1,0:T(8,128)(2,1)S(1)}) custom-call(s32[24,128]{1,0:T(8,128)S(1)} %get-tuple-element.38.tab, bf16[16,128]{1,0:T(8,128)(2,1)S(1)} %get-tuple-element.39.row, ...), custom_call_target="tpu_custom_call" | custom-call | flops 33554432 | bytes 524288 | tf_op jit(solution)/shard_map/slope/pallas_call | solution.py:395
  16.5 0.1 collective-permute-start.1
  16.6 1.6 %collective-permute-start.2 = (bf16[272,128]{1,0:T(8,128)(2,1)S(1)}, bf16[272,128]{1,0:T(8,128)(2,1)S(1)}, u32[]{:S(2)}, u32[]{:S(2)}) collective-permute-start(bf16[272,128]{1,0:T(8,128)(2,1)S(1)} %get-tuple-element.46), channel_id=1, source_target_pairs={{0,2},{1,3},{2,0},{3,1},{4,6},{5,7},{6,4},{7,5},{8,10},{9,11},{10,... | collective-permute-start | bytes 208904 | tf_op jit(solution)/shard_map/ppermute | solution.py:55
  18.2 0.2 collective-permute-start.3
  18.4 0.7 %collective-permute-done.5.refs_0_ = bf16[1024,128]{1,0:T(8,128)(2,1)S(1)} collective-permute-done((bf16[1024,128]{1,0:T(8,128)(2,1)S(1)}, bf16[1024,128]{1,0:T(8,128)(2,1)S(1)}, u32[]{:S(2)}, u32[]{:S(2)}) %collective-permute-start.5) | collective-permute-done | bytes 262176 | tf_op jit(solution)/shard_map/ppermute | solution.py:55
  19.2 0.6 %back.1 = (bf16[256,128]{1,0:T(8,128)(2,1)S(1)}, bf16[256,128]{1,0:T(8,128)(2,1)S(1)}, bf16[256,128]{1,0:T(8,128)(2,1)S(1)}, bf16[256,128]{1,0:T(8,128)(2,1)S(1)...) custom-call(s32[24,128]{1,0:T(8,128)S(1)} %get-tuple-element.38.tab,, ...), custom_call_target="tpu_custom_call" | custom-call | flops 33554432 | bytes 524288 | tf_op jit(solution)/shard_map/back/pallas_call | solution.py:405
  19.8 2.7 %collective-permute-start.6 = (bf16[272,128]{1,0:T(8,128)(2,1)S(1)}, bf16[272,128]{1,0:T(8,128)(2,1)S(1)}, u32[]{:S(2)}, u32[]{:S(2)}) collective-permute-start(bf16[272,128]{1,0:T(8,128)(2,1)S(1)} %get-tuple-element.60), channel_id=1, source_target_pairs={{0,16},{8,24},{16,0},{24,8},{1,17},{9,25},{17,1},{25,9},{2,18},{10... | collective-permute-start | bytes 208904 | tf_op jit(solution)/shard_map/ppermute | solution.py:55
  22.4 0.0 collective-permute-done.1.refs_1_.refs_2_
  22.4 0.1 collective-permute-done.2.refs_2_.refs_3_
  22.6 0.0 collective-permute-done.3.refs_3_.refs_4_
  22.6 0.0 collective-permute-done.4.half
  22.6 1.6 %collective-permute-start.8 = (bf16[512,128]{1,0:T(8,128)(2,1)S(1)}, bf16[512,128]{1,0:T(8,128)(2,1)S(1)}, u32[]{:S(2)}, u32[]{:S(2)}) collective-permute-start(bf16[512,128]{1,0:T(8,128)(2,1)S(1)} %get-tuple-element.62), channel_id=1, source_target_pairs={{0,8},{8,0},{16,24},{24,16},{1,9},{9,1},{17,25},{25,17},{2,10},{10... | collective-permute-start | bytes 393224 | tf_op jit(solution)/shard_map/ppermute | solution.py:55
  24.2 1.0 %collective-permute-start.7 = (bf16[272,128]{1,0:T(8,128)(2,1)S(1)}, bf16[272,128]{1,0:T(8,128)(2,1)S(1)}, u32[]{:S(2)}, u32[]{:S(2)}) collective-permute-start(bf16[272,128]{1,0:T(8,128)(2,1)S(1)} %get-tuple-element.61), channel_id=1, source_target_pairs={{0,24},{8,16},{16,8},{24,0},{1,25},{9,17},{17,9},{25,1},{2,26},{10... | collective-permute-start | bytes 208904 | tf_op jit(solution)/shard_map/ppermute | solution.py:55
  25.3 0.2 collective-permute-start.9
  25.5 1.4 %collective-permute-start.10 = (bf16[256,128]{1,0:T(8,128)(2,1)S(1)}, bf16[256,128]{1,0:T(8,128)(2,1)S(1)}, u32[]{:S(2)}, u32[]{:S(2)}) collective-permute-start(bf16[256,128]{1,0:T(8,128)(2,1)S(1)} %get-tuple-element.67), channel_id=1, source_target_pairs={{0,2},{1,3},{2,0},{3,1},{4,6},{5,7},{6,4},{7,5},{8,10},{9,11},{10,... | collective-permute-start | bytes 196616 | tf_op jit(solution)/shard_map/ppermute | solution.py:55
  26.8 0.0 collective-permute-done.6.refs_1_
  26.8 0.3 collective-permute-start.11
  27.1 1.0 %add_outputs.1 = (bf16[32,4096]{1,0:T(8,128)(2,1)}, s32[8,128]{1,0:T(8,128)S(1)}) custom-call(bf16[272,128]{1,0:T(8,128)(2,1)S(1)} %get-tuple-element.44.refs_0_, bf16[272,128]{1,0:T(8,128)(2,1)S(1)} %collective-permute-done.1.refs_1_.refs_2_, bf16[272,128]{1,0:T(8,128)(2,1)S(1)} %collective-permute-done.2.refs_2_.refs_3_, ...), custom_call_target="tpu_custom_call" | custom-call | flops 33554432 | bytes 524288 | tf_op jit(solution)/shard_map/add_outputs/pallas_call | solution.py:440
  28.1 2.2 %collective-permute-done.7.refs_2_ = bf16[272,128]{1,0:T(8,128)(2,1)S(1)} collective-permute-done((bf16[272,128]{1,0:T(8,128)(2,1)S(1)}, bf16[272,128]{1,0:T(8,128)(2,1)S(1)}, u32[]{:S(2)}, u32[]{:S(2)}) %collective-permute-start.7) | collective-permute-done | bytes 69664 | tf_op jit(solution)/shard_map/ppermute | solution.py:55
  30.4 0.0 collective-permute-done.8.refs_3_
  30.4 0.1 add_grads.1
  30.4 0.0 collective-permute-done.9.refs_5_
  30.4 0.6 %collective-permute-done.10.refs_6_ = bf16[256,128]{1,0:T(8,128)(2,1)S(1)} collective-permute-done((bf16[256,128]{1,0:T(8,128)(2,1)S(1)}, bf16[256,128]{1,0:T(8,128)(2,1)S(1)}, u32[]{:S(2)}, u32[]{:S(2)}) %collective-permute-start.10) | collective-permute-done | bytes 65568 | tf_op jit(solution)/shard_map/ppermute | solution.py:55
  31.1 0.0 collective-permute-done.11.refs_7_
  31.1 1.0 %add_inputs.1 = (bf16[32,4096]{1,0:T(8,128)(2,1)}, f32[8,32,128]{2,1,0:T(8,128)}, f32[8,32,128]{2,1,0:T(8,128)}) custom-call(s32[8,128]{1,0:T(8,128)S(1)} %get-tuple-element.49.after, f32[8,32,128]{2,1,0:T(8,128)S(1)} %get-tuple-element.63.sum1, f32[8,32,128]{2,1,0:T(8,128)S(1)} %get-tuple-element.64.sum2, bf16[272,128]{1,0:T(8,128)(2,1)S(1)} %get-tuple-element.44.refs_0_, ...), custom_call_target="tpu_custom_call" | custom-call | flops 33554432 | bytes 524288 | tf_op jit(solution)/shard_map/add_inputs/pallas_call | solution.py:448
  (1 shorter events, 0.0 us)
Async XLA Ops:
  0.6 5.5 %copy-start = (bf16[128,4096]{1,0:T(8,128)(2,1)S(1)}, bf16[128,4096]{1,0:T(8,128)(2,1)}, u32[]{:S(2)}) copy-start(bf16[128,4096]{1,0:T(8,128)(2,1)} %tokens.3) | copy-start | bytes 3145732
  0.6 5.5 %copy-start.1 = (bf16[1,1,8,128,128]{4,3,2,1,0:T(8,128)(2,1)S(1)}, bf16[1,1,8,128,128]{4,3,2,1,0:T(8,128)(2,1)}, u32[]{:S(2)}) copy-start(bf16[1,1,8,128,128]{4,3,2,1,0:T(8,128)(2,1)} %param.9) | copy-start | bytes 786436
  0.7 5.4 %copy-start.2 = (bf16[1,1,8,128,128]{4,3,2,1,0:T(8,128)(2,1)S(1)}, bf16[1,1,8,128,128]{4,3,2,1,0:T(8,128)(2,1)}, u32[]{:S(2)}) copy-start(bf16[1,1,8,128,128]{4,3,2,1,0:T(8,128)(2,1)} %param.12) | copy-start | bytes 786436
  0.7 5.4 %copy-start.7 = (s32[1,1,8]{2,1,0:T(1,128)S(1)}, s32[1,1,8]{2,1,0:T(1,128)}, u32[]{:S(2)}) copy-start(s32[1,1,8]{2,1,0:T(1,128)} %param.14) | copy-start | bytes 100
  3.0 3.1 %copy-start.4 = (s32[1,1,8]{2,1,0:T(1,128)S(1)}, s32[1,1,8]{2,1,0:T(1,128)}, u32[]{:S(2)}) copy-start(s32[1,1,8]{2,1,0:T(1,128)} %param.10) | copy-start | bytes 100
  3.1 3.1 %copy-start.5 = (s32[1,1,8]{2,1,0:T(1,128)S(1)}, s32[1,1,8]{2,1,0:T(1,128)}, u32[]{:S(2)}) copy-start(s32[1,1,8]{2,1,0:T(1,128)} %param.11) | copy-start | bytes 100
  3.1 3.1 %copy-start.6 = (s32[1,1,8]{2,1,0:T(1,128)S(1)}, s32[1,1,8]{2,1,0:T(1,128)}, u32[]{:S(2)}) copy-start(s32[1,1,8]{2,1,0:T(1,128)} %param.13) | copy-start | bytes 100
  3.1 9.6 %collective-permute-start = (bf16[1040,128]{1,0:T(8,128)(2,1)}, bf16[1040,128]{1,0:T(8,128)(2,1)S(1)}, u32[]{:S(2)}, u32[]{:S(2)}) collective-permute-start(bf16[1040,128]{1,0:T(8,128)(2,1)} %take_tokens.1), channel_id=1, source_target_pairs={{0,4},{4,0},{1,5},{5,1},{2,6},{6,2},{3,7},{7,3},{8,12},{12,8},{9,1... | collective-permute-start | bytes 798728 | tf_op jit(solution)/shard_map/ppermute | solution.py:55
  6.1 1.2 %copy-start.3 = (bf16[128,4096]{1,0:T(8,128)(2,1)S(1)}, bf16[128,4096]{1,0:T(8,128)(2,1)}, u32[]{:S(2)}) copy-start(bf16[128,4096]{1,0:T(8,128)(2,1)} %grad_out.1) | copy-start | bytes 3145732
  11.3 7.8 %collective-permute-start.5 = (bf16[1024,128]{1,0:T(8,128)(2,1)S(1)}, bf16[1024,128]{1,0:T(8,128)(2,1)S(1)}, u32[]{:S(2)}, u32[]{:S(2)}) collective-permute-start(bf16[1024,128]{1,0:T(8,128)(2,1)S(1)} %get-tuple-element.54), channel_id=1, source_target_pairs={{0,4},{4,0},{1,5},{5,1},{2,6},{6,2},{3,7},{7,3},{8,12},{12,8},{9,1... | collective-permute-start | bytes 786440 | tf_op jit(solution)/shard_map/ppermute | solution.py:55
  13.2 9.3 %collective-permute-start.4 = (bf16[512,128]{1,0:T(8,128)(2,1)S(1)}, bf16[512,128]{1,0:T(8,128)(2,1)S(1)}, u32[]{:S(2)}, u32[]{:S(2)}) collective-permute-start(bf16[512,128]{1,0:T(8,128)(2,1)S(1)} %get-tuple-element.51), channel_id=1, source_target_pairs={{0,16},{8,24},{16,0},{24,8},{1,17},{9,25},{17,1},{25,9},{2,18},{10... | collective-permute-start | bytes 393224 | tf_op jit(solution)/shard_map/ppermute | solution.py:393
  16.5 5.9 %collective-permute-start.1 = (bf16[272,128]{1,0:T(8,128)(2,1)S(1)}, bf16[272,128]{1,0:T(8,128)(2,1)S(1)}, u32[]{:S(2)}, u32[]{:S(2)}) collective-permute-start(bf16[272,128]{1,0:T(8,128)(2,1)S(1)} %get-tuple-element.45), channel_id=1, source_target_pairs={{0,3},{1,2},{2,1},{3,0},{4,7},{5,6},{6,5},{7,4},{8,11},{9,10},{10,... | collective-permute-start | bytes 208904 | tf_op jit(solution)/shard_map/ppermute | solution.py:55
  16.6 6.0 %collective-permute-start.2 = (bf16[272,128]{1,0:T(8,128)(2,1)S(1)}, bf16[272,128]{1,0:T(8,128)(2,1)S(1)}, u32[]{:S(2)}, u32[]{:S(2)}) collective-permute-start(bf16[272,128]{1,0:T(8,128)(2,1)S(1)} %get-tuple-element.46), channel_id=1, source_target_pairs={{0,2},{1,3},{2,0},{3,1},{4,6},{5,7},{6,4},{7,5},{8,10},{9,11},{10,... | collective-permute-start | bytes 208904 | tf_op jit(solution)/shard_map/ppermute | solution.py:55
  18.2 4.4 %collective-permute-start.3 = (bf16[272,128]{1,0:T(8,128)(2,1)S(1)}, bf16[272,128]{1,0:T(8,128)(2,1)S(1)}, u32[]{:S(2)}, u32[]{:S(2)}) collective-permute-start(bf16[272,128]{1,0:T(8,128)(2,1)S(1)} %get-tuple-element.47), channel_id=1, source_target_pairs={{0,1},{1,0},{2,3},{3,2},{4,5},{5,4},{6,7},{7,6},{8,9},{9,8},{10,11... | collective-permute-start | bytes 208904 | tf_op jit(solution)/shard_map/ppermute | solution.py:55
  19.8 7.1 %collective-permute-start.6 = (bf16[272,128]{1,0:T(8,128)(2,1)S(1)}, bf16[272,128]{1,0:T(8,128)(2,1)S(1)}, u32[]{:S(2)}, u32[]{:S(2)}) collective-permute-start(bf16[272,128]{1,0:T(8,128)(2,1)S(1)} %get-tuple-element.60), channel_id=1, source_target_pairs={{0,16},{8,24},{16,0},{24,8},{1,17},{9,25},{17,1},{25,9},{2,18},{10... | collective-permute-start | bytes 208904 | tf_op jit(solution)/shard_map/ppermute | solution.py:55
  22.6 7.8 %collective-permute-start.8 = (bf16[512,128]{1,0:T(8,128)(2,1)S(1)}, bf16[512,128]{1,0:T(8,128)(2,1)S(1)}, u32[]{:S(2)}, u32[]{:S(2)}) collective-permute-start(bf16[512,128]{1,0:T(8,128)(2,1)S(1)} %get-tuple-element.62), channel_id=1, source_target_pairs={{0,8},{8,0},{16,24},{24,16},{1,9},{9,1},{17,25},{25,17},{2,10},{10... | collective-permute-start | bytes 393224 | tf_op jit(solution)/shard_map/ppermute | solution.py:55
  24.2 6.1 %collective-permute-start.7 = (bf16[272,128]{1,0:T(8,128)(2,1)S(1)}, bf16[272,128]{1,0:T(8,128)(2,1)S(1)}, u32[]{:S(2)}, u32[]{:S(2)}) collective-permute-start(bf16[272,128]{1,0:T(8,128)(2,1)S(1)} %get-tuple-element.61), channel_id=1, source_target_pairs={{0,24},{8,16},{16,8},{24,0},{1,25},{9,17},{17,9},{25,1},{2,26},{10... | collective-permute-start | bytes 208904 | tf_op jit(solution)/shard_map/ppermute | solution.py:55
  25.3 5.1 %collective-permute-start.9 = (bf16[256,128]{1,0:T(8,128)(2,1)S(1)}, bf16[256,128]{1,0:T(8,128)(2,1)S(1)}, u32[]{:S(2)}, u32[]{:S(2)}) collective-permute-start(bf16[256,128]{1,0:T(8,128)(2,1)S(1)} %get-tuple-element.66), channel_id=1, source_target_pairs={{0,3},{1,2},{2,1},{3,0},{4,7},{5,6},{6,5},{7,4},{8,11},{9,10},{10,... | collective-permute-start | bytes 196616 | tf_op jit(solution)/shard_map/ppermute | solution.py:55
  25.5 5.6 %collective-permute-start.10 = (bf16[256,128]{1,0:T(8,128)(2,1)S(1)}, bf16[256,128]{1,0:T(8,128)(2,1)S(1)}, u32[]{:S(2)}, u32[]{:S(2)}) collective-permute-start(bf16[256,128]{1,0:T(8,128)(2,1)S(1)} %get-tuple-element.67), channel_id=1, source_target_pairs={{0,2},{1,3},{2,0},{3,1},{4,6},{5,7},{6,4},{7,5},{8,10},{9,11},{10,... | collective-permute-start | bytes 196616 | tf_op jit(solution)/shard_map/ppermute | solution.py:55
  26.8 4.2 %collective-permute-start.11 = (bf16[256,128]{1,0:T(8,128)(2,1)S(1)}, bf16[256,128]{1,0:T(8,128)(2,1)S(1)}, u32[]{:S(2)}, u32[]{:S(2)}) collective-permute-start(bf16[256,128]{1,0:T(8,128)(2,1)S(1)} %get-tuple-element.68), channel_id=1, source_target_pairs={{0,1},{1,0},{2,3},{3,2},{4,5},{5,4},{6,7},{7,6},{8,9},{9,8},{10,11... | collective-permute-start | bytes 196616 | tf_op jit(solution)/shard_map/ppermute | solution.py:55

commit v20 on v15

--- a/solution.py
+++ b/solution.py
@@ -400,7 +400,7 @@
         out_specs=(VMEM,) * (1 + n_col),
         scratch_shapes=[pltpu.VMEM((slots, rows, blk), f32)],
     )(tab, row, active, hid, w2)
-    o_parts = [send(o_sent[d], "col", d) for d in near_last(n_col)]
+    o_parts = [send(o_sent[d], "col", d) for d in [0] + near_last(n_col)[-2:0:-1] + [1][: n_col - 1]]
 
     sent = call(
         functools.partial(back_kernel, dims),
@@ -452,7 +452,7 @@
         in_specs=[ANY] + [VMEM] * len([*sums, *o_parts, *i_parts]),
         out_specs=(HBM,) * 3,
         scratch_shapes=[pltpu.VMEM(result.shape, bf16), acc, pltpu.SemaphoreType.DMA((3,))],
-    )(last, *sums, *o_parts, *i_parts)
+    )(last, *sums, o_parts[0], *o_parts[-2:0:-1], *o_parts[1:][-1:], *i_parts)
     return (output, grad_in, gw1.reshape(1, 1, slots, part, blk), gw2.reshape(1, 1, slots, part, blk))
 
 

time: 32.1 us -> 32.1 us (level)
  waiting for transfers between devices: 3.69 us -> 4.12 us
  starting transfers between devices: 16.3 us -> 15.9 us
    ppermute x11, waiting for transfers between devices: 3.69 us -> 4.11 us  [send(): lax.ppermute(x, axis, [(i, partner(i, d, n)) for i in range(n)])]
    ppermute x11, starting transfers between devices: 13.4 us -> 13 us  [send(): lax.ppermute(x, axis, [(i, partner(i, d, n)) for i in range(n)])]
  transfers between devices with their start and end apart: 12 -> 12, of which waited for: 4 -> 5; matrix products, arithmetic and copies ran while one was open for 0% -> 0% of each run, Pallas kernels for 20% -> 20%
where the time goes in v20:
time: 32.1 us; the launch traced here: 31.9 us
  starting transfers between devices  15.9 us (50%)
  Pallas kernels  9.86 us (31%)
  waiting for transfers between devices  4.12 us (13%)
  local copies, waits for them, and re-layouts  1.26 us (4%)
  between operations  0.8 us (2%)
    ppermute x11, starting transfers between devices, send(): lax.ppermute(x, axis, [(i, partner(i, d, n)) for i in range(n)])  13 us
    ppermute x11, waiting for transfers between devices, send(): lax.ppermute(x, axis, [(i, partner(i, d, n)) for i in range(n)])  4.11 us
    pallas_call x1, Pallas kernels, shards(): call(cotangent_kernel, 'take_cotangent', out_shape=(S((slots * rows, blk)...  3.96 us
    ppermute x1, starting transfers between devices, shards(): lax.ppermute(half, 'tok', [(i, (i + side) % n_tok) for i in range(n_tok)])  2.91 us
    pallas_call x1, Pallas kernels, shards(): call(token_kernel, 'take_tokens', TAKE_LIMIT, out_shape=message, in_specs...  2.37 us
    unnamed x16, local copies, waits for them, and re-layouts  1.26 us
    pallas_call x1, Pallas kernels, shards(): call(functools.partial(input_kernel, dims), 'add_inputs', out_shape=(resu...  0.98 us
    pallas_call x1, Pallas kernels, shards(): call(functools.partial(output_kernel, dims), 'add_outputs', out_shape=(re...  0.96 us
  transfers between devices with their start and end apart: 12, of which 5 were waited for; matrix products, arithmetic and copies ran while one was open for 0% of the time, Pallas kernels for 20%

profile of v20, /device:TPU:0, one launch (start us, length us, event | category | flops | bytes accessed | tf_op | source)
XLA Modules:
  0.0 31.9 jit_solution(6310103813611290548)
XLA Ops:
  0.6 0.0 copy-start
  0.6 0.0 copy-start.1
  0.7 0.0 copy-start.2
  0.7 0.0 copy-start.7
  0.7 2.4 %take_tokens.1 = bf16[1040,128]{1,0:T(8,128)(2,1)} custom-call(s32[8]{0:T(128)} %bitcast.13, s32[8]{0:T(128)} %bitcast.15, s32[8]{0:T(128)} %bitcast.17, s32[8]{0:T(128)} %bitcast.19, bf16[128,4096]{1,0:T(8,128)(2,1)} %tokens.3, bf16[8,128,128]{2,1,0:T(8,128)(2,1)} %bitcast.8), custom_call_target="tpu_custom_call" | custom-call | flops 33554432 | bytes 524288 | tf_op jit(solution)/shard_map/take_tokens/pallas_call | solution.py:334
  3.0 0.0 copy-start.4
  3.1 0.0 copy-start.5
  3.1 0.0 copy-start.6
  3.1 3.0 %collective-permute-start = (bf16[1040,128]{1,0:T(8,128)(2,1)}, bf16[1040,128]{1,0:T(8,128)(2,1)S(1)}, u32[]{:S(2)}, u32[]{:S(2)}) collective-permute-start(bf16[1040,128]{1,0:T(8,128)(2,1)} %take_tokens.1), channel_id=1, source_target_pairs={{0,4},{4,0},{1,5},{5,1},{2,6},{6,2},{3,7},{7,3},{8,12},{12,8},{9,1... | collective-permute-start | bytes 798728 | tf_op jit(solution)/shard_map/ppermute | solution.py:55
  6.1 0.0 copy-done
  6.1 0.0 copy-done.1
  6.1 0.0 copy-done.2
  6.1 0.0 copy-done.7
  6.1 0.0 copy-done.4
  6.1 0.0 copy-done.5
  6.1 0.0 copy-done.6
  6.1 0.0 copy-start.3
  6.1 1.2 %copy-done.3 = bf16[128,4096]{1,0:T(8,128)(2,1)S(1)} copy-done((bf16[128,4096]{1,0:T(8,128)(2,1)S(1)}, bf16[128,4096]{1,0:T(8,128)(2,1)}, u32[]{:S(2)}) %copy-start.3) | copy-done | bytes 1048600
  7.4 4.0 %take_cotangent.1 = (bf16[1024,128]{1,0:T(8,128)(2,1)S(1)}, bf16[8,128,128]{2,1,0:T(8,128)(2,1)S(1)}, bf16[8,128,128]{2,1,0:T(8,128)(2,1)S(1)}, f32[16,128,128]{...) custom-call(s32[8]{0:T(128)S(1)} %bitcast.14, s32[8]{0:T(128)S(1)} %bitcast.16, ...), custom_call_target="tpu_custom_call" | custom-call | flops 33554432 | bytes 524288 | tf_op jit(solution)/shard_map/take_cotangent/pallas_call | solution.py:351
  11.3 0.6 %collective-permute-start.5 = (bf16[1024,128]{1,0:T(8,128)(2,1)S(1)}, bf16[1024,128]{1,0:T(8,128)(2,1)S(1)}, u32[]{:S(2)}, u32[]{:S(2)}) collective-permute-start(bf16[1024,128]{1,0:T(8,128)(2,1)S(1)} %get-tuple-element.54), channel_id=1, source_target_pairs={{0,4},{4,0},{1,5},{5,1},{2,6},{6,2},{3,7},{7,3},{8,12},{12,8},{9,1... | collective-permute-start | bytes 786440 | tf_op jit(solution)/shard_map/ppermute | solution.py:55
  11.9 0.8 %collective-permute-done.refs_0_ = bf16[1040,128]{1,0:T(8,128)(2,1)S(1)} collective-permute-done((bf16[1040,128]{1,0:T(8,128)(2,1)}, bf16[1040,128]{1,0:T(8,128)(2,1)S(1)}, u32[]{:S(2)}, u32[]{:S(2)}) %collective-permute-start) | collective-permute-done | bytes 266272 | tf_op jit(solution)/shard_map/ppermute | solution.py:55
  12.7 0.5 %hidden.1 = (bf16[8,128,128]{2,1,0:T(8,128)(2,1)S(1)}, f32[16,128,128]{2,1,0:T(8,128)S(1)}, s32[8,128]{1,0:T(8,128)S(1)}, f32[8,128,128]{2,1,0:T(8,128)S(1)}, bf16[512,128]{1,0:T(8,128)(2,1)S(1)}) custom-call(s32[24,128]{1,0:T(8,128)S(1)} %get-tuple-element.38.tab, f32[16,128,128]{2,1,0:T(8,128)S(1)} %get-tuple-element.40.own, ...), custom_call_target="tpu_custom_call" | custom-call | flops 33554432 | bytes 524288 | tf_op jit(solution)/shard_map/hidden/pallas_call | solution.py:379
  13.2 2.9 %collective-permute-start.4 = (bf16[512,128]{1,0:T(8,128)(2,1)S(1)}, bf16[512,128]{1,0:T(8,128)(2,1)S(1)}, u32[]{:S(2)}, u32[]{:S(2)}) collective-permute-start(bf16[512,128]{1,0:T(8,128)(2,1)S(1)} %get-tuple-element.51), channel_id=1, source_target_pairs={{0,16},{8,24},{16,0},{24,8},{1,17},{9,25},{17,1},{25,9},{2,18},{10... | collective-permute-start | bytes 393224 | tf_op jit(solution)/shard_map/ppermute | solution.py:393
  16.1 0.4 %slope.1 = (f32[8,128,128]{2,1,0:T(8,128)S(1)}, bf16[272,128]{1,0:T(8,128)(2,1)S(1)}, bf16[272,128]{1,0:T(8,128)(2,1)S(1)}, bf16[272,128]{1,0:T(8,128)(2,1)S(1)}, bf16[272,128]{1,0:T(8,128)(2,1)S(1)}) custom-call(s32[24,128]{1,0:T(8,128)S(1)} %get-tuple-element.38.tab, bf16[16,128]{1,0:T(8,128)(2,1)S(1)} %get-tuple-element.39.row, ...), custom_call_target="tpu_custom_call" | custom-call | flops 33554432 | bytes 524288 | tf_op jit(solution)/shard_map/slope/pallas_call | solution.py:395
  16.5 0.1 collective-permute-start.1
  16.6 1.6 %collective-permute-start.2 = (bf16[272,128]{1,0:T(8,128)(2,1)S(1)}, bf16[272,128]{1,0:T(8,128)(2,1)S(1)}, u32[]{:S(2)}, u32[]{:S(2)}) collective-permute-start(bf16[272,128]{1,0:T(8,128)(2,1)S(1)} %get-tuple-element.46), channel_id=1, source_target_pairs={{0,2},{1,3},{2,0},{3,1},{4,6},{5,7},{6,4},{7,5},{8,10},{9,11},{10,... | collective-permute-start | bytes 208904 | tf_op jit(solution)/shard_map/ppermute | solution.py:55
  18.2 0.3 collective-permute-start.3
  18.4 0.7 %collective-permute-done.5.refs_0_ = bf16[1024,128]{1,0:T(8,128)(2,1)S(1)} collective-permute-done((bf16[1024,128]{1,0:T(8,128)(2,1)S(1)}, bf16[1024,128]{1,0:T(8,128)(2,1)S(1)}, u32[]{:S(2)}, u32[]{:S(2)}) %collective-permute-start.5) | collective-permute-done | bytes 262176 | tf_op jit(solution)/shard_map/ppermute | solution.py:55
  19.2 0.6 %back.1 = (bf16[256,128]{1,0:T(8,128)(2,1)S(1)}, bf16[256,128]{1,0:T(8,128)(2,1)S(1)}, bf16[256,128]{1,0:T(8,128)(2,1)S(1)}, bf16[256,128]{1,0:T(8,128)(2,1)S(1)...) custom-call(s32[24,128]{1,0:T(8,128)S(1)} %get-tuple-element.38.tab,, ...), custom_call_target="tpu_custom_call" | custom-call | flops 33554432 | bytes 524288 | tf_op jit(solution)/shard_map/back/pallas_call | solution.py:405
  19.8 2.7 %collective-permute-start.6 = (bf16[272,128]{1,0:T(8,128)(2,1)S(1)}, bf16[272,128]{1,0:T(8,128)(2,1)S(1)}, u32[]{:S(2)}, u32[]{:S(2)}) collective-permute-start(bf16[272,128]{1,0:T(8,128)(2,1)S(1)} %get-tuple-element.60), channel_id=1, source_target_pairs={{0,16},{8,24},{16,0},{24,8},{1,17},{9,25},{17,1},{25,9},{2,18},{10... | collective-permute-start | bytes 208904 | tf_op jit(solution)/shard_map/ppermute | solution.py:55
  22.4 0.0 collective-permute-done.1.refs_1_.refs_2_
  22.4 0.1 collective-permute-done.2.refs_2_.refs_3_.refs_1_
  22.6 0.0 collective-permute-done.3.refs_3_.refs_4_
  22.6 0.0 collective-permute-done.4.half
  22.6 1.6 %collective-permute-start.8 = (bf16[512,128]{1,0:T(8,128)(2,1)S(1)}, bf16[512,128]{1,0:T(8,128)(2,1)S(1)}, u32[]{:S(2)}, u32[]{:S(2)}) collective-permute-start(bf16[512,128]{1,0:T(8,128)(2,1)S(1)} %get-tuple-element.62), channel_id=1, source_target_pairs={{0,8},{8,0},{16,24},{24,16},{1,9},{9,1},{17,25},{25,17},{2,10},{10... | collective-permute-start | bytes 393224 | tf_op jit(solution)/shard_map/ppermute | solution.py:55
  24.3 1.0 %collective-permute-start.7 = (bf16[272,128]{1,0:T(8,128)(2,1)S(1)}, bf16[272,128]{1,0:T(8,128)(2,1)S(1)}, u32[]{:S(2)}, u32[]{:S(2)}) collective-permute-start(bf16[272,128]{1,0:T(8,128)(2,1)S(1)} %get-tuple-element.61), channel_id=1, source_target_pairs={{0,24},{8,16},{16,8},{24,0},{1,25},{9,17},{17,9},{25,1},{2,26},{10... | collective-permute-start | bytes 208904 | tf_op jit(solution)/shard_map/ppermute | solution.py:55
  25.3 1.5 %collective-permute-start.9 = (bf16[256,128]{1,0:T(8,128)(2,1)S(1)}, bf16[256,128]{1,0:T(8,128)(2,1)S(1)}, u32[]{:S(2)}, u32[]{:S(2)}) collective-permute-start(bf16[256,128]{1,0:T(8,128)(2,1)S(1)} %get-tuple-element.66), channel_id=1, source_target_pairs={{0,2},{1,3},{2,0},{3,1},{4,6},{5,7},{6,4},{7,5},{8,10},{9,11},{10,... | collective-permute-start | bytes 196616 | tf_op jit(solution)/shard_map/ppermute | solution.py:55
  26.8 0.0 collective-permute-start.10
  26.8 0.0 collective-permute-done.6.refs_1_
  26.8 0.6 %collective-permute-start.11 = (bf16[256,128]{1,0:T(8,128)(2,1)S(1)}, bf16[256,128]{1,0:T(8,128)(2,1)S(1)}, u32[]{:S(2)}, u32[]{:S(2)}) collective-permute-start(bf16[256,128]{1,0:T(8,128)(2,1)S(1)} %get-tuple-element.68), channel_id=1, source_target_pairs={{0,1},{1,0},{2,3},{3,2},{4,5},{5,4},{6,7},{7,6},{8,9},{9,8},{10,11... | collective-permute-start | bytes 196616 | tf_op jit(solution)/shard_map/ppermute | solution.py:55
  27.4 1.0 %add_outputs.1 = (bf16[32,4096]{1,0:T(8,128)(2,1)}, s32[8,128]{1,0:T(8,128)S(1)}) custom-call(bf16[272,128]{1,0:T(8,128)(2,1)S(1)} %get-tuple-element.44.refs_0_, bf16[272,128]{1,0:T(8,128)(2,1)S(1)} %collective-permute-done.1.refs_1_.refs_2_, bf16[272,128]{1,0:T(8,128)(2,1)S(1)} %collective-permute-done.2.refs_2_.refs_3_.refs_1_, ...), custom_call_target="tpu_custom_call" | custom-call | flops 33554432 | bytes 524288 | tf_op jit(solution)/shard_map/add_outputs/pallas_call | solution.py:440
  28.4 2.0 %collective-permute-done.7.refs_2_ = bf16[272,128]{1,0:T(8,128)(2,1)S(1)} collective-permute-done((bf16[272,128]{1,0:T(8,128)(2,1)S(1)}, bf16[272,128]{1,0:T(8,128)(2,1)S(1)}, u32[]{:S(2)}, u32[]{:S(2)}) %collective-permute-start.7) | collective-permute-done | bytes 69664 | tf_op jit(solution)/shard_map/ppermute | solution.py:55
  30.4 0.0 collective-permute-done.8.refs_3_
  30.4 0.1 add_grads.1
  30.4 0.0 collective-permute-done.9.refs_5_
  30.4 0.5 %collective-permute-done.10.refs_6_ = bf16[256,128]{1,0:T(8,128)(2,1)S(1)} collective-permute-done((bf16[256,128]{1,0:T(8,128)(2,1)S(1)}, bf16[256,128]{1,0:T(8,128)(2,1)S(1)}, u32[]{:S(2)}, u32[]{:S(2)}) %collective-permute-start.10) | collective-permute-done | bytes 65568 | tf_op jit(solution)/shard_map/ppermute | solution.py:55
  31.0 0.0 collective-permute-done.11.refs_7_
  31.0 1.0 %add_inputs.1 = (bf16[32,4096]{1,0:T(8,128)(2,1)}, f32[8,32,128]{2,1,0:T(8,128)}, f32[8,32,128]{2,1,0:T(8,128)}) custom-call(s32[8,128]{1,0:T(8,128)S(1)} %get-tuple-element.49.after, f32[8,32,128]{2,1,0:T(8,128)S(1)} %get-tuple-element.63.sum1, f32[8,32,128]{2,1,0:T(8,128)S(1)} %get-tuple-element.64.sum2, bf16[272,128]{1,0:T(8,128)(2,1)S(1)} %get-tuple-element.44.refs_0_, ...), custom_call_target="tpu_custom_call" | custom-call | flops 33554432 | bytes 524288 | tf_op jit(solution)/shard_map/add_inputs/pallas_call | solution.py:448
  (1 shorter events, 0.0 us)
Async XLA Ops:
  0.6 5.5 %copy-start = (bf16[128,4096]{1,0:T(8,128)(2,1)S(1)}, bf16[128,4096]{1,0:T(8,128)(2,1)}, u32[]{:S(2)}) copy-start(bf16[128,4096]{1,0:T(8,128)(2,1)} %tokens.3) | copy-start | bytes 3145732
  0.6 5.5 %copy-start.1 = (bf16[1,1,8,128,128]{4,3,2,1,0:T(8,128)(2,1)S(1)}, bf16[1,1,8,128,128]{4,3,2,1,0:T(8,128)(2,1)}, u32[]{:S(2)}) copy-start(bf16[1,1,8,128,128]{4,3,2,1,0:T(8,128)(2,1)} %param.9) | copy-start | bytes 786436
  0.7 5.4 %copy-start.2 = (bf16[1,1,8,128,128]{4,3,2,1,0:T(8,128)(2,1)S(1)}, bf16[1,1,8,128,128]{4,3,2,1,0:T(8,128)(2,1)}, u32[]{:S(2)}) copy-start(bf16[1,1,8,128,128]{4,3,2,1,0:T(8,128)(2,1)} %param.12) | copy-start | bytes 786436
  0.7 5.4 %copy-start.7 = (s32[1,1,8]{2,1,0:T(1,128)S(1)}, s32[1,1,8]{2,1,0:T(1,128)}, u32[]{:S(2)}) copy-start(s32[1,1,8]{2,1,0:T(1,128)} %param.14) | copy-start | bytes 100
  3.0 3.1 %copy-start.4 = (s32[1,1,8]{2,1,0:T(1,128)S(1)}, s32[1,1,8]{2,1,0:T(1,128)}, u32[]{:S(2)}) copy-start(s32[1,1,8]{2,1,0:T(1,128)} %param.10) | copy-start | bytes 100
  3.1 3.1 %copy-start.5 = (s32[1,1,8]{2,1,0:T(1,128)S(1)}, s32[1,1,8]{2,1,0:T(1,128)}, u32[]{:S(2)}) copy-start(s32[1,1,8]{2,1,0:T(1,128)} %param.11) | copy-start | bytes 100
  3.1 3.1 %copy-start.6 = (s32[1,1,8]{2,1,0:T(1,128)S(1)}, s32[1,1,8]{2,1,0:T(1,128)}, u32[]{:S(2)}) copy-start(s32[1,1,8]{2,1,0:T(1,128)} %param.13) | copy-start | bytes 100
  3.1 9.6 %collective-permute-start = (bf16[1040,128]{1,0:T(8,128)(2,1)}, bf16[1040,128]{1,0:T(8,128)(2,1)S(1)}, u32[]{:S(2)}, u32[]{:S(2)}) collective-permute-start(bf16[1040,128]{1,0:T(8,128)(2,1)} %take_tokens.1), channel_id=1, source_target_pairs={{0,4},{4,0},{1,5},{5,1},{2,6},{6,2},{3,7},{7,3},{8,12},{12,8},{9,1... | collective-permute-start | bytes 798728 | tf_op jit(solution)/shard_map/ppermute | solution.py:55
  6.1 1.2 %copy-start.3 = (bf16[128,4096]{1,0:T(8,128)(2,1)S(1)}, bf16[128,4096]{1,0:T(8,128)(2,1)}, u32[]{:S(2)}) copy-start(bf16[128,4096]{1,0:T(8,128)(2,1)} %grad_out.1) | copy-start | bytes 3145732
  11.3 7.8 %collective-permute-start.5 = (bf16[1024,128]{1,0:T(8,128)(2,1)S(1)}, bf16[1024,128]{1,0:T(8,128)(2,1)S(1)}, u32[]{:S(2)}, u32[]{:S(2)}) collective-permute-start(bf16[1024,128]{1,0:T(8,128)(2,1)S(1)} %get-tuple-element.54), channel_id=1, source_target_pairs={{0,4},{4,0},{1,5},{5,1},{2,6},{6,2},{3,7},{7,3},{8,12},{12,8},{9,1... | collective-permute-start | bytes 786440 | tf_op jit(solution)/shard_map/ppermute | solution.py:55
  13.2 9.3 %collective-permute-start.4 = (bf16[512,128]{1,0:T(8,128)(2,1)S(1)}, bf16[512,128]{1,0:T(8,128)(2,1)S(1)}, u32[]{:S(2)}, u32[]{:S(2)}) collective-permute-start(bf16[512,128]{1,0:T(8,128)(2,1)S(1)} %get-tuple-element.51), channel_id=1, source_target_pairs={{0,16},{8,24},{16,0},{24,8},{1,17},{9,25},{17,1},{25,9},{2,18},{10... | collective-permute-start | bytes 393224 | tf_op jit(solution)/shard_map/ppermute | solution.py:393
  16.5 5.9 %collective-permute-start.1 = (bf16[272,128]{1,0:T(8,128)(2,1)S(1)}, bf16[272,128]{1,0:T(8,128)(2,1)S(1)}, u32[]{:S(2)}, u32[]{:S(2)}) collective-permute-start(bf16[272,128]{1,0:T(8,128)(2,1)S(1)} %get-tuple-element.45), channel_id=1, source_target_pairs={{0,3},{1,2},{2,1},{3,0},{4,7},{5,6},{6,5},{7,4},{8,11},{9,10},{10,... | collective-permute-start | bytes 208904 | tf_op jit(solution)/shard_map/ppermute | solution.py:55
  16.6 6.0 %collective-permute-start.2 = (bf16[272,128]{1,0:T(8,128)(2,1)S(1)}, bf16[272,128]{1,0:T(8,128)(2,1)S(1)}, u32[]{:S(2)}, u32[]{:S(2)}) collective-permute-start(bf16[272,128]{1,0:T(8,128)(2,1)S(1)} %get-tuple-element.46), channel_id=1, source_target_pairs={{0,2},{1,3},{2,0},{3,1},{4,6},{5,7},{6,4},{7,5},{8,10},{9,11},{10,... | collective-permute-start | bytes 208904 | tf_op jit(solution)/shard_map/ppermute | solution.py:55
  18.2 4.4 %collective-permute-start.3 = (bf16[272,128]{1,0:T(8,128)(2,1)S(1)}, bf16[272,128]{1,0:T(8,128)(2,1)S(1)}, u32[]{:S(2)}, u32[]{:S(2)}) collective-permute-start(bf16[272,128]{1,0:T(8,128)(2,1)S(1)} %get-tuple-element.47), channel_id=1, source_target_pairs={{0,1},{1,0},{2,3},{3,2},{4,5},{5,4},{6,7},{7,6},{8,9},{9,8},{10,11... | collective-permute-start | bytes 208904 | tf_op jit(solution)/shard_map/ppermute | solution.py:55
  19.8 7.0 %collective-permute-start.6 = (bf16[272,128]{1,0:T(8,128)(2,1)S(1)}, bf16[272,128]{1,0:T(8,128)(2,1)S(1)}, u32[]{:S(2)}, u32[]{:S(2)}) collective-permute-start(bf16[272,128]{1,0:T(8,128)(2,1)S(1)} %get-tuple-element.60), channel_id=1, source_target_pairs={{0,16},{8,24},{16,0},{24,8},{1,17},{9,25},{17,1},{25,9},{2,18},{10... | collective-permute-start | bytes 208904 | tf_op jit(solution)/shard_map/ppermute | solution.py:55
  22.6 7.8 %collective-permute-start.8 = (bf16[512,128]{1,0:T(8,128)(2,1)S(1)}, bf16[512,128]{1,0:T(8,128)(2,1)S(1)}, u32[]{:S(2)}, u32[]{:S(2)}) collective-permute-start(bf16[512,128]{1,0:T(8,128)(2,1)S(1)} %get-tuple-element.62), channel_id=1, source_target_pairs={{0,8},{8,0},{16,24},{24,16},{1,9},{9,1},{17,25},{25,17},{2,10},{10... | collective-permute-start | bytes 393224 | tf_op jit(solution)/shard_map/ppermute | solution.py:55
  24.3 6.1 %collective-permute-start.7 = (bf16[272,128]{1,0:T(8,128)(2,1)S(1)}, bf16[272,128]{1,0:T(8,128)(2,1)S(1)}, u32[]{:S(2)}, u32[]{:S(2)}) collective-permute-start(bf16[272,128]{1,0:T(8,128)(2,1)S(1)} %get-tuple-element.61), channel_id=1, source_target_pairs={{0,24},{8,16},{16,8},{24,0},{1,25},{9,17},{17,9},{25,1},{2,26},{10... | collective-permute-start | bytes 208904 | tf_op jit(solution)/shard_map/ppermute | solution.py:55
  25.3 5.1 %collective-permute-start.9 = (bf16[256,128]{1,0:T(8,128)(2,1)S(1)}, bf16[256,128]{1,0:T(8,128)(2,1)S(1)}, u32[]{:S(2)}, u32[]{:S(2)}) collective-permute-start(bf16[256,128]{1,0:T(8,128)(2,1)S(1)} %get-tuple-element.66), channel_id=1, source_target_pairs={{0,2},{1,3},{2,0},{3,1},{4,6},{5,7},{6,4},{7,5},{8,10},{9,11},{10,... | collective-permute-start | bytes 196616 | tf_op jit(solution)/shard_map/ppermute | solution.py:55
  26.8 4.2 %collective-permute-start.10 = (bf16[256,128]{1,0:T(8,128)(2,1)S(1)}, bf16[256,128]{1,0:T(8,128)(2,1)S(1)}, u32[]{:S(2)}, u32[]{:S(2)}) collective-permute-start(bf16[256,128]{1,0:T(8,128)(2,1)S(1)} %get-tuple-element.67), channel_id=1, source_target_pairs={{0,3},{1,2},{2,1},{3,0},{4,7},{5,6},{6,5},{7,4},{8,11},{9,10},{10,... | collective-permute-start | bytes 196616 | tf_op jit(solution)/shard_map/ppermute | solution.py:55
  26.8 4.2 %collective-permute-start.11 = (bf16[256,128]{1,0:T(8,128)(2,1)S(1)}, bf16[256,128]{1,0:T(8,128)(2,1)S(1)}, u32[]{:S(2)}, u32[]{:S(2)}) collective-permute-start(bf16[256,128]{1,0:T(8,128)(2,1)S(1)} %get-tuple-element.68), channel_id=1, source_target_pairs={{0,1},{1,0},{2,3},{3,2},{4,5},{5,4},{6,7},{7,6},{8,9},{9,8},{10,11... | collective-permute-start | bytes 196616 | tf_op jit(solution)/shard_map/ppermute | solution.py:55
